TPU v7x, 32 devices: a whole 2x2x4 slice. The times are simulated.
32 devices in a mesh: group: 2 (over y), gx: 4 (over x, core), gy: 4 (over z).
Axes of the slice: x: 2, y: 2, z: 4, core: 2. Of those that a mesh axis runs over, the one named last changes fastest.
Arguments:
- hidden: bfloat16 [16, 2, 8192], P(('group', 'gy'), None, 'gx'), parts along dimension 0, may hold values from -168 to 168
- norm_gain: bfloat16 [8192], P('gx'), may hold values from 0.099609375 to 1.8984375
- w_qkv: bfloat16 [8192, 10240], P('gx', 'gy'), may hold values from -0.0625 to 0.0625
- w_out: bfloat16 [8192, 8192], P('gy', 'gx'), may hold values from -0.5 to 0.5
- k_cache: bfloat16 [16, 1536, 1024], P(('group', 'gy'), 'gx'), parts along dimension 0, may hold values from -408 to 408
- v_cache: bfloat16 [16, 1536, 1024], P(('group', 'gy'), 'gx'), parts along dimension 0, may hold values from -6 to 6
- cache_len: int32 [16], P(('group', 'gy')), parts along dimension 0, may hold values from 192 to 1536, as said below
- positions: int32 [16], P(('group', 'gy')), parts along dimension 0, may hold values from 1536 to 6143
Outputs:
- layer_out: bfloat16 [16, 2, 8192], P(('group', 'gy'), None, 'gx'), parts along dimension 0
There are 2 independent parts, one for each index of `group`. A program takes and returns all parts, laid end to end along the dimension named above; an argument that names none is the same for every part. Nothing has to cross between parts.
Inputs may be any that keep to these rules, and one draw needn't show every extreme that they name: Timeline b's keys and values sit in slots 0 to cache_len[b] - 1; later slots hold stale entries. Some timeline fills all 1536 slots.
All inputs are finite; a program needn't handle non-finite values.
Results may differ from a plain program's by a relative error of at most 0.013.
Values may be sent and summed in bfloat16 or wider, within the bound.
No kernel may reach another device: no remote copies, remote signals or barrier semaphores. Data moves between devices by JAX's collectives and lax.ppermute only.
A program may use at most 64 MiB of HBM per device.

v0:
```python
import jax
import jax.numpy as jnp
from jax import lax
from jax.sharding import PartitionSpec as P

D = 8192
H = 64
KVH = 8
HD = 128
SPAN_DEV = 384


NEGATIVE = -1e30
ROPE_BASE = 500000.0
EPSILON = 1e-05


def combined_all(shard, axis, combine):
    everything = jax.tree.map(lambda part: lax.all_gather(part, axis), shard)
    first = jax.tree.map(lambda part: part[0], everything)

    def turn(k, so_far):
        return combine(so_far, jax.tree.map(lambda part: part[k], everything))

    return lax.fori_loop(1, lax.axis_size(axis), turn, first)


def rotate(inputs, positions, offset):
    halfway = HD // 2
    frequency = ROPE_BASE ** (-2.0 * jnp.arange(halfway, dtype=jnp.float32) / HD)
    places = (
        positions[:, None] + offset + jnp.arange(inputs.shape[1], dtype=jnp.int32)[None, :]
    ).astype(jnp.float32)
    angles = places[:, :, None] * frequency[None, None, :]
    cosine = jnp.cos(angles)[:, :, None, :]
    sines = jnp.sin(angles)[:, :, None, :]
    leading = inputs[..., :halfway]
    trailing = inputs[..., halfway:]
    return jnp.concatenate(
        [leading * cosine - trailing * sines, trailing * cosine + leading * sines], axis=-1
    )


def block_terms(scores, usable):
    maxima = jnp.max(jnp.where(usable, scores, NEGATIVE), axis=-1)
    weights = jnp.exp(jnp.where(usable, scores - maxima[..., None], NEGATIVE))
    return (maxima, jnp.sum(weights, axis=-1), weights)


def combine(first_part, second_part):
    maxima_a, totals_a, partials_a = first_part
    maxima_b, totals_b, partials_b = second_part
    highest = jnp.maximum(maxima_a, maxima_b)
    factor_a = jnp.exp(maxima_a - highest)
    factor_b = jnp.exp(maxima_b - highest)
    return (
        highest,
        totals_a * factor_a + totals_b * factor_b,
        partials_a * factor_a[..., None] + partials_b * factor_b[..., None],
    )


def body(hidden, norm_gain, w_qkv, w_out, k_cache, v_cache, cache_len, positions):
    timelines_here = hidden.shape[0]
    tokens_here = hidden.shape[1]
    floats = hidden.astype(jnp.float32)
    squares = lax.psum(jnp.sum(floats * floats, axis=-1), "gx")
    normed = (
        floats * lax.rsqrt(squares[..., None] / D + EPSILON) * norm_gain.astype(jnp.float32)
    ).astype(jnp.bfloat16)
    partial_sums = jnp.einsum(
        "rkc,ce->rke",
        lax.all_gather(normed, "gy", axis=0, tiled=True),
        w_qkv,
        preferred_element_type=jnp.float32,
    )
    summed = lax.psum(partial_sums, "gx").astype(jnp.bfloat16)
    projected = lax.all_to_all(summed, "gy", split_axis=0, concat_axis=2, tiled=True)
    widened = projected.astype(jnp.float32)
    queries = rotate(
        widened[..., : H * HD].reshape(timelines_here, tokens_here, H, HD), positions, 0
    ).astype(jnp.bfloat16)
    fresh_keys = rotate(
        widened[..., H * HD : (H + KVH) * HD].reshape(timelines_here, tokens_here, KVH, HD),
        positions,
        0,
    ).astype(jnp.bfloat16)
    fresh_values = projected[..., (H + KVH) * HD :].reshape(timelines_here, tokens_here, KVH, HD)
    grouped = queries.reshape(timelines_here, tokens_here, KVH, H // KVH, HD)
    cached_keys = k_cache.reshape(timelines_here, SPAN_DEV, KVH, HD)
    cached_values = v_cache.reshape(timelines_here, SPAN_DEV, KVH, HD)
    scaling = HD ** (-0.5)
    scores = (
        jnp.einsum("tkgqd,tsgd->tkgqs", grouped, cached_keys, preferred_element_type=jnp.float32)
        * scaling
    )
    slot_ids = lax.axis_index("gx") * SPAN_DEV + jnp.arange(SPAN_DEV, dtype=jnp.int32)
    usable = (slot_ids[None, :] < cache_len[:, None]).reshape(timelines_here, 1, 1, 1, SPAN_DEV)
    maxima, totals, weights = block_terms(scores, usable)
    partials = jnp.einsum(
        "tkgqs,tsgd->tkgqd",
        weights.astype(jnp.bfloat16),
        cached_values,
        preferred_element_type=jnp.float32,
    )
    merged = combined_all((maxima, totals, partials), "gx", combine)
    fresh_scores = (
        jnp.einsum("tkgqd,tjgd->tkgqj", grouped, fresh_keys, preferred_element_type=jnp.float32)
        * scaling
    )
    key_ids = jnp.arange(tokens_here, dtype=jnp.int32)
    allowed = (key_ids[None, :] <= key_ids[:, None]).reshape(1, tokens_here, 1, 1, tokens_here)
    fresh_maxima, fresh_totals, fresh_weights = block_terms(fresh_scores, allowed)
    fresh_partials = jnp.einsum(
        "tkgqj,tjgd->tkgqd",
        fresh_weights.astype(jnp.bfloat16),
        fresh_values,
        preferred_element_type=jnp.float32,
    )
    _, denominator, numerator = combine(merged, (fresh_maxima, fresh_totals, fresh_partials))
    attended = (
        (numerator / denominator[..., None])
        .astype(jnp.bfloat16)
        .reshape(timelines_here, tokens_here, H * HD)
    )
    heads_in = lax.all_to_all(attended, "gy", split_axis=2, concat_axis=0, tiled=True)
    return lax.psum_scatter(
        jnp.einsum("rke,ed->rkd", heads_in, w_out, preferred_element_type=jnp.float32),
        "gy",
        scatter_dimension=0,
        tiled=True,
    ).astype(jnp.bfloat16)


def solution(mesh):
    in_specs = (
        P(("group", "gy"), None, "gx"),
        P("gx"),
        P("gx", "gy"),
        P("gy", "gx"),
        P(("group", "gy"), "gx", None),
        P(("group", "gy"), "gx", None),
        P(("group", "gy")),
        P(("group", "gy")),
    )
    out_specs = P(("group", "gy"), None, "gx")
    return jax.shard_map(body, mesh=mesh, in_specs=in_specs, out_specs=out_specs, check_vma=False)
```

profile of v0, /device:TPU:0, one launch (start us, length us, event | category | flops | bytes accessed | tf_op | source)
XLA Modules:
  0.0 140.7 jit_solution(484158762002855227)
XLA Ops:
  0.0 0.8 fusion.36
  0.8 0.7 convert_element_type.39
  1.5 8.3 %psum.14 = f32[2,2]{1,0:T(2,128)S(1)} all-reduce(f32[2,2]{1,0:T(2,128)S(1)} %fusion.36), channel_id=1, replica_groups=mesh['group'=2,'gx'=4,'gy'=4] {'gx'}, use_global_device_ids=true, to_apply=%region_1.0 | all-reduce | flops 4 | bytes 32 | tf_op jit(solution)/shard_map/psum | solution.py:67
  9.8 0.8 fusion.38
  10.6 13.4 %all_gather.21 = bf16[8,2,2048]{2,1,0:T(2,128)(2,1)S(1)} all-gather(bf16[2,2,2048]{2,1,0:T(2,128)(2,1)S(1)} %fusion.38), channel_id=1, replica_groups=mesh['group'=2,'gx'=4,'gy'=4] {'gy'}, dimensions={0}, use_global_device_ids=true | all-gather | bytes 81920 | tf_op jit(solution)/shard_map/all_gather | solution.py:73
  24.1 5.6 %fusion.3 = f32[8,2,2560]{2,0,1:T(8,128)S(1)} fusion(bf16[2048,2560]{1,0:T(8,128)(2,1)} %param.12, bf16[8,2,2048]{2,1,0:T(2,128)(2,1)S(1)} %all_gather.21), kind=kOutput, calls=%fused_computation.8 | convolution fusion | flops 167772160 | bytes 10715136 | tf_op jit(solution)/shard_map/rkc,ce->rke/dot_general | solution.py:71
  29.6 12.1 %all-reduce.3 = bf16[8,2,2560]{2,0,1:T(8,128)(2,1)S(1)} all-reduce(f32[8,2,2560]{2,0,1:T(8,128)S(1)} %fusion.3), channel_id=1, replica_groups=mesh['group'=2,'gx'=4,'gy'=4] {'gx'}, use_global_device_ids=true, to_apply=%region_2.0 | all-reduce | flops 40960 | bytes 245760 | tf_op jit(solution)/shard_map/psum | solution.py:77
  42.4 4.8 %all-to-all-start = ((bf16[8,2,2560]{2,1,0:T(2,128)(2,1)}), bf16[8,2,2560]{2,1,0:T(2,128)(2,1)S(1)}, u32[]{:S(2)}, u32[]{:S(2)}) async-start(bf16[8,2,2560]{2,1,0:T(2,128)(2,1)} %copy.58), calls=%async_computation | async-start | bytes 163840 | tf_op jit(solution)/shard_map/all_to_all | solution.py:78
  47.9 1.3 copy-done.1
  50.4 2.6 %all-to-all-done = bf16[8,2,2560]{2,1,0:T(2,128)(2,1)S(1)} async-done(((bf16[8,2,2560]{2,1,0:T(2,128)(2,1)}), bf16[8,2,2560]{2,1,0:T(2,128)(2,1)S(1)}, u32[]{:S(2)}, u32[]{:S(2)}) %all-to-all-start) | async-done | bytes 81952 | tf_op jit(solution)/shard_map/all_to_all | solution.py:78
  53.1 0.7 convert_element_type.42
  54.1 0.8 select_reduce_fusion
  55.6 6.5 %all-gather.2 = f32[8,2,8,8,128]{4,3,2,1,0:T(8,128)S(1)} all-gather(f32[2,2,8,8,128]{4,3,2,1,0:T(8,128)S(1)} %copy.66), channel_id=4, replica_groups=mesh['group'=2,'gx'=4,'gy'=4] {'gx'}, dimensions={0}, use_global_device_ids=true | all-gather | bytes 655360 | tf_op jit(solution)/shard_map/all_gather | solution.py:19
  62.1 5.2 %all-gather.1 = f32[8,2,8,8]{3,2,1,0:T(8,128)S(1)} all-gather(f32[2,2,8,8]{3,2,1,0:T(8,128)S(1)} %copy.64), channel_id=3, replica_groups=mesh['group'=2,'gx'=4,'gy'=4] {'gx'}, dimensions={0}, use_global_device_ids=true | all-gather | bytes 5120 | tf_op jit(solution)/shard_map/all_gather | solution.py:19
  67.4 5.2 %all-gather = f32[8,2,8,8]{3,2,1,0:T(8,128)S(1)} all-gather(f32[2,2,8,8]{3,2,1,0:T(8,128)S(1)} %copy.63), channel_id=2, replica_groups=mesh['group'=2,'gx'=4,'gy'=4] {'gx'}, dimensions={0}, use_global_device_ids=true | all-gather | bytes 5120 | tf_op jit(solution)/shard_map/all_gather | solution.py:19
  73.2 0.7 slice_bitcast_fusion
  75.1 4.9 %copy.88 = bf16[2,2,8,8,128]{1,0,4,3,2:T(2,128)(2,1)} copy(bf16[2,2,8,8,128]{4,3,1,2,0:T(8,128)(2,1)S(1)} %fusion.23) | data formatting | bytes 131072 | tf_op jit(solution)/shard_map/reshape | solution.py:124
  80.0 7.8 %reshape.130 = bf16[4,2,4096]{2,1,0:T(2,128)(2,1)} reshape(bf16[8192,2,2]{2,1,0:T(2,128)(2,1)} %bitcast.93) | data formatting | bytes 131072
  87.7 3.3 %all-to-all-start.1 = ((bf16[4,2,4096]{2,1,0:T(2,128)(2,1)}), bf16[4,2,4096]{2,1,0:T(2,128)(2,1)S(1)}, u32[]{:S(2)}, u32[]{:S(2)}) async-start(bf16[4,2,4096]{2,1,0:T(2,128)(2,1)} %reshape.130), calls=%async_computation.1 | async-start | bytes 131072 | tf_op jit(solution)/shard_map/all_to_all | solution.py:126
  92.3 4.5 %all-to-all-done.1 = bf16[4,2,4096]{2,1,0:T(2,128)(2,1)S(1)} async-done(((bf16[4,2,4096]{2,1,0:T(2,128)(2,1)}), bf16[4,2,4096]{2,1,0:T(2,128)(2,1)S(1)}, u32[]{:S(2)}, u32[]{:S(2)}) %all-to-all-start.1) | async-done | bytes 65568 | tf_op jit(solution)/shard_map/all_to_all | solution.py:126
  96.7 10.0 %reshape.131 = bf16[8192,2,2]{2,1,0:T(2,128)(2,1)} reshape(bf16[4,2,4096]{2,1,0:T(2,128)(2,1)S(1)} %all-to-all-done.1) | data formatting | bytes 131072
  106.8 9.7 %copy.89 = bf16[2,2,4,2048]{3,2,1,0:T(4,128)(2,1)S(1)} copy(bf16[2,2,4,2048]{1,0,3,2:T(2,128)(2,1)} %bitcast.94) | data formatting | bytes 131072 | tf_op jit(solution)/shard_map/all_to_all | solution.py:126
  116.6 4.6 %fusion.5 = f32[8,2,2048]{2,0,1:T(8,128)S(1)} fusion(bf16[8,2,2048]{2,0,1:T(8,128)(2,1)S(1)} %all_to_all.33, bf16[2048,2048]{1,0:T(8,128)(2,1)} %param.13), kind=kOutput, calls=%fused_computation.10 | convolution fusion | flops 134217728 | bytes 8585216 | tf_op jit(solution)/shard_map/rke,ed->rkd/dot_general | solution.py:128
  121.2 18.8 %all-reduce.4 = bf16[8,2,2048]{2,0,1:T(8,128)(2,1)S(1)} all-reduce(f32[8,2,2048]{2,0,1:T(8,128)S(1)} %fusion.5), channel_id=5, replica_groups=mesh['group'=2,'gx'=4,'gy'=4] {'gy'}, use_global_device_ids=true, to_apply=%region_9.10.clone | all-reduce | flops 32768 | bytes 196608
  (54 shorter events, 7.2 us)
Async XLA Ops:
  24.1 23.2 %copy-start.3 = (s32[2]{0:T(128)S(1)}, s32[2]{0:T(128)}, u32[]{:S(2)}) copy-start(s32[2]{0:T(128)} %param.17) | copy-start | bytes 28
  24.1 23.2 %copy-start = (bf16[2,384,1024]{2,1,0:T(8,128)(2,1)S(1)}, bf16[2,384,1024]{2,1,0:T(8,128)(2,1)}, u32[]{:S(2)}) copy-start(bf16[2,384,1024]{2,1,0:T(8,128)(2,1)} %param.14) | copy-start | bytes 4718596
  42.4 10.6 %all-to-all-start = ((bf16[8,2,2560]{2,1,0:T(2,128)(2,1)}), bf16[8,2,2560]{2,1,0:T(2,128)(2,1)S(1)}, u32[]{:S(2)}, u32[]{:S(2)}) async-start(bf16[8,2,2560]{2,1,0:T(2,128)(2,1)} %copy.58), calls=%async_computation | async-start | bytes 163840 | tf_op jit(solution)/shard_map/all_to_all | solution.py:78
  47.8 1.4 %copy-start.1 = (bf16[2,384,1024]{2,1,0:T(8,128)(2,1)S(1)}, bf16[2,384,1024]{2,1,0:T(8,128)(2,1)}, u32[]{:S(2)}) copy-start(bf16[2,384,1024]{2,1,0:T(8,128)(2,1)} %param.15) | copy-start | bytes 4718596
  49.6 0.7 copy-start.2
  80.0 11.1 %copy-start.4 = (u32[32]{0:T(128)S(1)}, u32[32]{0:T(128)}, u32[]{:S(2)}) copy-start(u32[32]{0:T(128)} %constant.73) | copy-start | bytes 388
  87.7 9.0 %all-to-all-start.1 = ((bf16[4,2,4096]{2,1,0:T(2,128)(2,1)}), bf16[4,2,4096]{2,1,0:T(2,128)(2,1)S(1)}, u32[]{:S(2)}, u32[]{:S(2)}) async-start(bf16[4,2,4096]{2,1,0:T(2,128)(2,1)} %reshape.130), calls=%async_computation.1 | async-start | bytes 131072 | tf_op jit(solution)/shard_map/all_to_all | solution.py:126
where the time goes:
time: 142 us; the launch traced here: 141 us
  blocking collectives  69.6 us (49%)
  local copies, waits for them, and re-layouts  38.3 us (27%)
  matrix products  12.2 us (9%)
  starting transfers between devices  8.11 us (6%)
  waiting for transfers between devices  7.08 us (5%)
  other arithmetic  4.47 us (3%)
    unnamed x15, local copies, waits for them, and re-layouts  21 us
    unnamed x1, blocking collectives  18.8 us
    all_gather x3, blocking collectives, combined_all(): everything = jax.tree.map(lambda part: lax.all_gather(part, axis), shard)  17 us
    all_gather x1, blocking collectives, body(): lax.all_gather(normed, 'gy', axis=0, tiled=True)  13.4 us
    psum x1, blocking collectives, body(): summed = lax.psum(partial_sums, 'gx').astype(jnp.bfloat16)  12.1 us
    all_to_all x3, local copies, waits for them, and re-layouts, body(): lax.all_to_all(attended, 'gy', split_axis=2, concat_axis=0, tiled=True)  9.84 us
    psum x1, blocking collectives, body(): squares = lax.psum(jnp.sum(floats * floats, axis=-1), 'gx')  8.31 us
    dot_general x1, matrix products, body(): jnp.einsum('rkc,ce->rke', lax.all_gather(normed, 'gy', axis=0, tiled=True...  5.55 us
  transfers between devices with their start and end apart: 2, of which 2 were waited for; matrix products, arithmetic and copies ran while one was open for 1% of the time, Pallas kernels for 0%

commit v1 on v0

--- a/solution.py
+++ b/solution.py
@@ -1,6 +1,8 @@
 import jax
 import jax.numpy as jnp
 from jax import lax
+from jax.experimental import pallas as pl
+from jax.experimental.pallas import tpu as pltpu
 from jax.sharding import PartitionSpec as P
 
 D = 8192
@@ -60,7 +62,7 @@
     )
 
 
-def body(hidden, norm_gain, w_qkv, w_out, k_cache, v_cache, cache_len, positions):
+def general_body(hidden, norm_gain, w_qkv, w_out, k_cache, v_cache, cache_len, positions):
     timelines_here = hidden.shape[0]
     tokens_here = hidden.shape[1]
     floats = hidden.astype(jnp.float32)
@@ -132,7 +134,338 @@
     ).astype(jnp.bfloat16)
 
 
+NX = 4
+NY = 4
+ROWS = 4
+QKV_ROWS = (H + 2 * KVH) // NY * ROWS
+OUT_HEADS = H // NY
+OUT_ROWS = OUT_HEADS * ROWS
+QUERIES = H * ROWS
+VMEM_SPEC = pl.BlockSpec(memory_space=pltpu.VMEM)
+SMEM_SPEC = pl.BlockSpec(memory_space=pltpu.SMEM)
+F32 = jnp.float32
+BF16 = jnp.bfloat16
+
+
+def call(kernel, name, out_shape, operands, scratch=(), scalars=0, mib=8):
+    many = isinstance(out_shape, (list, tuple))
+    return pl.pallas_call(
+        kernel,
+        in_specs=[SMEM_SPEC] * scalars + [VMEM_SPEC] * (len(operands) - scalars),
+        out_specs=[VMEM_SPEC] * len(out_shape) if many else VMEM_SPEC,
+        out_shape=out_shape,
+        scratch_shapes=list(scratch),
+        compiler_params=pltpu.CompilerParams(vmem_limit_bytes=mib << 20),
+        name=name,
+    )(*operands)
+
+
+def high_rest(values):
+    high = values.astype(BF16).astype(F32)
+    return high, values - high
+
+
+def square_kernel(h0, h1, h2, h3, out):
+    for shift, hidden in enumerate((h0, h1, h2, h3)):
+        for timeline in range(2):
+            wide = hidden[timeline].astype(F32)
+            total = jnp.sum(wide * wide, axis=-1, keepdims=True)
+            at = ROWS * shift + 2 * timeline
+            out[at : at + 2, :] = jnp.broadcast_to(total, (2, HD))
+
+
+def project_kernel(h0, h1, h2, h3, s0, s1, s2, s3, gain, w, out, rows):
+    for shift, hidden in enumerate((h0, h1, h2, h3)):
+        for timeline in range(2):
+            at = ROWS * shift + 2 * timeline
+            rows[at : at + 2, :] = hidden[timeline].astype(F32)
+    squares = ((s0[...] + s1[...]) + (s2[...] + s3[...]))[:, 0:1]
+    normed = rows[...] * lax.rsqrt(squares / D + EPSILON) * gain[...].astype(F32)
+    normed = normed.astype(BF16)
+    width = 512
+    for step in range(w.shape[1] // width):
+        part = jnp.dot(
+            normed, w[:, width * step : width * (step + 1)], preferred_element_type=F32
+        )
+        for head in range(width // HD):
+            at = (step * (width // HD) + head) * ROWS
+            for shift in range(NY):
+                out[shift, at : at + ROWS, :] = part[
+                    ROWS * shift : ROWS * (shift + 1), HD * head : HD * (head + 1)
+                ]
+
+
+def add_kernel(a, b, out):
+    out[...] = a[...] + b[...]
+
+
+def round_kernel(a, b, *outs):
+    for shift, out in enumerate(outs):
+        out[...] = (a[shift] + b[shift]).astype(BF16)
+
+
+def attend_kernel(
+    lengths, r0, r1, r2, r3, cosine, sine, keys, values, out, projected, turns, spread
+):
+    my_x = lax.axis_index("gx")
+    my_y = lax.axis_index("gy")
+    for shift, received in enumerate((r0, r1, r2, r3)):
+        at = pl.multiple_of((my_y ^ shift) * QKV_ROWS, 16)
+        projected[pl.ds(at, QKV_ROWS), :] = received[...].astype(F32)
+    for t in range(4):
+        turns[0, 2 * t : 2 * t + 2, :] = cosine[t % 2]
+        turns[1, 2 * t : 2 * t + 2, :] = sine[t % 2]
+    turned = projected[: QUERIES + KVH * ROWS, :]
+    swapped = pltpu.roll(turned, HD // 2, 1)
+    turned = (
+        turned.reshape(-1, 8, HD) * turns[0][None] + swapped.reshape(-1, 8, HD) * turns[1][None]
+    ).reshape(-1, HD)
+    queries = turned[:QUERIES].astype(BF16)
+    new_keys = turned[QUERIES:].astype(BF16)
+    new_values = projected[QUERIES + KVH * ROWS :, :].astype(BF16)
+
+    row = lax.broadcasted_iota(jnp.int32, (QUERIES, 1), 0)
+    token = row & 1
+    timeline = (row >> 1) & 1
+    group_rows = QUERIES // KVH
+    spread[...] = jnp.zeros_like(spread)
+    scores = jnp.zeros((QUERIES, SPAN_DEV), F32)
+    for t in range(2):
+        mine = jnp.where(timeline == t, queries, jnp.zeros_like(queries))
+        for g in range(KVH):
+            at = slice(group_rows * g, group_rows * (g + 1))
+            spread[t, at, HD * g : HD * (g + 1)] = mine[at]
+        scores += lax.dot_general(
+            spread[t], keys[t], (((1,), (1,)), ((), ())), preferred_element_type=F32
+        )
+    scaling = HD ** (-0.5)
+    scores = scores * scaling
+    slot = my_x * SPAN_DEV + lax.broadcasted_iota(jnp.int32, (QUERIES, SPAN_DEV), 1)
+    usable = slot < jnp.where(timeline == 0, lengths[0], lengths[1])
+    maxima = jnp.max(jnp.where(usable, scores, NEGATIVE), axis=-1, keepdims=True)
+
+    wide_queries = queries.astype(F32)
+    column = lax.broadcasted_iota(jnp.int32, (QUERIES, KVH * ROWS), 1)
+    fresh = []
+    for j in range(2):
+        pick = jnp.where(column == (row // group_rows) * ROWS + timeline * 2 + j, 1.0, 0.0)
+        pick = pick.astype(BF16)
+        key = jnp.dot(pick, new_keys, preferred_element_type=F32)
+        value = jnp.dot(pick, new_values, preferred_element_type=F32)
+        score = jnp.sum(wide_queries * key, axis=-1, keepdims=True) * scaling
+        allowed = (token >= j) & (my_x == 0)
+        maxima = jnp.maximum(maxima, jnp.where(allowed, score, NEGATIVE))
+        fresh.append((score, allowed, value))
+    weights = jnp.exp(jnp.where(usable, scores - maxima, NEGATIVE))
+    totals = jnp.sum(weights, axis=-1, keepdims=True)
+    rounded = weights.astype(BF16)
+    added = jnp.zeros((QUERIES, HD), F32)
+    for score, allowed, value in fresh:
+        weight = jnp.exp(jnp.where(allowed, score - maxima, NEGATIVE))
+        totals += weight
+        added += weight.astype(BF16).astype(F32) * value
+    sums = jnp.zeros((QUERIES, KVH * HD), F32)
+    for t in range(2):
+        mine = jnp.where(timeline == t, rounded, jnp.zeros_like(rounded))
+        sums += jnp.dot(mine, values[t], preferred_element_type=F32)
+    for g in range(KVH):
+        at = slice(group_rows * g, group_rows * (g + 1))
+        out[at, :] = sums[at, HD * g : HD * (g + 1)] + added[at]
+
+    lane = lax.broadcasted_iota(jnp.int32, (QUERIES, HD), 1)
+    sheet = jnp.where(lane == 0, maxima, jnp.where(lane == 1, totals, 0.0))
+    flat = jnp.transpose(sheet)[0:8]
+    out[QUERIES : QUERIES + 8, :] = flat[:, :HD]
+    out[QUERIES + 8 : QUERIES + 16, :] = flat[:, HD:]
+
+
+def factor_columns(rows, sheets):
+    columns = []
+    for half in range(2):
+        sheets[half] = jnp.zeros((HD, HD), F32)
+        for k in range(2):
+            sheets[half, k : k + 1, :] = rows[half][k]
+    turned = [jnp.transpose(sheets[half]) for half in range(2)]
+    for k in range(2):
+        columns.append(
+            jnp.concatenate([turned[half][:, k : k + 1] for half in range(2)], axis=0)
+        )
+    return columns
+
+
+def merge_kernel(a, b, kept, sent, sheets):
+    rows = []
+    for half in range(2):
+        at = QUERIES + 8 * half
+        highest = jnp.maximum(a[at : at + 1, :], b[at : at + 1, :])
+        high, rest = high_rest(highest)
+        middle, low = high_rest(rest)
+        power_a = jnp.exp(a[at : at + 1, :] - highest)
+        power_b = jnp.exp(b[at : at + 1, :] - highest)
+        total = a[at + 1 : at + 2, :] * power_a + b[at + 1 : at + 2, :] * power_b
+        line = lax.broadcasted_iota(jnp.int32, (8, HD), 0)
+        stats = jnp.zeros((8, HD), F32)
+        for k, piece in enumerate((high, middle, low, *high_rest(total))):
+            stats = jnp.where(line == k, piece, stats)
+        kept[at : at + 8, :] = jnp.where(line == 0, highest, jnp.where(line == 1, total, 0.0))
+        sheets[half, 0:8, :] = stats
+        rows.append((power_a, power_b))
+    sent[QUERIES : QUERIES + 16, :] = jnp.concatenate(
+        [sheets[0, 0:8, :], sheets[1, 0:8, :]], axis=0
+    ).astype(BF16)
+    factor_a, factor_b = factor_columns(rows, sheets)
+    merged = a[:QUERIES, :] * factor_a + b[:QUERIES, :] * factor_b
+    kept[:QUERIES, :] = merged
+    sent[:QUERIES, :] = merged.astype(BF16)
+
+
+def settle_kernel(a, b, o0, o1, o2, o3, attended, sheets):
+    my_y = lax.axis_index("gy")
+    other = b[QUERIES : QUERIES + 16, :].astype(F32)
+    rows = []
+    for half in range(2):
+        at = QUERIES + 8 * half
+        stats = other[8 * half : 8 * half + 8]
+        maximum = (stats[0:1] + stats[1:2]) + stats[2:3]
+        total = stats[3:4] + stats[4:5]
+        own_maximum, own_total = a[at : at + 1, :], a[at + 1 : at + 2, :]
+        highest = jnp.maximum(own_maximum, maximum)
+        power_a = jnp.exp(own_maximum - highest)
+        power_b = jnp.exp(maximum - highest)
+        whole = own_total * power_a + total * power_b
+        rows.append((power_a / whole, power_b / whole))
+    factor_a, factor_b = factor_columns(rows, sheets)
+    attended[...] = a[:QUERIES, :] * factor_a + b[:QUERIES, :].astype(F32) * factor_b
+    for shift, out in enumerate((o0, o1, o2, o3)):
+        at = pl.multiple_of((my_y ^ shift) * OUT_ROWS, OUT_ROWS)
+        out[...] = attended[pl.ds(at, OUT_ROWS), :].astype(BF16)
+
+
+def output_kernel(a0, a1, a2, a3, w, o0, o1, o2, o3, wide, sums):
+    for shift, attended in enumerate((a0, a1, a2, a3)):
+        block = attended[...].astype(F32)
+        for head in range(OUT_HEADS):
+            wide[ROWS * shift : ROWS * (shift + 1), HD * head : HD * (head + 1)] = block[
+                ROWS * head : ROWS * (head + 1)
+            ]
+    left = wide[...].astype(BF16)
+    width = 512
+    for step in range(w.shape[1] // width):
+        part = jnp.dot(left, w[:, width * step : width * (step + 1)], preferred_element_type=F32)
+        for chunk in range(width // HD):
+            at = (step * (width // HD) + chunk) * ROWS
+            for shift in range(NY):
+                sums[shift, at : at + ROWS, :] = part[
+                    ROWS * shift : ROWS * (shift + 1), HD * chunk : HD * (chunk + 1)
+                ]
+    o0[...] = sums[0]
+    for shift, out in ((1, o1), (2, o2), (3, o3)):
+        out[...] = sums[shift].astype(BF16)
+
+
+def finish_kernel(a, b, c, d, out, total):
+    total[...] = (a[...] + b[...].astype(F32)) + (c[...].astype(F32) + d[...].astype(F32))
+    for chunk in range(out.shape[2] // HD):
+        for timeline in range(2):
+            at = ROWS * chunk + 2 * timeline
+            out[timeline, :, HD * chunk : HD * (chunk + 1)] = total[at : at + 2, :].astype(BF16)
+
+
+def rotation(positions):
+    halfway = HD // 2
+    frequency = ROPE_BASE ** (-2.0 * jnp.arange(halfway, dtype=F32) / HD)
+    places = positions[:, None] + jnp.arange(2, dtype=jnp.int32)[None, :]
+    angles = places.astype(F32)[:, :, None] * frequency[None, None, :]
+    cosine, sine = jnp.cos(angles), jnp.sin(angles)
+    return jnp.concatenate([cosine, cosine], axis=2), jnp.concatenate([-sine, sine], axis=2)
+
+
+def partner(part, axis, distance):
+    if distance == 0:
+        return part
+    return lax.ppermute(part, axis, [(k, k ^ distance) for k in range(lax.axis_size(axis))])
+
+
+def small_body(hidden, norm_gain, w_qkv, w_out, k_cache, v_cache, cache_len, positions):
+    def shape(*dims, dtype=BF16):
+        return jax.ShapeDtypeStruct(dims, dtype)
+
+    columns = w_out.shape[1]
+    features = hidden.shape[2]
+    w_qkv = pltpu.with_memory_space_constraint(w_qkv, pltpu.VMEM)
+    k_cache = pltpu.with_memory_space_constraint(k_cache, pltpu.VMEM)
+    v_cache = pltpu.with_memory_space_constraint(v_cache, pltpu.VMEM)
+    w_out = pltpu.with_memory_space_constraint(w_out, pltpu.VMEM)
+    cosine, sine = rotation(positions)
+    hiddens = [partner(hidden, "gy", y) for y in range(NY)]
+    squares = call(square_kernel, "square", shape(NY * ROWS, HD, dtype=F32), hiddens)
+    squares = [partner(squares, "gx", x) for x in range(NX)]
+    sums = call(
+        project_kernel,
+        "project",
+        shape(NY, QKV_ROWS, HD, dtype=F32),
+        [*hiddens, *squares, norm_gain[None], w_qkv],
+        [pltpu.VMEM((NY * ROWS, features), F32)],
+    )
+    sums = call(
+        add_kernel, "add", shape(NY, QKV_ROWS, HD, dtype=F32), [sums, partner(sums, "gx", 1)]
+    )
+    blocks = call(
+        round_kernel, "round", [shape(QKV_ROWS, HD)] * NY, [sums, partner(sums, "gx", 2)]
+    )
+    blocks = [partner(block, "gy", y) for y, block in enumerate(blocks)]
+    partial = call(
+        attend_kernel,
+        "attend",
+        shape(QUERIES + 16, HD, dtype=F32),
+        [cache_len, *blocks, cosine, sine, k_cache, v_cache],
+        [
+            pltpu.VMEM((NY * QKV_ROWS, HD), F32),
+            pltpu.VMEM((2, 8, HD), F32),
+            pltpu.VMEM((2, QUERIES, KVH * HD), BF16),
+        ],
+        scalars=1,
+        mib=16,
+    )
+    kept, sent = call(
+        merge_kernel,
+        "merge",
+        [shape(QUERIES + 16, HD, dtype=F32), shape(QUERIES + 16, HD)],
+        [partial, partner(partial, "gx", 1)],
+        [pltpu.VMEM((2, HD, HD), F32)],
+    )
+    blocks = call(
+        settle_kernel,
+        "settle",
+        [shape(OUT_ROWS, HD)] * NY,
+        [kept, partner(sent, "gx", 2)],
+        [pltpu.VMEM((QUERIES, HD), F32), pltpu.VMEM((2, HD, HD), F32)],
+    )
+    blocks = [partner(block, "gy", y) for y, block in enumerate(blocks)]
+    count = columns // HD * ROWS
+    blocks = call(
+        output_kernel,
+        "output",
+        [shape(count, HD, dtype=F32)] + [shape(count, HD)] * (NY - 1),
+        [*blocks, w_out],
+        [
+            pltpu.VMEM((NY * ROWS, w_out.shape[0]), F32),
+            pltpu.VMEM((NY, count, HD), F32),
+        ],
+    )
+    blocks = [partner(block, "gy", y) for y, block in enumerate(blocks)]
+    return call(
+        finish_kernel,
+        "finish",
+        shape(2, 2, columns),
+        blocks,
+        [pltpu.VMEM((count, HD), F32)],
+    )
+
+
 def solution(mesh):
+    small = mesh.shape["gx"] == NX and mesh.shape["gy"] == NY
+    body = small_body if small else general_body
     in_specs = (
         P(("group", "gy"), None, "gx"),
         P("gx"),

time: 142 us -> 64.1 us (0.45)
  blocking collectives: 69.6 us -> 0 us
  local copies, waits for them, and re-layouts: 38.3 us -> 6.12 us
  waiting for transfers between devices: 7.08 us -> 28.5 us
  starting transfers between devices: 8.11 us -> 22.5 us
  matrix products: 12.2 us -> 0 us
  Pallas kernels: 0 us -> 6.32 us
  other arithmetic: 4.47 us -> 0.27 us
    all_gather x4 -> x0, blocking collectives: 30.4 us -> none  [the longest x3 17 us: combined_all(): everything = jax.tree.map(lambda part: lax.all_gather(part, axis), shard)]
    ppermute x0 -> x19, waiting for transfers between devices: none -> 28.5 us  [partner(): lax.ppermute(part, axis, [(k, k ^ distance) for k in range(lax.axis_size(...]
    ppermute x0 -> x19, starting transfers between devices: none -> 22.5 us  [partner(): lax.ppermute(part, axis, [(k, k ^ distance) for k in range(lax.axis_size(...]
    psum x2 -> x0, blocking collectives: 20.4 us -> none  [the longest x1 12.1 us: body(): summed = lax.psum(partial_sums, 'gx').astype(jnp.bfloat16)]
    unnamed x1 -> x0, blocking collectives: 18.8 us -> none
    unnamed x15 -> x16, local copies, waits for them, and re-layouts: 21 us -> 5.43 us
    dot_general x6 -> x0, matrix products: 12.2 us -> none  [the longest x1 5.55 us: body(): jnp.einsum('rkc,ce->rke', lax.all_gather(normed, 'gy', axis=0, tiled=True...]
    all_to_all x5 -> x0, local copies, waits for them, and re-layouts: 9.9 us -> none  [the longest x3 9.84 us: body(): lax.all_to_all(attended, 'gy', split_axis=2, concat_axis=0, tiled=True)]
  transfers between devices with their start and end apart: 2 -> 19, of which waited for: 2 -> 14; matrix products, arithmetic and copies ran while one was open for 1% -> 2% of each run, Pallas kernels for 0% -> 0%
where the time goes in v1:
time: 64.1 us; the launch traced here: 63.7 us
  waiting for transfers between devices  28.5 us (44%)
  starting transfers between devices  22.5 us (35%)
  Pallas kernels  6.32 us (10%)
  local copies, waits for them, and re-layouts  6.12 us (10%)
    ppermute x19, waiting for transfers between devices, partner(): lax.ppermute(part, axis, [(k, k ^ distance) for k in range(lax.axis_size(...  28.5 us
    ppermute x19, starting transfers between devices, partner(): lax.ppermute(part, axis, [(k, k ^ distance) for k in range(lax.axis_size(...  22.5 us
    pallas_call x9, Pallas kernels, call(): pl.pallas_call(kernel, in_specs=[SMEM_SPEC] * scalars + [VMEM_SPEC] * (le...  6.32 us
    unnamed x16, local copies, waits for them, and re-layouts  5.43 us
  transfers between devices with their start and end apart: 19, of which 14 were waited for; matrix products, arithmetic and copies ran while one was open for 2% of the time, Pallas kernels for 0%

profile of v1, /device:TPU:0, one launch (start us, length us, event | category | flops | bytes accessed | tf_op | source)
XLA Modules:
  0.0 63.7 jit_solution(2299986523034361819)
XLA Ops:
  0.0 3.0 %collective-permute-start = (bf16[2,2,2048]{2,1,0:T(2,128)(2,1)}, bf16[2,2,2048]{2,1,0:T(2,128)(2,1)S(1)}, u32[]{:S(2)}, u32[]{:S(2)}) collective-permute-start(bf16[2,2,2048]{2,1,0:T(2,128)(2,1)} %h0.3), channel_id=1, source_target_pairs={{0,1},{1,0},{2,3},{3,2},{4,5},{5,4},{6,7},{7,6},{8,9},{9,8},{10,11... | collective-permute-start | bytes 49160 | tf_op jit(solution)/shard_map/ppermute | solution.py:386
  3.0 2.6 %collective-permute-start.1 = (bf16[2,2,2048]{2,1,0:T(2,128)(2,1)}, bf16[2,2,2048]{2,1,0:T(2,128)(2,1)S(1)}, u32[]{:S(2)}, u32[]{:S(2)}) collective-permute-start(bf16[2,2,2048]{2,1,0:T(2,128)(2,1)} %h0.3), channel_id=1, source_target_pairs={{0,2},{1,3},{2,0},{3,1},{4,6},{5,7},{6,4},{7,5},{8,10},{9,11},{10,... | collective-permute-start | bytes 49160 | tf_op jit(solution)/shard_map/ppermute | solution.py:386
  5.6 2.3 %collective-permute-done.1.h2 = bf16[2,2,2048]{2,1,0:T(2,128)(2,1)S(1)} collective-permute-done((bf16[2,2,2048]{2,1,0:T(2,128)(2,1)}, bf16[2,2,2048]{2,1,0:T(2,128)(2,1)S(1)}, u32[]{:S(2)}, u32[]{:S(2)}) %collective-permute-start.1) | collective-permute-done | bytes 16416 | tf_op jit(solution)/shard_map/ppermute | solution.py:386
  8.0 3.4 %collective-permute-done.2.h3 = bf16[2,2,2048]{2,1,0:T(2,128)(2,1)S(1)} collective-permute-done((bf16[2,2,2048]{2,1,0:T(2,128)(2,1)}, bf16[2,2,2048]{2,1,0:T(2,128)(2,1)S(1)}, u32[]{:S(2)}, u32[]{:S(2)}) %collective-permute-start.2) | collective-permute-done | bytes 16416 | tf_op jit(solution)/shard_map/ppermute | solution.py:386
  12.3 1.6 %collective-permute-start.4 = (f32[16,128]{1,0:T(8,128)S(1)}, f32[16,128]{1,0:T(8,128)S(1)}, u32[]{:S(2)}, u32[]{:S(2)}) collective-permute-start(f32[16,128]{1,0:T(8,128)S(1)} %square.1.s0), channel_id=1, source_target_pairs={{0,8},{4,12},{8,0},{12,4},{1,9},{5,13},{9,1},{13,5},{2,10},{6,14},... | collective-permute-start | bytes 24584 | tf_op jit(solution)/shard_map/ppermute | solution.py:386
  14.8 1.2 %collective-permute-done.4.s2 = f32[16,128]{1,0:T(8,128)S(1)} collective-permute-done((f32[16,128]{1,0:T(8,128)S(1)}, f32[16,128]{1,0:T(8,128)S(1)}, u32[]{:S(2)}, u32[]{:S(2)}) %collective-permute-start.4) | collective-permute-done | bytes 8224 | tf_op jit(solution)/shard_map/ppermute | solution.py:386
  16.0 0.9 %collective-permute-done.5.s3 = f32[16,128]{1,0:T(8,128)S(1)} collective-permute-done((f32[16,128]{1,0:T(8,128)S(1)}, f32[16,128]{1,0:T(8,128)S(1)}, u32[]{:S(2)}, u32[]{:S(2)}) %collective-permute-start.5) | collective-permute-done | bytes 8224 | tf_op jit(solution)/shard_map/ppermute | solution.py:386
  16.9 4.0 %copy-done = bf16[2048,2560]{1,0:T(8,128)(2,1)S(1)} copy-done((bf16[2048,2560]{1,0:T(8,128)(2,1)S(1)}, bf16[2048,2560]{1,0:T(8,128)(2,1)}, u32[]{:S(2)}) %copy-start) | copy-done | bytes 10485784
  21.6 1.5 %project.1.a = f32[4,80,128]{2,1,0:T(8,128)S(1)} custom-call(bf16[2,2,2048]{2,1,0:T(2,128)(2,1)S(1)} %copy-done.5, bf16[2,2,2048]{2,1,0:T(2,128)(2,1)S(1)} %collective-permute-done.h1, bf16[2,2,2048]{2,1,0:T(2,128)(2,1)S(1)} %collective-permute-done.1.h2, bf16[2,2,2048]{2,1,0:T(2,128)(2,1)S(1)} %collective-permute-done.2.h3, f32[16,128]{1,0:T(8,128)S(1)} %square.1.s0, ...), custom_call_target="tpu_custom_call" | custom-call | tf_op jit(solution)/shard_map/project/pallas_call | solution.py:152
  23.4 1.1 %collective-permute-done.6.b = f32[4,80,128]{2,1,0:T(8,128)S(1)} collective-permute-done((f32[4,80,128]{2,1,0:T(8,128)S(1)}, f32[4,80,128]{2,1,0:T(8,128)S(1)}, u32[]{:S(2)}, u32[]{:S(2)}) %collective-permute-start.6) | collective-permute-done | bytes 163872 | tf_op jit(solution)/shard_map/ppermute | solution.py:386
  25.3 5.5 %collective-permute-done.7.b = f32[4,80,128]{2,1,0:T(8,128)S(1)} collective-permute-done((f32[4,80,128]{2,1,0:T(8,128)S(1)}, f32[4,80,128]{2,1,0:T(8,128)S(1)}, u32[]{:S(2)}, u32[]{:S(2)}) %collective-permute-start.7) | collective-permute-done | bytes 163872 | tf_op jit(solution)/shard_map/ppermute | solution.py:386
  31.2 4.2 %collective-permute-start.9 = (bf16[80,128]{1,0:T(8,128)(2,1)S(1)}, bf16[80,128]{1,0:T(8,128)(2,1)S(1)}, u32[]{:S(2)}, u32[]{:S(2)}) collective-permute-start(bf16[80,128]{1,0:T(8,128)(2,1)S(1)} %get-tuple-element.21), channel_id=1, source_target_pairs={{0,2},{1,3},{2,0},{3,1},{4,6},{5,7},{6,4},{7,5},{8,10},{9,11},{10,... | collective-permute-start | bytes 61448 | tf_op jit(solution)/shard_map/ppermute | solution.py:386
  35.4 1.1 %collective-permute-done.10.r3 = bf16[80,128]{1,0:T(8,128)(2,1)S(1)} collective-permute-done((bf16[80,128]{1,0:T(8,128)(2,1)S(1)}, bf16[80,128]{1,0:T(8,128)(2,1)S(1)}, u32[]{:S(2)}, u32[]{:S(2)}) %collective-permute-start.10) | collective-permute-done | bytes 20512 | tf_op jit(solution)/shard_map/ppermute | solution.py:386
  37.1 2.3 %attend.1.a = f32[272,128]{1,0:T(8,128)S(1)} custom-call(s32[2]{0:T(128)S(1)} %copy-done.6, bf16[80,128]{1,0:T(8,128)(2,1)S(1)} %get-tuple-element.19.r0, bf16[80,128]{1,0:T(8,128)(2,1)S(1)} %collective-permute-done.8.r1, bf16[80,128]{1,0:T(8,128)(2,1)S(1)} %collective-permute-done.9.r2, bf16[80,128]{1,0:T(8,128)(2,1)S(1)} %collective-permute-done.10.r3, ...), custom_call_target="tpu_custom_call" | custom-call | tf_op jit(solution)/shard_map/attend/pallas_call | solution.py:152
  39.5 1.3 %collective-permute-done.11.b = f32[272,128]{1,0:T(8,128)S(1)} collective-permute-done((f32[272,128]{1,0:T(8,128)S(1)}, f32[272,128]{1,0:T(8,128)S(1)}, u32[]{:S(2)}, u32[]{:S(2)}) %collective-permute-start.11) | collective-permute-done | bytes 139296 | tf_op jit(solution)/shard_map/ppermute | solution.py:386
  41.8 3.7 %collective-permute-done.12.b = bf16[272,128]{1,0:T(8,128)(2,1)S(1)} collective-permute-done((bf16[272,128]{1,0:T(8,128)(2,1)S(1)}, bf16[272,128]{1,0:T(8,128)(2,1)S(1)}, u32[]{:S(2)}, u32[]{:S(2)}) %collective-permute-start.12) | collective-permute-done | bytes 69664 | tf_op jit(solution)/shard_map/ppermute | solution.py:386
  46.6 2.2 %collective-permute-start.14 = (bf16[64,128]{1,0:T(8,128)(2,1)S(1)}, bf16[64,128]{1,0:T(8,128)(2,1)S(1)}, u32[]{:S(2)}, u32[]{:S(2)}) collective-permute-start(bf16[64,128]{1,0:T(8,128)(2,1)S(1)} %get-tuple-element.27), channel_id=1, source_target_pairs={{0,2},{1,3},{2,0},{3,1},{4,6},{5,7},{6,4},{7,5},{8,10},{9,11},{10,... | collective-permute-start | bytes 49160 | tf_op jit(solution)/shard_map/ppermute | solution.py:386
  48.8 1.4 %collective-permute-start.15 = (bf16[64,128]{1,0:T(8,128)(2,1)S(1)}, bf16[64,128]{1,0:T(8,128)(2,1)S(1)}, u32[]{:S(2)}, u32[]{:S(2)}) collective-permute-start(bf16[64,128]{1,0:T(8,128)(2,1)S(1)} %get-tuple-element.28), channel_id=1, source_target_pairs={{0,3},{1,2},{2,1},{3,0},{4,7},{5,6},{6,5},{7,4},{8,11},{9,10},{10,... | collective-permute-start | bytes 49160 | tf_op jit(solution)/shard_map/ppermute | solution.py:386
  50.2 1.0 %collective-permute-done.14.a2 = bf16[64,128]{1,0:T(8,128)(2,1)S(1)} collective-permute-done((bf16[64,128]{1,0:T(8,128)(2,1)S(1)}, bf16[64,128]{1,0:T(8,128)(2,1)S(1)}, u32[]{:S(2)}, u32[]{:S(2)}) %collective-permute-start.14) | collective-permute-done | bytes 16416 | tf_op jit(solution)/shard_map/ppermute | solution.py:386
  51.2 3.1 %collective-permute-done.15.a3 = bf16[64,128]{1,0:T(8,128)(2,1)S(1)} collective-permute-done((bf16[64,128]{1,0:T(8,128)(2,1)S(1)}, bf16[64,128]{1,0:T(8,128)(2,1)S(1)}, u32[]{:S(2)}, u32[]{:S(2)}) %collective-permute-start.15) | collective-permute-done | bytes 16416 | tf_op jit(solution)/shard_map/ppermute | solution.py:386
  54.3 1.2 %output.1 = (f32[64,128]{1,0:T(8,128)S(1)}, bf16[64,128]{1,0:T(8,128)(2,1)S(1)}, bf16[64,128]{1,0:T(8,128)(2,1)S(1)}, bf16[64,128]{1,0:T(8,128)(2,1)S(1)}) custom-call(bf16[64,128]{1,0:T(8,128)(2,1)S(1)} %get-tuple-element.25.a0, bf16[64,128]{1,0:T(8,128)(2,1)S(1)} %collective-permute-done.13.a1, bf16[64,128]{1,0:T(8,128)(2,1)S(1)} %collective-permute-done.14.a2, ...), custom_call_target="tpu_custom_call" | custom-call | tf_op jit(solution)/shard_map/output/pallas_call | solution.py:152
  55.8 1.8 %collective-permute-start.17 = (bf16[64,128]{1,0:T(8,128)(2,1)S(1)}, bf16[64,128]{1,0:T(8,128)(2,1)S(1)}, u32[]{:S(2)}, u32[]{:S(2)}) collective-permute-start(bf16[64,128]{1,0:T(8,128)(2,1)S(1)} %get-tuple-element.31), channel_id=1, source_target_pairs={{0,2},{1,3},{2,0},{3,1},{4,6},{5,7},{6,4},{7,5},{8,10},{9,11},{10,... | collective-permute-start | bytes 49160 | tf_op jit(solution)/shard_map/ppermute | solution.py:386
  57.6 2.4 %collective-permute-start.18 = (bf16[64,128]{1,0:T(8,128)(2,1)S(1)}, bf16[64,128]{1,0:T(8,128)(2,1)S(1)}, u32[]{:S(2)}, u32[]{:S(2)}) collective-permute-start(bf16[64,128]{1,0:T(8,128)(2,1)S(1)} %get-tuple-element.32), channel_id=1, source_target_pairs={{0,3},{1,2},{2,1},{3,0},{4,7},{5,6},{6,5},{7,4},{8,11},{9,10},{10,... | collective-permute-start | bytes 49160 | tf_op jit(solution)/shard_map/ppermute | solution.py:386
  60.4 2.7 %collective-permute-done.18.d = bf16[64,128]{1,0:T(8,128)(2,1)S(1)} collective-permute-done((bf16[64,128]{1,0:T(8,128)(2,1)S(1)}, bf16[64,128]{1,0:T(8,128)(2,1)S(1)}, u32[]{:S(2)}, u32[]{:S(2)}) %collective-permute-start.18) | collective-permute-done | bytes 16416 | tf_op jit(solution)/shard_map/ppermute | solution.py:386
  (44 shorter events, 8.0 us)
Async XLA Ops:
  0.0 5.6 %collective-permute-start = (bf16[2,2,2048]{2,1,0:T(2,128)(2,1)}, bf16[2,2,2048]{2,1,0:T(2,128)(2,1)S(1)}, u32[]{:S(2)}, u32[]{:S(2)}) collective-permute-start(bf16[2,2,2048]{2,1,0:T(2,128)(2,1)} %h0.3), channel_id=1, source_target_pairs={{0,1},{1,0},{2,3},{3,2},{4,5},{5,4},{6,7},{7,6},{8,9},{9,8},{10,11... | collective-permute-start | bytes 49160 | tf_op jit(solution)/shard_map/ppermute | solution.py:386
  3.0 4.9 %collective-permute-start.1 = (bf16[2,2,2048]{2,1,0:T(2,128)(2,1)}, bf16[2,2,2048]{2,1,0:T(2,128)(2,1)S(1)}, u32[]{:S(2)}, u32[]{:S(2)}) collective-permute-start(bf16[2,2,2048]{2,1,0:T(2,128)(2,1)} %h0.3), channel_id=1, source_target_pairs={{0,2},{1,3},{2,0},{3,1},{4,6},{5,7},{6,4},{7,5},{8,10},{9,11},{10,... | collective-permute-start | bytes 49160 | tf_op jit(solution)/shard_map/ppermute | solution.py:386
  5.6 5.7 %collective-permute-start.2 = (bf16[2,2,2048]{2,1,0:T(2,128)(2,1)}, bf16[2,2,2048]{2,1,0:T(2,128)(2,1)S(1)}, u32[]{:S(2)}, u32[]{:S(2)}) collective-permute-start(bf16[2,2,2048]{2,1,0:T(2,128)(2,1)} %h0.3), channel_id=1, source_target_pairs={{0,3},{1,2},{2,1},{3,0},{4,7},{5,6},{6,5},{7,4},{8,11},{9,10},{10,... | collective-permute-start | bytes 49160 | tf_op jit(solution)/shard_map/ppermute | solution.py:386
  12.1 11.2 %copy-start.7 = (s32[2]{0:T(128)S(1)}, s32[2]{0:T(128)}, u32[]{:S(2)}) copy-start(s32[2]{0:T(128)} %param.15) | copy-start | bytes 28
  12.1 25.0 %copy-start.6 = (s32[2]{0:T(128)S(1)}, s32[2]{0:T(128)}, u32[]{:S(2)}) copy-start(s32[2]{0:T(128)} %lengths.1) | copy-start | bytes 28
  12.2 2.6 %collective-permute-start.3 = (f32[16,128]{1,0:T(8,128)S(1)}, f32[16,128]{1,0:T(8,128)S(1)}, u32[]{:S(2)}, u32[]{:S(2)}) collective-permute-start(f32[16,128]{1,0:T(8,128)S(1)} %square.1.s0), channel_id=1, source_target_pairs={{0,4},{4,0},{8,12},{12,8},{1,5},{5,1},{9,13},{13,9},{2,6},{6,2},{1... | collective-permute-start | bytes 24584 | tf_op jit(solution)/shard_map/ppermute | solution.py:386
  12.3 3.7 %collective-permute-start.4 = (f32[16,128]{1,0:T(8,128)S(1)}, f32[16,128]{1,0:T(8,128)S(1)}, u32[]{:S(2)}, u32[]{:S(2)}) collective-permute-start(f32[16,128]{1,0:T(8,128)S(1)} %square.1.s0), channel_id=1, source_target_pairs={{0,8},{4,12},{8,0},{12,4},{1,9},{5,13},{9,1},{13,5},{2,10},{6,14},... | collective-permute-start | bytes 24584 | tf_op jit(solution)/shard_map/ppermute | solution.py:386
  13.8 3.1 %collective-permute-start.5 = (f32[16,128]{1,0:T(8,128)S(1)}, f32[16,128]{1,0:T(8,128)S(1)}, u32[]{:S(2)}, u32[]{:S(2)}) collective-permute-start(f32[16,128]{1,0:T(8,128)S(1)} %square.1.s0), channel_id=1, source_target_pairs={{0,12},{4,8},{8,4},{12,0},{1,13},{5,9},{9,5},{13,1},{2,14},{6,10},... | collective-permute-start | bytes 24584 | tf_op jit(solution)/shard_map/ppermute | solution.py:386
  21.6 15.5 %copy-start.2 = (bf16[2,384,1024]{2,1,0:T(8,128)(2,1)S(1)}, bf16[2,384,1024]{2,1,0:T(8,128)(2,1)}, u32[]{:S(2)}) copy-start(bf16[2,384,1024]{2,1,0:T(8,128)(2,1)} %keys.1) | copy-start | bytes 4718596
  21.6 15.5 %copy-start.3 = (bf16[2,384,1024]{2,1,0:T(8,128)(2,1)S(1)}, bf16[2,384,1024]{2,1,0:T(8,128)(2,1)}, u32[]{:S(2)}) copy-start(bf16[2,384,1024]{2,1,0:T(8,128)(2,1)} %values.1) | copy-start | bytes 4718596
  21.6 32.7 %copy-start.1 = (bf16[2048,2048]{1,0:T(8,128)(2,1)S(1)}, bf16[2048,2048]{1,0:T(8,128)(2,1)}, u32[]{:S(2)}) copy-start(bf16[2048,2048]{1,0:T(8,128)(2,1)} %w.3) | copy-start | bytes 25165828
  23.1 1.4 %collective-permute-start.6 = (f32[4,80,128]{2,1,0:T(8,128)S(1)}, f32[4,80,128]{2,1,0:T(8,128)S(1)}, u32[]{:S(2)}, u32[]{:S(2)}) collective-permute-start(f32[4,80,128]{2,1,0:T(8,128)S(1)} %project.1.a), channel_id=1, source_target_pairs={{0,4},{4,0},{8,12},{12,8},{1,5},{5,1},{9,13},{13,9},{2,6},{6,2},{1... | collective-permute-start | bytes 491528 | tf_op jit(solution)/shard_map/ppermute | solution.py:386
  24.5 6.3 %collective-permute-start.7 = (f32[4,80,128]{2,1,0:T(8,128)S(1)}, f32[4,80,128]{2,1,0:T(8,128)S(1)}, u32[]{:S(2)}, u32[]{:S(2)}) collective-permute-start(f32[4,80,128]{2,1,0:T(8,128)S(1)} %add.24.a), channel_id=1, source_target_pairs={{0,8},{4,12},{8,0},{12,4},{1,9},{5,13},{9,1},{13,5},{2,10},{6,14},... | collective-permute-start | bytes 491528 | tf_op jit(solution)/shard_map/ppermute | solution.py:386
  30.9 5.6 %collective-permute-start.10 = (bf16[80,128]{1,0:T(8,128)(2,1)S(1)}, bf16[80,128]{1,0:T(8,128)(2,1)S(1)}, u32[]{:S(2)}, u32[]{:S(2)}) collective-permute-start(bf16[80,128]{1,0:T(8,128)(2,1)S(1)} %get-tuple-element.22), channel_id=1, source_target_pairs={{0,3},{1,2},{2,1},{3,0},{4,7},{5,6},{6,5},{7,4},{8,11},{9,10},{10,... | collective-permute-start | bytes 61448 | tf_op jit(solution)/shard_map/ppermute | solution.py:386
  31.2 5.4 %collective-permute-start.8 = (bf16[80,128]{1,0:T(8,128)(2,1)S(1)}, bf16[80,128]{1,0:T(8,128)(2,1)S(1)}, u32[]{:S(2)}, u32[]{:S(2)}) collective-permute-start(bf16[80,128]{1,0:T(8,128)(2,1)S(1)} %get-tuple-element.20), channel_id=1, source_target_pairs={{0,1},{1,0},{2,3},{3,2},{4,5},{5,4},{6,7},{7,6},{8,9},{9,8},{10,11... | collective-permute-start | bytes 61448 | tf_op jit(solution)/shard_map/ppermute | solution.py:386
  31.2 5.9 %collective-permute-start.9 = (bf16[80,128]{1,0:T(8,128)(2,1)S(1)}, bf16[80,128]{1,0:T(8,128)(2,1)S(1)}, u32[]{:S(2)}, u32[]{:S(2)}) collective-permute-start(bf16[80,128]{1,0:T(8,128)(2,1)S(1)} %get-tuple-element.21), channel_id=1, source_target_pairs={{0,2},{1,3},{2,0},{3,1},{4,6},{5,7},{6,4},{7,5},{8,10},{9,11},{10,... | collective-permute-start | bytes 61448 | tf_op jit(solution)/shard_map/ppermute | solution.py:386
  39.4 1.4 %collective-permute-start.11 = (f32[272,128]{1,0:T(8,128)S(1)}, f32[272,128]{1,0:T(8,128)S(1)}, u32[]{:S(2)}, u32[]{:S(2)}) collective-permute-start(f32[272,128]{1,0:T(8,128)S(1)} %attend.1.a), channel_id=1, source_target_pairs={{0,4},{4,0},{8,12},{12,8},{1,5},{5,1},{9,13},{13,9},{2,6},{6,2},{1... | collective-permute-start | bytes 417800 | tf_op jit(solution)/shard_map/ppermute | solution.py:386
  41.1 4.4 %collective-permute-start.12 = (bf16[272,128]{1,0:T(8,128)(2,1)S(1)}, bf16[272,128]{1,0:T(8,128)(2,1)S(1)}, u32[]{:S(2)}, u32[]{:S(2)}) collective-permute-start(bf16[272,128]{1,0:T(8,128)(2,1)S(1)} %get-tuple-element.24), channel_id=1, source_target_pairs={{0,8},{4,12},{8,0},{12,4},{1,9},{5,13},{9,1},{13,5},{2,10},{6,14},... | collective-permute-start | bytes 208904 | tf_op jit(solution)/shard_map/ppermute | solution.py:386
  45.7 4.5 %collective-permute-start.13 = (bf16[64,128]{1,0:T(8,128)(2,1)S(1)}, bf16[64,128]{1,0:T(8,128)(2,1)S(1)}, u32[]{:S(2)}, u32[]{:S(2)}) collective-permute-start(bf16[64,128]{1,0:T(8,128)(2,1)S(1)} %get-tuple-element.26), channel_id=1, source_target_pairs={{0,1},{1,0},{2,3},{3,2},{4,5},{5,4},{6,7},{7,6},{8,9},{9,8},{10,11... | collective-permute-start | bytes 49160 | tf_op jit(solution)/shard_map/ppermute | solution.py:386
  46.6 4.6 %collective-permute-start.14 = (bf16[64,128]{1,0:T(8,128)(2,1)S(1)}, bf16[64,128]{1,0:T(8,128)(2,1)S(1)}, u32[]{:S(2)}, u32[]{:S(2)}) collective-permute-start(bf16[64,128]{1,0:T(8,128)(2,1)S(1)} %get-tuple-element.27), channel_id=1, source_target_pairs={{0,2},{1,3},{2,0},{3,1},{4,6},{5,7},{6,4},{7,5},{8,10},{9,11},{10,... | collective-permute-start | bytes 49160 | tf_op jit(solution)/shard_map/ppermute | solution.py:386
  48.8 5.5 %collective-permute-start.15 = (bf16[64,128]{1,0:T(8,128)(2,1)S(1)}, bf16[64,128]{1,0:T(8,128)(2,1)S(1)}, u32[]{:S(2)}, u32[]{:S(2)}) collective-permute-start(bf16[64,128]{1,0:T(8,128)(2,1)S(1)} %get-tuple-element.28), channel_id=1, source_target_pairs={{0,3},{1,2},{2,1},{3,0},{4,7},{5,6},{6,5},{7,4},{8,11},{9,10},{10,... | collective-permute-start | bytes 49160 | tf_op jit(solution)/shard_map/ppermute | solution.py:386
  55.5 4.5 %collective-permute-start.16 = (bf16[64,128]{1,0:T(8,128)(2,1)S(1)}, bf16[64,128]{1,0:T(8,128)(2,1)S(1)}, u32[]{:S(2)}, u32[]{:S(2)}) collective-permute-start(bf16[64,128]{1,0:T(8,128)(2,1)S(1)} %get-tuple-element.30), channel_id=1, source_target_pairs={{0,1},{1,0},{2,3},{3,2},{4,5},{5,4},{6,7},{7,6},{8,9},{9,8},{10,11... | collective-permute-start | bytes 49160 | tf_op jit(solution)/shard_map/ppermute | solution.py:386
  55.8 4.6 %collective-permute-start.17 = (bf16[64,128]{1,0:T(8,128)(2,1)S(1)}, bf16[64,128]{1,0:T(8,128)(2,1)S(1)}, u32[]{:S(2)}, u32[]{:S(2)}) collective-permute-start(bf16[64,128]{1,0:T(8,128)(2,1)S(1)} %get-tuple-element.31), channel_id=1, source_target_pairs={{0,2},{1,3},{2,0},{3,1},{4,6},{5,7},{6,4},{7,5},{8,10},{9,11},{10,... | collective-permute-start | bytes 49160 | tf_op jit(solution)/shard_map/ppermute | solution.py:386
  57.6 5.5 %collective-permute-start.18 = (bf16[64,128]{1,0:T(8,128)(2,1)S(1)}, bf16[64,128]{1,0:T(8,128)(2,1)S(1)}, u32[]{:S(2)}, u32[]{:S(2)}) collective-permute-start(bf16[64,128]{1,0:T(8,128)(2,1)S(1)} %get-tuple-element.32), channel_id=1, source_target_pairs={{0,3},{1,2},{2,1},{3,0},{4,7},{5,6},{6,5},{7,4},{8,11},{9,10},{10,... | collective-permute-start | bytes 49160 | tf_op jit(solution)/shard_map/ppermute | solution.py:386
  (3 other events, 5.4 us)

commit v2 on v1

--- a/solution.py
+++ b/solution.py
@@ -147,7 +147,7 @@
 BF16 = jnp.bfloat16
 
 
-def call(kernel, name, out_shape, operands, scratch=(), scalars=0, mib=8):
+def call(kernel, name, out_shape, operands, scratch=(), scalars=0, mib=8, cost=None):
     many = isinstance(out_shape, (list, tuple))
     return pl.pallas_call(
         kernel,
@@ -156,6 +156,7 @@
         out_shape=out_shape,
         scratch_shapes=list(scratch),
         compiler_params=pltpu.CompilerParams(vmem_limit_bytes=mib << 20),
+        cost_estimate=cost,
         name=name,
     )(*operands)
 
@@ -165,21 +166,31 @@
     return high, values - high
 
 
-def square_kernel(h0, h1, h2, h3, out):
-    for shift, hidden in enumerate((h0, h1, h2, h3)):
-        for timeline in range(2):
-            wide = hidden[timeline].astype(F32)
+def pair_kernel(own, other, out):
+    out[0] = own[...]
+    out[1] = other[...]
+
+
+def add_kernel(a, b, out):
+    out[...] = a[...] + b[...]
+
+
+def square_kernel(near, far, out):
+    for half, pair in enumerate((near, far)):
+        for k in range(4):
+            wide = pair[k // 2, k % 2].astype(F32)
             total = jnp.sum(wide * wide, axis=-1, keepdims=True)
-            at = ROWS * shift + 2 * timeline
+            at = 8 * half + 2 * k
             out[at : at + 2, :] = jnp.broadcast_to(total, (2, HD))
 
 
-def project_kernel(h0, h1, h2, h3, s0, s1, s2, s3, gain, w, out, rows):
-    for shift, hidden in enumerate((h0, h1, h2, h3)):
-        for timeline in range(2):
-            at = ROWS * shift + 2 * timeline
-            rows[at : at + 2, :] = hidden[timeline].astype(F32)
-    squares = ((s0[...] + s1[...]) + (s2[...] + s3[...]))[:, 0:1]
+def project_kernel(near, far, s0, s1, gain, w, kept, sent, rows, sums):
+    mixed = lax.axis_index("gx") ^ lax.axis_index("gy")
+    for half, pair in enumerate((near, far)):
+        for k in range(4):
+            at = 8 * half + 2 * k
+            rows[at : at + 2, :] = pair[k // 2, k % 2].astype(F32)
+    squares = (s0[...] + s1[...])[:, 0:1]
     normed = rows[...] * lax.rsqrt(squares / D + EPSILON) * gain[...].astype(F32)
     normed = normed.astype(BF16)
     width = 512
@@ -190,28 +201,31 @@
         for head in range(width // HD):
             at = (step * (width // HD) + head) * ROWS
             for shift in range(NY):
-                out[shift, at : at + ROWS, :] = part[
+                sums[shift, at : at + ROWS, :] = part[
                     ROWS * shift : ROWS * (shift + 1), HD * head : HD * (head + 1)
                 ]
-
-
-def add_kernel(a, b, out):
-    out[...] = a[...] + b[...]
-
-
-def round_kernel(a, b, *outs):
-    for shift, out in enumerate(outs):
-        out[...] = (a[shift] + b[shift]).astype(BF16)
+    for k in range(2):
+        kept[k] = sums[mixed ^ (2 * k)]
+        sent[k] = sums[mixed ^ (2 * k + 1)]
+
+
+def halve_kernel(a, b, kept, sent):
+    kept[...] = a[0] + b[0].astype(F32)
+    sent[...] = (a[1] + b[1].astype(F32)).astype(sent.dtype)
+
+
+def round_kernel(a, b, out):
+    out[...] = (a[...] + b[...]).astype(BF16)
 
 
 def attend_kernel(
-    lengths, r0, r1, r2, r3, cosine, sine, keys, values, out, projected, turns, spread
+    lengths, near, far, cosine, sine, keys, values, kept, sent, projected, turns, spread, parts
 ):
     my_x = lax.axis_index("gx")
-    my_y = lax.axis_index("gy")
-    for shift, received in enumerate((r0, r1, r2, r3)):
-        at = pl.multiple_of((my_y ^ shift) * QKV_ROWS, 16)
-        projected[pl.ds(at, QKV_ROWS), :] = received[...].astype(F32)
+    for core, pair in enumerate((near, far)):
+        for k in range(2):
+            at = pl.multiple_of((my_x ^ (2 * k + core)) * QKV_ROWS, 16)
+            projected[pl.ds(at, QKV_ROWS), :] = pair[k].astype(F32)
     for t in range(4):
         turns[0, 2 * t : 2 * t + 2, :] = cosine[t % 2]
         turns[1, 2 * t : 2 * t + 2, :] = sine[t % 2]
@@ -270,83 +284,78 @@
         sums += jnp.dot(mine, values[t], preferred_element_type=F32)
     for g in range(KVH):
         at = slice(group_rows * g, group_rows * (g + 1))
-        out[at, :] = sums[at, HD * g : HD * (g + 1)] + added[at]
+        inside = group_rows * (g % 2)
+        parts[g // 2, inside : inside + group_rows, :] = (
+            sums[at, HD * g : HD * (g + 1)] + added[at]
+        )
 
     lane = lax.broadcasted_iota(jnp.int32, (QUERIES, HD), 1)
     sheet = jnp.where(lane == 0, maxima, jnp.where(lane == 1, totals, 0.0))
     flat = jnp.transpose(sheet)[0:8]
-    out[QUERIES : QUERIES + 8, :] = flat[:, :HD]
-    out[QUERIES + 8 : QUERIES + 16, :] = flat[:, HD:]
-
-
-def factor_columns(rows, sheets):
-    columns = []
-    for half in range(2):
-        sheets[half] = jnp.zeros((HD, HD), F32)
+    for q in range(NY):
+        half = flat[:, HD * (q // 2) : HD * (q // 2 + 1)]
+        parts[q, OUT_ROWS:, :] = half if q % 2 == 0 else pltpu.roll(half, OUT_ROWS, 1)
+    for k in range(2):
+        kept[k] = parts[my_x ^ (2 * k)]
+        sent[k] = parts[my_x ^ (2 * k + 1)]
+
+
+def columns_of(rows, sheet):
+    sheet[...] = jnp.zeros_like(sheet)
+    for k, row in enumerate(rows):
+        sheet[k : k + 1, :] = row
+    turned = jnp.transpose(sheet[...])[:OUT_ROWS]
+    return [turned[:, k : k + 1] for k in range(len(rows))]
+
+
+def merge_kernel(a, b, kept, sent, sheet):
+    line = lax.broadcasted_iota(jnp.int32, (8, HD), 0)
+    powers, stats = [], []
+    for k in range(2):
+        a_stats, b_stats = a[k, OUT_ROWS:, :], b[k, OUT_ROWS:, :]
+        highest = jnp.maximum(a_stats[0:1], b_stats[0:1])
+        power_a = jnp.exp(a_stats[0:1] - highest)
+        power_b = jnp.exp(b_stats[0:1] - highest)
+        powers += [power_a, power_b]
+        stats.append((highest, a_stats[1:2] * power_a + b_stats[1:2] * power_b))
+    factors = columns_of(powers, sheet)
+    merged = [
+        a[k, :OUT_ROWS, :] * factors[2 * k] + b[k, :OUT_ROWS, :] * factors[2 * k + 1]
+        for k in range(2)
+    ]
+    kept[:OUT_ROWS, :] = merged[0]
+    kept[OUT_ROWS:, :] = jnp.where(line == 0, stats[0][0], jnp.where(line == 1, stats[0][1], 0.0))
+    sent[:OUT_ROWS, :] = merged[1].astype(BF16)
+    high, rest = high_rest(stats[1][0])
+    middle, low = high_rest(rest)
+    pieces = jnp.zeros((8, HD), F32)
+    for k, piece in enumerate((high, middle, low, *high_rest(stats[1][1]))):
+        pieces = jnp.where(line == k, piece, pieces)
+    sent[OUT_ROWS:, :] = jnp.concatenate([pieces, jnp.zeros_like(pieces)], axis=0).astype(BF16)
+
+
+def settle_kernel(a, b, out, sheet):
+    pieces = b[OUT_ROWS:, :].astype(F32)
+    maximum = (pieces[0:1] + pieces[1:2]) + pieces[2:3]
+    total = pieces[3:4] + pieces[4:5]
+    own_maximum, own_total = a[OUT_ROWS : OUT_ROWS + 1, :], a[OUT_ROWS + 1 : OUT_ROWS + 2, :]
+    highest = jnp.maximum(own_maximum, maximum)
+    power_a = jnp.exp(own_maximum - highest)
+    power_b = jnp.exp(maximum - highest)
+    whole = own_total * power_a + total * power_b
+    factor_a, factor_b = columns_of([power_a / whole, power_b / whole], sheet)
+    out[...] = (a[:OUT_ROWS, :] * factor_a + b[:OUT_ROWS, :].astype(F32) * factor_b).astype(BF16)
+
+
+def output_kernel(near, far, w, kept, sent, blocks, wide, sums):
+    mixed = lax.axis_index("gx") ^ lax.axis_index("gy")
+    for core, pair in enumerate((near, far)):
         for k in range(2):
-            sheets[half, k : k + 1, :] = rows[half][k]
-    turned = [jnp.transpose(sheets[half]) for half in range(2)]
-    for k in range(2):
-        columns.append(
-            jnp.concatenate([turned[half][:, k : k + 1] for half in range(2)], axis=0)
-        )
-    return columns
-
-
-def merge_kernel(a, b, kept, sent, sheets):
-    rows = []
-    for half in range(2):
-        at = QUERIES + 8 * half
-        highest = jnp.maximum(a[at : at + 1, :], b[at : at + 1, :])
-        high, rest = high_rest(highest)
-        middle, low = high_rest(rest)
-        power_a = jnp.exp(a[at : at + 1, :] - highest)
-        power_b = jnp.exp(b[at : at + 1, :] - highest)
-        total = a[at + 1 : at + 2, :] * power_a + b[at + 1 : at + 2, :] * power_b
-        line = lax.broadcasted_iota(jnp.int32, (8, HD), 0)
-        stats = jnp.zeros((8, HD), F32)
-        for k, piece in enumerate((high, middle, low, *high_rest(total))):
-            stats = jnp.where(line == k, piece, stats)
-        kept[at : at + 8, :] = jnp.where(line == 0, highest, jnp.where(line == 1, total, 0.0))
-        sheets[half, 0:8, :] = stats
-        rows.append((power_a, power_b))
-    sent[QUERIES : QUERIES + 16, :] = jnp.concatenate(
-        [sheets[0, 0:8, :], sheets[1, 0:8, :]], axis=0
-    ).astype(BF16)
-    factor_a, factor_b = factor_columns(rows, sheets)
-    merged = a[:QUERIES, :] * factor_a + b[:QUERIES, :] * factor_b
-    kept[:QUERIES, :] = merged
-    sent[:QUERIES, :] = merged.astype(BF16)
-
-
-def settle_kernel(a, b, o0, o1, o2, o3, attended, sheets):
-    my_y = lax.axis_index("gy")
-    other = b[QUERIES : QUERIES + 16, :].astype(F32)
-    rows = []
-    for half in range(2):
-        at = QUERIES + 8 * half
-        stats = other[8 * half : 8 * half + 8]
-        maximum = (stats[0:1] + stats[1:2]) + stats[2:3]
-        total = stats[3:4] + stats[4:5]
-        own_maximum, own_total = a[at : at + 1, :], a[at + 1 : at + 2, :]
-        highest = jnp.maximum(own_maximum, maximum)
-        power_a = jnp.exp(own_maximum - highest)
-        power_b = jnp.exp(maximum - highest)
-        whole = own_total * power_a + total * power_b
-        rows.append((power_a / whole, power_b / whole))
-    factor_a, factor_b = factor_columns(rows, sheets)
-    attended[...] = a[:QUERIES, :] * factor_a + b[:QUERIES, :].astype(F32) * factor_b
-    for shift, out in enumerate((o0, o1, o2, o3)):
-        at = pl.multiple_of((my_y ^ shift) * OUT_ROWS, OUT_ROWS)
-        out[...] = attended[pl.ds(at, OUT_ROWS), :].astype(BF16)
-
-
-def output_kernel(a0, a1, a2, a3, w, o0, o1, o2, o3, wide, sums):
-    for shift, attended in enumerate((a0, a1, a2, a3)):
-        block = attended[...].astype(F32)
+            blocks[mixed ^ (2 * k + core)] = pair[k].astype(F32)
+    for shift in range(NY):
         for head in range(OUT_HEADS):
-            wide[ROWS * shift : ROWS * (shift + 1), HD * head : HD * (head + 1)] = block[
-                ROWS * head : ROWS * (head + 1)
+            wide[ROWS * shift : ROWS * (shift + 1), HD * head : HD * (head + 1)] = blocks[
+                shift, ROWS * head : ROWS * (head + 1), :
             ]
     left = wide[...].astype(BF16)
     width = 512
@@ -358,13 +367,13 @@
                 sums[shift, at : at + ROWS, :] = part[
                     ROWS * shift : ROWS * (shift + 1), HD * chunk : HD * (chunk + 1)
                 ]
-    o0[...] = sums[0]
-    for shift, out in ((1, o1), (2, o2), (3, o3)):
-        out[...] = sums[shift].astype(BF16)
-
-
-def finish_kernel(a, b, c, d, out, total):
-    total[...] = (a[...] + b[...].astype(F32)) + (c[...].astype(F32) + d[...].astype(F32))
+    for k in range(2):
+        kept[k] = sums[k]
+        sent[k] = sums[2 + k].astype(BF16)
+
+
+def finish_kernel(a, b, out, total):
+    total[...] = a[...] + b[...].astype(F32)
     for chunk in range(out.shape[2] // HD):
         for timeline in range(2):
             at = ROWS * chunk + 2 * timeline
@@ -381,48 +390,69 @@
 
 
 def partner(part, axis, distance):
-    if distance == 0:
-        return part
     return lax.ppermute(part, axis, [(k, k ^ distance) for k in range(lax.axis_size(axis))])
+
+
+def swapped(part):
+    pairs = [(x * NY + y, y * NY + x) for x in range(NX) for y in range(NY)]
+    return lax.ppermute(part, ("gx", "gy"), pairs)
+
+
+def paired(part, axis, distance):
+    return call(
+        pair_kernel,
+        "pair",
+        jax.ShapeDtypeStruct((2, *part.shape), part.dtype),
+        [part, partner(part, axis, distance)],
+    )
 
 
 def small_body(hidden, norm_gain, w_qkv, w_out, k_cache, v_cache, cache_len, positions):
     def shape(*dims, dtype=BF16):
         return jax.ShapeDtypeStruct(dims, dtype)
 
+    def pinned(array):
+        return pltpu.with_memory_space_constraint(array, pltpu.VMEM)
+
     columns = w_out.shape[1]
     features = hidden.shape[2]
-    w_qkv = pltpu.with_memory_space_constraint(w_qkv, pltpu.VMEM)
-    k_cache = pltpu.with_memory_space_constraint(k_cache, pltpu.VMEM)
-    v_cache = pltpu.with_memory_space_constraint(v_cache, pltpu.VMEM)
-    w_out = pltpu.with_memory_space_constraint(w_out, pltpu.VMEM)
+    count = columns // HD * ROWS
+    w_qkv, w_out, k_cache, v_cache = map(pinned, (w_qkv, w_out, k_cache, v_cache))
     cosine, sine = rotation(positions)
-    hiddens = [partner(hidden, "gy", y) for y in range(NY)]
-    squares = call(square_kernel, "square", shape(NY * ROWS, HD, dtype=F32), hiddens)
-    squares = [partner(squares, "gx", x) for x in range(NX)]
-    sums = call(
+
+    near = paired(hidden, "gy", 1)
+    far = partner(near, "gy", 2)
+    squares = call(
+        square_kernel, "square", shape(NY * ROWS, HD, dtype=F32), [near, far]
+    )
+    squares = call(
+        add_kernel, "add", shape(NY * ROWS, HD, dtype=F32), [squares, partner(squares, "gx", 1)]
+    )
+    half = shape(2, QKV_ROWS, HD, dtype=F32)
+    kept, sent = call(
         project_kernel,
         "project",
-        shape(NY, QKV_ROWS, HD, dtype=F32),
-        [*hiddens, *squares, norm_gain[None], w_qkv],
-        [pltpu.VMEM((NY * ROWS, features), F32)],
-    )
-    sums = call(
-        add_kernel, "add", shape(NY, QKV_ROWS, HD, dtype=F32), [sums, partner(sums, "gx", 1)]
-    )
-    blocks = call(
-        round_kernel, "round", [shape(QKV_ROWS, HD)] * NY, [sums, partner(sums, "gx", 2)]
-    )
-    blocks = [partner(block, "gy", y) for y, block in enumerate(blocks)]
-    partial = call(
+        [half, half],
+        [near, far, squares, partner(squares, "gx", 2), norm_gain[None], w_qkv],
+        [pltpu.VMEM((NY * ROWS, features), F32), pltpu.VMEM((NY, QKV_ROWS, HD), F32)],
+    )
+    quarter = shape(QKV_ROWS, HD, dtype=F32)
+    kept, sent = call(halve_kernel, "halve", [quarter, quarter], [kept, partner(sent, "gx", 1)])
+    block = call(round_kernel, "round", shape(QKV_ROWS, HD), [kept, partner(sent, "gx", 2)])
+    near = paired(swapped(block), "gx", 2)
+    far = partner(near, "gx", 1)
+
+    half = shape(2, OUT_ROWS + 8, HD, dtype=F32)
+    kept, sent = call(
         attend_kernel,
         "attend",
-        shape(QUERIES + 16, HD, dtype=F32),
-        [cache_len, *blocks, cosine, sine, k_cache, v_cache],
+        [half, half],
+        [cache_len, near, far, cosine, sine, k_cache, v_cache],
         [
             pltpu.VMEM((NY * QKV_ROWS, HD), F32),
             pltpu.VMEM((2, 8, HD), F32),
             pltpu.VMEM((2, QUERIES, KVH * HD), BF16),
+            pltpu.VMEM((NY, OUT_ROWS + 8, HD), F32),
         ],
         scalars=1,
         mib=16,
@@ -430,35 +460,42 @@
     kept, sent = call(
         merge_kernel,
         "merge",
-        [shape(QUERIES + 16, HD, dtype=F32), shape(QUERIES + 16, HD)],
-        [partial, partner(partial, "gx", 1)],
-        [pltpu.VMEM((2, HD, HD), F32)],
-    )
-    blocks = call(
+        [shape(OUT_ROWS + 8, HD, dtype=F32), shape(OUT_ROWS + 16, HD)],
+        [kept, partner(sent, "gx", 1)],
+        [pltpu.VMEM((HD, HD), F32)],
+    )
+    block = call(
         settle_kernel,
         "settle",
-        [shape(OUT_ROWS, HD)] * NY,
+        shape(OUT_ROWS, HD),
         [kept, partner(sent, "gx", 2)],
-        [pltpu.VMEM((QUERIES, HD), F32), pltpu.VMEM((2, HD, HD), F32)],
-    )
-    blocks = [partner(block, "gy", y) for y, block in enumerate(blocks)]
-    count = columns // HD * ROWS
-    blocks = call(
+        [pltpu.VMEM((HD, HD), F32)],
+    )
+    near = paired(swapped(block), "gx", 2)
+    far = partner(near, "gx", 1)
+
+    kept, sent = call(
         output_kernel,
         "output",
-        [shape(count, HD, dtype=F32)] + [shape(count, HD)] * (NY - 1),
-        [*blocks, w_out],
+        [shape(2, count, HD, dtype=F32), shape(2, count, HD)],
+        [near, far, w_out],
         [
+            pltpu.VMEM((NY, OUT_ROWS, HD), F32),
             pltpu.VMEM((NY * ROWS, w_out.shape[0]), F32),
             pltpu.VMEM((NY, count, HD), F32),
         ],
     )
-    blocks = [partner(block, "gy", y) for y, block in enumerate(blocks)]
+    kept, sent = call(
+        halve_kernel,
+        "halve",
+        [shape(count, HD, dtype=F32), shape(count, HD)],
+        [kept, partner(sent, "gy", 2)],
+    )
     return call(
         finish_kernel,
         "finish",
         shape(2, 2, columns),
-        blocks,
+        [kept, partner(sent, "gy", 1)],
         [pltpu.VMEM((count, HD), F32)],
     )
 

time: 64.1 us -> 72.1 us (1.12)
  starting transfers between devices: 22.5 us -> 36.6 us
  waiting for transfers between devices: 28.5 us -> 21.7 us
    ppermute x19 -> x14, starting transfers between devices: 22.5 us -> 35.3 us  [partner(): lax.ppermute(part, axis, [(k, k ^ distance) for k in range(lax.axis_size(...]
    ppermute x19 -> x14, waiting for transfers between devices: 28.5 us -> 21.7 us  [partner(): lax.ppermute(part, axis, [(k, k ^ distance) for k in range(lax.axis_size(...]
    ppermute x0 -> x2, starting transfers between devices: none -> 1.32 us  [swapped(): return lax.ppermute(part, ('gx', 'gy'), pairs)]
    unnamed x16 -> x14, local copies, waits for them, and re-layouts: 5.43 us -> 6.12 us
    pallas_call x9 -> x14, Pallas kernels: 6.32 us -> 6.33 us  [call(): pl.pallas_call(kernel, in_specs=[SMEM_SPEC] * scalars + [VMEM_SPEC] * (le...]
  transfers between devices with their start and end apart: 19 -> 16, of which waited for: 14 -> 14; matrix products, arithmetic and copies ran while one was open for 2% -> 1% of each run, Pallas kernels for 0% -> 0%
where the time goes in v2:
time: 72.1 us; the launch traced here: 71.8 us
  starting transfers between devices  36.6 us (51%)
  waiting for transfers between devices  21.7 us (30%)
  local copies, waits for them, and re-layouts  6.81 us (9%)
  Pallas kernels  6.33 us (9%)
    ppermute x14, starting transfers between devices, partner(): lax.ppermute(part, axis, [(k, k ^ distance) for k in range(lax.axis_size(...  35.3 us
    ppermute x14, waiting for transfers between devices, partner(): lax.ppermute(part, axis, [(k, k ^ distance) for k in range(lax.axis_size(...  21.7 us
    pallas_call x14, Pallas kernels, call(): pl.pallas_call(kernel, in_specs=[SMEM_SPEC] * scalars + [VMEM_SPEC] * (le...  6.33 us
    unnamed x14, local copies, waits for them, and re-layouts  6.12 us
  transfers between devices with their start and end apart: 16, of which 14 were waited for; matrix products, arithmetic and copies ran while one was open for 1% of the time, Pallas kernels for 0%

profile of v2, /device:TPU:0, one launch (start us, length us, event | category | flops | bytes accessed | tf_op | source)
XLA Modules:
  0.0 71.8 jit_solution(14342707675094215562)
XLA Ops:
  0.0 3.0 %collective-permute-start = (bf16[2,2,2048]{2,1,0:T(2,128)(2,1)}, bf16[2,2,2048]{2,1,0:T(2,128)(2,1)S(1)}, u32[]{:S(2)}, u32[]{:S(2)}) collective-permute-start(bf16[2,2,2048]{2,1,0:T(2,128)(2,1)} %own.1), channel_id=1, source_target_pairs={{0,1},{1,0},{2,3},{3,2},{4,5},{5,4},{6,7},{7,6},{8,9},{9,8},{10,11... | collective-permute-start | bytes 49160 | tf_op jit(solution)/shard_map/ppermute | solution.py:393
  3.0 1.9 %collective-permute-done.other = bf16[2,2,2048]{2,1,0:T(2,128)(2,1)S(1)} collective-permute-done((bf16[2,2,2048]{2,1,0:T(2,128)(2,1)}, bf16[2,2,2048]{2,1,0:T(2,128)(2,1)S(1)}, u32[]{:S(2)}, u32[]{:S(2)}) %collective-permute-start) | collective-permute-done | bytes 16416 | tf_op jit(solution)/shard_map/ppermute | solution.py:393
  5.7 3.1 %collective-permute-start.1 = (bf16[2,2,2,2048]{3,2,1,0:T(2,128)(2,1)S(1)}, bf16[2,2,2,2048]{3,2,1,0:T(2,128)(2,1)S(1)}, u32[]{:S(2)}, u32[]{:S(2)}) collective-permute-start(bf16[2,2,2,2048]{3,2,1,0:T(2,128)(2,1)S(1)} %pair.3.near), channel_id=1, source_target_pairs={{0,2},{1,3},{2,0},{3,1},{4,6},{5,7},{6,4},{7,5},{8,10},{9,11},{10,... | collective-permute-start | bytes 98312 | tf_op jit(solution)/shard_map/ppermute | solution.py:393
  8.8 1.9 %collective-permute-done.1.far = bf16[2,2,2,2048]{3,2,1,0:T(2,128)(2,1)S(1)} collective-permute-done((bf16[2,2,2,2048]{3,2,1,0:T(2,128)(2,1)S(1)}, bf16[2,2,2,2048]{3,2,1,0:T(2,128)(2,1)S(1)}, u32[]{:S(2)}, u32[]{:S(2)}) %collective-permute-start.1) | collective-permute-done | bytes 32800 | tf_op jit(solution)/shard_map/ppermute | solution.py:393
  12.0 1.8 %collective-permute-start.3 = (f32[16,128]{1,0:T(8,128)S(1)}, f32[16,128]{1,0:T(8,128)S(1)}, u32[]{:S(2)}, u32[]{:S(2)}) collective-permute-start(f32[16,128]{1,0:T(8,128)S(1)} %add.24.s0), channel_id=1, source_target_pairs={{0,8},{4,12},{8,0},{12,4},{1,9},{5,13},{9,1},{13,5},{2,10},{6,14},... | collective-permute-start | bytes 24584 | tf_op jit(solution)/shard_map/ppermute | solution.py:393
  15.7 4.0 %copy-done = bf16[2048,2560]{1,0:T(8,128)(2,1)S(1)} copy-done((bf16[2048,2560]{1,0:T(8,128)(2,1)S(1)}, bf16[2048,2560]{1,0:T(8,128)(2,1)}, u32[]{:S(2)}) %copy-start) | copy-done | bytes 10485784
  19.6 1.5 %project.1 = (f32[2,80,128]{2,1,0:T(8,128)S(1)}, f32[2,80,128]{2,1,0:T(8,128)S(1)}) custom-call(bf16[2,2,2,2048]{3,2,1,0:T(2,128)(2,1)S(1)} %pair.3.near, bf16[2,2,2,2048]{3,2,1,0:T(2,128)(2,1)S(1)} %collective-permute-done.1.far, f32[16,128]{1,0:T(8,128)S(1)} %add.24.s0, f32[16,128]{1,0:T(8,128)S(1)} %collective-permute-done.3.s1, ...), custom_call_target="tpu_custom_call" | custom-call | tf_op jit(solution)/shard_map/project/pallas_call | solution.py:152
  21.3 1.3 %collective-permute-done.4.b = f32[2,80,128]{2,1,0:T(8,128)S(1)} collective-permute-done((f32[2,80,128]{2,1,0:T(8,128)S(1)}, f32[2,80,128]{2,1,0:T(8,128)S(1)}, u32[]{:S(2)}, u32[]{:S(2)}) %collective-permute-start.4) | collective-permute-done | bytes 81952 | tf_op jit(solution)/shard_map/ppermute | solution.py:393
  22.5 1.9 %collective-permute-start.5 = (f32[80,128]{1,0:T(8,128)S(1)}, f32[80,128]{1,0:T(8,128)S(1)}, u32[]{:S(2)}, u32[]{:S(2)}) collective-permute-start(f32[80,128]{1,0:T(8,128)S(1)} %get-tuple-element.20), channel_id=1, source_target_pairs={{0,8},{4,12},{8,0},{12,4},{1,9},{5,13},{9,1},{13,5},{2,10},{6,14},... | collective-permute-start | bytes 122888 | tf_op jit(solution)/shard_map/ppermute | solution.py:393
  24.5 2.1 %collective-permute-done.5.b = f32[80,128]{1,0:T(8,128)S(1)} collective-permute-done((f32[80,128]{1,0:T(8,128)S(1)}, f32[80,128]{1,0:T(8,128)S(1)}, u32[]{:S(2)}, u32[]{:S(2)}) %collective-permute-start.5) | collective-permute-done | bytes 40992 | tf_op jit(solution)/shard_map/ppermute | solution.py:393
  27.3 8.8 %collective-permute-start.7 = (bf16[80,128]{1,0:T(8,128)(2,1)S(1)}, bf16[80,128]{1,0:T(8,128)(2,1)S(1)}, u32[]{:S(2)}, u32[]{:S(2)}) collective-permute-start(bf16[80,128]{1,0:T(8,128)(2,1)S(1)} %collective-permute-done.6.own), channel_id=1, source_target_pairs={{0,8},{4,12},{8,0},{12,4},{1,9},{5,13},{9,1},{13,5},{2,10},{6,14},... | collective-permute-start | bytes 61448 | tf_op jit(solution)/shard_map/ppermute | solution.py:393
  36.2 1.6 %collective-permute-done.7.other = bf16[80,128]{1,0:T(8,128)(2,1)S(1)} collective-permute-done((bf16[80,128]{1,0:T(8,128)(2,1)S(1)}, bf16[80,128]{1,0:T(8,128)(2,1)S(1)}, u32[]{:S(2)}, u32[]{:S(2)}) %collective-permute-start.7) | collective-permute-done | bytes 20512 | tf_op jit(solution)/shard_map/ppermute | solution.py:393
  39.1 1.4 %copy-done.3 = bf16[2,384,1024]{2,1,0:T(8,128)(2,1)S(1)} copy-done((bf16[2,384,1024]{2,1,0:T(8,128)(2,1)S(1)}, bf16[2,384,1024]{2,1,0:T(8,128)(2,1)}, u32[]{:S(2)}) %copy-start.3) | copy-done | bytes 1572888
  40.5 2.3 %attend.1 = (f32[2,72,128]{2,1,0:T(8,128)S(1)}, f32[2,72,128]{2,1,0:T(8,128)S(1)}) custom-call(s32[2]{0:T(128)S(1)} %copy-done.5, bf16[2,80,128]{2,1,0:T(8,128)(2,1)S(1)} %pair.4.near, bf16[2,80,128]{2,1,0:T(8,128)(2,1)S(1)} %collective-permute-done.8.far, f32[2,2,128]{2,1,0:T(2,128)S(1)} %get-tuple-element.32.cosine, ...), custom_call_target="tpu_custom_call" | custom-call | tf_op jit(solution)/shard_map/attend/pallas_call | solution.py:152
  44.4 2.1 %collective-permute-start.10 = (bf16[80,128]{1,0:T(8,128)(2,1)S(1)}, bf16[80,128]{1,0:T(8,128)(2,1)S(1)}, u32[]{:S(2)}, u32[]{:S(2)}) collective-permute-start(bf16[80,128]{1,0:T(8,128)(2,1)S(1)} %get-tuple-element.24), channel_id=1, source_target_pairs={{0,8},{4,12},{8,0},{12,4},{1,9},{5,13},{9,1},{13,5},{2,10},{6,14},... | collective-permute-start | bytes 61448 | tf_op jit(solution)/shard_map/ppermute | solution.py:393
  46.5 1.8 %collective-permute-done.10.b = bf16[80,128]{1,0:T(8,128)(2,1)S(1)} collective-permute-done((bf16[80,128]{1,0:T(8,128)(2,1)S(1)}, bf16[80,128]{1,0:T(8,128)(2,1)S(1)}, u32[]{:S(2)}, u32[]{:S(2)}) %collective-permute-start.10) | collective-permute-done | bytes 20512 | tf_op jit(solution)/shard_map/ppermute | solution.py:393
  49.2 8.8 %collective-permute-start.12 = (bf16[64,128]{1,0:T(8,128)(2,1)S(1)}, bf16[64,128]{1,0:T(8,128)(2,1)S(1)}, u32[]{:S(2)}, u32[]{:S(2)}) collective-permute-start(bf16[64,128]{1,0:T(8,128)(2,1)S(1)} %collective-permute-done.11.own), channel_id=1, source_target_pairs={{0,8},{4,12},{8,0},{12,4},{1,9},{5,13},{9,1},{13,5},{2,10},{6,14},... | collective-permute-start | bytes 49160 | tf_op jit(solution)/shard_map/ppermute | solution.py:393
  57.9 1.7 %collective-permute-done.12.other = bf16[64,128]{1,0:T(8,128)(2,1)S(1)} collective-permute-done((bf16[64,128]{1,0:T(8,128)(2,1)S(1)}, bf16[64,128]{1,0:T(8,128)(2,1)S(1)}, u32[]{:S(2)}, u32[]{:S(2)}) %collective-permute-start.12) | collective-permute-done | bytes 16416 | tf_op jit(solution)/shard_map/ppermute | solution.py:393
  59.7 1.2 %collective-permute-done.13.far = bf16[2,64,128]{2,1,0:T(8,128)(2,1)S(1)} collective-permute-done((bf16[2,64,128]{2,1,0:T(8,128)(2,1)S(1)}, bf16[2,64,128]{2,1,0:T(8,128)(2,1)S(1)}, u32[]{:S(2)}, u32[]{:S(2)}) %collective-permute-start.13) | collective-permute-done | bytes 32800 | tf_op jit(solution)/shard_map/ppermute | solution.py:393
  60.9 1.2 %output.1 = (f32[2,64,128]{2,1,0:T(8,128)S(1)}, bf16[2,64,128]{2,1,0:T(8,128)(2,1)S(1)}) custom-call(bf16[2,64,128]{2,1,0:T(8,128)(2,1)S(1)} %pair.5.near, bf16[2,64,128]{2,1,0:T(8,128)(2,1)S(1)} %collective-permute-done.13.far, bf16[2048,2048]{1,0:T(8,128)(2,1)S(1)} %copy-done.1), custom_call_target="tpu_custom_call" | custom-call | tf_op jit(solution)/shard_map/output/pallas_call | solution.py:152
  62.1 3.0 %collective-permute-start.14 = (bf16[2,64,128]{2,1,0:T(8,128)(2,1)S(1)}, bf16[2,64,128]{2,1,0:T(8,128)(2,1)S(1)}, u32[]{:S(2)}, u32[]{:S(2)}) collective-permute-start(bf16[2,64,128]{2,1,0:T(8,128)(2,1)S(1)} %get-tuple-element.26), channel_id=1, source_target_pairs={{0,2},{1,3},{2,0},{3,1},{4,6},{5,7},{6,4},{7,5},{8,10},{9,11},{10,... | collective-permute-start | bytes 98312 | tf_op jit(solution)/shard_map/ppermute | solution.py:393
  65.1 1.9 %collective-permute-done.14.b = bf16[2,64,128]{2,1,0:T(8,128)(2,1)S(1)} collective-permute-done((bf16[2,64,128]{2,1,0:T(8,128)(2,1)S(1)}, bf16[2,64,128]{2,1,0:T(8,128)(2,1)S(1)}, u32[]{:S(2)}, u32[]{:S(2)}) %collective-permute-start.14) | collective-permute-done | bytes 32800 | tf_op jit(solution)/shard_map/ppermute | solution.py:393
  67.0 2.5 %collective-permute-start.15 = (bf16[64,128]{1,0:T(8,128)(2,1)S(1)}, bf16[64,128]{1,0:T(8,128)(2,1)S(1)}, u32[]{:S(2)}, u32[]{:S(2)}) collective-permute-start(bf16[64,128]{1,0:T(8,128)(2,1)S(1)} %get-tuple-element.28), channel_id=1, source_target_pairs={{0,1},{1,0},{2,3},{3,2},{4,5},{5,4},{6,7},{7,6},{8,9},{9,8},{10,11... | collective-permute-start | bytes 49160 | tf_op jit(solution)/shard_map/ppermute | solution.py:393
  69.5 1.7 %collective-permute-done.15.b = bf16[64,128]{1,0:T(8,128)(2,1)S(1)} collective-permute-done((bf16[64,128]{1,0:T(8,128)(2,1)S(1)}, bf16[64,128]{1,0:T(8,128)(2,1)S(1)}, u32[]{:S(2)}, u32[]{:S(2)}) %collective-permute-start.15) | collective-permute-done | bytes 16416 | tf_op jit(solution)/shard_map/ppermute | solution.py:393
  (41 shorter events, 9.1 us)
Async XLA Ops:
  0.0 5.0 %collective-permute-start = (bf16[2,2,2048]{2,1,0:T(2,128)(2,1)}, bf16[2,2,2048]{2,1,0:T(2,128)(2,1)S(1)}, u32[]{:S(2)}, u32[]{:S(2)}) collective-permute-start(bf16[2,2,2048]{2,1,0:T(2,128)(2,1)} %own.1), channel_id=1, source_target_pairs={{0,1},{1,0},{2,3},{3,2},{4,5},{5,4},{6,7},{7,6},{8,9},{9,8},{10,11... | collective-permute-start | bytes 49160 | tf_op jit(solution)/shard_map/ppermute | solution.py:393
  5.0 0.7 copy-start.4
  5.7 18.8 %copy-start.6 = (s32[2]{0:T(128)S(1)}, s32[2]{0:T(128)}, u32[]{:S(2)}) copy-start(s32[2]{0:T(128)} %param.15) | copy-start | bytes 28
  5.7 33.4 %copy-start.5 = (s32[2]{0:T(128)S(1)}, s32[2]{0:T(128)}, u32[]{:S(2)}) copy-start(s32[2]{0:T(128)} %lengths.1) | copy-start | bytes 28
  5.7 5.0 %collective-permute-start.1 = (bf16[2,2,2,2048]{3,2,1,0:T(2,128)(2,1)S(1)}, bf16[2,2,2,2048]{3,2,1,0:T(2,128)(2,1)S(1)}, u32[]{:S(2)}, u32[]{:S(2)}) collective-permute-start(bf16[2,2,2,2048]{3,2,1,0:T(2,128)(2,1)S(1)} %pair.3.near), channel_id=1, source_target_pairs={{0,2},{1,3},{2,0},{3,1},{4,6},{5,7},{6,4},{7,5},{8,10},{9,11},{10,... | collective-permute-start | bytes 98312 | tf_op jit(solution)/shard_map/ppermute | solution.py:393
  10.8 1.2 %collective-permute-start.2 = (f32[16,128]{1,0:T(8,128)S(1)}, f32[16,128]{1,0:T(8,128)S(1)}, u32[]{:S(2)}, u32[]{:S(2)}) collective-permute-start(f32[16,128]{1,0:T(8,128)S(1)} %square.1.a), channel_id=1, source_target_pairs={{0,4},{4,0},{8,12},{12,8},{1,5},{5,1},{9,13},{13,9},{2,6},{6,2},{1... | collective-permute-start | bytes 24584 | tf_op jit(solution)/shard_map/ppermute | solution.py:393
  12.0 3.7 %collective-permute-start.3 = (f32[16,128]{1,0:T(8,128)S(1)}, f32[16,128]{1,0:T(8,128)S(1)}, u32[]{:S(2)}, u32[]{:S(2)}) collective-permute-start(f32[16,128]{1,0:T(8,128)S(1)} %add.24.s0), channel_id=1, source_target_pairs={{0,8},{4,12},{8,0},{12,4},{1,9},{5,13},{9,1},{13,5},{2,10},{6,14},... | collective-permute-start | bytes 24584 | tf_op jit(solution)/shard_map/ppermute | solution.py:393
  15.7 4.0 %copy-start = (bf16[2048,2560]{1,0:T(8,128)(2,1)S(1)}, bf16[2048,2560]{1,0:T(8,128)(2,1)}, u32[]{:S(2)}) copy-start(bf16[2048,2560]{1,0:T(8,128)(2,1)} %w.2) | copy-start | bytes 31457284
  19.6 19.5 %copy-start.2 = (bf16[2,384,1024]{2,1,0:T(8,128)(2,1)S(1)}, bf16[2,384,1024]{2,1,0:T(8,128)(2,1)}, u32[]{:S(2)}) copy-start(bf16[2,384,1024]{2,1,0:T(8,128)(2,1)} %keys.1) | copy-start | bytes 4718596
  19.6 41.2 %copy-start.1 = (bf16[2048,2048]{1,0:T(8,128)(2,1)S(1)}, bf16[2048,2048]{1,0:T(8,128)(2,1)}, u32[]{:S(2)}) copy-start(bf16[2048,2048]{1,0:T(8,128)(2,1)} %w.3) | copy-start | bytes 25165828
  21.2 1.3 %collective-permute-start.4 = (f32[2,80,128]{2,1,0:T(8,128)S(1)}, f32[2,80,128]{2,1,0:T(8,128)S(1)}, u32[]{:S(2)}, u32[]{:S(2)}) collective-permute-start(f32[2,80,128]{2,1,0:T(8,128)S(1)} %get-tuple-element.18), channel_id=1, source_target_pairs={{0,4},{4,0},{8,12},{12,8},{1,5},{5,1},{9,13},{13,9},{2,6},{6,2},{1... | collective-permute-start | bytes 245768 | tf_op jit(solution)/shard_map/ppermute | solution.py:393
  22.5 4.1 %collective-permute-start.5 = (f32[80,128]{1,0:T(8,128)S(1)}, f32[80,128]{1,0:T(8,128)S(1)}, u32[]{:S(2)}, u32[]{:S(2)}) collective-permute-start(f32[80,128]{1,0:T(8,128)S(1)} %get-tuple-element.20), channel_id=1, source_target_pairs={{0,8},{4,12},{8,0},{12,4},{1,9},{5,13},{9,1},{13,5},{2,10},{6,14},... | collective-permute-start | bytes 122888 | tf_op jit(solution)/shard_map/ppermute | solution.py:393
  26.6 0.7 collective-permute-start.6
  27.3 10.6 %collective-permute-start.7 = (bf16[80,128]{1,0:T(8,128)(2,1)S(1)}, bf16[80,128]{1,0:T(8,128)(2,1)S(1)}, u32[]{:S(2)}, u32[]{:S(2)}) collective-permute-start(bf16[80,128]{1,0:T(8,128)(2,1)S(1)} %collective-permute-done.6.own), channel_id=1, source_target_pairs={{0,8},{4,12},{8,0},{12,4},{1,9},{5,13},{9,1},{13,5},{2,10},{6,14},... | collective-permute-start | bytes 61448 | tf_op jit(solution)/shard_map/ppermute | solution.py:393
  37.9 1.2 %collective-permute-start.8 = (bf16[2,80,128]{2,1,0:T(8,128)(2,1)S(1)}, bf16[2,80,128]{2,1,0:T(8,128)(2,1)S(1)}, u32[]{:S(2)}, u32[]{:S(2)}) collective-permute-start(bf16[2,80,128]{2,1,0:T(8,128)(2,1)S(1)} %pair.4.near), channel_id=1, source_target_pairs={{0,4},{4,0},{8,12},{12,8},{1,5},{5,1},{9,13},{13,9},{2,6},{6,2},{1... | collective-permute-start | bytes 122888 | tf_op jit(solution)/shard_map/ppermute | solution.py:393
  39.1 1.4 %copy-start.3 = (bf16[2,384,1024]{2,1,0:T(8,128)(2,1)S(1)}, bf16[2,384,1024]{2,1,0:T(8,128)(2,1)}, u32[]{:S(2)}) copy-start(bf16[2,384,1024]{2,1,0:T(8,128)(2,1)} %values.1) | copy-start | bytes 4718596
  42.9 1.3 %collective-permute-start.9 = (f32[2,72,128]{2,1,0:T(8,128)S(1)}, f32[2,72,128]{2,1,0:T(8,128)S(1)}, u32[]{:S(2)}, u32[]{:S(2)}) collective-permute-start(f32[2,72,128]{2,1,0:T(8,128)S(1)} %get-tuple-element.22), channel_id=1, source_target_pairs={{0,4},{4,0},{8,12},{12,8},{1,5},{5,1},{9,13},{13,9},{2,6},{6,2},{1... | collective-permute-start | bytes 221192 | tf_op jit(solution)/shard_map/ppermute | solution.py:393
  44.4 3.8 %collective-permute-start.10 = (bf16[80,128]{1,0:T(8,128)(2,1)S(1)}, bf16[80,128]{1,0:T(8,128)(2,1)S(1)}, u32[]{:S(2)}, u32[]{:S(2)}) collective-permute-start(bf16[80,128]{1,0:T(8,128)(2,1)S(1)} %get-tuple-element.24), channel_id=1, source_target_pairs={{0,8},{4,12},{8,0},{12,4},{1,9},{5,13},{9,1},{13,5},{2,10},{6,14},... | collective-permute-start | bytes 61448 | tf_op jit(solution)/shard_map/ppermute | solution.py:393
  48.5 0.7 collective-permute-start.11
  49.2 10.5 %collective-permute-start.12 = (bf16[64,128]{1,0:T(8,128)(2,1)S(1)}, bf16[64,128]{1,0:T(8,128)(2,1)S(1)}, u32[]{:S(2)}, u32[]{:S(2)}) collective-permute-start(bf16[64,128]{1,0:T(8,128)(2,1)S(1)} %collective-permute-done.11.own), channel_id=1, source_target_pairs={{0,8},{4,12},{8,0},{12,4},{1,9},{5,13},{9,1},{13,5},{2,10},{6,14},... | collective-permute-start | bytes 49160 | tf_op jit(solution)/shard_map/ppermute | solution.py:393
  59.7 1.2 %collective-permute-start.13 = (bf16[2,64,128]{2,1,0:T(8,128)(2,1)S(1)}, bf16[2,64,128]{2,1,0:T(8,128)(2,1)S(1)}, u32[]{:S(2)}, u32[]{:S(2)}) collective-permute-start(bf16[2,64,128]{2,1,0:T(8,128)(2,1)S(1)} %pair.5.near), channel_id=1, source_target_pairs={{0,4},{4,0},{8,12},{12,8},{1,5},{5,1},{9,13},{13,9},{2,6},{6,2},{1... | collective-permute-start | bytes 98312 | tf_op jit(solution)/shard_map/ppermute | solution.py:393
  62.1 4.9 %collective-permute-start.14 = (bf16[2,64,128]{2,1,0:T(8,128)(2,1)S(1)}, bf16[2,64,128]{2,1,0:T(8,128)(2,1)S(1)}, u32[]{:S(2)}, u32[]{:S(2)}) collective-permute-start(bf16[2,64,128]{2,1,0:T(8,128)(2,1)S(1)} %get-tuple-element.26), channel_id=1, source_target_pairs={{0,2},{1,3},{2,0},{3,1},{4,6},{5,7},{6,4},{7,5},{8,10},{9,11},{10,... | collective-permute-start | bytes 98312 | tf_op jit(solution)/shard_map/ppermute | solution.py:393
  67.0 4.2 %collective-permute-start.15 = (bf16[64,128]{1,0:T(8,128)(2,1)S(1)}, bf16[64,128]{1,0:T(8,128)(2,1)S(1)}, u32[]{:S(2)}, u32[]{:S(2)}) collective-permute-start(bf16[64,128]{1,0:T(8,128)(2,1)S(1)} %get-tuple-element.28), channel_id=1, source_target_pairs={{0,1},{1,0},{2,3},{3,2},{4,5},{5,4},{6,7},{7,6},{8,9},{9,8},{10,11... | collective-permute-start | bytes 49160 | tf_op jit(solution)/shard_map/ppermute | solution.py:393

commit v3 on v1

--- a/solution.py
+++ b/solution.py
@@ -1,3 +1,5 @@
+import functools
+
 import jax
 import jax.numpy as jnp
 from jax import lax
@@ -163,6 +165,32 @@
 def high_rest(values):
     high = values.astype(BF16).astype(F32)
     return high, values - high
+
+
+def fetch_kernel(count, *refs):
+    sources, outs, done = refs[:count], refs[count : 2 * count], refs[2 * count]
+    copies = [
+        pltpu.make_async_copy(source, out, done.at[k])
+        for k, (source, out) in enumerate(zip(sources, outs))
+    ]
+    for copy in copies:
+        copy.start()
+    for copy in copies:
+        copy.wait()
+
+
+def fetch(*arrays):
+    size = sum(array.size * array.dtype.itemsize for array in arrays)
+    return pl.pallas_call(
+        functools.partial(fetch_kernel, len(arrays)),
+        in_specs=[pl.BlockSpec(memory_space=pltpu.HBM)] * len(arrays),
+        out_specs=[VMEM_SPEC] * len(arrays),
+        out_shape=[pltpu.VMEM(array.shape, array.dtype) for array in arrays],
+        scratch_shapes=[pltpu.SemaphoreType.DMA((len(arrays),))],
+        compiler_params=pltpu.CompilerParams(vmem_limit_bytes=1 << 20),
+        cost_estimate=pl.CostEstimate(flops=0, bytes_accessed=size, transcendentals=0),
+        name="fetch",
+    )(*(pltpu.with_memory_space_constraint(array, pltpu.HBM) for array in arrays))
 
 
 def square_kernel(h0, h1, h2, h3, out):
@@ -392,12 +420,12 @@
 
     columns = w_out.shape[1]
     features = hidden.shape[2]
-    w_qkv = pltpu.with_memory_space_constraint(w_qkv, pltpu.VMEM)
+    w_qkv, own = fetch(w_qkv, hidden)
     k_cache = pltpu.with_memory_space_constraint(k_cache, pltpu.VMEM)
     v_cache = pltpu.with_memory_space_constraint(v_cache, pltpu.VMEM)
     w_out = pltpu.with_memory_space_constraint(w_out, pltpu.VMEM)
     cosine, sine = rotation(positions)
-    hiddens = [partner(hidden, "gy", y) for y in range(NY)]
+    hiddens = [own] + [partner(hidden, "gy", y) for y in range(1, NY)]
     squares = call(square_kernel, "square", shape(NY * ROWS, HD, dtype=F32), hiddens)
     squares = [partner(squares, "gx", x) for x in range(NX)]
     sums = call(

time: 64.1 us -> 59.2 us (0.924)
  local copies, waits for them, and re-layouts: 6.12 us -> 0.04 us
  Pallas kernels: 6.32 us -> 10.3 us
  waiting for transfers between devices: 28.5 us -> 25.8 us
    unnamed x16 -> x14, local copies, waits for them, and re-layouts: 5.43 us -> 0.04 us
    pallas_call x0 -> x1, Pallas kernels: none -> 4 us  [fetch(): pl.pallas_call(functools.partial(fetch_kernel, len(arrays)), in_specs=[pl...]
    ppermute x19, waiting for transfers between devices: 28.5 us -> 25.8 us  [partner(): lax.ppermute(part, axis, [(k, k ^ distance) for k in range(lax.axis_size(...]
    broadcast_in_dim x1, local copies, waits for them, and re-layouts: 0.69 us -> 0.01 us  [small_body(): norm_gain[None]]
  transfers between devices with their start and end apart: 19 -> 19, of which waited for: 14 -> 14; matrix products, arithmetic and copies ran while one was open for 2% -> 0% of each run, Pallas kernels for 0% -> 7%
where the time goes in v3:
time: 59.2 us; the launch traced here: 59.1 us
  waiting for transfers between devices  25.8 us (44%)
  starting transfers between devices  22.5 us (38%)
  Pallas kernels  10.3 us (17%)
    ppermute x19, waiting for transfers between devices, partner(): lax.ppermute(part, axis, [(k, k ^ distance) for k in range(lax.axis_size(...  25.8 us
    ppermute x19, starting transfers between devices, partner(): lax.ppermute(part, axis, [(k, k ^ distance) for k in range(lax.axis_size(...  22.5 us
    pallas_call x9, Pallas kernels, call(): pl.pallas_call(kernel, in_specs=[SMEM_SPEC] * scalars + [VMEM_SPEC] * (le...  6.33 us
    pallas_call x1, Pallas kernels, fetch(): pl.pallas_call(functools.partial(fetch_kernel, len(arrays)), in_specs=[pl...  4 us
  transfers between devices with their start and end apart: 19, of which 14 were waited for; matrix products, arithmetic and copies ran while one was open for 0% of the time, Pallas kernels for 7%

profile of v3, /device:TPU:0, one launch (start us, length us, event | category | flops | bytes accessed | tf_op | source)
XLA Modules:
  0.0 59.1 jit_solution(13158647376798963480)
XLA Ops:
  0.0 3.0 %collective-permute-start = (bf16[2,2,2048]{2,1,0:T(2,128)(2,1)}, bf16[2,2,2048]{2,1,0:T(2,128)(2,1)S(1)}, u32[]{:S(2)}, u32[]{:S(2)}) collective-permute-start(bf16[2,2,2048]{2,1,0:T(2,128)(2,1)} %refs_1_.1), channel_id=1, source_target_pairs={{0,1},{1,0},{2,3},{3,2},{4,5},{5,4},{6,7},{7,6},{8,9},{9,8},{10,11... | collective-permute-start | bytes 49160 | tf_op jit(solution)/shard_map/ppermute | solution.py:414
  3.0 2.6 %collective-permute-start.1 = (bf16[2,2,2048]{2,1,0:T(2,128)(2,1)}, bf16[2,2,2048]{2,1,0:T(2,128)(2,1)S(1)}, u32[]{:S(2)}, u32[]{:S(2)}) collective-permute-start(bf16[2,2,2048]{2,1,0:T(2,128)(2,1)} %refs_1_.1), channel_id=1, source_target_pairs={{0,2},{1,3},{2,0},{3,1},{4,6},{5,7},{6,4},{7,5},{8,10},{9,11},{10,... | collective-permute-start | bytes 49160 | tf_op jit(solution)/shard_map/ppermute | solution.py:414
  5.6 4.0 %fetch.1 = (bf16[2048,2560]{1,0:T(8,128)(2,1)S(1)}, bf16[2,2,2048]{2,1,0:T(2,128)(2,1)S(1)}) custom-call(bf16[2048,2560]{1,0:T(8,128)(2,1)} %refs_0_.1, bf16[2,2,2048]{2,1,0:T(2,128)(2,1)} %refs_1_.1), custom_call_target="tpu_custom_call" | custom-call | bytes 10502144 | tf_op jit(solution)/shard_map/fetch/pallas_call | solution.py:184
  9.7 1.7 %collective-permute-done.2.h3 = bf16[2,2,2048]{2,1,0:T(2,128)(2,1)S(1)} collective-permute-done((bf16[2,2,2048]{2,1,0:T(2,128)(2,1)}, bf16[2,2,2048]{2,1,0:T(2,128)(2,1)S(1)}, u32[]{:S(2)}, u32[]{:S(2)}) %collective-permute-start.2) | collective-permute-done | bytes 16416 | tf_op jit(solution)/shard_map/ppermute | solution.py:414
  11.5 1.6 %collective-permute-start.4 = (f32[16,128]{1,0:T(8,128)S(1)}, f32[16,128]{1,0:T(8,128)S(1)}, u32[]{:S(2)}, u32[]{:S(2)}) collective-permute-start(f32[16,128]{1,0:T(8,128)S(1)} %square.1.s0), channel_id=1, source_target_pairs={{0,8},{4,12},{8,0},{12,4},{1,9},{5,13},{9,1},{13,5},{2,10},{6,14},... | collective-permute-start | bytes 24584 | tf_op jit(solution)/shard_map/ppermute | solution.py:414
  13.4 1.8 %collective-permute-done.4.s2 = f32[16,128]{1,0:T(8,128)S(1)} collective-permute-done((f32[16,128]{1,0:T(8,128)S(1)}, f32[16,128]{1,0:T(8,128)S(1)}, u32[]{:S(2)}, u32[]{:S(2)}) %collective-permute-start.4) | collective-permute-done | bytes 8224 | tf_op jit(solution)/shard_map/ppermute | solution.py:414
  15.3 0.9 %collective-permute-done.5.s3 = f32[16,128]{1,0:T(8,128)S(1)} collective-permute-done((f32[16,128]{1,0:T(8,128)S(1)}, f32[16,128]{1,0:T(8,128)S(1)}, u32[]{:S(2)}, u32[]{:S(2)}) %collective-permute-start.5) | collective-permute-done | bytes 8224 | tf_op jit(solution)/shard_map/ppermute | solution.py:414
  16.2 1.5 %project.1.a = f32[4,80,128]{2,1,0:T(8,128)S(1)} custom-call(bf16[2,2,2048]{2,1,0:T(2,128)(2,1)S(1)} %get-tuple-element.21.h0, bf16[2,2,2048]{2,1,0:T(2,128)(2,1)S(1)} %collective-permute-done.h1, bf16[2,2,2048]{2,1,0:T(2,128)(2,1)S(1)} %collective-permute-done.1.h2, bf16[2,2,2048]{2,1,0:T(2,128)(2,1)S(1)} %collective-permute-done.2.h3, ...), custom_call_target="tpu_custom_call" | custom-call | tf_op jit(solution)/shard_map/project/pallas_call | solution.py:154
  17.9 1.1 %collective-permute-done.6.b = f32[4,80,128]{2,1,0:T(8,128)S(1)} collective-permute-done((f32[4,80,128]{2,1,0:T(8,128)S(1)}, f32[4,80,128]{2,1,0:T(8,128)S(1)}, u32[]{:S(2)}, u32[]{:S(2)}) %collective-permute-start.6) | collective-permute-done | bytes 163872 | tf_op jit(solution)/shard_map/ppermute | solution.py:414
  19.9 5.5 %collective-permute-done.7.b = f32[4,80,128]{2,1,0:T(8,128)S(1)} collective-permute-done((f32[4,80,128]{2,1,0:T(8,128)S(1)}, f32[4,80,128]{2,1,0:T(8,128)S(1)}, u32[]{:S(2)}, u32[]{:S(2)}) %collective-permute-start.7) | collective-permute-done | bytes 163872 | tf_op jit(solution)/shard_map/ppermute | solution.py:414
  25.5 2.2 %collective-permute-start.10 = (bf16[80,128]{1,0:T(8,128)(2,1)S(1)}, bf16[80,128]{1,0:T(8,128)(2,1)S(1)}, u32[]{:S(2)}, u32[]{:S(2)}) collective-permute-start(bf16[80,128]{1,0:T(8,128)(2,1)S(1)} %get-tuple-element.26), channel_id=1, source_target_pairs={{0,3},{1,2},{2,1},{3,0},{4,7},{5,6},{6,5},{7,4},{8,11},{9,10},{10,... | collective-permute-start | bytes 61448 | tf_op jit(solution)/shard_map/ppermute | solution.py:414
  27.7 2.2 %collective-permute-start.9 = (bf16[80,128]{1,0:T(8,128)(2,1)S(1)}, bf16[80,128]{1,0:T(8,128)(2,1)S(1)}, u32[]{:S(2)}, u32[]{:S(2)}) collective-permute-start(bf16[80,128]{1,0:T(8,128)(2,1)S(1)} %get-tuple-element.25), channel_id=1, source_target_pairs={{0,2},{1,3},{2,0},{3,1},{4,6},{5,7},{6,4},{7,5},{8,10},{9,11},{10,... | collective-permute-start | bytes 61448 | tf_op jit(solution)/shard_map/ppermute | solution.py:414
  30.0 1.1 %collective-permute-done.10.r3 = bf16[80,128]{1,0:T(8,128)(2,1)S(1)} collective-permute-done((bf16[80,128]{1,0:T(8,128)(2,1)S(1)}, bf16[80,128]{1,0:T(8,128)(2,1)S(1)}, u32[]{:S(2)}, u32[]{:S(2)}) %collective-permute-start.10) | collective-permute-done | bytes 20512 | tf_op jit(solution)/shard_map/ppermute | solution.py:414
  32.4 2.3 %attend.1.a = f32[272,128]{1,0:T(8,128)S(1)} custom-call(s32[2]{0:T(128)S(1)} %copy-done.2, bf16[80,128]{1,0:T(8,128)(2,1)S(1)} %get-tuple-element.23.r0, bf16[80,128]{1,0:T(8,128)(2,1)S(1)} %collective-permute-done.8.r1, bf16[80,128]{1,0:T(8,128)(2,1)S(1)} %collective-permute-done.9.r2, bf16[80,128]{1,0:T(8,128)(2,1)S(1)} %collective-permute-done.10.r3, ...), custom_call_target="tpu_custom_call" | custom-call | tf_op jit(solution)/shard_map/attend/pallas_call | solution.py:154
  34.8 1.3 %collective-permute-done.11.b = f32[272,128]{1,0:T(8,128)S(1)} collective-permute-done((f32[272,128]{1,0:T(8,128)S(1)}, f32[272,128]{1,0:T(8,128)S(1)}, u32[]{:S(2)}, u32[]{:S(2)}) %collective-permute-start.11) | collective-permute-done | bytes 139296 | tf_op jit(solution)/shard_map/ppermute | solution.py:414
  37.0 3.7 %collective-permute-done.12.b = bf16[272,128]{1,0:T(8,128)(2,1)S(1)} collective-permute-done((bf16[272,128]{1,0:T(8,128)(2,1)S(1)}, bf16[272,128]{1,0:T(8,128)(2,1)S(1)}, u32[]{:S(2)}, u32[]{:S(2)}) %collective-permute-start.12) | collective-permute-done | bytes 69664 | tf_op jit(solution)/shard_map/ppermute | solution.py:414
  41.0 2.1 %collective-permute-start.13 = (bf16[64,128]{1,0:T(8,128)(2,1)S(1)}, bf16[64,128]{1,0:T(8,128)(2,1)S(1)}, u32[]{:S(2)}, u32[]{:S(2)}) collective-permute-start(bf16[64,128]{1,0:T(8,128)(2,1)S(1)} %get-tuple-element.30), channel_id=1, source_target_pairs={{0,1},{1,0},{2,3},{3,2},{4,5},{5,4},{6,7},{7,6},{8,9},{9,8},{10,11... | collective-permute-start | bytes 49160 | tf_op jit(solution)/shard_map/ppermute | solution.py:414
  43.4 2.2 %collective-permute-start.15 = (bf16[64,128]{1,0:T(8,128)(2,1)S(1)}, bf16[64,128]{1,0:T(8,128)(2,1)S(1)}, u32[]{:S(2)}, u32[]{:S(2)}) collective-permute-start(bf16[64,128]{1,0:T(8,128)(2,1)S(1)} %get-tuple-element.32), channel_id=1, source_target_pairs={{0,3},{1,2},{2,1},{3,0},{4,7},{5,6},{6,5},{7,4},{8,11},{9,10},{10,... | collective-permute-start | bytes 49160 | tf_op jit(solution)/shard_map/ppermute | solution.py:414
  45.5 2.2 %collective-permute-done.14.a2 = bf16[64,128]{1,0:T(8,128)(2,1)S(1)} collective-permute-done((bf16[64,128]{1,0:T(8,128)(2,1)S(1)}, bf16[64,128]{1,0:T(8,128)(2,1)S(1)}, u32[]{:S(2)}, u32[]{:S(2)}) %collective-permute-start.14) | collective-permute-done | bytes 16416 | tf_op jit(solution)/shard_map/ppermute | solution.py:414
  47.7 1.2 %collective-permute-done.15.a3 = bf16[64,128]{1,0:T(8,128)(2,1)S(1)} collective-permute-done((bf16[64,128]{1,0:T(8,128)(2,1)S(1)}, bf16[64,128]{1,0:T(8,128)(2,1)S(1)}, u32[]{:S(2)}, u32[]{:S(2)}) %collective-permute-start.15) | collective-permute-done | bytes 16416 | tf_op jit(solution)/shard_map/ppermute | solution.py:414
  48.9 1.2 %output.1 = (f32[64,128]{1,0:T(8,128)S(1)}, bf16[64,128]{1,0:T(8,128)(2,1)S(1)}, bf16[64,128]{1,0:T(8,128)(2,1)S(1)}, bf16[64,128]{1,0:T(8,128)(2,1)S(1)}) custom-call(bf16[64,128]{1,0:T(8,128)(2,1)S(1)} %get-tuple-element.29.a0, bf16[64,128]{1,0:T(8,128)(2,1)S(1)} %collective-permute-done.13.a1, bf16[64,128]{1,0:T(8,128)(2,1)S(1)} %collective-permute-done.14.a2, ...), custom_call_target="tpu_custom_call" | custom-call | tf_op jit(solution)/shard_map/output/pallas_call | solution.py:154
  50.3 2.6 %collective-permute-start.17 = (bf16[64,128]{1,0:T(8,128)(2,1)S(1)}, bf16[64,128]{1,0:T(8,128)(2,1)S(1)}, u32[]{:S(2)}, u32[]{:S(2)}) collective-permute-start(bf16[64,128]{1,0:T(8,128)(2,1)S(1)} %get-tuple-element.35), channel_id=1, source_target_pairs={{0,2},{1,3},{2,0},{3,1},{4,6},{5,7},{6,4},{7,5},{8,10},{9,11},{10,... | collective-permute-start | bytes 49160 | tf_op jit(solution)/shard_map/ppermute | solution.py:414
  52.9 1.7 %collective-permute-start.18 = (bf16[64,128]{1,0:T(8,128)(2,1)S(1)}, bf16[64,128]{1,0:T(8,128)(2,1)S(1)}, u32[]{:S(2)}, u32[]{:S(2)}) collective-permute-start(bf16[64,128]{1,0:T(8,128)(2,1)S(1)} %get-tuple-element.36), channel_id=1, source_target_pairs={{0,3},{1,2},{2,1},{3,0},{4,7},{5,6},{6,5},{7,4},{8,11},{9,10},{10,... | collective-permute-start | bytes 49160 | tf_op jit(solution)/shard_map/ppermute | solution.py:414
  55.0 3.5 %collective-permute-done.18.d = bf16[64,128]{1,0:T(8,128)(2,1)S(1)} collective-permute-done((bf16[64,128]{1,0:T(8,128)(2,1)S(1)}, bf16[64,128]{1,0:T(8,128)(2,1)S(1)}, u32[]{:S(2)}, u32[]{:S(2)}) %collective-permute-start.18) | collective-permute-done | bytes 16416 | tf_op jit(solution)/shard_map/ppermute | solution.py:414
  (44 shorter events, 5.7 us)
Async XLA Ops:
  0.0 9.7 %collective-permute-start = (bf16[2,2,2048]{2,1,0:T(2,128)(2,1)}, bf16[2,2,2048]{2,1,0:T(2,128)(2,1)S(1)}, u32[]{:S(2)}, u32[]{:S(2)}) collective-permute-start(bf16[2,2,2048]{2,1,0:T(2,128)(2,1)} %refs_1_.1), channel_id=1, source_target_pairs={{0,1},{1,0},{2,3},{3,2},{4,5},{5,4},{6,7},{7,6},{8,9},{9,8},{10,11... | collective-permute-start | bytes 49160 | tf_op jit(solution)/shard_map/ppermute | solution.py:414
  3.0 6.7 %collective-permute-start.1 = (bf16[2,2,2048]{2,1,0:T(2,128)(2,1)}, bf16[2,2,2048]{2,1,0:T(2,128)(2,1)S(1)}, u32[]{:S(2)}, u32[]{:S(2)}) collective-permute-start(bf16[2,2,2048]{2,1,0:T(2,128)(2,1)} %refs_1_.1), channel_id=1, source_target_pairs={{0,2},{1,3},{2,0},{3,1},{4,6},{5,7},{6,4},{7,5},{8,10},{9,11},{10,... | collective-permute-start | bytes 49160 | tf_op jit(solution)/shard_map/ppermute | solution.py:414
  5.6 5.7 %collective-permute-start.2 = (bf16[2,2,2048]{2,1,0:T(2,128)(2,1)}, bf16[2,2,2048]{2,1,0:T(2,128)(2,1)S(1)}, u32[]{:S(2)}, u32[]{:S(2)}) collective-permute-start(bf16[2,2,2048]{2,1,0:T(2,128)(2,1)} %refs_1_.1), channel_id=1, source_target_pairs={{0,3},{1,2},{2,1},{3,0},{4,7},{5,6},{6,5},{7,4},{8,11},{9,10},{10,... | collective-permute-start | bytes 49160 | tf_op jit(solution)/shard_map/ppermute | solution.py:414
  9.6 22.8 %copy-start = (bf16[2,384,1024]{2,1,0:T(8,128)(2,1)S(1)}, bf16[2,384,1024]{2,1,0:T(8,128)(2,1)}, u32[]{:S(2)}) copy-start(bf16[2,384,1024]{2,1,0:T(8,128)(2,1)} %keys.1) | copy-start | bytes 4718596
  9.6 22.8 %copy-start.1 = (bf16[2,384,1024]{2,1,0:T(8,128)(2,1)S(1)}, bf16[2,384,1024]{2,1,0:T(8,128)(2,1)}, u32[]{:S(2)}) copy-start(bf16[2,384,1024]{2,1,0:T(8,128)(2,1)} %values.1) | copy-start | bytes 4718596
  9.7 22.7 %copy-start.2 = (s32[2]{0:T(128)S(1)}, s32[2]{0:T(128)}, u32[]{:S(2)}) copy-start(s32[2]{0:T(128)} %lengths.1) | copy-start | bytes 28
  9.7 39.2 %slice-start = ((s8[8388608]{0:T(1024)(128)(4,1)}), s8[4194304]{0:T(1024)(128)(4,1)S(1)}, s32[]{:S(2)}) async-start(s8[8388608]{0:T(1024)(128)(4,1)} %bitcast), calls=%async_computation | async-start | bytes 8388608
  11.5 1.9 %collective-permute-start.3 = (f32[16,128]{1,0:T(8,128)S(1)}, f32[16,128]{1,0:T(8,128)S(1)}, u32[]{:S(2)}, u32[]{:S(2)}) collective-permute-start(f32[16,128]{1,0:T(8,128)S(1)} %square.1.s0), channel_id=1, source_target_pairs={{0,4},{4,0},{8,12},{12,8},{1,5},{5,1},{9,13},{13,9},{2,6},{6,2},{1... | collective-permute-start | bytes 24584 | tf_op jit(solution)/shard_map/ppermute | solution.py:414
  11.5 3.7 %collective-permute-start.4 = (f32[16,128]{1,0:T(8,128)S(1)}, f32[16,128]{1,0:T(8,128)S(1)}, u32[]{:S(2)}, u32[]{:S(2)}) collective-permute-start(f32[16,128]{1,0:T(8,128)S(1)} %square.1.s0), channel_id=1, source_target_pairs={{0,8},{4,12},{8,0},{12,4},{1,9},{5,13},{9,1},{13,5},{2,10},{6,14},... | collective-permute-start | bytes 24584 | tf_op jit(solution)/shard_map/ppermute | solution.py:414
  13.1 3.1 %collective-permute-start.5 = (f32[16,128]{1,0:T(8,128)S(1)}, f32[16,128]{1,0:T(8,128)S(1)}, u32[]{:S(2)}, u32[]{:S(2)}) collective-permute-start(f32[16,128]{1,0:T(8,128)S(1)} %square.1.s0), channel_id=1, source_target_pairs={{0,12},{4,8},{8,4},{12,0},{1,13},{5,9},{9,5},{13,1},{2,14},{6,10},... | collective-permute-start | bytes 24584 | tf_op jit(solution)/shard_map/ppermute | solution.py:414
  16.2 32.7 %slice-start.1 = ((s8[8388608]{0:T(1024)(128)(4,1)}), s8[4194304]{0:T(1024)(128)(4,1)S(1)}, s32[]{:S(2)}) async-start(s8[8388608]{0:T(1024)(128)(4,1)} %bitcast), calls=%async_computation.1 | async-start | bytes 8388608
  17.7 1.4 %collective-permute-start.6 = (f32[4,80,128]{2,1,0:T(8,128)S(1)}, f32[4,80,128]{2,1,0:T(8,128)S(1)}, u32[]{:S(2)}, u32[]{:S(2)}) collective-permute-start(f32[4,80,128]{2,1,0:T(8,128)S(1)} %project.1.a), channel_id=1, source_target_pairs={{0,4},{4,0},{8,12},{12,8},{1,5},{5,1},{9,13},{13,9},{2,6},{6,2},{1... | collective-permute-start | bytes 491528 | tf_op jit(solution)/shard_map/ppermute | solution.py:414
  19.1 6.3 %collective-permute-start.7 = (f32[4,80,128]{2,1,0:T(8,128)S(1)}, f32[4,80,128]{2,1,0:T(8,128)S(1)}, u32[]{:S(2)}, u32[]{:S(2)}) collective-permute-start(f32[4,80,128]{2,1,0:T(8,128)S(1)} %add.24.a), channel_id=1, source_target_pairs={{0,8},{4,12},{8,0},{12,4},{1,9},{5,13},{9,1},{13,5},{2,10},{6,14},... | collective-permute-start | bytes 491528 | tf_op jit(solution)/shard_map/ppermute | solution.py:414
  25.5 5.6 %collective-permute-start.10 = (bf16[80,128]{1,0:T(8,128)(2,1)S(1)}, bf16[80,128]{1,0:T(8,128)(2,1)S(1)}, u32[]{:S(2)}, u32[]{:S(2)}) collective-permute-start(bf16[80,128]{1,0:T(8,128)(2,1)S(1)} %get-tuple-element.26), channel_id=1, source_target_pairs={{0,3},{1,2},{2,1},{3,0},{4,7},{5,6},{6,5},{7,4},{8,11},{9,10},{10,... | collective-permute-start | bytes 61448 | tf_op jit(solution)/shard_map/ppermute | solution.py:414
  27.7 3.8 %collective-permute-start.8 = (bf16[80,128]{1,0:T(8,128)(2,1)S(1)}, bf16[80,128]{1,0:T(8,128)(2,1)S(1)}, u32[]{:S(2)}, u32[]{:S(2)}) collective-permute-start(bf16[80,128]{1,0:T(8,128)(2,1)S(1)} %get-tuple-element.24), channel_id=1, source_target_pairs={{0,1},{1,0},{2,3},{3,2},{4,5},{5,4},{6,7},{7,6},{8,9},{9,8},{10,11... | collective-permute-start | bytes 61448 | tf_op jit(solution)/shard_map/ppermute | solution.py:414
  27.7 4.7 %collective-permute-start.9 = (bf16[80,128]{1,0:T(8,128)(2,1)S(1)}, bf16[80,128]{1,0:T(8,128)(2,1)S(1)}, u32[]{:S(2)}, u32[]{:S(2)}) collective-permute-start(bf16[80,128]{1,0:T(8,128)(2,1)S(1)} %get-tuple-element.25), channel_id=1, source_target_pairs={{0,2},{1,3},{2,0},{3,1},{4,6},{5,7},{6,4},{7,5},{8,10},{9,11},{10,... | collective-permute-start | bytes 61448 | tf_op jit(solution)/shard_map/ppermute | solution.py:414
  34.7 1.4 %collective-permute-start.11 = (f32[272,128]{1,0:T(8,128)S(1)}, f32[272,128]{1,0:T(8,128)S(1)}, u32[]{:S(2)}, u32[]{:S(2)}) collective-permute-start(f32[272,128]{1,0:T(8,128)S(1)} %attend.1.a), channel_id=1, source_target_pairs={{0,4},{4,0},{8,12},{12,8},{1,5},{5,1},{9,13},{13,9},{2,6},{6,2},{1... | collective-permute-start | bytes 417800 | tf_op jit(solution)/shard_map/ppermute | solution.py:414
  36.4 4.4 %collective-permute-start.12 = (bf16[272,128]{1,0:T(8,128)(2,1)S(1)}, bf16[272,128]{1,0:T(8,128)(2,1)S(1)}, u32[]{:S(2)}, u32[]{:S(2)}) collective-permute-start(bf16[272,128]{1,0:T(8,128)(2,1)S(1)} %get-tuple-element.28), channel_id=1, source_target_pairs={{0,8},{4,12},{8,0},{12,4},{1,9},{5,13},{9,1},{13,5},{2,10},{6,14},... | collective-permute-start | bytes 208904 | tf_op jit(solution)/shard_map/ppermute | solution.py:414
  41.0 4.5 %collective-permute-start.13 = (bf16[64,128]{1,0:T(8,128)(2,1)S(1)}, bf16[64,128]{1,0:T(8,128)(2,1)S(1)}, u32[]{:S(2)}, u32[]{:S(2)}) collective-permute-start(bf16[64,128]{1,0:T(8,128)(2,1)S(1)} %get-tuple-element.30), channel_id=1, source_target_pairs={{0,1},{1,0},{2,3},{3,2},{4,5},{5,4},{6,7},{7,6},{8,9},{9,8},{10,11... | collective-permute-start | bytes 49160 | tf_op jit(solution)/shard_map/ppermute | solution.py:414
  43.1 4.6 %collective-permute-start.14 = (bf16[64,128]{1,0:T(8,128)(2,1)S(1)}, bf16[64,128]{1,0:T(8,128)(2,1)S(1)}, u32[]{:S(2)}, u32[]{:S(2)}) collective-permute-start(bf16[64,128]{1,0:T(8,128)(2,1)S(1)} %get-tuple-element.31), channel_id=1, source_target_pairs={{0,2},{1,3},{2,0},{3,1},{4,6},{5,7},{6,4},{7,5},{8,10},{9,11},{10,... | collective-permute-start | bytes 49160 | tf_op jit(solution)/shard_map/ppermute | solution.py:414
  43.4 5.5 %collective-permute-start.15 = (bf16[64,128]{1,0:T(8,128)(2,1)S(1)}, bf16[64,128]{1,0:T(8,128)(2,1)S(1)}, u32[]{:S(2)}, u32[]{:S(2)}) collective-permute-start(bf16[64,128]{1,0:T(8,128)(2,1)S(1)} %get-tuple-element.32), channel_id=1, source_target_pairs={{0,3},{1,2},{2,1},{3,0},{4,7},{5,6},{6,5},{7,4},{8,11},{9,10},{10,... | collective-permute-start | bytes 49160 | tf_op jit(solution)/shard_map/ppermute | solution.py:414
  50.1 4.5 %collective-permute-start.16 = (bf16[64,128]{1,0:T(8,128)(2,1)S(1)}, bf16[64,128]{1,0:T(8,128)(2,1)S(1)}, u32[]{:S(2)}, u32[]{:S(2)}) collective-permute-start(bf16[64,128]{1,0:T(8,128)(2,1)S(1)} %get-tuple-element.34), channel_id=1, source_target_pairs={{0,1},{1,0},{2,3},{3,2},{4,5},{5,4},{6,7},{7,6},{8,9},{9,8},{10,11... | collective-permute-start | bytes 49160 | tf_op jit(solution)/shard_map/ppermute | solution.py:414
  50.3 4.6 %collective-permute-start.17 = (bf16[64,128]{1,0:T(8,128)(2,1)S(1)}, bf16[64,128]{1,0:T(8,128)(2,1)S(1)}, u32[]{:S(2)}, u32[]{:S(2)}) collective-permute-start(bf16[64,128]{1,0:T(8,128)(2,1)S(1)} %get-tuple-element.35), channel_id=1, source_target_pairs={{0,2},{1,3},{2,0},{3,1},{4,6},{5,7},{6,4},{7,5},{8,10},{9,11},{10,... | collective-permute-start | bytes 49160 | tf_op jit(solution)/shard_map/ppermute | solution.py:414
  52.9 5.5 %collective-permute-start.18 = (bf16[64,128]{1,0:T(8,128)(2,1)S(1)}, bf16[64,128]{1,0:T(8,128)(2,1)S(1)}, u32[]{:S(2)}, u32[]{:S(2)}) collective-permute-start(bf16[64,128]{1,0:T(8,128)(2,1)S(1)} %get-tuple-element.36), channel_id=1, source_target_pairs={{0,3},{1,2},{2,1},{3,0},{4,7},{5,6},{6,5},{7,4},{8,11},{9,10},{10,... | collective-permute-start | bytes 49160 | tf_op jit(solution)/shard_map/ppermute | solution.py:414
  (2 other events, 31.3 us)

commit v4 on v2

--- a/solution.py
+++ b/solution.py
@@ -1,3 +1,5 @@
+import functools
+
 import jax
 import jax.numpy as jnp
 from jax import lax
@@ -141,13 +143,14 @@
 OUT_HEADS = H // NY
 OUT_ROWS = OUT_HEADS * ROWS
 QUERIES = H * ROWS
+GROUP_ROWS = QUERIES // KVH
 VMEM_SPEC = pl.BlockSpec(memory_space=pltpu.VMEM)
 SMEM_SPEC = pl.BlockSpec(memory_space=pltpu.SMEM)
 F32 = jnp.float32
 BF16 = jnp.bfloat16
 
 
-def call(kernel, name, out_shape, operands, scratch=(), scalars=0, mib=8, cost=None):
+def call(kernel, name, out_shape, operands, scratch=(), scalars=0, mib=8):
     many = isinstance(out_shape, (list, tuple))
     return pl.pallas_call(
         kernel,
@@ -156,7 +159,6 @@
         out_shape=out_shape,
         scratch_shapes=list(scratch),
         compiler_params=pltpu.CompilerParams(vmem_limit_bytes=mib << 20),
-        cost_estimate=cost,
         name=name,
     )(*operands)
 
@@ -166,38 +168,65 @@
     return high, values - high
 
 
-def pair_kernel(own, other, out):
-    out[0] = own[...]
-    out[1] = other[...]
+def fetch_kernel(pieces, source, out, done):
+    rows = source.shape[0] // pieces
+    copies = [
+        pltpu.make_async_copy(
+            source.at[pl.ds(rows * k, rows)], out.at[pl.ds(rows * k, rows)], done.at[k]
+        )
+        for k in range(pieces)
+    ]
+    for copy in copies:
+        copy.start()
+    for copy in copies:
+        copy.wait()
+
+
+def fetch(array, pieces=8):
+    size = array.size * array.dtype.itemsize
+    return pl.pallas_call(
+        functools.partial(fetch_kernel, pieces),
+        in_specs=[pl.BlockSpec(memory_space=pltpu.HBM)],
+        out_specs=VMEM_SPEC,
+        out_shape=pltpu.VMEM(array.shape, array.dtype),
+        scratch_shapes=[pltpu.SemaphoreType.DMA((pieces,))],
+        compiler_params=pltpu.CompilerParams(vmem_limit_bytes=1 << 20),
+        cost_estimate=pl.CostEstimate(flops=0, bytes_accessed=size, transcendentals=0),
+        name="fetch",
+    )(pltpu.with_memory_space_constraint(array, pltpu.HBM))
+
+
+def square_kernel(hidden, out, held):
+    out[...] = jnp.zeros_like(out)
+    held[...] = hidden[...]
+    for timeline in range(2):
+        wide = hidden[timeline].astype(F32)
+        total = jnp.sum(wide * wide, axis=-1, keepdims=True)
+        out[2 * timeline : 2 * timeline + 2, :] = jnp.broadcast_to(total, (2, HD))
 
 
 def add_kernel(a, b, out):
     out[...] = a[...] + b[...]
 
 
-def square_kernel(near, far, out):
-    for half, pair in enumerate((near, far)):
-        for k in range(4):
-            wide = pair[k // 2, k % 2].astype(F32)
-            total = jnp.sum(wide * wide, axis=-1, keepdims=True)
-            at = 8 * half + 2 * k
-            out[at : at + 2, :] = jnp.broadcast_to(total, (2, HD))
-
-
-def project_kernel(near, far, s0, s1, gain, w, kept, sent, rows, sums):
-    mixed = lax.axis_index("gx") ^ lax.axis_index("gy")
-    for half, pair in enumerate((near, far)):
-        for k in range(4):
-            at = 8 * half + 2 * k
-            rows[at : at + 2, :] = pair[k // 2, k % 2].astype(F32)
-    squares = (s0[...] + s1[...])[:, 0:1]
-    normed = rows[...] * lax.rsqrt(squares / D + EPSILON) * gain[...].astype(F32)
-    normed = normed.astype(BF16)
+def norm_kernel(hidden, a, b, gain, out):
+    squares = (a[...] + b[...])[:, 0:1]
+    wide_gain = gain[...].astype(F32)
+    for timeline in range(2):
+        scale = lax.rsqrt(squares[2 * timeline : 2 * timeline + 2] / D + EPSILON)
+        out[timeline] = (hidden[timeline].astype(F32) * scale * wide_gain).astype(BF16)
+
+
+def project_kernel(n0, n1, n2, n3, w, kept, sent, rows, sums):
+    core = lax.axis_index("gx") & 1
+    for shift, normed in enumerate((n0, n1, n2, n3)):
+        for timeline in range(2):
+            at = ROWS * shift + 2 * timeline
+            rows[at : at + 2, :] = normed[timeline].astype(F32)
+    left = rows[...].astype(BF16)
     width = 512
     for step in range(w.shape[1] // width):
-        part = jnp.dot(
-            normed, w[:, width * step : width * (step + 1)], preferred_element_type=F32
-        )
+        part = jnp.dot(left, w[:, width * step : width * (step + 1)], preferred_element_type=F32)
         for head in range(width // HD):
             at = (step * (width // HD) + head) * ROWS
             for shift in range(NY):
@@ -205,26 +234,29 @@
                     ROWS * shift : ROWS * (shift + 1), HD * head : HD * (head + 1)
                 ]
     for k in range(2):
-        kept[k] = sums[mixed ^ (2 * k)]
-        sent[k] = sums[mixed ^ (2 * k + 1)]
-
-
-def halve_kernel(a, b, kept, sent):
-    kept[...] = a[0] + b[0].astype(F32)
-    sent[...] = (a[1] + b[1].astype(F32)).astype(sent.dtype)
-
-
-def round_kernel(a, b, out):
-    out[...] = (a[...] + b[...]).astype(BF16)
+        kept[k] = sums[(3 * k) ^ core]
+        sent[k] = sums[(3 * k) ^ core ^ 1]
+
+
+def chip_kernel(a, b, *outs):
+    for k, out in enumerate(outs):
+        out[...] = a[k] + b[k]
+
+
+def round_kernel(a0, b0, a1, b1, out):
+    out[0] = (a0[...] + b0[...]).astype(BF16)
+    out[1] = (a1[...] + b1[...]).astype(BF16)
 
 
 def attend_kernel(
-    lengths, near, far, cosine, sine, keys, values, kept, sent, projected, turns, spread, parts
+    lengths, near, far, cosine, sine, keys, values, kept, sent, projected, turns, table, parts
 ):
     my_x = lax.axis_index("gx")
-    for core, pair in enumerate((near, far)):
+    my_y = lax.axis_index("gy")
+    core = my_x & 1
+    for other, pair in enumerate((near, far)):
         for k in range(2):
-            at = pl.multiple_of((my_x ^ (2 * k + core)) * QKV_ROWS, 16)
+            at = pl.multiple_of((my_y ^ (3 * k) ^ core ^ other) * QKV_ROWS, 16)
             projected[pl.ds(at, QKV_ROWS), :] = pair[k].astype(F32)
     for t in range(4):
         turns[0, 2 * t : 2 * t + 2, :] = cosine[t % 2]
@@ -241,19 +273,22 @@
     row = lax.broadcasted_iota(jnp.int32, (QUERIES, 1), 0)
     token = row & 1
     timeline = (row >> 1) & 1
-    group_rows = QUERIES // KVH
-    spread[...] = jnp.zeros_like(spread)
-    scores = jnp.zeros((QUERIES, SPAN_DEV), F32)
-    for t in range(2):
-        mine = jnp.where(timeline == t, queries, jnp.zeros_like(queries))
-        for g in range(KVH):
-            at = slice(group_rows * g, group_rows * (g + 1))
-            spread[t, at, HD * g : HD * (g + 1)] = mine[at]
-        scores += lax.dot_general(
-            spread[t], keys[t], (((1,), (1,)), ((), ())), preferred_element_type=F32
-        )
+    group_rows = GROUP_ROWS
+    first = timeline[:GROUP_ROWS] == 0
+    for g in range(KVH):
+        at = slice(GROUP_ROWS * g, GROUP_ROWS * (g + 1))
+        both = [
+            lax.dot_general(
+                queries[at],
+                keys[t, :, HD * g : HD * (g + 1)],
+                (((1,), (1,)), ((), ())),
+                preferred_element_type=F32,
+            )
+            for t in range(2)
+        ]
+        table[at, :] = jnp.where(first, both[0], both[1])
     scaling = HD ** (-0.5)
-    scores = scores * scaling
+    scores = table[...] * scaling
     slot = my_x * SPAN_DEV + lax.broadcasted_iota(jnp.int32, (QUERIES, SPAN_DEV), 1)
     usable = slot < jnp.where(timeline == 0, lengths[0], lengths[1])
     maxima = jnp.max(jnp.where(usable, scores, NEGATIVE), axis=-1, keepdims=True)
@@ -278,16 +313,16 @@
         weight = jnp.exp(jnp.where(allowed, score - maxima, NEGATIVE))
         totals += weight
         added += weight.astype(BF16).astype(F32) * value
-    sums = jnp.zeros((QUERIES, KVH * HD), F32)
-    for t in range(2):
-        mine = jnp.where(timeline == t, rounded, jnp.zeros_like(rounded))
-        sums += jnp.dot(mine, values[t], preferred_element_type=F32)
+    mine = [jnp.where(timeline == t, rounded, jnp.zeros_like(rounded)) for t in range(2)]
     for g in range(KVH):
-        at = slice(group_rows * g, group_rows * (g + 1))
-        inside = group_rows * (g % 2)
-        parts[g // 2, inside : inside + group_rows, :] = (
-            sums[at, HD * g : HD * (g + 1)] + added[at]
-        )
+        at = slice(GROUP_ROWS * g, GROUP_ROWS * (g + 1))
+        total = added[at]
+        for t in range(2):
+            total += jnp.dot(
+                mine[t][at], values[t, :, HD * g : HD * (g + 1)], preferred_element_type=F32
+            )
+        inside = GROUP_ROWS * (g % 2)
+        parts[g // 2, inside : inside + GROUP_ROWS, :] = total
 
     lane = lax.broadcasted_iota(jnp.int32, (QUERIES, HD), 1)
     sheet = jnp.where(lane == 0, maxima, jnp.where(lane == 1, totals, 0.0))
@@ -296,8 +331,8 @@
         half = flat[:, HD * (q // 2) : HD * (q // 2 + 1)]
         parts[q, OUT_ROWS:, :] = half if q % 2 == 0 else pltpu.roll(half, OUT_ROWS, 1)
     for k in range(2):
-        kept[k] = parts[my_x ^ (2 * k)]
-        sent[k] = parts[my_x ^ (2 * k + 1)]
+        kept[k] = parts[my_y ^ (3 * k) ^ core]
+        sent[k] = parts[my_y ^ (3 * k) ^ core ^ 1]
 
 
 def columns_of(rows, sheet):
@@ -308,7 +343,7 @@
     return [turned[:, k : k + 1] for k in range(len(rows))]
 
 
-def merge_kernel(a, b, kept, sent, sheet):
+def merge_kernel(a, b, o0, o1, sheet):
     line = lax.broadcasted_iota(jnp.int32, (8, HD), 0)
     powers, stats = [], []
     for k in range(2):
@@ -319,39 +354,41 @@
         powers += [power_a, power_b]
         stats.append((highest, a_stats[1:2] * power_a + b_stats[1:2] * power_b))
     factors = columns_of(powers, sheet)
-    merged = [
-        a[k, :OUT_ROWS, :] * factors[2 * k] + b[k, :OUT_ROWS, :] * factors[2 * k + 1]
-        for k in range(2)
-    ]
-    kept[:OUT_ROWS, :] = merged[0]
-    kept[OUT_ROWS:, :] = jnp.where(line == 0, stats[0][0], jnp.where(line == 1, stats[0][1], 0.0))
-    sent[:OUT_ROWS, :] = merged[1].astype(BF16)
-    high, rest = high_rest(stats[1][0])
-    middle, low = high_rest(rest)
-    pieces = jnp.zeros((8, HD), F32)
-    for k, piece in enumerate((high, middle, low, *high_rest(stats[1][1]))):
-        pieces = jnp.where(line == k, piece, pieces)
-    sent[OUT_ROWS:, :] = jnp.concatenate([pieces, jnp.zeros_like(pieces)], axis=0).astype(BF16)
-
-
-def settle_kernel(a, b, out, sheet):
-    pieces = b[OUT_ROWS:, :].astype(F32)
-    maximum = (pieces[0:1] + pieces[1:2]) + pieces[2:3]
-    total = pieces[3:4] + pieces[4:5]
-    own_maximum, own_total = a[OUT_ROWS : OUT_ROWS + 1, :], a[OUT_ROWS + 1 : OUT_ROWS + 2, :]
-    highest = jnp.maximum(own_maximum, maximum)
-    power_a = jnp.exp(own_maximum - highest)
-    power_b = jnp.exp(maximum - highest)
-    whole = own_total * power_a + total * power_b
-    factor_a, factor_b = columns_of([power_a / whole, power_b / whole], sheet)
-    out[...] = (a[:OUT_ROWS, :] * factor_a + b[:OUT_ROWS, :].astype(F32) * factor_b).astype(BF16)
-
-
-def output_kernel(near, far, w, kept, sent, blocks, wide, sums):
-    mixed = lax.axis_index("gx") ^ lax.axis_index("gy")
-    for core, pair in enumerate((near, far)):
+    for k, out in enumerate((o0, o1)):
+        merged = a[k, :OUT_ROWS, :] * factors[2 * k] + b[k, :OUT_ROWS, :] * factors[2 * k + 1]
+        out[:OUT_ROWS, :] = merged.astype(BF16)
+        high, rest = high_rest(stats[k][0])
+        middle, low = high_rest(rest)
+        pieces = jnp.zeros((8, HD), F32)
+        for m, piece in enumerate((high, middle, low, *high_rest(stats[k][1]))):
+            pieces = jnp.where(line == m, piece, pieces)
+        out[OUT_ROWS:, :] = jnp.concatenate([pieces, jnp.zeros_like(pieces)], axis=0).astype(BF16)
+
+
+def settle_kernel(a0, b0, a1, b1, out, sheet):
+    factors = []
+    for pair in ((a0, b0), (a1, b1)):
+        maxima, totals = [], []
+        for part in pair:
+            pieces = part[OUT_ROWS:, :].astype(F32)
+            maxima.append((pieces[0:1] + pieces[1:2]) + pieces[2:3])
+            totals.append(pieces[3:4] + pieces[4:5])
+        highest = jnp.maximum(*maxima)
+        powers = [jnp.exp(maximum - highest) for maximum in maxima]
+        whole = totals[0] * powers[0] + totals[1] * powers[1]
+        factors += [power / whole for power in powers]
+    columns = columns_of(factors, sheet)
+    for k, (a, b) in enumerate(((a0, b0), (a1, b1))):
+        attended = a[:OUT_ROWS, :].astype(F32) * columns[2 * k]
+        attended += b[:OUT_ROWS, :].astype(F32) * columns[2 * k + 1]
+        out[k] = attended.astype(BF16)
+
+
+def output_kernel(near, far, w, o0, o1, o2, o3, blocks, wide, sums):
+    core = lax.axis_index("gx") & 1
+    for other, pair in enumerate((near, far)):
         for k in range(2):
-            blocks[mixed ^ (2 * k + core)] = pair[k].astype(F32)
+            blocks[(3 * k) ^ core ^ other] = pair[k].astype(F32)
     for shift in range(NY):
         for head in range(OUT_HEADS):
             wide[ROWS * shift : ROWS * (shift + 1), HD * head : HD * (head + 1)] = blocks[
@@ -367,13 +404,13 @@
                 sums[shift, at : at + ROWS, :] = part[
                     ROWS * shift : ROWS * (shift + 1), HD * chunk : HD * (chunk + 1)
                 ]
-    for k in range(2):
-        kept[k] = sums[k]
-        sent[k] = sums[2 + k].astype(BF16)
-
-
-def finish_kernel(a, b, out, total):
-    total[...] = a[...] + b[...].astype(F32)
+    o0[...] = sums[0]
+    for shift, out in ((1, o1), (2, o2), (3, o3)):
+        out[...] = sums[shift].astype(BF16)
+
+
+def finish_kernel(a, b, c, d, out, total):
+    total[...] = (a[...] + b[...].astype(F32)) + (c[...].astype(F32) + d[...].astype(F32))
     for chunk in range(out.shape[2] // HD):
         for timeline in range(2):
             at = ROWS * chunk + 2 * timeline
@@ -393,18 +430,22 @@
     return lax.ppermute(part, axis, [(k, k ^ distance) for k in range(lax.axis_size(axis))])
 
 
-def swapped(part):
-    pairs = [(x * NY + y, y * NY + x) for x in range(NX) for y in range(NY)]
-    return lax.ppermute(part, ("gx", "gy"), pairs)
-
-
-def paired(part, axis, distance):
-    return call(
-        pair_kernel,
-        "pair",
-        jax.ShapeDtypeStruct((2, *part.shape), part.dtype),
-        [part, partner(part, axis, distance)],
-    )
+def on_gy(parts):
+    far = {y: partner(parts[y], "gy", y) for y in (3, 2, 1)}
+    return [parts[0], far[1], far[2], far[3]]
+
+
+def on_chips(parts):
+    received = {}
+    for k in (1, 0):
+        for far_x in (1, 0):
+            pairs = [
+                (x * NY + y, (x ^ (2 * far_x)) * NY + (y ^ (3 * k) ^ (x & 1)))
+                for x in range(NX)
+                for y in range(NY)
+            ]
+            received[k, far_x] = lax.ppermute(parts[k], ("gx", "gy"), pairs)
+    return [received[k, far_x] for k in range(2) for far_x in range(2)]
 
 
 def small_body(hidden, norm_gain, w_qkv, w_out, k_cache, v_cache, cache_len, positions):
@@ -417,85 +458,77 @@
     columns = w_out.shape[1]
     features = hidden.shape[2]
     count = columns // HD * ROWS
-    w_qkv, w_out, k_cache, v_cache = map(pinned, (w_qkv, w_out, k_cache, v_cache))
+    hidden, w_out, k_cache, v_cache = map(pinned, (hidden, w_out, k_cache, v_cache))
+    w_qkv = fetch(w_qkv)
     cosine, sine = rotation(positions)
 
-    near = paired(hidden, "gy", 1)
-    far = partner(near, "gy", 2)
-    squares = call(
-        square_kernel, "square", shape(NY * ROWS, HD, dtype=F32), [near, far]
-    )
-    squares = call(
-        add_kernel, "add", shape(NY * ROWS, HD, dtype=F32), [squares, partner(squares, "gx", 1)]
+    line = shape(8, HD, dtype=F32)
+    squares, hidden = call(square_kernel, "square", [line, shape(*hidden.shape)], [hidden])
+    squares = call(add_kernel, "add", line, [squares, partner(squares, "gx", 1)])
+    normed = call(
+        norm_kernel,
+        "norm",
+        shape(*hidden.shape),
+        [hidden, squares, partner(squares, "gx", 2), norm_gain[None]],
     )
     half = shape(2, QKV_ROWS, HD, dtype=F32)
     kept, sent = call(
         project_kernel,
         "project",
         [half, half],
-        [near, far, squares, partner(squares, "gx", 2), norm_gain[None], w_qkv],
+        [*on_gy([normed] * NY), w_qkv],
         [pltpu.VMEM((NY * ROWS, features), F32), pltpu.VMEM((NY, QKV_ROWS, HD), F32)],
     )
-    quarter = shape(QKV_ROWS, HD, dtype=F32)
-    kept, sent = call(halve_kernel, "halve", [quarter, quarter], [kept, partner(sent, "gx", 1)])
-    block = call(round_kernel, "round", shape(QKV_ROWS, HD), [kept, partner(sent, "gx", 2)])
-    near = paired(swapped(block), "gx", 2)
-    far = partner(near, "gx", 1)
+    block = shape(QKV_ROWS, HD, dtype=F32)
+    sums = call(chip_kernel, "chip", [block, block], [kept, partner(sent, "gx", 1)])
+    near = call(round_kernel, "round", shape(2, QKV_ROWS, HD), on_chips(sums))
 
     half = shape(2, OUT_ROWS + 8, HD, dtype=F32)
     kept, sent = call(
         attend_kernel,
         "attend",
         [half, half],
-        [cache_len, near, far, cosine, sine, k_cache, v_cache],
+        [cache_len, near, partner(near, "gx", 1), cosine, sine, k_cache, v_cache],
         [
             pltpu.VMEM((NY * QKV_ROWS, HD), F32),
             pltpu.VMEM((2, 8, HD), F32),
-            pltpu.VMEM((2, QUERIES, KVH * HD), BF16),
+            pltpu.VMEM((QUERIES, SPAN_DEV), F32),
             pltpu.VMEM((NY, OUT_ROWS + 8, HD), F32),
         ],
         scalars=1,
         mib=16,
     )
-    kept, sent = call(
+    block = shape(OUT_ROWS + 16, HD)
+    merged = call(
         merge_kernel,
         "merge",
-        [shape(OUT_ROWS + 8, HD, dtype=F32), shape(OUT_ROWS + 16, HD)],
+        [block, block],
         [kept, partner(sent, "gx", 1)],
         [pltpu.VMEM((HD, HD), F32)],
     )
-    block = call(
+    near = call(
         settle_kernel,
         "settle",
-        shape(OUT_ROWS, HD),
-        [kept, partner(sent, "gx", 2)],
+        shape(2, OUT_ROWS, HD),
+        on_chips(merged),
         [pltpu.VMEM((HD, HD), F32)],
     )
-    near = paired(swapped(block), "gx", 2)
-    far = partner(near, "gx", 1)
-
-    kept, sent = call(
+    blocks = call(
         output_kernel,
         "output",
-        [shape(2, count, HD, dtype=F32), shape(2, count, HD)],
-        [near, far, w_out],
+        [shape(count, HD, dtype=F32)] + [shape(count, HD)] * (NY - 1),
+        [near, partner(near, "gx", 1), w_out],
         [
             pltpu.VMEM((NY, OUT_ROWS, HD), F32),
             pltpu.VMEM((NY * ROWS, w_out.shape[0]), F32),
             pltpu.VMEM((NY, count, HD), F32),
         ],
     )
-    kept, sent = call(
-        halve_kernel,
-        "halve",
-        [shape(count, HD, dtype=F32), shape(count, HD)],
-        [kept, partner(sent, "gy", 2)],
-    )
     return call(
         finish_kernel,
         "finish",
         shape(2, 2, columns),
-        [kept, partner(sent, "gy", 1)],
+        on_gy(blocks),
         [pltpu.VMEM((count, HD), F32)],
     )
 

time: 72.1 us -> 59.1 us (0.82)
  starting transfers between devices: 36.6 us -> 25 us
  local copies, waits for them, and re-layouts: 6.81 us -> 1.44 us
  Pallas kernels: 6.33 us -> 10.6 us
  waiting for transfers between devices: 21.7 us -> 20.6 us
  other arithmetic: 0.28 us -> 1.08 us
    ppermute x14 -> x12, starting transfers between devices: 35.3 us -> 12.9 us  [partner(): lax.ppermute(part, axis, [(k, k ^ distance) for k in range(lax.axis_size(...]
    ppermute x14 -> x12, waiting for transfers between devices: 21.7 us -> 10.7 us  [partner(): lax.ppermute(part, axis, [(k, k ^ distance) for k in range(lax.axis_size(...]
    ppermute x2 -> x8, starting transfers between devices: 1.32 us -> 12 us  [on_chips(): received[k, far_x] = lax.ppermute(parts[k], ('gx', 'gy'), pairs)]
    ppermute x2 -> x8, waiting for transfers between devices: 0.01 us -> 9.91 us  [on_chips(): received[k, far_x] = lax.ppermute(parts[k], ('gx', 'gy'), pairs)]
    unnamed x14 -> x12, local copies, waits for them, and re-layouts: 6.12 us -> 0.74 us
    pallas_call x0 -> x1, Pallas kernels: none -> 4.48 us  [fetch(): pl.pallas_call(functools.partial(fetch_kernel, pieces), in_specs=[pl.Bloc...]
    convert_element_type x1, other arithmetic: 0.07 us -> 0.88 us  [rotation(): angles = places.astype(F32)[:, :, None] * frequency[None, None, :]]
    pallas_call x14 -> x11, Pallas kernels: 6.33 us -> 6.09 us  [call(): pl.pallas_call(kernel, in_specs=[SMEM_SPEC] * scalars + [VMEM_SPEC] * (le...]
  transfers between devices with their start and end apart: 16 -> 20, of which waited for: 14 -> 13; matrix products, arithmetic and copies ran while one was open for 1% -> 3% of each run, Pallas kernels for 0% -> 8%
where the time goes in v4:
time: 59.1 us; the launch traced here: 58.8 us
  starting transfers between devices  25 us (42%)
  waiting for transfers between devices  20.6 us (35%)
  Pallas kernels  10.6 us (18%)
  local copies, waits for them, and re-layouts  1.44 us (2%)
  other arithmetic  1.08 us (2%)
    ppermute x12, starting transfers between devices, partner(): lax.ppermute(part, axis, [(k, k ^ distance) for k in range(lax.axis_size(...  12.9 us
    ppermute x8, starting transfers between devices, on_chips(): received[k, far_x] = lax.ppermute(parts[k], ('gx', 'gy'), pairs)  12 us
    ppermute x12, waiting for transfers between devices, partner(): lax.ppermute(part, axis, [(k, k ^ distance) for k in range(lax.axis_size(...  10.7 us
    ppermute x8, waiting for transfers between devices, on_chips(): received[k, far_x] = lax.ppermute(parts[k], ('gx', 'gy'), pairs)  9.91 us
    pallas_call x11, Pallas kernels, call(): pl.pallas_call(kernel, in_specs=[SMEM_SPEC] * scalars + [VMEM_SPEC] * (le...  6.09 us
    pallas_call x1, Pallas kernels, fetch(): pl.pallas_call(functools.partial(fetch_kernel, pieces), in_specs=[pl.Bloc...  4.48 us
  transfers between devices with their start and end apart: 20, of which 13 were waited for; matrix products, arithmetic and copies ran while one was open for 3% of the time, Pallas kernels for 8%

profile of v4, /device:TPU:0, one launch (start us, length us, event | category | flops | bytes accessed | tf_op | source)
XLA Modules:
  0.0 58.8 jit_solution(10089147935854329260)
XLA Ops:
  2.1 2.8 %collective-permute-start.1 = (f32[8,128]{1,0:T(8,128)S(1)}, f32[8,128]{1,0:T(8,128)S(1)}, u32[]{:S(2)}, u32[]{:S(2)}) collective-permute-start(f32[8,128]{1,0:T(8,128)S(1)} %add.24.a), channel_id=1, source_target_pairs={{0,8},{4,12},{8,0},{12,4},{1,9},{5,13},{9,1},{13,5},{2,10},{6,14},... | collective-permute-start | bytes 12296 | tf_op jit(solution)/shard_map/ppermute | solution.py:430
  5.6 0.9 %collective-permute-done.1.b = f32[8,128]{1,0:T(8,128)S(1)} collective-permute-done((f32[8,128]{1,0:T(8,128)S(1)}, f32[8,128]{1,0:T(8,128)S(1)}, u32[]{:S(2)}, u32[]{:S(2)}) %collective-permute-start.1) | collective-permute-done | bytes 4128 | tf_op jit(solution)/shard_map/ppermute | solution.py:430
  6.6 2.2 %collective-permute-start.2 = (bf16[2,2,2048]{2,1,0:T(2,128)(2,1)S(1)}, bf16[2,2,2048]{2,1,0:T(2,128)(2,1)S(1)}, u32[]{:S(2)}, u32[]{:S(2)}) collective-permute-start(bf16[2,2,2048]{2,1,0:T(2,128)(2,1)S(1)} %norm.1.n0), channel_id=1, source_target_pairs={{0,1},{1,0},{2,3},{3,2},{4,5},{5,4},{6,7},{7,6},{8,9},{9,8},{10,11... | collective-permute-start | bytes 49160 | tf_op jit(solution)/shard_map/ppermute | solution.py:430
  8.8 2.6 %collective-permute-start.3 = (bf16[2,2,2048]{2,1,0:T(2,128)(2,1)S(1)}, bf16[2,2,2048]{2,1,0:T(2,128)(2,1)S(1)}, u32[]{:S(2)}, u32[]{:S(2)}) collective-permute-start(bf16[2,2,2048]{2,1,0:T(2,128)(2,1)S(1)} %norm.1.n0), channel_id=1, source_target_pairs={{0,2},{1,3},{2,0},{3,1},{4,6},{5,7},{6,4},{7,5},{8,10},{9,11},{10,... | collective-permute-start | bytes 49160 | tf_op jit(solution)/shard_map/ppermute | solution.py:430
  11.4 0.9 %add_convert_fusion = f32[2,2]{1,0:T(2,128)S(1)} fusion(s32[2]{0:T(128)} %param.15), kind=kLoop, calls=%fused_computation.4 | loop fusion | flops 8 | bytes 24 | tf_op jit(solution)/shard_map/convert_element_type | solution.py:424
  12.3 4.5 %fetch.1.w = bf16[2048,2560]{1,0:T(8,128)(2,1)S(1)} custom-call(bf16[2048,2560]{1,0:T(8,128)(2,1)} %source.1), custom_call_target="tpu_custom_call" | custom-call | bytes 10485760 | tf_op jit(solution)/shard_map/fetch/pallas_call | solution.py:187
  16.9 1.5 %project.1 = (f32[2,80,128]{2,1,0:T(8,128)S(1)}, f32[2,80,128]{2,1,0:T(8,128)S(1)}) custom-call(bf16[2,2,2048]{2,1,0:T(2,128)(2,1)S(1)} %norm.1.n0, bf16[2,2,2048]{2,1,0:T(2,128)(2,1)S(1)} %collective-permute-done.2.n1, bf16[2,2,2048]{2,1,0:T(2,128)(2,1)S(1)} %collective-permute-done.3.n2, bf16[2,2,2048]{2,1,0:T(2,128)(2,1)S(1)} %collective-permute-done.4.n3, ...), custom_call_target="tpu_custom_call" | custom-call | tf_op jit(solution)/shard_map/project/pallas_call | solution.py:155
  18.5 1.2 %collective-permute-done.5.b = f32[2,80,128]{2,1,0:T(8,128)S(1)} collective-permute-done((f32[2,80,128]{2,1,0:T(8,128)S(1)}, f32[2,80,128]{2,1,0:T(8,128)S(1)}, u32[]{:S(2)}, u32[]{:S(2)}) %collective-permute-start.5) | collective-permute-done | bytes 81952 | tf_op jit(solution)/shard_map/ppermute | solution.py:430
  20.4 1.7 %collective-permute-start.7 = (f32[80,128]{1,0:T(8,128)S(1)}, f32[80,128]{1,0:T(8,128)S(1)}, u32[]{:S(2)}, u32[]{:S(2)}) collective-permute-start(f32[80,128]{1,0:T(8,128)S(1)} %get-tuple-element.23), channel_id=1, source_target_pairs={{0,8},{1,9},{2,10},{3,11},{4,13},{5,12},{6,15},{7,14},{8,0},{9,1},... | collective-permute-start | bytes 122888 | tf_op jit(solution)/shard_map/ppermute | solution.py:447
  22.1 3.6 %collective-permute-start.8 = (f32[80,128]{1,0:T(8,128)S(1)}, f32[80,128]{1,0:T(8,128)S(1)}, u32[]{:S(2)}, u32[]{:S(2)}) collective-permute-start(f32[80,128]{1,0:T(8,128)S(1)} %get-tuple-element.24), channel_id=1, source_target_pairs={{0,3},{1,2},{2,1},{3,0},{4,6},{5,7},{6,4},{7,5},{8,11},{9,10},{10,... | collective-permute-start | bytes 122888 | tf_op jit(solution)/shard_map/ppermute | solution.py:447
  25.9 2.1 %collective-permute-done.8.a1 = f32[80,128]{1,0:T(8,128)S(1)} collective-permute-done((f32[80,128]{1,0:T(8,128)S(1)}, f32[80,128]{1,0:T(8,128)S(1)}, u32[]{:S(2)}, u32[]{:S(2)}) %collective-permute-start.8) | collective-permute-done | bytes 40992 | tf_op jit(solution)/shard_map/ppermute | solution.py:447
  28.0 4.7 %collective-permute-done.9.b1 = f32[80,128]{1,0:T(8,128)S(1)} collective-permute-done((f32[80,128]{1,0:T(8,128)S(1)}, f32[80,128]{1,0:T(8,128)S(1)}, u32[]{:S(2)}, u32[]{:S(2)}) %collective-permute-start.9) | collective-permute-done | bytes 40992 | tf_op jit(solution)/shard_map/ppermute | solution.py:447
  32.9 1.1 %collective-permute-done.10.far = bf16[2,80,128]{2,1,0:T(8,128)(2,1)S(1)} collective-permute-done((bf16[2,80,128]{2,1,0:T(8,128)(2,1)S(1)}, bf16[2,80,128]{2,1,0:T(8,128)(2,1)S(1)}, u32[]{:S(2)}, u32[]{:S(2)}) %collective-permute-start.10) | collective-permute-done | bytes 40992 | tf_op jit(solution)/shard_map/ppermute | solution.py:430
  34.0 2.1 %attend.1 = (f32[2,72,128]{2,1,0:T(8,128)S(1)}, f32[2,72,128]{2,1,0:T(8,128)S(1)}) custom-call(s32[2]{0:T(128)S(1)} %copy-done.3, bf16[2,80,128]{2,1,0:T(8,128)(2,1)S(1)} %round.1.near, bf16[2,80,128]{2,1,0:T(8,128)(2,1)S(1)} %collective-permute-done.10.far, f32[2,2,128]{2,1,0:T(2,128)S(1)} %get-tuple-element.36.cosine, ...), custom_call_target="tpu_custom_call" | custom-call | tf_op jit(solution)/shard_map/attend/pallas_call | solution.py:155
  36.3 1.1 %collective-permute-done.11.b = f32[2,72,128]{2,1,0:T(8,128)S(1)} collective-permute-done((f32[2,72,128]{2,1,0:T(8,128)S(1)}, f32[2,72,128]{2,1,0:T(8,128)S(1)}, u32[]{:S(2)}, u32[]{:S(2)}) %collective-permute-start.11) | collective-permute-done | bytes 73760 | tf_op jit(solution)/shard_map/ppermute | solution.py:430
  38.9 1.4 %collective-permute-start.14 = (bf16[80,128]{1,0:T(8,128)(2,1)S(1)}, bf16[80,128]{1,0:T(8,128)(2,1)S(1)}, u32[]{:S(2)}, u32[]{:S(2)}) collective-permute-start(bf16[80,128]{1,0:T(8,128)(2,1)S(1)} %get-tuple-element.28), channel_id=1, source_target_pairs={{0,3},{1,2},{2,1},{3,0},{4,6},{5,7},{6,4},{7,5},{8,11},{9,10},{10,... | collective-permute-start | bytes 61448 | tf_op jit(solution)/shard_map/ppermute | solution.py:447
  40.3 3.3 %collective-permute-start.15 = (bf16[80,128]{1,0:T(8,128)(2,1)S(1)}, bf16[80,128]{1,0:T(8,128)(2,1)S(1)}, u32[]{:S(2)}, u32[]{:S(2)}) collective-permute-start(bf16[80,128]{1,0:T(8,128)(2,1)S(1)} %get-tuple-element.28), channel_id=1, source_target_pairs={{0,11},{1,10},{2,9},{3,8},{4,14},{5,15},{6,12},{7,13},{8,3},{9,2},... | collective-permute-start | bytes 61448 | tf_op jit(solution)/shard_map/ppermute | solution.py:447
  44.5 2.3 %collective-permute-done.15.b1 = bf16[80,128]{1,0:T(8,128)(2,1)S(1)} collective-permute-done((bf16[80,128]{1,0:T(8,128)(2,1)S(1)}, bf16[80,128]{1,0:T(8,128)(2,1)S(1)}, u32[]{:S(2)}, u32[]{:S(2)}) %collective-permute-start.15) | collective-permute-done | bytes 20512 | tf_op jit(solution)/shard_map/ppermute | solution.py:447
  47.1 1.2 %collective-permute-done.16.far = bf16[2,64,128]{2,1,0:T(8,128)(2,1)S(1)} collective-permute-done((bf16[2,64,128]{2,1,0:T(8,128)(2,1)S(1)}, bf16[2,64,128]{2,1,0:T(8,128)(2,1)S(1)}, u32[]{:S(2)}, u32[]{:S(2)}) %collective-permute-start.16) | collective-permute-done | bytes 32800 | tf_op jit(solution)/shard_map/ppermute | solution.py:430
  48.3 1.2 %output.1 = (f32[64,128]{1,0:T(8,128)S(1)}, bf16[64,128]{1,0:T(8,128)(2,1)S(1)}, bf16[64,128]{1,0:T(8,128)(2,1)S(1)}, bf16[64,128]{1,0:T(8,128)(2,1)S(1)}) custom-call(bf16[2,64,128]{2,1,0:T(8,128)(2,1)S(1)} %settle.1.near, bf16[2,64,128]{2,1,0:T(8,128)(2,1)S(1)} %collective-permute-done.16.far, bf16[2048,2048]{1,0:T(8,128)(2,1)S(1)} %bitcast.1), custom_call_target="tpu_custom_call" | custom-call | tf_op jit(solution)/shard_map/output/pallas_call | solution.py:155
  50.0 2.6 %collective-permute-start.18 = (bf16[64,128]{1,0:T(8,128)(2,1)S(1)}, bf16[64,128]{1,0:T(8,128)(2,1)S(1)}, u32[]{:S(2)}, u32[]{:S(2)}) collective-permute-start(bf16[64,128]{1,0:T(8,128)(2,1)S(1)} %get-tuple-element.31), channel_id=1, source_target_pairs={{0,2},{1,3},{2,0},{3,1},{4,6},{5,7},{6,4},{7,5},{8,10},{9,11},{10,... | collective-permute-start | bytes 49160 | tf_op jit(solution)/shard_map/ppermute | solution.py:430
  52.7 1.4 %collective-permute-start.19 = (bf16[64,128]{1,0:T(8,128)(2,1)S(1)}, bf16[64,128]{1,0:T(8,128)(2,1)S(1)}, u32[]{:S(2)}, u32[]{:S(2)}) collective-permute-start(bf16[64,128]{1,0:T(8,128)(2,1)S(1)} %get-tuple-element.32), channel_id=1, source_target_pairs={{0,3},{1,2},{2,1},{3,0},{4,7},{5,6},{6,5},{7,4},{8,11},{9,10},{10,... | collective-permute-start | bytes 49160 | tf_op jit(solution)/shard_map/ppermute | solution.py:430
  54.0 0.9 %collective-permute-done.18.c = bf16[64,128]{1,0:T(8,128)(2,1)S(1)} collective-permute-done((bf16[64,128]{1,0:T(8,128)(2,1)S(1)}, bf16[64,128]{1,0:T(8,128)(2,1)S(1)}, u32[]{:S(2)}, u32[]{:S(2)}) %collective-permute-start.18) | collective-permute-done | bytes 16416 | tf_op jit(solution)/shard_map/ppermute | solution.py:430
  54.9 3.2 %collective-permute-done.19.d = bf16[64,128]{1,0:T(8,128)(2,1)S(1)} collective-permute-done((bf16[64,128]{1,0:T(8,128)(2,1)S(1)}, bf16[64,128]{1,0:T(8,128)(2,1)S(1)}, u32[]{:S(2)}, u32[]{:S(2)}) %collective-permute-start.19) | collective-permute-done | bytes 16416 | tf_op jit(solution)/shard_map/ppermute | solution.py:430
  (46 shorter events, 8.1 us)
Async XLA Ops:
  0.8 1.3 %collective-permute-start = (f32[8,128]{1,0:T(8,128)S(1)}, f32[8,128]{1,0:T(8,128)S(1)}, u32[]{:S(2)}, u32[]{:S(2)}) collective-permute-start(f32[8,128]{1,0:T(8,128)S(1)} %get-tuple-element.20.a), channel_id=1, source_target_pairs={{0,4},{4,0},{8,12},{12,8},{1,5},{5,1},{9,13},{13,9},{2,6},{6,2},{1... | collective-permute-start | bytes 12296 | tf_op jit(solution)/shard_map/ppermute | solution.py:430
  2.1 4.4 %collective-permute-start.1 = (f32[8,128]{1,0:T(8,128)S(1)}, f32[8,128]{1,0:T(8,128)S(1)}, u32[]{:S(2)}, u32[]{:S(2)}) collective-permute-start(f32[8,128]{1,0:T(8,128)S(1)} %add.24.a), channel_id=1, source_target_pairs={{0,8},{4,12},{8,0},{12,4},{1,9},{5,13},{9,1},{13,5},{2,10},{6,14},... | collective-permute-start | bytes 12296 | tf_op jit(solution)/shard_map/ppermute | solution.py:430
  6.6 10.2 %collective-permute-start.2 = (bf16[2,2,2048]{2,1,0:T(2,128)(2,1)S(1)}, bf16[2,2,2048]{2,1,0:T(2,128)(2,1)S(1)}, u32[]{:S(2)}, u32[]{:S(2)}) collective-permute-start(bf16[2,2,2048]{2,1,0:T(2,128)(2,1)S(1)} %norm.1.n0), channel_id=1, source_target_pairs={{0,1},{1,0},{2,3},{3,2},{4,5},{5,4},{6,7},{7,6},{8,9},{9,8},{10,11... | collective-permute-start | bytes 49160 | tf_op jit(solution)/shard_map/ppermute | solution.py:430
  8.8 8.0 %collective-permute-start.3 = (bf16[2,2,2048]{2,1,0:T(2,128)(2,1)S(1)}, bf16[2,2,2048]{2,1,0:T(2,128)(2,1)S(1)}, u32[]{:S(2)}, u32[]{:S(2)}) collective-permute-start(bf16[2,2,2048]{2,1,0:T(2,128)(2,1)S(1)} %norm.1.n0), channel_id=1, source_target_pairs={{0,2},{1,3},{2,0},{3,1},{4,6},{5,7},{6,4},{7,5},{8,10},{9,11},{10,... | collective-permute-start | bytes 49160 | tf_op jit(solution)/shard_map/ppermute | solution.py:430
  11.4 5.5 %collective-permute-start.4 = (bf16[2,2,2048]{2,1,0:T(2,128)(2,1)S(1)}, bf16[2,2,2048]{2,1,0:T(2,128)(2,1)S(1)}, u32[]{:S(2)}, u32[]{:S(2)}) collective-permute-start(bf16[2,2,2048]{2,1,0:T(2,128)(2,1)S(1)} %norm.1.n0), channel_id=1, source_target_pairs={{0,3},{1,2},{2,1},{3,0},{4,7},{5,6},{6,5},{7,4},{8,11},{9,10},{10,... | collective-permute-start | bytes 49160 | tf_op jit(solution)/shard_map/ppermute | solution.py:430
  11.4 36.9 %slice-start = ((s8[8388608]{0:T(1024)(128)(4,1)}), s8[4194304]{0:T(1024)(128)(4,1)S(1)}, s32[]{:S(2)}) async-start(s8[8388608]{0:T(1024)(128)(4,1)} %bitcast), calls=%async_computation | async-start | bytes 8388608
  12.3 36.1 %slice-start.1 = ((s8[8388608]{0:T(1024)(128)(4,1)}), s8[4194304]{0:T(1024)(128)(4,1)S(1)}, s32[]{:S(2)}) async-start(s8[8388608]{0:T(1024)(128)(4,1)} %bitcast), calls=%async_computation.1 | async-start | bytes 8388608
  16.7 17.3 %copy-start = (bf16[2,384,1024]{2,1,0:T(8,128)(2,1)S(1)}, bf16[2,384,1024]{2,1,0:T(8,128)(2,1)}, u32[]{:S(2)}) copy-start(bf16[2,384,1024]{2,1,0:T(8,128)(2,1)} %keys.1) | copy-start | bytes 4718596
  16.8 17.2 %copy-start.1 = (bf16[2,384,1024]{2,1,0:T(8,128)(2,1)S(1)}, bf16[2,384,1024]{2,1,0:T(8,128)(2,1)}, u32[]{:S(2)}) copy-start(bf16[2,384,1024]{2,1,0:T(8,128)(2,1)} %values.1) | copy-start | bytes 4718596
  18.4 1.3 %collective-permute-start.5 = (f32[2,80,128]{2,1,0:T(8,128)S(1)}, f32[2,80,128]{2,1,0:T(8,128)S(1)}, u32[]{:S(2)}, u32[]{:S(2)}) collective-permute-start(f32[2,80,128]{2,1,0:T(8,128)S(1)} %get-tuple-element.22), channel_id=1, source_target_pairs={{0,4},{4,0},{8,12},{12,8},{1,5},{5,1},{9,13},{13,9},{2,6},{6,2},{1... | collective-permute-start | bytes 245768 | tf_op jit(solution)/shard_map/ppermute | solution.py:430
  19.8 6.1 %collective-permute-start.6 = (f32[80,128]{1,0:T(8,128)S(1)}, f32[80,128]{1,0:T(8,128)S(1)}, u32[]{:S(2)}, u32[]{:S(2)}) collective-permute-start(f32[80,128]{1,0:T(8,128)S(1)} %get-tuple-element.23), channel_id=1, source_target_pairs={{0,0},{1,1},{2,2},{3,3},{4,5},{5,4},{6,7},{7,6},{8,8},{9,9},{10,10... | collective-permute-start | bytes 122888 | tf_op jit(solution)/shard_map/ppermute | solution.py:447
  20.4 5.5 %collective-permute-start.7 = (f32[80,128]{1,0:T(8,128)S(1)}, f32[80,128]{1,0:T(8,128)S(1)}, u32[]{:S(2)}, u32[]{:S(2)}) collective-permute-start(f32[80,128]{1,0:T(8,128)S(1)} %get-tuple-element.23), channel_id=1, source_target_pairs={{0,8},{1,9},{2,10},{3,11},{4,13},{5,12},{6,15},{7,14},{8,0},{9,1},... | collective-permute-start | bytes 122888 | tf_op jit(solution)/shard_map/ppermute | solution.py:447
  22.1 5.9 %collective-permute-start.8 = (f32[80,128]{1,0:T(8,128)S(1)}, f32[80,128]{1,0:T(8,128)S(1)}, u32[]{:S(2)}, u32[]{:S(2)}) collective-permute-start(f32[80,128]{1,0:T(8,128)S(1)} %get-tuple-element.24), channel_id=1, source_target_pairs={{0,3},{1,2},{2,1},{3,0},{4,6},{5,7},{6,4},{7,5},{8,11},{9,10},{10,... | collective-permute-start | bytes 122888 | tf_op jit(solution)/shard_map/ppermute | solution.py:447
  25.7 7.0 %collective-permute-start.9 = (f32[80,128]{1,0:T(8,128)S(1)}, f32[80,128]{1,0:T(8,128)S(1)}, u32[]{:S(2)}, u32[]{:S(2)}) collective-permute-start(f32[80,128]{1,0:T(8,128)S(1)} %get-tuple-element.24), channel_id=1, source_target_pairs={{0,11},{1,10},{2,9},{3,8},{4,14},{5,15},{6,12},{7,13},{8,3},{9,2},... | collective-permute-start | bytes 122888 | tf_op jit(solution)/shard_map/ppermute | solution.py:447
  32.7 1.3 %collective-permute-start.10 = (bf16[2,80,128]{2,1,0:T(8,128)(2,1)S(1)}, bf16[2,80,128]{2,1,0:T(8,128)(2,1)S(1)}, u32[]{:S(2)}, u32[]{:S(2)}) collective-permute-start(bf16[2,80,128]{2,1,0:T(8,128)(2,1)S(1)} %round.1.near), channel_id=1, source_target_pairs={{0,4},{4,0},{8,12},{12,8},{1,5},{5,1},{9,13},{13,9},{2,6},{6,2},{1... | collective-permute-start | bytes 122888 | tf_op jit(solution)/shard_map/ppermute | solution.py:430
  36.1 1.3 %collective-permute-start.11 = (f32[2,72,128]{2,1,0:T(8,128)S(1)}, f32[2,72,128]{2,1,0:T(8,128)S(1)}, u32[]{:S(2)}, u32[]{:S(2)}) collective-permute-start(f32[2,72,128]{2,1,0:T(8,128)S(1)} %get-tuple-element.26), channel_id=1, source_target_pairs={{0,4},{4,0},{8,12},{12,8},{1,5},{5,1},{9,13},{13,9},{2,6},{6,2},{1... | collective-permute-start | bytes 221192 | tf_op jit(solution)/shard_map/ppermute | solution.py:430
  37.6 6.0 %collective-permute-start.12 = (bf16[80,128]{1,0:T(8,128)(2,1)S(1)}, bf16[80,128]{1,0:T(8,128)(2,1)S(1)}, u32[]{:S(2)}, u32[]{:S(2)}) collective-permute-start(bf16[80,128]{1,0:T(8,128)(2,1)S(1)} %get-tuple-element.27), channel_id=1, source_target_pairs={{0,0},{1,1},{2,2},{3,3},{4,5},{5,4},{6,7},{7,6},{8,8},{9,9},{10,10... | collective-permute-start | bytes 61448 | tf_op jit(solution)/shard_map/ppermute | solution.py:447
  38.3 5.4 %collective-permute-start.13 = (bf16[80,128]{1,0:T(8,128)(2,1)S(1)}, bf16[80,128]{1,0:T(8,128)(2,1)S(1)}, u32[]{:S(2)}, u32[]{:S(2)}) collective-permute-start(bf16[80,128]{1,0:T(8,128)(2,1)S(1)} %get-tuple-element.27), channel_id=1, source_target_pairs={{0,8},{1,9},{2,10},{3,11},{4,13},{5,12},{6,15},{7,14},{8,0},{9,1},... | collective-permute-start | bytes 61448 | tf_op jit(solution)/shard_map/ppermute | solution.py:447
  38.9 5.6 %collective-permute-start.14 = (bf16[80,128]{1,0:T(8,128)(2,1)S(1)}, bf16[80,128]{1,0:T(8,128)(2,1)S(1)}, u32[]{:S(2)}, u32[]{:S(2)}) collective-permute-start(bf16[80,128]{1,0:T(8,128)(2,1)S(1)} %get-tuple-element.28), channel_id=1, source_target_pairs={{0,3},{1,2},{2,1},{3,0},{4,6},{5,7},{6,4},{7,5},{8,11},{9,10},{10,... | collective-permute-start | bytes 61448 | tf_op jit(solution)/shard_map/ppermute | solution.py:447
  40.3 6.5 %collective-permute-start.15 = (bf16[80,128]{1,0:T(8,128)(2,1)S(1)}, bf16[80,128]{1,0:T(8,128)(2,1)S(1)}, u32[]{:S(2)}, u32[]{:S(2)}) collective-permute-start(bf16[80,128]{1,0:T(8,128)(2,1)S(1)} %get-tuple-element.28), channel_id=1, source_target_pairs={{0,11},{1,10},{2,9},{3,8},{4,14},{5,15},{6,12},{7,13},{8,3},{9,2},... | collective-permute-start | bytes 61448 | tf_op jit(solution)/shard_map/ppermute | solution.py:447
  47.0 1.3 %collective-permute-start.16 = (bf16[2,64,128]{2,1,0:T(8,128)(2,1)S(1)}, bf16[2,64,128]{2,1,0:T(8,128)(2,1)S(1)}, u32[]{:S(2)}, u32[]{:S(2)}) collective-permute-start(bf16[2,64,128]{2,1,0:T(8,128)(2,1)S(1)} %settle.1.near), channel_id=1, source_target_pairs={{0,4},{4,0},{8,12},{12,8},{1,5},{5,1},{9,13},{13,9},{2,6},{6,2},{1... | collective-permute-start | bytes 98312 | tf_op jit(solution)/shard_map/ppermute | solution.py:430
  49.6 4.5 %collective-permute-start.17 = (bf16[64,128]{1,0:T(8,128)(2,1)S(1)}, bf16[64,128]{1,0:T(8,128)(2,1)S(1)}, u32[]{:S(2)}, u32[]{:S(2)}) collective-permute-start(bf16[64,128]{1,0:T(8,128)(2,1)S(1)} %get-tuple-element.30), channel_id=1, source_target_pairs={{0,1},{1,0},{2,3},{3,2},{4,5},{5,4},{6,7},{7,6},{8,9},{9,8},{10,11... | collective-permute-start | bytes 49160 | tf_op jit(solution)/shard_map/ppermute | solution.py:430
  50.0 4.9 %collective-permute-start.18 = (bf16[64,128]{1,0:T(8,128)(2,1)S(1)}, bf16[64,128]{1,0:T(8,128)(2,1)S(1)}, u32[]{:S(2)}, u32[]{:S(2)}) collective-permute-start(bf16[64,128]{1,0:T(8,128)(2,1)S(1)} %get-tuple-element.31), channel_id=1, source_target_pairs={{0,2},{1,3},{2,0},{3,1},{4,6},{5,7},{6,4},{7,5},{8,10},{9,11},{10,... | collective-permute-start | bytes 49160 | tf_op jit(solution)/shard_map/ppermute | solution.py:430
  52.7 5.5 %collective-permute-start.19 = (bf16[64,128]{1,0:T(8,128)(2,1)S(1)}, bf16[64,128]{1,0:T(8,128)(2,1)S(1)}, u32[]{:S(2)}, u32[]{:S(2)}) collective-permute-start(bf16[64,128]{1,0:T(8,128)(2,1)S(1)} %get-tuple-element.32), channel_id=1, source_target_pairs={{0,3},{1,2},{2,1},{3,0},{4,7},{5,6},{6,5},{7,4},{8,11},{9,10},{10,... | collective-permute-start | bytes 49160 | tf_op jit(solution)/shard_map/ppermute | solution.py:430
  (2 other events, 18.0 us)

commit v5 on v4

--- a/solution.py
+++ b/solution.py
@@ -1,5 +1,3 @@
-import functools
-
 import jax
 import jax.numpy as jnp
 from jax import lax
@@ -145,22 +143,25 @@
 QUERIES = H * ROWS
 GROUP_ROWS = QUERIES // KVH
 VMEM_SPEC = pl.BlockSpec(memory_space=pltpu.VMEM)
+HBM_SPEC = pl.BlockSpec(memory_space=pltpu.HBM)
 SMEM_SPEC = pl.BlockSpec(memory_space=pltpu.SMEM)
 F32 = jnp.float32
 BF16 = jnp.bfloat16
 
 
-def call(kernel, name, out_shape, operands, scratch=(), scalars=0, mib=8):
+def call(kernel, name, out_shape, operands, scratch=(), scalars=0, mib=8, later=()):
     many = isinstance(out_shape, (list, tuple))
     return pl.pallas_call(
         kernel,
-        in_specs=[SMEM_SPEC] * scalars + [VMEM_SPEC] * (len(operands) - scalars),
+        in_specs=[SMEM_SPEC] * scalars
+        + [VMEM_SPEC] * (len(operands) - scalars)
+        + [HBM_SPEC] * len(later),
         out_specs=[VMEM_SPEC] * len(out_shape) if many else VMEM_SPEC,
         out_shape=out_shape,
         scratch_shapes=list(scratch),
         compiler_params=pltpu.CompilerParams(vmem_limit_bytes=mib << 20),
         name=name,
-    )(*operands)
+    )(*operands, *(pltpu.with_memory_space_constraint(array, pltpu.HBM) for array in later))
 
 
 def high_rest(values):
@@ -168,35 +169,7 @@
     return high, values - high
 
 
-def fetch_kernel(pieces, source, out, done):
-    rows = source.shape[0] // pieces
-    copies = [
-        pltpu.make_async_copy(
-            source.at[pl.ds(rows * k, rows)], out.at[pl.ds(rows * k, rows)], done.at[k]
-        )
-        for k in range(pieces)
-    ]
-    for copy in copies:
-        copy.start()
-    for copy in copies:
-        copy.wait()
-
-
-def fetch(array, pieces=8):
-    size = array.size * array.dtype.itemsize
-    return pl.pallas_call(
-        functools.partial(fetch_kernel, pieces),
-        in_specs=[pl.BlockSpec(memory_space=pltpu.HBM)],
-        out_specs=VMEM_SPEC,
-        out_shape=pltpu.VMEM(array.shape, array.dtype),
-        scratch_shapes=[pltpu.SemaphoreType.DMA((pieces,))],
-        compiler_params=pltpu.CompilerParams(vmem_limit_bytes=1 << 20),
-        cost_estimate=pl.CostEstimate(flops=0, bytes_accessed=size, transcendentals=0),
-        name="fetch",
-    )(pltpu.with_memory_space_constraint(array, pltpu.HBM))
-
-
-def square_kernel(hidden, out, held):
+def square_kernel(hidden, later, out, held):
     out[...] = jnp.zeros_like(out)
     held[...] = hidden[...]
     for timeline in range(2):
@@ -217,7 +190,7 @@
         out[timeline] = (hidden[timeline].astype(F32) * scale * wide_gain).astype(BF16)
 
 
-def project_kernel(n0, n1, n2, n3, w, kept, sent, rows, sums):
+def project_kernel(n3, n2, n1, n0, w, kept, sent, rows, sums):
     core = lax.axis_index("gx") & 1
     for shift, normed in enumerate((n0, n1, n2, n3)):
         for timeline in range(2):
@@ -243,7 +216,7 @@
         out[...] = a[k] + b[k]
 
 
-def round_kernel(a0, b0, a1, b1, out):
+def round_kernel(b1, a1, b0, a0, out):
     out[0] = (a0[...] + b0[...]).astype(BF16)
     out[1] = (a1[...] + b1[...]).astype(BF16)
 
@@ -365,7 +338,7 @@
         out[OUT_ROWS:, :] = jnp.concatenate([pieces, jnp.zeros_like(pieces)], axis=0).astype(BF16)
 
 
-def settle_kernel(a0, b0, a1, b1, out, sheet):
+def settle_kernel(b1, a1, b0, a0, out, sheet):
     factors = []
     for pair in ((a0, b0), (a1, b1)):
         maxima, totals = [], []
@@ -409,7 +382,7 @@
         out[...] = sums[shift].astype(BF16)
 
 
-def finish_kernel(a, b, c, d, out, total):
+def finish_kernel(d, c, b, a, out, total):
     total[...] = (a[...] + b[...].astype(F32)) + (c[...].astype(F32) + d[...].astype(F32))
     for chunk in range(out.shape[2] // HD):
         for timeline in range(2):
@@ -431,8 +404,7 @@
 
 
 def on_gy(parts):
-    far = {y: partner(parts[y], "gy", y) for y in (3, 2, 1)}
-    return [parts[0], far[1], far[2], far[3]]
+    return [partner(parts[y], "gy", y) if y else parts[y] for y in (3, 2, 1, 0)]
 
 
 def on_chips(parts):
@@ -445,7 +417,7 @@
                 for y in range(NY)
             ]
             received[k, far_x] = lax.ppermute(parts[k], ("gx", "gy"), pairs)
-    return [received[k, far_x] for k in range(2) for far_x in range(2)]
+    return [received[k, far_x] for k in (1, 0) for far_x in (1, 0)]
 
 
 def small_body(hidden, norm_gain, w_qkv, w_out, k_cache, v_cache, cache_len, positions):
@@ -458,12 +430,14 @@
     columns = w_out.shape[1]
     features = hidden.shape[2]
     count = columns // HD * ROWS
+    pinned_w_qkv = pinned(w_qkv)
     hidden, w_out, k_cache, v_cache = map(pinned, (hidden, w_out, k_cache, v_cache))
-    w_qkv = fetch(w_qkv)
     cosine, sine = rotation(positions)
 
     line = shape(8, HD, dtype=F32)
-    squares, hidden = call(square_kernel, "square", [line, shape(*hidden.shape)], [hidden])
+    squares, hidden = call(
+        square_kernel, "square", [line, shape(*hidden.shape)], [hidden], later=[w_qkv]
+    )
     squares = call(add_kernel, "add", line, [squares, partner(squares, "gx", 1)])
     normed = call(
         norm_kernel,
@@ -476,7 +450,7 @@
         project_kernel,
         "project",
         [half, half],
-        [*on_gy([normed] * NY), w_qkv],
+        [*on_gy([normed] * NY), pinned_w_qkv],
         [pltpu.VMEM((NY * ROWS, features), F32), pltpu.VMEM((NY, QKV_ROWS, HD), F32)],
     )
     block = shape(QKV_ROWS, HD, dtype=F32)

time: 59.1 us -> 51.4 us (0.87)
  Pallas kernels: 10.6 us -> 6.04 us
  waiting for transfers between devices: 20.6 us -> 16.6 us
  local copies, waits for them, and re-layouts: 1.44 us -> 2.33 us
    pallas_call x1 -> x0, Pallas kernels: 4.48 us -> none  [fetch(): pl.pallas_call(functools.partial(fetch_kernel, pieces), in_specs=[pl.Bloc...]
    ppermute x8, waiting for transfers between devices: 9.91 us -> 5.51 us  [on_chips(): received[k, far_x] = lax.ppermute(parts[k], ('gx', 'gy'), pairs)]
    broadcast_in_dim x1, local copies, waits for them, and re-layouts: 0.69 us -> 1.44 us  [small_body(): norm_gain[None]]
  transfers between devices with their start and end apart: 20 -> 20, of which waited for: 13 -> 15; matrix products, arithmetic and copies ran while one was open for 3% -> 5% of each run, Pallas kernels for 8% -> 0%
where the time goes in v5:
time: 51.4 us; the launch traced here: 51.1 us
  starting transfers between devices  25.2 us (49%)
  waiting for transfers between devices  16.6 us (32%)
  Pallas kernels  6.04 us (12%)
  local copies, waits for them, and re-layouts  2.33 us (5%)
  other arithmetic  0.93 us (2%)
    ppermute x12, starting transfers between devices, partner(): lax.ppermute(part, axis, [(k, k ^ distance) for k in range(lax.axis_size(...  13.2 us
    ppermute x8, starting transfers between devices, on_chips(): received[k, far_x] = lax.ppermute(parts[k], ('gx', 'gy'), pairs)  12 us
    ppermute x12, waiting for transfers between devices, partner(): lax.ppermute(part, axis, [(k, k ^ distance) for k in range(lax.axis_size(...  11 us
    pallas_call x11, Pallas kernels, call(): pl.pallas_call(kernel, in_specs=[SMEM_SPEC] * scalars + [VMEM_SPEC] * (le...  6.04 us
    ppermute x8, waiting for transfers between devices, on_chips(): received[k, far_x] = lax.ppermute(parts[k], ('gx', 'gy'), pairs)  5.51 us
    broadcast_in_dim x1, local copies, waits for them, and re-layouts, small_body(): norm_gain[None]  1.44 us
  transfers between devices with their start and end apart: 20, of which 15 were waited for; matrix products, arithmetic and copies ran while one was open for 5% of the time, Pallas kernels for 0%

profile of v5, /device:TPU:0, one launch (start us, length us, event | category | flops | bytes accessed | tf_op | source)
XLA Modules:
  0.0 51.1 jit_solution(15127287097562574607)
XLA Ops:
  0.0 0.9 %copy-done.4 = bf16[2,2,2048]{2,1,0:T(2,128)(2,1)S(1)} copy-done((bf16[2,2,2048]{2,1,0:T(2,128)(2,1)S(1)}, bf16[2,2,2048]{2,1,0:T(2,128)(2,1)}, u32[]{:S(2)}) %copy-start.4) | copy-done | bytes 16408
  1.4 0.8 %collective-permute-done.b = f32[8,128]{1,0:T(8,128)S(1)} collective-permute-done((f32[8,128]{1,0:T(8,128)S(1)}, f32[8,128]{1,0:T(8,128)S(1)}, u32[]{:S(2)}, u32[]{:S(2)}) %collective-permute-start) | collective-permute-done | bytes 4128 | tf_op jit(solution)/shard_map/ppermute | solution.py:403
  2.3 2.8 %collective-permute-start.1 = (f32[8,128]{1,0:T(8,128)S(1)}, f32[8,128]{1,0:T(8,128)S(1)}, u32[]{:S(2)}, u32[]{:S(2)}) collective-permute-start(f32[8,128]{1,0:T(8,128)S(1)} %add.24.a), channel_id=1, source_target_pairs={{0,8},{4,12},{8,0},{12,4},{1,9},{5,13},{9,1},{13,5},{2,10},{6,14},... | collective-permute-start | bytes 12296 | tf_op jit(solution)/shard_map/ppermute | solution.py:403
  5.1 1.4 %broadcast_in_dim.2.gain = bf16[1,2048]{1,0:T(2,128)(2,1)S(1)} reshape(bf16[2048]{0:T(1024)(128)(2,1)} %param.9) | data formatting | bytes 8192 | tf_op jit(solution)/shard_map/broadcast_in_dim | solution.py:446
  6.8 4.2 %collective-permute-start.2 = (bf16[2,2,2048]{2,1,0:T(2,128)(2,1)S(1)}, bf16[2,2,2048]{2,1,0:T(2,128)(2,1)S(1)}, u32[]{:S(2)}, u32[]{:S(2)}) collective-permute-start(bf16[2,2,2048]{2,1,0:T(2,128)(2,1)S(1)} %norm.1.n0), channel_id=1, source_target_pairs={{0,3},{1,2},{2,1},{3,0},{4,7},{5,6},{6,5},{7,4},{8,11},{9,10},{10,... | collective-permute-start | bytes 49160 | tf_op jit(solution)/shard_map/ppermute | solution.py:403
  11.6 0.7 %add_convert_fusion = f32[2,2]{1,0:T(2,128)S(1)} fusion(s32[2]{0:T(128)} %param.15), kind=kLoop, calls=%fused_computation.4 | loop fusion | flops 8 | bytes 24 | tf_op jit(solution)/shard_map/convert_element_type | solution.py:397
  12.9 2.7 %collective-permute-done.3.n2 = bf16[2,2,2048]{2,1,0:T(2,128)(2,1)S(1)} collective-permute-done((bf16[2,2,2048]{2,1,0:T(2,128)(2,1)S(1)}, bf16[2,2,2048]{2,1,0:T(2,128)(2,1)S(1)}, u32[]{:S(2)}, u32[]{:S(2)}) %collective-permute-start.3) | collective-permute-done | bytes 16416 | tf_op jit(solution)/shard_map/ppermute | solution.py:403
  15.6 1.5 %project.1 = (f32[2,80,128]{2,1,0:T(8,128)S(1)}, f32[2,80,128]{2,1,0:T(8,128)S(1)}) custom-call(bf16[2,2,2048]{2,1,0:T(2,128)(2,1)S(1)} %collective-permute-done.2.n3, bf16[2,2,2048]{2,1,0:T(2,128)(2,1)S(1)} %collective-permute-done.3.n2, bf16[2,2,2048]{2,1,0:T(2,128)(2,1)S(1)} %collective-permute-done.4.n1, bf16[2,2,2048]{2,1,0:T(2,128)(2,1)S(1)} %norm.1.n0, ...), custom_call_target="tpu_custom_call" | custom-call | tf_op jit(solution)/shard_map/project/pallas_call | solution.py:154
  17.2 1.2 %collective-permute-done.5.b = f32[2,80,128]{2,1,0:T(8,128)S(1)} collective-permute-done((f32[2,80,128]{2,1,0:T(8,128)S(1)}, f32[2,80,128]{2,1,0:T(8,128)S(1)}, u32[]{:S(2)}, u32[]{:S(2)}) %collective-permute-start.5) | collective-permute-done | bytes 81952 | tf_op jit(solution)/shard_map/ppermute | solution.py:403
  18.5 2.5 %collective-permute-start.6 = (f32[80,128]{1,0:T(8,128)S(1)}, f32[80,128]{1,0:T(8,128)S(1)}, u32[]{:S(2)}, u32[]{:S(2)}) collective-permute-start(f32[80,128]{1,0:T(8,128)S(1)} %get-tuple-element.23), channel_id=1, source_target_pairs={{0,11},{1,10},{2,9},{3,8},{4,14},{5,15},{6,12},{7,13},{8,3},{9,2},... | collective-permute-start | bytes 122888 | tf_op jit(solution)/shard_map/ppermute | solution.py:419
  20.9 2.4 %collective-permute-start.7 = (f32[80,128]{1,0:T(8,128)S(1)}, f32[80,128]{1,0:T(8,128)S(1)}, u32[]{:S(2)}, u32[]{:S(2)}) collective-permute-start(f32[80,128]{1,0:T(8,128)S(1)} %get-tuple-element.23), channel_id=1, source_target_pairs={{0,3},{1,2},{2,1},{3,0},{4,6},{5,7},{6,4},{7,5},{8,11},{9,10},{10,... | collective-permute-start | bytes 122888 | tf_op jit(solution)/shard_map/ppermute | solution.py:419
  25.3 1.6 %collective-permute-done.7.a1 = f32[80,128]{1,0:T(8,128)S(1)} collective-permute-done((f32[80,128]{1,0:T(8,128)S(1)}, f32[80,128]{1,0:T(8,128)S(1)}, u32[]{:S(2)}, u32[]{:S(2)}) %collective-permute-start.7) | collective-permute-done | bytes 40992 | tf_op jit(solution)/shard_map/ppermute | solution.py:419
  27.5 1.1 %collective-permute-done.10.far = bf16[2,80,128]{2,1,0:T(8,128)(2,1)S(1)} collective-permute-done((bf16[2,80,128]{2,1,0:T(8,128)(2,1)S(1)}, bf16[2,80,128]{2,1,0:T(8,128)(2,1)S(1)}, u32[]{:S(2)}, u32[]{:S(2)}) %collective-permute-start.10) | collective-permute-done | bytes 40992 | tf_op jit(solution)/shard_map/ppermute | solution.py:403
  28.6 2.0 %attend.1 = (f32[2,72,128]{2,1,0:T(8,128)S(1)}, f32[2,72,128]{2,1,0:T(8,128)S(1)}) custom-call(s32[2]{0:T(128)S(1)} %copy-done.5, bf16[2,80,128]{2,1,0:T(8,128)(2,1)S(1)} %round.1.near, bf16[2,80,128]{2,1,0:T(8,128)(2,1)S(1)} %collective-permute-done.10.far, f32[2,2,128]{2,1,0:T(2,128)S(1)} %get-tuple-element.36.cosine, ...), custom_call_target="tpu_custom_call" | custom-call | tf_op jit(solution)/shard_map/attend/pallas_call | solution.py:154
  30.9 1.1 %collective-permute-done.11.b = f32[2,72,128]{2,1,0:T(8,128)S(1)} collective-permute-done((f32[2,72,128]{2,1,0:T(8,128)S(1)}, f32[2,72,128]{2,1,0:T(8,128)S(1)}, u32[]{:S(2)}, u32[]{:S(2)}) %collective-permute-start.11) | collective-permute-done | bytes 73760 | tf_op jit(solution)/shard_map/ppermute | solution.py:403
  32.2 3.2 %collective-permute-start.12 = (bf16[80,128]{1,0:T(8,128)(2,1)S(1)}, bf16[80,128]{1,0:T(8,128)(2,1)S(1)}, u32[]{:S(2)}, u32[]{:S(2)}) collective-permute-start(bf16[80,128]{1,0:T(8,128)(2,1)S(1)} %get-tuple-element.27), channel_id=1, source_target_pairs={{0,11},{1,10},{2,9},{3,8},{4,14},{5,15},{6,12},{7,13},{8,3},{9,2},... | collective-permute-start | bytes 61448 | tf_op jit(solution)/shard_map/ppermute | solution.py:419
  36.1 1.5 %collective-permute-start.14 = (bf16[80,128]{1,0:T(8,128)(2,1)S(1)}, bf16[80,128]{1,0:T(8,128)(2,1)S(1)}, u32[]{:S(2)}, u32[]{:S(2)}) collective-permute-start(bf16[80,128]{1,0:T(8,128)(2,1)S(1)} %get-tuple-element.28), channel_id=1, source_target_pairs={{0,8},{1,9},{2,10},{3,11},{4,13},{5,12},{6,15},{7,14},{8,0},{9,1},... | collective-permute-start | bytes 61448 | tf_op jit(solution)/shard_map/ppermute | solution.py:419
  38.8 2.2 %collective-permute-done.13.a1 = bf16[80,128]{1,0:T(8,128)(2,1)S(1)} collective-permute-done((bf16[80,128]{1,0:T(8,128)(2,1)S(1)}, bf16[80,128]{1,0:T(8,128)(2,1)S(1)}, u32[]{:S(2)}, u32[]{:S(2)}) %collective-permute-start.13) | collective-permute-done | bytes 20512 | tf_op jit(solution)/shard_map/ppermute | solution.py:419
  41.4 1.1 %collective-permute-done.16.far = bf16[2,64,128]{2,1,0:T(8,128)(2,1)S(1)} collective-permute-done((bf16[2,64,128]{2,1,0:T(8,128)(2,1)S(1)}, bf16[2,64,128]{2,1,0:T(8,128)(2,1)S(1)}, u32[]{:S(2)}, u32[]{:S(2)}) %collective-permute-start.16) | collective-permute-done | bytes 32800 | tf_op jit(solution)/shard_map/ppermute | solution.py:403
  42.6 1.2 %output.1 = (f32[64,128]{1,0:T(8,128)S(1)}, bf16[64,128]{1,0:T(8,128)(2,1)S(1)}, bf16[64,128]{1,0:T(8,128)(2,1)S(1)}, bf16[64,128]{1,0:T(8,128)(2,1)S(1)}) custom-call(bf16[2,64,128]{2,1,0:T(8,128)(2,1)S(1)} %settle.1.near, bf16[2,64,128]{2,1,0:T(8,128)(2,1)S(1)} %collective-permute-done.16.far, bf16[2048,2048]{1,0:T(8,128)(2,1)S(1)} %copy-done.1), custom_call_target="tpu_custom_call" | custom-call | tf_op jit(solution)/shard_map/output/pallas_call | solution.py:154
  43.8 2.1 %collective-permute-start.17 = (bf16[64,128]{1,0:T(8,128)(2,1)S(1)}, bf16[64,128]{1,0:T(8,128)(2,1)S(1)}, u32[]{:S(2)}, u32[]{:S(2)}) collective-permute-start(bf16[64,128]{1,0:T(8,128)(2,1)S(1)} %get-tuple-element.29), channel_id=1, source_target_pairs={{0,3},{1,2},{2,1},{3,0},{4,7},{5,6},{6,5},{7,4},{8,11},{9,10},{10,... | collective-permute-start | bytes 49160 | tf_op jit(solution)/shard_map/ppermute | solution.py:403
  45.9 2.4 %collective-permute-start.19 = (bf16[64,128]{1,0:T(8,128)(2,1)S(1)}, bf16[64,128]{1,0:T(8,128)(2,1)S(1)}, u32[]{:S(2)}, u32[]{:S(2)}) collective-permute-start(bf16[64,128]{1,0:T(8,128)(2,1)S(1)} %get-tuple-element.31), channel_id=1, source_target_pairs={{0,1},{1,0},{2,3},{3,2},{4,5},{5,4},{6,7},{7,6},{8,9},{9,8},{10,11... | collective-permute-start | bytes 49160 | tf_op jit(solution)/shard_map/ppermute | solution.py:403
  48.2 1.2 %collective-permute-done.17.d = bf16[64,128]{1,0:T(8,128)(2,1)S(1)} collective-permute-done((bf16[64,128]{1,0:T(8,128)(2,1)S(1)}, bf16[64,128]{1,0:T(8,128)(2,1)S(1)}, u32[]{:S(2)}, u32[]{:S(2)}) %collective-permute-start.17) | collective-permute-done | bytes 16416 | tf_op jit(solution)/shard_map/ppermute | solution.py:403
  49.4 1.1 %collective-permute-done.18.c = bf16[64,128]{1,0:T(8,128)(2,1)S(1)} collective-permute-done((bf16[64,128]{1,0:T(8,128)(2,1)S(1)}, bf16[64,128]{1,0:T(8,128)(2,1)S(1)}, u32[]{:S(2)}, u32[]{:S(2)}) %collective-permute-start.18) | collective-permute-done | bytes 16416 | tf_op jit(solution)/shard_map/ppermute | solution.py:403
  (44 shorter events, 8.1 us)
Async XLA Ops:
  0.0 28.6 %copy-start.2 = (bf16[2,384,1024]{2,1,0:T(8,128)(2,1)S(1)}, bf16[2,384,1024]{2,1,0:T(8,128)(2,1)}, u32[]{:S(2)}) copy-start(bf16[2,384,1024]{2,1,0:T(8,128)(2,1)} %keys.1) | copy-start | bytes 4718596
  0.0 28.6 %copy-start.3 = (bf16[2,384,1024]{2,1,0:T(8,128)(2,1)S(1)}, bf16[2,384,1024]{2,1,0:T(8,128)(2,1)}, u32[]{:S(2)}) copy-start(bf16[2,384,1024]{2,1,0:T(8,128)(2,1)} %values.1) | copy-start | bytes 4718596
  0.9 27.7 %copy-start.5 = (s32[2]{0:T(128)S(1)}, s32[2]{0:T(128)}, u32[]{:S(2)}) copy-start(s32[2]{0:T(128)} %lengths.1) | copy-start | bytes 28
  1.0 41.6 %copy-start.1 = (bf16[2048,2048]{1,0:T(8,128)(2,1)S(1)}, bf16[2048,2048]{1,0:T(8,128)(2,1)}, u32[]{:S(2)}) copy-start(bf16[2048,2048]{1,0:T(8,128)(2,1)} %w.3) | copy-start | bytes 25165828
  1.0 1.3 %collective-permute-start = (f32[8,128]{1,0:T(8,128)S(1)}, f32[8,128]{1,0:T(8,128)S(1)}, u32[]{:S(2)}, u32[]{:S(2)}) collective-permute-start(f32[8,128]{1,0:T(8,128)S(1)} %get-tuple-element.20.a), channel_id=1, source_target_pairs={{0,4},{4,0},{8,12},{12,8},{1,5},{5,1},{9,13},{13,9},{2,6},{6,2},{1... | collective-permute-start | bytes 12296 | tf_op jit(solution)/shard_map/ppermute | solution.py:403
  2.3 4.4 %collective-permute-start.1 = (f32[8,128]{1,0:T(8,128)S(1)}, f32[8,128]{1,0:T(8,128)S(1)}, u32[]{:S(2)}, u32[]{:S(2)}) collective-permute-start(f32[8,128]{1,0:T(8,128)S(1)} %add.24.a), channel_id=1, source_target_pairs={{0,8},{4,12},{8,0},{12,4},{1,9},{5,13},{9,1},{13,5},{2,10},{6,14},... | collective-permute-start | bytes 12296 | tf_op jit(solution)/shard_map/ppermute | solution.py:403
  6.8 6.1 %collective-permute-start.2 = (bf16[2,2,2048]{2,1,0:T(2,128)(2,1)S(1)}, bf16[2,2,2048]{2,1,0:T(2,128)(2,1)S(1)}, u32[]{:S(2)}, u32[]{:S(2)}) collective-permute-start(bf16[2,2,2048]{2,1,0:T(2,128)(2,1)S(1)} %norm.1.n0), channel_id=1, source_target_pairs={{0,3},{1,2},{2,1},{3,0},{4,7},{5,6},{6,5},{7,4},{8,11},{9,10},{10,... | collective-permute-start | bytes 49160 | tf_op jit(solution)/shard_map/ppermute | solution.py:403
  11.0 4.6 %collective-permute-start.3 = (bf16[2,2,2048]{2,1,0:T(2,128)(2,1)S(1)}, bf16[2,2,2048]{2,1,0:T(2,128)(2,1)S(1)}, u32[]{:S(2)}, u32[]{:S(2)}) collective-permute-start(bf16[2,2,2048]{2,1,0:T(2,128)(2,1)S(1)} %norm.1.n0), channel_id=1, source_target_pairs={{0,2},{1,3},{2,0},{3,1},{4,6},{5,7},{6,4},{7,5},{8,10},{9,11},{10,... | collective-permute-start | bytes 49160 | tf_op jit(solution)/shard_map/ppermute | solution.py:403
  11.0 4.6 %collective-permute-start.4 = (bf16[2,2,2048]{2,1,0:T(2,128)(2,1)S(1)}, bf16[2,2,2048]{2,1,0:T(2,128)(2,1)S(1)}, u32[]{:S(2)}, u32[]{:S(2)}) collective-permute-start(bf16[2,2,2048]{2,1,0:T(2,128)(2,1)S(1)} %norm.1.n0), channel_id=1, source_target_pairs={{0,1},{1,0},{2,3},{3,2},{4,5},{5,4},{6,7},{7,6},{8,9},{9,8},{10,11... | collective-permute-start | bytes 49160 | tf_op jit(solution)/shard_map/ppermute | solution.py:403
  17.1 1.3 %collective-permute-start.5 = (f32[2,80,128]{2,1,0:T(8,128)S(1)}, f32[2,80,128]{2,1,0:T(8,128)S(1)}, u32[]{:S(2)}, u32[]{:S(2)}) collective-permute-start(f32[2,80,128]{2,1,0:T(8,128)S(1)} %get-tuple-element.22), channel_id=1, source_target_pairs={{0,4},{4,0},{8,12},{12,8},{1,5},{5,1},{9,13},{13,9},{2,6},{6,2},{1... | collective-permute-start | bytes 245768 | tf_op jit(solution)/shard_map/ppermute | solution.py:403
  18.5 6.8 %collective-permute-start.6 = (f32[80,128]{1,0:T(8,128)S(1)}, f32[80,128]{1,0:T(8,128)S(1)}, u32[]{:S(2)}, u32[]{:S(2)}) collective-permute-start(f32[80,128]{1,0:T(8,128)S(1)} %get-tuple-element.23), channel_id=1, source_target_pairs={{0,11},{1,10},{2,9},{3,8},{4,14},{5,15},{6,12},{7,13},{8,3},{9,2},... | collective-permute-start | bytes 122888 | tf_op jit(solution)/shard_map/ppermute | solution.py:419
  20.9 6.0 %collective-permute-start.7 = (f32[80,128]{1,0:T(8,128)S(1)}, f32[80,128]{1,0:T(8,128)S(1)}, u32[]{:S(2)}, u32[]{:S(2)}) collective-permute-start(f32[80,128]{1,0:T(8,128)S(1)} %get-tuple-element.23), channel_id=1, source_target_pairs={{0,3},{1,2},{2,1},{3,0},{4,6},{5,7},{6,4},{7,5},{8,11},{9,10},{10,... | collective-permute-start | bytes 122888 | tf_op jit(solution)/shard_map/ppermute | solution.py:419
  23.3 4.0 %collective-permute-start.8 = (f32[80,128]{1,0:T(8,128)S(1)}, f32[80,128]{1,0:T(8,128)S(1)}, u32[]{:S(2)}, u32[]{:S(2)}) collective-permute-start(f32[80,128]{1,0:T(8,128)S(1)} %get-tuple-element.24), channel_id=1, source_target_pairs={{0,8},{1,9},{2,10},{3,11},{4,13},{5,12},{6,15},{7,14},{8,0},{9,1},... | collective-permute-start | bytes 122888 | tf_op jit(solution)/shard_map/ppermute | solution.py:419
  23.8 3.5 %collective-permute-start.9 = (f32[80,128]{1,0:T(8,128)S(1)}, f32[80,128]{1,0:T(8,128)S(1)}, u32[]{:S(2)}, u32[]{:S(2)}) collective-permute-start(f32[80,128]{1,0:T(8,128)S(1)} %get-tuple-element.24), channel_id=1, source_target_pairs={{0,0},{1,1},{2,2},{3,3},{4,5},{5,4},{6,7},{7,6},{8,8},{9,9},{10,10... | collective-permute-start | bytes 122888 | tf_op jit(solution)/shard_map/ppermute | solution.py:419
  27.3 1.3 %collective-permute-start.10 = (bf16[2,80,128]{2,1,0:T(8,128)(2,1)S(1)}, bf16[2,80,128]{2,1,0:T(8,128)(2,1)S(1)}, u32[]{:S(2)}, u32[]{:S(2)}) collective-permute-start(bf16[2,80,128]{2,1,0:T(8,128)(2,1)S(1)} %round.1.near), channel_id=1, source_target_pairs={{0,4},{4,0},{8,12},{12,8},{1,5},{5,1},{9,13},{13,9},{2,6},{6,2},{1... | collective-permute-start | bytes 122888 | tf_op jit(solution)/shard_map/ppermute | solution.py:403
  30.6 1.3 %collective-permute-start.11 = (f32[2,72,128]{2,1,0:T(8,128)S(1)}, f32[2,72,128]{2,1,0:T(8,128)S(1)}, u32[]{:S(2)}, u32[]{:S(2)}) collective-permute-start(f32[2,72,128]{2,1,0:T(8,128)S(1)} %get-tuple-element.26), channel_id=1, source_target_pairs={{0,4},{4,0},{8,12},{12,8},{1,5},{5,1},{9,13},{13,9},{2,6},{6,2},{1... | collective-permute-start | bytes 221192 | tf_op jit(solution)/shard_map/ppermute | solution.py:403
  32.2 6.6 %collective-permute-start.12 = (bf16[80,128]{1,0:T(8,128)(2,1)S(1)}, bf16[80,128]{1,0:T(8,128)(2,1)S(1)}, u32[]{:S(2)}, u32[]{:S(2)}) collective-permute-start(bf16[80,128]{1,0:T(8,128)(2,1)S(1)} %get-tuple-element.27), channel_id=1, source_target_pairs={{0,11},{1,10},{2,9},{3,8},{4,14},{5,15},{6,12},{7,13},{8,3},{9,2},... | collective-permute-start | bytes 61448 | tf_op jit(solution)/shard_map/ppermute | solution.py:419
  35.4 5.6 %collective-permute-start.13 = (bf16[80,128]{1,0:T(8,128)(2,1)S(1)}, bf16[80,128]{1,0:T(8,128)(2,1)S(1)}, u32[]{:S(2)}, u32[]{:S(2)}) collective-permute-start(bf16[80,128]{1,0:T(8,128)(2,1)S(1)} %get-tuple-element.27), channel_id=1, source_target_pairs={{0,3},{1,2},{2,1},{3,0},{4,6},{5,7},{6,4},{7,5},{8,11},{9,10},{10,... | collective-permute-start | bytes 61448 | tf_op jit(solution)/shard_map/ppermute | solution.py:419
  36.1 5.0 %collective-permute-start.14 = (bf16[80,128]{1,0:T(8,128)(2,1)S(1)}, bf16[80,128]{1,0:T(8,128)(2,1)S(1)}, u32[]{:S(2)}, u32[]{:S(2)}) collective-permute-start(bf16[80,128]{1,0:T(8,128)(2,1)S(1)} %get-tuple-element.28), channel_id=1, source_target_pairs={{0,8},{1,9},{2,10},{3,11},{4,13},{5,12},{6,15},{7,14},{8,0},{9,1},... | collective-permute-start | bytes 61448 | tf_op jit(solution)/shard_map/ppermute | solution.py:419
  37.6 3.5 %collective-permute-start.15 = (bf16[80,128]{1,0:T(8,128)(2,1)S(1)}, bf16[80,128]{1,0:T(8,128)(2,1)S(1)}, u32[]{:S(2)}, u32[]{:S(2)}) collective-permute-start(bf16[80,128]{1,0:T(8,128)(2,1)S(1)} %get-tuple-element.28), channel_id=1, source_target_pairs={{0,0},{1,1},{2,2},{3,3},{4,5},{5,4},{6,7},{7,6},{8,8},{9,9},{10,10... | collective-permute-start | bytes 61448 | tf_op jit(solution)/shard_map/ppermute | solution.py:419
  41.3 1.3 %collective-permute-start.16 = (bf16[2,64,128]{2,1,0:T(8,128)(2,1)S(1)}, bf16[2,64,128]{2,1,0:T(8,128)(2,1)S(1)}, u32[]{:S(2)}, u32[]{:S(2)}) collective-permute-start(bf16[2,64,128]{2,1,0:T(8,128)(2,1)S(1)} %settle.1.near), channel_id=1, source_target_pairs={{0,4},{4,0},{8,12},{12,8},{1,5},{5,1},{9,13},{13,9},{2,6},{6,2},{1... | collective-permute-start | bytes 98312 | tf_op jit(solution)/shard_map/ppermute | solution.py:403
  43.8 5.6 %collective-permute-start.17 = (bf16[64,128]{1,0:T(8,128)(2,1)S(1)}, bf16[64,128]{1,0:T(8,128)(2,1)S(1)}, u32[]{:S(2)}, u32[]{:S(2)}) collective-permute-start(bf16[64,128]{1,0:T(8,128)(2,1)S(1)} %get-tuple-element.29), channel_id=1, source_target_pairs={{0,3},{1,2},{2,1},{3,0},{4,7},{5,6},{6,5},{7,4},{8,11},{9,10},{10,... | collective-permute-start | bytes 49160 | tf_op jit(solution)/shard_map/ppermute | solution.py:403
  45.9 4.6 %collective-permute-start.18 = (bf16[64,128]{1,0:T(8,128)(2,1)S(1)}, bf16[64,128]{1,0:T(8,128)(2,1)S(1)}, u32[]{:S(2)}, u32[]{:S(2)}) collective-permute-start(bf16[64,128]{1,0:T(8,128)(2,1)S(1)} %get-tuple-element.30), channel_id=1, source_target_pairs={{0,2},{1,3},{2,0},{3,1},{4,6},{5,7},{6,4},{7,5},{8,10},{9,11},{10,... | collective-permute-start | bytes 49160 | tf_op jit(solution)/shard_map/ppermute | solution.py:403
  45.9 4.6 %collective-permute-start.19 = (bf16[64,128]{1,0:T(8,128)(2,1)S(1)}, bf16[64,128]{1,0:T(8,128)(2,1)S(1)}, u32[]{:S(2)}, u32[]{:S(2)}) collective-permute-start(bf16[64,128]{1,0:T(8,128)(2,1)S(1)} %get-tuple-element.31), channel_id=1, source_target_pairs={{0,1},{1,0},{2,3},{3,2},{4,5},{5,4},{6,7},{7,6},{8,9},{9,8},{10,11... | collective-permute-start | bytes 49160 | tf_op jit(solution)/shard_map/ppermute | solution.py:403
  (2 other events, 16.5 us)

commit v6 on v5

--- a/solution.py
+++ b/solution.py
@@ -169,17 +169,15 @@
     return high, values - high
 
 
-def square_kernel(hidden, later, out, held):
+def square_kernel(hidden, other, later, out, held):
     out[...] = jnp.zeros_like(out)
     held[...] = hidden[...]
     for timeline in range(2):
-        wide = hidden[timeline].astype(F32)
-        total = jnp.sum(wide * wide, axis=-1, keepdims=True)
+        total = jnp.zeros((2, 1), F32)
+        for part in (hidden, other):
+            wide = part[timeline].astype(F32)
+            total += jnp.sum(wide * wide, axis=-1, keepdims=True)
         out[2 * timeline : 2 * timeline + 2, :] = jnp.broadcast_to(total, (2, HD))
-
-
-def add_kernel(a, b, out):
-    out[...] = a[...] + b[...]
 
 
 def norm_kernel(hidden, a, b, gain, out):
@@ -222,7 +220,21 @@
 
 
 def attend_kernel(
-    lengths, near, far, cosine, sine, keys, values, kept, sent, projected, turns, table, parts
+    lengths,
+    near,
+    far,
+    cosine,
+    sine,
+    keys,
+    far_keys,
+    values,
+    far_values,
+    o0,
+    o1,
+    projected,
+    turns,
+    table,
+    parts,
 ):
     my_x = lax.axis_index("gx")
     my_y = lax.axis_index("gy")
@@ -234,78 +246,100 @@
     for t in range(4):
         turns[0, 2 * t : 2 * t + 2, :] = cosine[t % 2]
         turns[1, 2 * t : 2 * t + 2, :] = sine[t % 2]
-    turned = projected[: QUERIES + KVH * ROWS, :]
-    swapped = pltpu.roll(turned, HD // 2, 1)
-    turned = (
-        turned.reshape(-1, 8, HD) * turns[0][None] + swapped.reshape(-1, 8, HD) * turns[1][None]
-    ).reshape(-1, HD)
-    queries = turned[:QUERIES].astype(BF16)
-    new_keys = turned[QUERIES:].astype(BF16)
-    new_values = projected[QUERIES + KVH * ROWS :, :].astype(BF16)
-
-    row = lax.broadcasted_iota(jnp.int32, (QUERIES, 1), 0)
+
+    def mine(start, count):
+        return projected[pl.ds(pl.multiple_of(start + core * count, 16), count), :]
+
+    def turned(wide):
+        swapped = pltpu.roll(wide, HD // 2, 1)
+        wide, swapped = wide.reshape(-1, 8, HD), swapped.reshape(-1, 8, HD)
+        return (wide * turns[0][None] + swapped * turns[1][None]).reshape(-1, HD).astype(BF16)
+
+    count = QUERIES // 2
+    fresh_count = KVH * ROWS // 2
+    queries = turned(mine(0, count))
+    new_keys = turned(mine(QUERIES, fresh_count))
+    new_values = mine(QUERIES + KVH * ROWS, fresh_count).astype(BF16)
+    row = lax.broadcasted_iota(jnp.int32, (count, 1), 0)
     token = row & 1
     timeline = (row >> 1) & 1
-    group_rows = GROUP_ROWS
     first = timeline[:GROUP_ROWS] == 0
-    for g in range(KVH):
-        at = slice(GROUP_ROWS * g, GROUP_ROWS * (g + 1))
-        both = [
-            lax.dot_general(
-                queries[at],
-                keys[t, :, HD * g : HD * (g + 1)],
-                (((1,), (1,)), ((), ())),
-                preferred_element_type=F32,
-            )
-            for t in range(2)
-        ]
-        table[at, :] = jnp.where(first, both[0], both[1])
+    groups = [
+        (
+            slice(GROUP_ROWS * g, GROUP_ROWS * (g + 1)),
+            pl.ds(pl.multiple_of(core * (KVH // 2 * HD) + HD * g, HD), HD),
+        )
+        for g in range(KVH // 2)
+    ]
+    for at, lanes in groups:
+        for block, cache in enumerate((keys, far_keys)):
+            both = [
+                lax.dot_general(
+                    queries[at],
+                    cache[t, :, lanes],
+                    (((1,), (1,)), ((), ())),
+                    preferred_element_type=F32,
+                )
+                for t in range(2)
+            ]
+            table[at, SPAN_DEV * block : SPAN_DEV * (block + 1)] = jnp.where(first, *both)
     scaling = HD ** (-0.5)
-    scores = table[...] * scaling
-    slot = my_x * SPAN_DEV + lax.broadcasted_iota(jnp.int32, (QUERIES, SPAN_DEV), 1)
+    lane = lax.broadcasted_iota(jnp.int32, (1, 2 * SPAN_DEV), 1)
+    slot = jnp.where(
+        lane < SPAN_DEV, my_x * SPAN_DEV + lane, (my_x ^ 1) * SPAN_DEV + lane - SPAN_DEV
+    )
     usable = slot < jnp.where(timeline == 0, lengths[0], lengths[1])
-    maxima = jnp.max(jnp.where(usable, scores, NEGATIVE), axis=-1, keepdims=True)
+    scores = jnp.where(usable, table[...] * scaling, NEGATIVE)
+    maxima = jnp.maximum(jnp.max(scores, axis=-1, keepdims=True), NEGATIVE / 10)
 
     wide_queries = queries.astype(F32)
-    column = lax.broadcasted_iota(jnp.int32, (QUERIES, KVH * ROWS), 1)
+    column = lax.broadcasted_iota(jnp.int32, (count, fresh_count), 1)
     fresh = []
     for j in range(2):
-        pick = jnp.where(column == (row // group_rows) * ROWS + timeline * 2 + j, 1.0, 0.0)
+        pick = jnp.where(column == (row // GROUP_ROWS) * ROWS + timeline * 2 + j, 1.0, 0.0)
         pick = pick.astype(BF16)
         key = jnp.dot(pick, new_keys, preferred_element_type=F32)
         value = jnp.dot(pick, new_values, preferred_element_type=F32)
         score = jnp.sum(wide_queries * key, axis=-1, keepdims=True) * scaling
-        allowed = (token >= j) & (my_x == 0)
-        maxima = jnp.maximum(maxima, jnp.where(allowed, score, NEGATIVE))
-        fresh.append((score, allowed, value))
-    weights = jnp.exp(jnp.where(usable, scores - maxima, NEGATIVE))
+        score = jnp.where((token >= j) & (my_x < 2), score, NEGATIVE)
+        maxima = jnp.maximum(maxima, score)
+        fresh.append((score, value))
+    weights = jnp.exp(scores - maxima)
     totals = jnp.sum(weights, axis=-1, keepdims=True)
     rounded = weights.astype(BF16)
-    added = jnp.zeros((QUERIES, HD), F32)
-    for score, allowed, value in fresh:
-        weight = jnp.exp(jnp.where(allowed, score - maxima, NEGATIVE))
+    added = jnp.zeros((count, HD), F32)
+    for score, value in fresh:
+        weight = jnp.exp(score - maxima)
         totals += weight
         added += weight.astype(BF16).astype(F32) * value
-    mine = [jnp.where(timeline == t, rounded, jnp.zeros_like(rounded)) for t in range(2)]
-    for g in range(KVH):
-        at = slice(GROUP_ROWS * g, GROUP_ROWS * (g + 1))
-        total = added[at]
-        for t in range(2):
-            total += jnp.dot(
-                mine[t][at], values[t, :, HD * g : HD * (g + 1)], preferred_element_type=F32
+    for g, (at, lanes) in enumerate(groups):
+        both = [
+            sum(
+                jnp.dot(
+                    rounded[at, SPAN_DEV * block : SPAN_DEV * (block + 1)],
+                    cache[t, :, lanes],
+                    preferred_element_type=F32,
+                )
+                for block, cache in enumerate((values, far_values))
             )
+            for t in range(2)
+        ]
         inside = GROUP_ROWS * (g % 2)
-        parts[g // 2, inside : inside + GROUP_ROWS, :] = total
-
-    lane = lax.broadcasted_iota(jnp.int32, (QUERIES, HD), 1)
+        parts[g // 2, inside : inside + GROUP_ROWS, :] = added[at] + jnp.where(first, *both)
+
+    lane = lax.broadcasted_iota(jnp.int32, (count, HD), 1)
     sheet = jnp.where(lane == 0, maxima, jnp.where(lane == 1, totals, 0.0))
-    flat = jnp.transpose(sheet)[0:8]
-    for q in range(NY):
-        half = flat[:, HD * (q // 2) : HD * (q // 2 + 1)]
-        parts[q, OUT_ROWS:, :] = half if q % 2 == 0 else pltpu.roll(half, OUT_ROWS, 1)
-    for k in range(2):
-        kept[k] = parts[my_y ^ (3 * k) ^ core]
-        sent[k] = parts[my_y ^ (3 * k) ^ core ^ 1]
+    flat = jnp.transpose(sheet)
+    high, rest = high_rest(flat[0:1])
+    middle, low = high_rest(rest)
+    line = lax.broadcasted_iota(jnp.int32, (16, HD), 0)
+    pieces = jnp.zeros((16, HD), F32)
+    for m, piece in enumerate((high, middle, low, *high_rest(flat[1:2]))):
+        pieces = jnp.where(line == m, piece, pieces)
+    parts[0, OUT_ROWS:, :] = pieces
+    parts[1, OUT_ROWS:, :] = pltpu.roll(pieces, OUT_ROWS, 1)
+    o0[...] = parts[my_y & 1].astype(BF16)
+    o1[...] = parts[(my_y & 1) ^ 1].astype(BF16)
 
 
 def columns_of(rows, sheet):
@@ -314,28 +348,6 @@
         sheet[k : k + 1, :] = row
     turned = jnp.transpose(sheet[...])[:OUT_ROWS]
     return [turned[:, k : k + 1] for k in range(len(rows))]
-
-
-def merge_kernel(a, b, o0, o1, sheet):
-    line = lax.broadcasted_iota(jnp.int32, (8, HD), 0)
-    powers, stats = [], []
-    for k in range(2):
-        a_stats, b_stats = a[k, OUT_ROWS:, :], b[k, OUT_ROWS:, :]
-        highest = jnp.maximum(a_stats[0:1], b_stats[0:1])
-        power_a = jnp.exp(a_stats[0:1] - highest)
-        power_b = jnp.exp(b_stats[0:1] - highest)
-        powers += [power_a, power_b]
-        stats.append((highest, a_stats[1:2] * power_a + b_stats[1:2] * power_b))
-    factors = columns_of(powers, sheet)
-    for k, out in enumerate((o0, o1)):
-        merged = a[k, :OUT_ROWS, :] * factors[2 * k] + b[k, :OUT_ROWS, :] * factors[2 * k + 1]
-        out[:OUT_ROWS, :] = merged.astype(BF16)
-        high, rest = high_rest(stats[k][0])
-        middle, low = high_rest(rest)
-        pieces = jnp.zeros((8, HD), F32)
-        for m, piece in enumerate((high, middle, low, *high_rest(stats[k][1]))):
-            pieces = jnp.where(line == m, piece, pieces)
-        out[OUT_ROWS:, :] = jnp.concatenate([pieces, jnp.zeros_like(pieces)], axis=0).astype(BF16)
 
 
 def settle_kernel(b1, a1, b0, a0, out, sheet):
@@ -358,10 +370,12 @@
 
 
 def output_kernel(near, far, w, o0, o1, o2, o3, blocks, wide, sums):
+    my_y = lax.axis_index("gy")
     core = lax.axis_index("gx") & 1
     for other, pair in enumerate((near, far)):
         for k in range(2):
-            blocks[(3 * k) ^ core ^ other] = pair[k].astype(F32)
+            source = 2 * (core ^ other) + ((my_y & 1) ^ k)
+            blocks[source ^ my_y] = pair[k].astype(F32)
     for shift in range(NY):
         for head in range(OUT_HEADS):
             wide[ROWS * shift : ROWS * (shift + 1), HD * head : HD * (head + 1)] = blocks[
@@ -407,17 +421,25 @@
     return [partner(parts[y], "gy", y) if y else parts[y] for y in (3, 2, 1, 0)]
 
 
-def on_chips(parts):
-    received = {}
+def on_chips(parts, target):
+    received = []
     for k in (1, 0):
-        for far_x in (1, 0):
-            pairs = [
-                (x * NY + y, (x ^ (2 * far_x)) * NY + (y ^ (3 * k) ^ (x & 1)))
-                for x in range(NX)
-                for y in range(NY)
-            ]
-            received[k, far_x] = lax.ppermute(parts[k], ("gx", "gy"), pairs)
-    return [received[k, far_x] for k in (1, 0) for far_x in (1, 0)]
+        for far_x in (2, 0):
+            pairs = []
+            for x in range(NX):
+                for y in range(NY):
+                    core, there = target(x & 1, y, k)
+                    pairs.append((x * NY + y, ((x & 2 ^ far_x) + core) * NY + there))
+            received.append(lax.ppermute(parts[k], ("gx", "gy"), pairs))
+    return received
+
+
+def by_distance(core, y, k):
+    return core, y ^ (3 * k) ^ core
+
+
+def by_heads(core, y, k):
+    return y >> 1, 2 * core + ((y & 1) ^ k)
 
 
 def small_body(hidden, norm_gain, w_qkv, w_out, k_cache, v_cache, cache_len, positions):
@@ -431,14 +453,18 @@
     features = hidden.shape[2]
     count = columns // HD * ROWS
     pinned_w_qkv = pinned(w_qkv)
-    hidden, w_out, k_cache, v_cache = map(pinned, (hidden, w_out, k_cache, v_cache))
+    w_out = pinned(w_out)
+    caches = [(pinned(cache), pinned(partner(cache, "gx", 1))) for cache in (k_cache, v_cache)]
     cosine, sine = rotation(positions)
 
     line = shape(8, HD, dtype=F32)
     squares, hidden = call(
-        square_kernel, "square", [line, shape(*hidden.shape)], [hidden], later=[w_qkv]
-    )
-    squares = call(add_kernel, "add", line, [squares, partner(squares, "gx", 1)])
+        square_kernel,
+        "square",
+        [line, shape(*hidden.shape)],
+        [pinned(hidden), partner(hidden, "gx", 1)],
+        later=[w_qkv],
+    )
     normed = call(
         norm_kernel,
         "norm",
@@ -455,36 +481,28 @@
     )
     block = shape(QKV_ROWS, HD, dtype=F32)
     sums = call(chip_kernel, "chip", [block, block], [kept, partner(sent, "gx", 1)])
-    near = call(round_kernel, "round", shape(2, QKV_ROWS, HD), on_chips(sums))
-
-    half = shape(2, OUT_ROWS + 8, HD, dtype=F32)
-    kept, sent = call(
+    near = call(round_kernel, "round", shape(2, QKV_ROWS, HD), on_chips(sums, by_distance))
+
+    block = shape(OUT_ROWS + 16, HD)
+    partials = call(
         attend_kernel,
         "attend",
-        [half, half],
-        [cache_len, near, partner(near, "gx", 1), cosine, sine, k_cache, v_cache],
+        [block, block],
+        [cache_len, near, partner(near, "gx", 1), cosine, sine, *caches[0], *caches[1]],
         [
             pltpu.VMEM((NY * QKV_ROWS, HD), F32),
             pltpu.VMEM((2, 8, HD), F32),
-            pltpu.VMEM((QUERIES, SPAN_DEV), F32),
-            pltpu.VMEM((NY, OUT_ROWS + 8, HD), F32),
+            pltpu.VMEM((QUERIES // 2, 2 * SPAN_DEV), F32),
+            pltpu.VMEM((2, OUT_ROWS + 16, HD), F32),
         ],
         scalars=1,
         mib=16,
-    )
-    block = shape(OUT_ROWS + 16, HD)
-    merged = call(
-        merge_kernel,
-        "merge",
-        [block, block],
-        [kept, partner(sent, "gx", 1)],
-        [pltpu.VMEM((HD, HD), F32)],
     )
     near = call(
         settle_kernel,
         "settle",
         shape(2, OUT_ROWS, HD),
-        on_chips(merged),
+        on_chips(partials, by_heads),
         [pltpu.VMEM((HD, HD), F32)],
     )
     blocks = call(

time: 51.4 us -> 61 us (1.19)
  waiting for transfers between devices: 16.6 us -> 22.4 us
  starting transfers between devices: 25.2 us -> 28.5 us
  local copies, waits for them, and re-layouts: 2.33 us -> 3.63 us
  other arithmetic: 0.93 us -> 0.28 us
    ppermute x12 -> x13, waiting for transfers between devices: 11 us -> 16.2 us  [partner(): lax.ppermute(part, axis, [(k, k ^ distance) for k in range(lax.axis_size(...]
    ppermute x12 -> x13, starting transfers between devices: 13.2 us -> 17.3 us  [partner(): lax.ppermute(part, axis, [(k, k ^ distance) for k in range(lax.axis_size(...]
    unnamed x12 -> x16, local copies, waits for them, and re-layouts: 0.89 us -> 2.15 us
    ppermute x8, starting transfers between devices: 12 us -> 11.2 us  [on_chips(): received.append(lax.ppermute(parts[k], ('gx', 'gy'), pairs))]
    convert_element_type x1, other arithmetic: 0.73 us -> 0.07 us  [rotation(): angles = places.astype(F32)[:, :, None] * frequency[None, None, :]]
    ppermute x8, waiting for transfers between devices: 5.51 us -> 6.14 us  [on_chips(): received.append(lax.ppermute(parts[k], ('gx', 'gy'), pairs))]
    pallas_call x11 -> x9, Pallas kernels: 6.04 us -> 5.74 us  [call(): pl.pallas_call(kernel, in_specs=[SMEM_SPEC] * scalars + [VMEM_SPEC] * (le...]
  transfers between devices with their start and end apart: 20 -> 21, of which waited for: 15 -> 14; matrix products, arithmetic and copies ran while one was open for 5% -> 3% of each run, Pallas kernels for 0% -> 3%
where the time goes in v6:
time: 61 us; the launch traced here: 60.7 us
  starting transfers between devices  28.5 us (47%)
  waiting for transfers between devices  22.4 us (37%)
  Pallas kernels  5.74 us (9%)
  local copies, waits for them, and re-layouts  3.63 us (6%)
    ppermute x13, starting transfers between devices, partner(): lax.ppermute(part, axis, [(k, k ^ distance) for k in range(lax.axis_size(...  17.3 us
    ppermute x13, waiting for transfers between devices, partner(): lax.ppermute(part, axis, [(k, k ^ distance) for k in range(lax.axis_size(...  16.2 us
    ppermute x8, starting transfers between devices, on_chips(): received.append(lax.ppermute(parts[k], ('gx', 'gy'), pairs))  11.2 us
    ppermute x8, waiting for transfers between devices, on_chips(): received.append(lax.ppermute(parts[k], ('gx', 'gy'), pairs))  6.14 us
    pallas_call x9, Pallas kernels, call(): pl.pallas_call(kernel, in_specs=[SMEM_SPEC] * scalars + [VMEM_SPEC] * (le...  5.74 us
    unnamed x16, local copies, waits for them, and re-layouts  2.15 us
    broadcast_in_dim x1, local copies, waits for them, and re-layouts, small_body(): norm_gain[None]  1.47 us
  transfers between devices with their start and end apart: 21, of which 14 were waited for; matrix products, arithmetic and copies ran while one was open for 3% of the time, Pallas kernels for 3%

profile of v6, /device:TPU:0, one launch (start us, length us, event | category | flops | bytes accessed | tf_op | source)
XLA Modules:
  0.0 60.7 jit_solution(9248965978799382215)
XLA Ops:
  1.0 5.0 %collective-permute-done.other = bf16[2,2,2048]{2,1,0:T(2,128)(2,1)S(1)} collective-permute-done((bf16[2,2,2048]{2,1,0:T(2,128)(2,1)}, bf16[2,2,2048]{2,1,0:T(2,128)(2,1)S(1)}, u32[]{:S(2)}, u32[]{:S(2)}) %collective-permute-start) | collective-permute-done | bytes 16416 | tf_op jit(solution)/shard_map/ppermute | solution.py:417
  6.8 2.9 %collective-permute-start.1 = (f32[8,128]{1,0:T(8,128)S(1)}, f32[8,128]{1,0:T(8,128)S(1)}, u32[]{:S(2)}, u32[]{:S(2)}) collective-permute-start(f32[8,128]{1,0:T(8,128)S(1)} %get-tuple-element.18.a), channel_id=1, source_target_pairs={{0,8},{4,12},{8,0},{12,4},{1,9},{5,13},{9,1},{13,5},{2,10},{6,14},... | collective-permute-start | bytes 12296 | tf_op jit(solution)/shard_map/ppermute | solution.py:417
  9.7 1.5 %broadcast_in_dim.2.gain = bf16[1,2048]{1,0:T(2,128)(2,1)S(1)} reshape(bf16[2048]{0:T(1024)(128)(2,1)} %param.9) | data formatting | bytes 8192 | tf_op jit(solution)/shard_map/broadcast_in_dim | solution.py:472
  11.4 2.2 %collective-permute-start.4 = (bf16[2,2,2048]{2,1,0:T(2,128)(2,1)S(1)}, bf16[2,2,2048]{2,1,0:T(2,128)(2,1)S(1)}, u32[]{:S(2)}, u32[]{:S(2)}) collective-permute-start(bf16[2,2,2048]{2,1,0:T(2,128)(2,1)S(1)} %norm.1.n0), channel_id=1, source_target_pairs={{0,1},{1,0},{2,3},{3,2},{4,5},{5,4},{6,7},{7,6},{8,9},{9,8},{10,11... | collective-permute-start | bytes 49160 | tf_op jit(solution)/shard_map/ppermute | solution.py:417
  13.6 2.6 %collective-permute-start.3 = (bf16[2,2,2048]{2,1,0:T(2,128)(2,1)S(1)}, bf16[2,2,2048]{2,1,0:T(2,128)(2,1)S(1)}, u32[]{:S(2)}, u32[]{:S(2)}) collective-permute-start(bf16[2,2,2048]{2,1,0:T(2,128)(2,1)S(1)} %norm.1.n0), channel_id=1, source_target_pairs={{0,2},{1,3},{2,0},{3,1},{4,6},{5,7},{6,4},{7,5},{8,10},{9,11},{10,... | collective-permute-start | bytes 49160 | tf_op jit(solution)/shard_map/ppermute | solution.py:417
  16.2 2.0 %collective-permute-done.3.n2 = bf16[2,2,2048]{2,1,0:T(2,128)(2,1)S(1)} collective-permute-done((bf16[2,2,2048]{2,1,0:T(2,128)(2,1)S(1)}, bf16[2,2,2048]{2,1,0:T(2,128)(2,1)S(1)}, u32[]{:S(2)}, u32[]{:S(2)}) %collective-permute-start.3) | collective-permute-done | bytes 16416 | tf_op jit(solution)/shard_map/ppermute | solution.py:417
  18.2 3.5 %collective-permute-done.2.n3 = bf16[2,2,2048]{2,1,0:T(2,128)(2,1)S(1)} collective-permute-done((bf16[2,2,2048]{2,1,0:T(2,128)(2,1)S(1)}, bf16[2,2,2048]{2,1,0:T(2,128)(2,1)S(1)}, u32[]{:S(2)}, u32[]{:S(2)}) %collective-permute-start.2) | collective-permute-done | bytes 16416 | tf_op jit(solution)/shard_map/ppermute | solution.py:417
  21.7 1.5 %project.1 = (f32[2,80,128]{2,1,0:T(8,128)S(1)}, f32[2,80,128]{2,1,0:T(8,128)S(1)}) custom-call(bf16[2,2,2048]{2,1,0:T(2,128)(2,1)S(1)} %collective-permute-done.2.n3, bf16[2,2,2048]{2,1,0:T(2,128)(2,1)S(1)} %collective-permute-done.3.n2, bf16[2,2,2048]{2,1,0:T(2,128)(2,1)S(1)} %collective-permute-done.4.n1, bf16[2,2,2048]{2,1,0:T(2,128)(2,1)S(1)} %norm.1.n0, ...), custom_call_target="tpu_custom_call" | custom-call | tf_op jit(solution)/shard_map/project/pallas_call | solution.py:154
  23.4 1.2 %collective-permute-done.5.b = f32[2,80,128]{2,1,0:T(8,128)S(1)} collective-permute-done((f32[2,80,128]{2,1,0:T(8,128)S(1)}, f32[2,80,128]{2,1,0:T(8,128)S(1)}, u32[]{:S(2)}, u32[]{:S(2)}) %collective-permute-start.5) | collective-permute-done | bytes 81952 | tf_op jit(solution)/shard_map/ppermute | solution.py:417
  24.8 4.6 %collective-permute-start.6 = (f32[80,128]{1,0:T(8,128)S(1)}, f32[80,128]{1,0:T(8,128)S(1)}, u32[]{:S(2)}, u32[]{:S(2)}) collective-permute-start(f32[80,128]{1,0:T(8,128)S(1)} %get-tuple-element.21), channel_id=1, source_target_pairs={{0,11},{1,10},{2,9},{3,8},{4,14},{5,15},{6,12},{7,13},{8,3},{9,2},... | collective-permute-start | bytes 122888 | tf_op jit(solution)/shard_map/ppermute | solution.py:433
  30.4 1.5 %collective-permute-start.8 = (f32[80,128]{1,0:T(8,128)S(1)}, f32[80,128]{1,0:T(8,128)S(1)}, u32[]{:S(2)}, u32[]{:S(2)}) collective-permute-start(f32[80,128]{1,0:T(8,128)S(1)} %get-tuple-element.22), channel_id=1, source_target_pairs={{0,8},{1,9},{2,10},{3,11},{4,13},{5,12},{6,15},{7,14},{8,0},{9,1},... | collective-permute-start | bytes 122888 | tf_op jit(solution)/shard_map/ppermute | solution.py:433
  32.1 2.4 %collective-permute-done.8.b0 = f32[80,128]{1,0:T(8,128)S(1)} collective-permute-done((f32[80,128]{1,0:T(8,128)S(1)}, f32[80,128]{1,0:T(8,128)S(1)}, u32[]{:S(2)}, u32[]{:S(2)}) %collective-permute-start.8) | collective-permute-done | bytes 40992 | tf_op jit(solution)/shard_map/ppermute | solution.py:433
  34.6 1.1 %collective-permute-done.10.far = bf16[2,80,128]{2,1,0:T(8,128)(2,1)S(1)} collective-permute-done((bf16[2,80,128]{2,1,0:T(8,128)(2,1)S(1)}, bf16[2,80,128]{2,1,0:T(8,128)(2,1)S(1)}, u32[]{:S(2)}, u32[]{:S(2)}) %collective-permute-start.10) | collective-permute-done | bytes 40992 | tf_op jit(solution)/shard_map/ppermute | solution.py:417
  35.8 1.4 %copy-done.2 = bf16[2,384,1024]{2,1,0:T(8,128)(2,1)S(1)} copy-done((bf16[2,384,1024]{2,1,0:T(8,128)(2,1)S(1)}, bf16[2,384,1024]{2,1,0:T(8,128)(2,1)}, u32[]{:S(2)}) %copy-start.2) | copy-done | bytes 1572888
  37.2 1.9 %attend.1 = (bf16[80,128]{1,0:T(8,128)(2,1)S(1)}, bf16[80,128]{1,0:T(8,128)(2,1)S(1)}) custom-call(s32[2]{0:T(128)S(1)} %copy-done.4, bf16[2,80,128]{2,1,0:T(8,128)(2,1)S(1)} %round.1.near, bf16[2,80,128]{2,1,0:T(8,128)(2,1)S(1)} %collective-permute-done.10.far, f32[2,2,128]{2,1,0:T(2,128)S(1)} %get-tuple-element.32.cosine, ...), custom_call_target="tpu_custom_call" | custom-call | tf_op jit(solution)/shard_map/attend/pallas_call | solution.py:154
  40.0 2.2 %collective-permute-start.13 = (bf16[80,128]{1,0:T(8,128)(2,1)S(1)}, bf16[80,128]{1,0:T(8,128)(2,1)S(1)}, u32[]{:S(2)}, u32[]{:S(2)}) collective-permute-start(bf16[80,128]{1,0:T(8,128)(2,1)S(1)} %get-tuple-element.23), channel_id=1, source_target_pairs={{0,9},{1,8},{2,13},{3,12},{4,11},{5,10},{6,15},{7,14},{8,1},{9,0},... | collective-permute-start | bytes 61448 | tf_op jit(solution)/shard_map/ppermute | solution.py:433
  43.4 1.2 %collective-permute-done.13.b1 = bf16[80,128]{1,0:T(8,128)(2,1)S(1)} collective-permute-done((bf16[80,128]{1,0:T(8,128)(2,1)S(1)}, bf16[80,128]{1,0:T(8,128)(2,1)S(1)}, u32[]{:S(2)}, u32[]{:S(2)}) %collective-permute-start.13) | collective-permute-done | bytes 20512 | tf_op jit(solution)/shard_map/ppermute | solution.py:433
  44.7 2.1 %collective-permute-done.15.b0 = bf16[80,128]{1,0:T(8,128)(2,1)S(1)} collective-permute-done((bf16[80,128]{1,0:T(8,128)(2,1)S(1)}, bf16[80,128]{1,0:T(8,128)(2,1)S(1)}, u32[]{:S(2)}, u32[]{:S(2)}) %collective-permute-start.15) | collective-permute-done | bytes 20512 | tf_op jit(solution)/shard_map/ppermute | solution.py:433
  47.0 4.1 %collective-permute-start.17 = (bf16[2,64,128]{2,1,0:T(8,128)(2,1)S(1)}, bf16[2,64,128]{2,1,0:T(8,128)(2,1)S(1)}, u32[]{:S(2)}, u32[]{:S(2)}) collective-permute-start(bf16[2,64,128]{2,1,0:T(8,128)(2,1)S(1)} %settle.1.near), channel_id=1, source_target_pairs={{0,4},{4,0},{8,12},{12,8},{1,5},{5,1},{9,13},{13,9},{2,6},{6,2},{1... | collective-permute-start | bytes 98312 | tf_op jit(solution)/shard_map/ppermute | solution.py:417
  52.0 1.2 %output.1 = (f32[64,128]{1,0:T(8,128)S(1)}, bf16[64,128]{1,0:T(8,128)(2,1)S(1)}, bf16[64,128]{1,0:T(8,128)(2,1)S(1)}, bf16[64,128]{1,0:T(8,128)(2,1)S(1)}) custom-call(bf16[2,64,128]{2,1,0:T(8,128)(2,1)S(1)} %settle.1.near, bf16[2,64,128]{2,1,0:T(8,128)(2,1)S(1)} %collective-permute-done.17.far, bf16[2048,2048]{1,0:T(8,128)(2,1)S(1)} %bitcast.1), custom_call_target="tpu_custom_call" | custom-call | tf_op jit(solution)/shard_map/output/pallas_call | solution.py:154
  53.2 1.3 %collective-permute-start.18 = (bf16[64,128]{1,0:T(8,128)(2,1)S(1)}, bf16[64,128]{1,0:T(8,128)(2,1)S(1)}, u32[]{:S(2)}, u32[]{:S(2)}) collective-permute-start(bf16[64,128]{1,0:T(8,128)(2,1)S(1)} %get-tuple-element.25), channel_id=1, source_target_pairs={{0,3},{1,2},{2,1},{3,0},{4,7},{5,6},{6,5},{7,4},{8,11},{9,10},{10,... | collective-permute-start | bytes 49160 | tf_op jit(solution)/shard_map/ppermute | solution.py:417
  54.5 1.8 %collective-permute-start.19 = (bf16[64,128]{1,0:T(8,128)(2,1)S(1)}, bf16[64,128]{1,0:T(8,128)(2,1)S(1)}, u32[]{:S(2)}, u32[]{:S(2)}) collective-permute-start(bf16[64,128]{1,0:T(8,128)(2,1)S(1)} %get-tuple-element.26), channel_id=1, source_target_pairs={{0,2},{1,3},{2,0},{3,1},{4,6},{5,7},{6,4},{7,5},{8,10},{9,11},{10,... | collective-permute-start | bytes 49160 | tf_op jit(solution)/shard_map/ppermute | solution.py:417
  56.3 1.3 %collective-permute-start.20 = (bf16[64,128]{1,0:T(8,128)(2,1)S(1)}, bf16[64,128]{1,0:T(8,128)(2,1)S(1)}, u32[]{:S(2)}, u32[]{:S(2)}) collective-permute-start(bf16[64,128]{1,0:T(8,128)(2,1)S(1)} %get-tuple-element.27), channel_id=1, source_target_pairs={{0,1},{1,0},{2,3},{3,2},{4,5},{5,4},{6,7},{7,6},{8,9},{9,8},{10,11... | collective-permute-start | bytes 49160 | tf_op jit(solution)/shard_map/ppermute | solution.py:417
  57.7 1.2 %collective-permute-done.18.d = bf16[64,128]{1,0:T(8,128)(2,1)S(1)} collective-permute-done((bf16[64,128]{1,0:T(8,128)(2,1)S(1)}, bf16[64,128]{1,0:T(8,128)(2,1)S(1)}, u32[]{:S(2)}, u32[]{:S(2)}) %collective-permute-start.18) | collective-permute-done | bytes 16416 | tf_op jit(solution)/shard_map/ppermute | solution.py:417
  (49 shorter events, 8.8 us)
Async XLA Ops:
  0.0 35.8 %collective-permute-start.11 = (bf16[2,384,1024]{2,1,0:T(8,128)(2,1)}, bf16[2,384,1024]{2,1,0:T(8,128)(2,1)S(1)}, u32[]{:S(2)}, u32[]{:S(2)}) collective-permute-start(bf16[2,384,1024]{2,1,0:T(8,128)(2,1)} %keys.1), channel_id=1, source_target_pairs={{0,4},{4,0},{8,12},{12,8},{1,5},{5,1},{9,13},{13,9},{2,6},{6,2},{1... | collective-permute-start | bytes 4718600 | tf_op jit(solution)/shard_map/ppermute | solution.py:417
  0.5 35.3 %collective-permute-start.12 = (bf16[2,384,1024]{2,1,0:T(8,128)(2,1)}, bf16[2,384,1024]{2,1,0:T(8,128)(2,1)S(1)}, u32[]{:S(2)}, u32[]{:S(2)}) collective-permute-start(bf16[2,384,1024]{2,1,0:T(8,128)(2,1)} %values.1), channel_id=1, source_target_pairs={{0,4},{4,0},{8,12},{12,8},{1,5},{5,1},{9,13},{13,9},{2,6},{6,2},{1... | collective-permute-start | bytes 4718600 | tf_op jit(solution)/shard_map/ppermute | solution.py:417
  0.5 5.5 %collective-permute-start = (bf16[2,2,2048]{2,1,0:T(2,128)(2,1)}, bf16[2,2,2048]{2,1,0:T(2,128)(2,1)S(1)}, u32[]{:S(2)}, u32[]{:S(2)}) collective-permute-start(bf16[2,2,2048]{2,1,0:T(2,128)(2,1)} %hidden.1), channel_id=1, source_target_pairs={{0,4},{4,0},{8,12},{12,8},{1,5},{5,1},{9,13},{13,9},{2,6},{6,2},{1... | collective-permute-start | bytes 49160 | tf_op jit(solution)/shard_map/ppermute | solution.py:417
  6.7 45.3 %slice-start = ((s8[8388608]{0:T(1024)(128)(4,1)}), s8[4194304]{0:T(1024)(128)(4,1)S(1)}, s32[]{:S(2)}) async-start(s8[8388608]{0:T(1024)(128)(4,1)} %bitcast), calls=%async_computation | async-start | bytes 8388608
  6.8 4.5 %collective-permute-start.1 = (f32[8,128]{1,0:T(8,128)S(1)}, f32[8,128]{1,0:T(8,128)S(1)}, u32[]{:S(2)}, u32[]{:S(2)}) collective-permute-start(f32[8,128]{1,0:T(8,128)S(1)} %get-tuple-element.18.a), channel_id=1, source_target_pairs={{0,8},{4,12},{8,0},{12,4},{1,9},{5,13},{9,1},{13,5},{2,10},{6,14},... | collective-permute-start | bytes 12296 | tf_op jit(solution)/shard_map/ppermute | solution.py:417
  11.4 24.4 %copy-start.1 = (bf16[2,384,1024]{2,1,0:T(8,128)(2,1)S(1)}, bf16[2,384,1024]{2,1,0:T(8,128)(2,1)}, u32[]{:S(2)}) copy-start(bf16[2,384,1024]{2,1,0:T(8,128)(2,1)} %keys.1) | copy-start | bytes 4718596
  11.4 40.6 %slice-start.1 = ((s8[8388608]{0:T(1024)(128)(4,1)}), s8[4194304]{0:T(1024)(128)(4,1)S(1)}, s32[]{:S(2)}) async-start(s8[8388608]{0:T(1024)(128)(4,1)} %bitcast), calls=%async_computation.1 | async-start | bytes 8388608
  11.4 4.8 %collective-permute-start.4 = (bf16[2,2,2048]{2,1,0:T(2,128)(2,1)S(1)}, bf16[2,2,2048]{2,1,0:T(2,128)(2,1)S(1)}, u32[]{:S(2)}, u32[]{:S(2)}) collective-permute-start(bf16[2,2,2048]{2,1,0:T(2,128)(2,1)S(1)} %norm.1.n0), channel_id=1, source_target_pairs={{0,1},{1,0},{2,3},{3,2},{4,5},{5,4},{6,7},{7,6},{8,9},{9,8},{10,11... | collective-permute-start | bytes 49160 | tf_op jit(solution)/shard_map/ppermute | solution.py:417
  13.6 4.6 %collective-permute-start.3 = (bf16[2,2,2048]{2,1,0:T(2,128)(2,1)S(1)}, bf16[2,2,2048]{2,1,0:T(2,128)(2,1)S(1)}, u32[]{:S(2)}, u32[]{:S(2)}) collective-permute-start(bf16[2,2,2048]{2,1,0:T(2,128)(2,1)S(1)} %norm.1.n0), channel_id=1, source_target_pairs={{0,2},{1,3},{2,0},{3,1},{4,6},{5,7},{6,4},{7,5},{8,10},{9,11},{10,... | collective-permute-start | bytes 49160 | tf_op jit(solution)/shard_map/ppermute | solution.py:417
  16.2 5.5 %collective-permute-start.2 = (bf16[2,2,2048]{2,1,0:T(2,128)(2,1)S(1)}, bf16[2,2,2048]{2,1,0:T(2,128)(2,1)S(1)}, u32[]{:S(2)}, u32[]{:S(2)}) collective-permute-start(bf16[2,2,2048]{2,1,0:T(2,128)(2,1)S(1)} %norm.1.n0), channel_id=1, source_target_pairs={{0,3},{1,2},{2,1},{3,0},{4,7},{5,6},{6,5},{7,4},{8,11},{9,10},{10,... | collective-permute-start | bytes 49160 | tf_op jit(solution)/shard_map/ppermute | solution.py:417
  23.2 1.3 %collective-permute-start.5 = (f32[2,80,128]{2,1,0:T(8,128)S(1)}, f32[2,80,128]{2,1,0:T(8,128)S(1)}, u32[]{:S(2)}, u32[]{:S(2)}) collective-permute-start(f32[2,80,128]{2,1,0:T(8,128)S(1)} %get-tuple-element.20), channel_id=1, source_target_pairs={{0,4},{4,0},{8,12},{12,8},{1,5},{5,1},{9,13},{13,9},{2,6},{6,2},{1... | collective-permute-start | bytes 245768 | tf_op jit(solution)/shard_map/ppermute | solution.py:417
  24.6 5.9 %collective-permute-start.7 = (f32[80,128]{1,0:T(8,128)S(1)}, f32[80,128]{1,0:T(8,128)S(1)}, u32[]{:S(2)}, u32[]{:S(2)}) collective-permute-start(f32[80,128]{1,0:T(8,128)S(1)} %get-tuple-element.21), channel_id=1, source_target_pairs={{0,3},{1,2},{2,1},{3,0},{4,6},{5,7},{6,4},{7,5},{8,11},{9,10},{10,... | collective-permute-start | bytes 122888 | tf_op jit(solution)/shard_map/ppermute | solution.py:433
  24.8 7.2 %collective-permute-start.6 = (f32[80,128]{1,0:T(8,128)S(1)}, f32[80,128]{1,0:T(8,128)S(1)}, u32[]{:S(2)}, u32[]{:S(2)}) collective-permute-start(f32[80,128]{1,0:T(8,128)S(1)} %get-tuple-element.21), channel_id=1, source_target_pairs={{0,11},{1,10},{2,9},{3,8},{4,14},{5,15},{6,12},{7,13},{8,3},{9,2},... | collective-permute-start | bytes 122888 | tf_op jit(solution)/shard_map/ppermute | solution.py:433
  29.4 2.7 %collective-permute-start.9 = (f32[80,128]{1,0:T(8,128)S(1)}, f32[80,128]{1,0:T(8,128)S(1)}, u32[]{:S(2)}, u32[]{:S(2)}) collective-permute-start(f32[80,128]{1,0:T(8,128)S(1)} %get-tuple-element.22), channel_id=1, source_target_pairs={{0,0},{1,1},{2,2},{3,3},{4,5},{5,4},{6,7},{7,6},{8,8},{9,9},{10,10... | collective-permute-start | bytes 122888 | tf_op jit(solution)/shard_map/ppermute | solution.py:433
  30.4 4.0 %collective-permute-start.8 = (f32[80,128]{1,0:T(8,128)S(1)}, f32[80,128]{1,0:T(8,128)S(1)}, u32[]{:S(2)}, u32[]{:S(2)}) collective-permute-start(f32[80,128]{1,0:T(8,128)S(1)} %get-tuple-element.22), channel_id=1, source_target_pairs={{0,8},{1,9},{2,10},{3,11},{4,13},{5,12},{6,15},{7,14},{8,0},{9,1},... | collective-permute-start | bytes 122888 | tf_op jit(solution)/shard_map/ppermute | solution.py:433
  34.5 1.3 %collective-permute-start.10 = (bf16[2,80,128]{2,1,0:T(8,128)(2,1)S(1)}, bf16[2,80,128]{2,1,0:T(8,128)(2,1)S(1)}, u32[]{:S(2)}, u32[]{:S(2)}) collective-permute-start(bf16[2,80,128]{2,1,0:T(8,128)(2,1)S(1)} %round.1.near), channel_id=1, source_target_pairs={{0,4},{4,0},{8,12},{12,8},{1,5},{5,1},{9,13},{13,9},{2,6},{6,2},{1... | collective-permute-start | bytes 122888 | tf_op jit(solution)/shard_map/ppermute | solution.py:417
  39.1 4.3 %collective-permute-start.14 = (bf16[80,128]{1,0:T(8,128)(2,1)S(1)}, bf16[80,128]{1,0:T(8,128)(2,1)S(1)}, u32[]{:S(2)}, u32[]{:S(2)}) collective-permute-start(bf16[80,128]{1,0:T(8,128)(2,1)S(1)} %get-tuple-element.23), channel_id=1, source_target_pairs={{0,1},{1,0},{2,5},{3,4},{4,3},{5,2},{6,7},{7,6},{8,9},{9,8},{10,13... | collective-permute-start | bytes 61448 | tf_op jit(solution)/shard_map/ppermute | solution.py:433
  40.0 4.7 %collective-permute-start.13 = (bf16[80,128]{1,0:T(8,128)(2,1)S(1)}, bf16[80,128]{1,0:T(8,128)(2,1)S(1)}, u32[]{:S(2)}, u32[]{:S(2)}) collective-permute-start(bf16[80,128]{1,0:T(8,128)(2,1)S(1)} %get-tuple-element.23), channel_id=1, source_target_pairs={{0,9},{1,8},{2,13},{3,12},{4,11},{5,10},{6,15},{7,14},{8,1},{9,0},... | collective-permute-start | bytes 61448 | tf_op jit(solution)/shard_map/ppermute | solution.py:433
  42.1 2.5 %collective-permute-start.16 = (bf16[80,128]{1,0:T(8,128)(2,1)S(1)}, bf16[80,128]{1,0:T(8,128)(2,1)S(1)}, u32[]{:S(2)}, u32[]{:S(2)}) collective-permute-start(bf16[80,128]{1,0:T(8,128)(2,1)S(1)} %get-tuple-element.24), channel_id=1, source_target_pairs={{0,0},{1,1},{2,4},{3,5},{4,2},{5,3},{6,6},{7,7},{8,8},{9,9},{10,12... | collective-permute-start | bytes 61448 | tf_op jit(solution)/shard_map/ppermute | solution.py:433
  42.8 4.0 %collective-permute-start.15 = (bf16[80,128]{1,0:T(8,128)(2,1)S(1)}, bf16[80,128]{1,0:T(8,128)(2,1)S(1)}, u32[]{:S(2)}, u32[]{:S(2)}) collective-permute-start(bf16[80,128]{1,0:T(8,128)(2,1)S(1)} %get-tuple-element.24), channel_id=1, source_target_pairs={{0,8},{1,9},{2,12},{3,13},{4,10},{5,11},{6,14},{7,15},{8,0},{9,1},... | collective-permute-start | bytes 61448 | tf_op jit(solution)/shard_map/ppermute | solution.py:433
  47.0 4.9 %collective-permute-start.17 = (bf16[2,64,128]{2,1,0:T(8,128)(2,1)S(1)}, bf16[2,64,128]{2,1,0:T(8,128)(2,1)S(1)}, u32[]{:S(2)}, u32[]{:S(2)}) collective-permute-start(bf16[2,64,128]{2,1,0:T(8,128)(2,1)S(1)} %settle.1.near), channel_id=1, source_target_pairs={{0,4},{4,0},{8,12},{12,8},{1,5},{5,1},{9,13},{13,9},{2,6},{6,2},{1... | collective-permute-start | bytes 98312 | tf_op jit(solution)/shard_map/ppermute | solution.py:417
  53.2 5.6 %collective-permute-start.18 = (bf16[64,128]{1,0:T(8,128)(2,1)S(1)}, bf16[64,128]{1,0:T(8,128)(2,1)S(1)}, u32[]{:S(2)}, u32[]{:S(2)}) collective-permute-start(bf16[64,128]{1,0:T(8,128)(2,1)S(1)} %get-tuple-element.25), channel_id=1, source_target_pairs={{0,3},{1,2},{2,1},{3,0},{4,7},{5,6},{6,5},{7,4},{8,11},{9,10},{10,... | collective-permute-start | bytes 49160 | tf_op jit(solution)/shard_map/ppermute | solution.py:417
  54.5 4.6 %collective-permute-start.19 = (bf16[64,128]{1,0:T(8,128)(2,1)S(1)}, bf16[64,128]{1,0:T(8,128)(2,1)S(1)}, u32[]{:S(2)}, u32[]{:S(2)}) collective-permute-start(bf16[64,128]{1,0:T(8,128)(2,1)S(1)} %get-tuple-element.26), channel_id=1, source_target_pairs={{0,2},{1,3},{2,0},{3,1},{4,6},{5,7},{6,4},{7,5},{8,10},{9,11},{10,... | collective-permute-start | bytes 49160 | tf_op jit(solution)/shard_map/ppermute | solution.py:417
  56.3 3.7 %collective-permute-start.20 = (bf16[64,128]{1,0:T(8,128)(2,1)S(1)}, bf16[64,128]{1,0:T(8,128)(2,1)S(1)}, u32[]{:S(2)}, u32[]{:S(2)}) collective-permute-start(bf16[64,128]{1,0:T(8,128)(2,1)S(1)} %get-tuple-element.27), channel_id=1, source_target_pairs={{0,1},{1,0},{2,3},{3,2},{4,5},{5,4},{6,7},{7,6},{8,9},{9,8},{10,11... | collective-permute-start | bytes 49160 | tf_op jit(solution)/shard_map/ppermute | solution.py:417
  (5 other events, 53.5 us)

commit v7 on v6

--- a/solution.py
+++ b/solution.py
@@ -180,6 +180,20 @@
         out[2 * timeline : 2 * timeline + 2, :] = jnp.broadcast_to(total, (2, HD))
 
 
+def cut_kernel(squares, keys, values, out, done):
+    width = KVH // 2 * HD
+    lanes = pl.ds(pl.multiple_of((1 - (lax.axis_index("gx") & 1)) * width, width), width)
+    copies = [
+        pltpu.make_async_copy(cache.at[t, :, lanes], out.at[k, t], done.at[k, t])
+        for k, cache in enumerate((keys, values))
+        for t in range(2)
+    ]
+    for copy in copies:
+        copy.start()
+    for copy in copies:
+        copy.wait()
+
+
 def norm_kernel(hidden, a, b, gain, out):
     squares = (a[...] + b[...])[:, 0:1]
     wide_gain = gain[...].astype(F32)
@@ -188,7 +202,7 @@
         out[timeline] = (hidden[timeline].astype(F32) * scale * wide_gain).astype(BF16)
 
 
-def project_kernel(n3, n2, n1, n0, w, kept, sent, rows, sums):
+def project_kernel(n3, n2, n1, n0, w, later, kept, sent, rows, sums):
     core = lax.axis_index("gx") & 1
     for shift, normed in enumerate((n0, n1, n2, n3)):
         for timeline in range(2):
@@ -226,9 +240,8 @@
     cosine,
     sine,
     keys,
-    far_keys,
     values,
-    far_values,
+    far_caches,
     o0,
     o1,
     projected,
@@ -264,19 +277,20 @@
     token = row & 1
     timeline = (row >> 1) & 1
     first = timeline[:GROUP_ROWS] == 0
-    groups = [
-        (
-            slice(GROUP_ROWS * g, GROUP_ROWS * (g + 1)),
-            pl.ds(pl.multiple_of(core * (KVH // 2 * HD) + HD * g, HD), HD),
-        )
-        for g in range(KVH // 2)
-    ]
-    for at, lanes in groups:
-        for block, cache in enumerate((keys, far_keys)):
+    groups = [slice(GROUP_ROWS * g, GROUP_ROWS * (g + 1)) for g in range(KVH // 2)]
+
+    def block_of(g, which, t):
+        lanes = pl.ds(pl.multiple_of(core * (KVH // 2 * HD) + HD * g, HD), HD)
+        own = (keys, values)[which][t, :, lanes]
+        return own, far_caches[which, t, :, HD * g : HD * (g + 1)]
+
+    for g, at in enumerate(groups):
+        blocks = [block_of(g, 0, t) for t in range(2)]
+        for block in range(2):
             both = [
                 lax.dot_general(
                     queries[at],
-                    cache[t, :, lanes],
+                    blocks[t][block],
                     (((1,), (1,)), ((), ())),
                     preferred_element_type=F32,
                 )
@@ -312,15 +326,15 @@
         weight = jnp.exp(score - maxima)
         totals += weight
         added += weight.astype(BF16).astype(F32) * value
-    for g, (at, lanes) in enumerate(groups):
+    for g, at in enumerate(groups):
         both = [
             sum(
                 jnp.dot(
                     rounded[at, SPAN_DEV * block : SPAN_DEV * (block + 1)],
-                    cache[t, :, lanes],
+                    part,
                     preferred_element_type=F32,
                 )
-                for block, cache in enumerate((values, far_values))
+                for block, part in enumerate(block_of(g, 1, t))
             )
             for t in range(2)
         ]
@@ -454,7 +468,7 @@
     count = columns // HD * ROWS
     pinned_w_qkv = pinned(w_qkv)
     w_out = pinned(w_out)
-    caches = [(pinned(cache), pinned(partner(cache, "gx", 1))) for cache in (k_cache, v_cache)]
+    pinned_caches = [pinned(k_cache), pinned(v_cache)]
     cosine, sine = rotation(positions)
 
     line = shape(8, HD, dtype=F32)
@@ -465,6 +479,16 @@
         [pinned(hidden), partner(hidden, "gx", 1)],
         later=[w_qkv],
     )
+    slots = k_cache.shape[1]
+    cut = call(
+        cut_kernel,
+        "cut",
+        shape(2, 2, slots, KVH // 2 * HD),
+        [squares],
+        [pltpu.SemaphoreType.DMA((2, 2))],
+        later=[k_cache, v_cache],
+    )
+    far_caches = pinned(partner(cut, "gx", 1))
     normed = call(
         norm_kernel,
         "norm",
@@ -476,7 +500,7 @@
         project_kernel,
         "project",
         [half, half],
-        [*on_gy([normed] * NY), pinned_w_qkv],
+        [*on_gy([normed] * NY), pinned_w_qkv, far_caches],
         [pltpu.VMEM((NY * ROWS, features), F32), pltpu.VMEM((NY, QKV_ROWS, HD), F32)],
     )
     block = shape(QKV_ROWS, HD, dtype=F32)
@@ -488,7 +512,7 @@
         attend_kernel,
         "attend",
         [block, block],
-        [cache_len, near, partner(near, "gx", 1), cosine, sine, *caches[0], *caches[1]],
+        [cache_len, near, partner(near, "gx", 1), cosine, sine, *pinned_caches, far_caches],
         [
             pltpu.VMEM((NY * QKV_ROWS, HD), F32),
             pltpu.VMEM((2, 8, HD), F32),

time: 61 us -> 55.3 us (0.907)
  waiting for transfers between devices: 22.4 us -> 18.3 us
  local copies, waits for them, and re-layouts: 3.63 us -> 0.75 us
  Pallas kernels: 5.74 us -> 7.21 us
    ppermute x13 -> x12, waiting for transfers between devices: 16.2 us -> 13.3 us  [partner(): lax.ppermute(part, axis, [(k, k ^ distance) for k in range(lax.axis_size(...]
    pallas_call x9 -> x10, Pallas kernels: 5.74 us -> 7.21 us  [call(): pl.pallas_call(kernel, in_specs=[SMEM_SPEC] * scalars + [VMEM_SPEC] * (le...]
    broadcast_in_dim x1, local copies, waits for them, and re-layouts: 1.47 us -> 0.01 us  [small_body(): norm_gain[None]]
    unnamed x16 -> x18, local copies, waits for them, and re-layouts: 2.15 us -> 0.75 us
    ppermute x8, waiting for transfers between devices: 6.14 us -> 4.97 us  [on_chips(): received.append(lax.ppermute(parts[k], ('gx', 'gy'), pairs))]
    ppermute x8, starting transfers between devices: 11.2 us -> 10.3 us  [on_chips(): received.append(lax.ppermute(parts[k], ('gx', 'gy'), pairs))]
    ppermute x13 -> x12, starting transfers between devices: 17.3 us -> 18.2 us  [partner(): lax.ppermute(part, axis, [(k, k ^ distance) for k in range(lax.axis_size(...]
  transfers between devices with their start and end apart: 21 -> 20, of which waited for: 14 -> 15; matrix products, arithmetic and copies ran while one was open for 3% -> 1% of each run, Pallas kernels for 3% -> 0%
where the time goes in v7:
time: 55.3 us; the launch traced here: 55.1 us
  starting transfers between devices  28.4 us (51%)
  waiting for transfers between devices  18.3 us (33%)
  Pallas kernels  7.21 us (13%)
  local copies, waits for them, and re-layouts  0.75 us (1%)
    ppermute x12, starting transfers between devices, partner(): lax.ppermute(part, axis, [(k, k ^ distance) for k in range(lax.axis_size(...  18.2 us
    ppermute x12, waiting for transfers between devices, partner(): lax.ppermute(part, axis, [(k, k ^ distance) for k in range(lax.axis_size(...  13.3 us
    ppermute x8, starting transfers between devices, on_chips(): received.append(lax.ppermute(parts[k], ('gx', 'gy'), pairs))  10.3 us
    pallas_call x10, Pallas kernels, call(): pl.pallas_call(kernel, in_specs=[SMEM_SPEC] * scalars + [VMEM_SPEC] * (le...  7.21 us
    ppermute x8, waiting for transfers between devices, on_chips(): received.append(lax.ppermute(parts[k], ('gx', 'gy'), pairs))  4.97 us
  transfers between devices with their start and end apart: 20, of which 15 were waited for; matrix products, arithmetic and copies ran while one was open for 1% of the time, Pallas kernels for 0%

profile of v7, /device:TPU:0, one launch (start us, length us, event | category | flops | bytes accessed | tf_op | source)
XLA Modules:
  0.0 55.1 jit_solution(14730224659242454530)
XLA Ops:
  0.5 1.0 %collective-permute-done.other = bf16[2,2,2048]{2,1,0:T(2,128)(2,1)S(1)} collective-permute-done((bf16[2,2,2048]{2,1,0:T(2,128)(2,1)}, bf16[2,2,2048]{2,1,0:T(2,128)(2,1)S(1)}, u32[]{:S(2)}, u32[]{:S(2)}) %collective-permute-start) | collective-permute-done | bytes 16416 | tf_op jit(solution)/shard_map/ppermute | solution.py:431
  2.3 1.5 %cut.1 = bf16[2,2,384,512]{3,2,1,0:T(8,128)(2,1)S(1)} custom-call(f32[8,128]{1,0:T(8,128)S(1)} %get-tuple-element.18.a.squares, bf16[2,384,1024]{2,1,0:T(8,128)(2,1)} %keys.3, bf16[2,384,1024]{2,1,0:T(8,128)(2,1)} %values.3), custom_call_target="tpu_custom_call" | custom-call | tf_op jit(solution)/shard_map/cut/pallas_call | solution.py:154
  4.3 2.7 %collective-permute-start.1 = (f32[8,128]{1,0:T(8,128)S(1)}, f32[8,128]{1,0:T(8,128)S(1)}, u32[]{:S(2)}, u32[]{:S(2)}) collective-permute-start(f32[8,128]{1,0:T(8,128)S(1)} %get-tuple-element.18.a.squares), channel_id=1, source_target_pairs={{0,8},{4,12},{8,0},{12,4},{1,9},{5,13},{9,1},{13,5},{2,10},{6,14},... | collective-permute-start | bytes 12296 | tf_op jit(solution)/shard_map/ppermute | solution.py:431
  7.0 1.6 %collective-permute-done.1.b = f32[8,128]{1,0:T(8,128)S(1)} collective-permute-done((f32[8,128]{1,0:T(8,128)S(1)}, f32[8,128]{1,0:T(8,128)S(1)}, u32[]{:S(2)}, u32[]{:S(2)}) %collective-permute-start.1) | collective-permute-done | bytes 4128 | tf_op jit(solution)/shard_map/ppermute | solution.py:431
  8.6 4.2 %collective-permute-start.2 = (bf16[2,2,2048]{2,1,0:T(2,128)(2,1)S(1)}, bf16[2,2,2048]{2,1,0:T(2,128)(2,1)S(1)}, u32[]{:S(2)}, u32[]{:S(2)}) collective-permute-start(bf16[2,2,2048]{2,1,0:T(2,128)(2,1)S(1)} %norm.1.n0), channel_id=1, source_target_pairs={{0,3},{1,2},{2,1},{3,0},{4,7},{5,6},{6,5},{7,4},{8,11},{9,10},{10,... | collective-permute-start | bytes 49160 | tf_op jit(solution)/shard_map/ppermute | solution.py:431
  13.6 1.1 %collective-permute-done.2.n3 = bf16[2,2,2048]{2,1,0:T(2,128)(2,1)S(1)} collective-permute-done((bf16[2,2,2048]{2,1,0:T(2,128)(2,1)S(1)}, bf16[2,2,2048]{2,1,0:T(2,128)(2,1)S(1)}, u32[]{:S(2)}, u32[]{:S(2)}) %collective-permute-start.2) | collective-permute-done | bytes 16416 | tf_op jit(solution)/shard_map/ppermute | solution.py:431
  14.7 2.8 %collective-permute-done.3.n2 = bf16[2,2,2048]{2,1,0:T(2,128)(2,1)S(1)} collective-permute-done((bf16[2,2,2048]{2,1,0:T(2,128)(2,1)S(1)}, bf16[2,2,2048]{2,1,0:T(2,128)(2,1)S(1)}, u32[]{:S(2)}, u32[]{:S(2)}) %collective-permute-start.3) | collective-permute-done | bytes 16416 | tf_op jit(solution)/shard_map/ppermute | solution.py:431
  17.5 1.5 %project.1 = (f32[2,80,128]{2,1,0:T(8,128)S(1)}, f32[2,80,128]{2,1,0:T(8,128)S(1)}) custom-call(bf16[2,2,2048]{2,1,0:T(2,128)(2,1)S(1)} %collective-permute-done.2.n3, bf16[2,2,2048]{2,1,0:T(2,128)(2,1)S(1)} %collective-permute-done.3.n2, bf16[2,2,2048]{2,1,0:T(2,128)(2,1)S(1)} %collective-permute-done.4.n1, bf16[2,2,2048]{2,1,0:T(2,128)(2,1)S(1)} %norm.1.n0, ...), custom_call_target="tpu_custom_call" | custom-call | tf_op jit(solution)/shard_map/project/pallas_call | solution.py:154
  19.1 1.2 %collective-permute-done.6.b = f32[2,80,128]{2,1,0:T(8,128)S(1)} collective-permute-done((f32[2,80,128]{2,1,0:T(8,128)S(1)}, f32[2,80,128]{2,1,0:T(8,128)S(1)}, u32[]{:S(2)}, u32[]{:S(2)}) %collective-permute-start.6) | collective-permute-done | bytes 81952 | tf_op jit(solution)/shard_map/ppermute | solution.py:431
  20.3 2.5 %collective-permute-start.7 = (f32[80,128]{1,0:T(8,128)S(1)}, f32[80,128]{1,0:T(8,128)S(1)}, u32[]{:S(2)}, u32[]{:S(2)}) collective-permute-start(f32[80,128]{1,0:T(8,128)S(1)} %get-tuple-element.21), channel_id=1, source_target_pairs={{0,11},{1,10},{2,9},{3,8},{4,14},{5,15},{6,12},{7,13},{8,3},{9,2},... | collective-permute-start | bytes 122888 | tf_op jit(solution)/shard_map/ppermute | solution.py:447
  22.8 2.4 %collective-permute-start.8 = (f32[80,128]{1,0:T(8,128)S(1)}, f32[80,128]{1,0:T(8,128)S(1)}, u32[]{:S(2)}, u32[]{:S(2)}) collective-permute-start(f32[80,128]{1,0:T(8,128)S(1)} %get-tuple-element.21), channel_id=1, source_target_pairs={{0,3},{1,2},{2,1},{3,0},{4,6},{5,7},{6,4},{7,5},{8,11},{9,10},{10,... | collective-permute-start | bytes 122888 | tf_op jit(solution)/shard_map/ppermute | solution.py:447
  27.2 1.5 %collective-permute-done.8.a1 = f32[80,128]{1,0:T(8,128)S(1)} collective-permute-done((f32[80,128]{1,0:T(8,128)S(1)}, f32[80,128]{1,0:T(8,128)S(1)}, u32[]{:S(2)}, u32[]{:S(2)}) %collective-permute-start.8) | collective-permute-done | bytes 40992 | tf_op jit(solution)/shard_map/ppermute | solution.py:447
  28.6 1.6 %collective-permute-done.9.b0 = f32[80,128]{1,0:T(8,128)S(1)} collective-permute-done((f32[80,128]{1,0:T(8,128)S(1)}, f32[80,128]{1,0:T(8,128)S(1)}, u32[]{:S(2)}, u32[]{:S(2)}) %collective-permute-start.9) | collective-permute-done | bytes 40992 | tf_op jit(solution)/shard_map/ppermute | solution.py:447
  30.4 1.1 %collective-permute-done.11.far = bf16[2,80,128]{2,1,0:T(8,128)(2,1)S(1)} collective-permute-done((bf16[2,80,128]{2,1,0:T(8,128)(2,1)S(1)}, bf16[2,80,128]{2,1,0:T(8,128)(2,1)S(1)}, u32[]{:S(2)}, u32[]{:S(2)}) %collective-permute-start.11) | collective-permute-done | bytes 40992 | tf_op jit(solution)/shard_map/ppermute | solution.py:431
  31.5 1.9 %attend.1 = (bf16[80,128]{1,0:T(8,128)(2,1)S(1)}, bf16[80,128]{1,0:T(8,128)(2,1)S(1)}) custom-call(s32[2]{0:T(128)S(1)} %copy-done.4, bf16[2,80,128]{2,1,0:T(8,128)(2,1)S(1)} %round.1.near, bf16[2,80,128]{2,1,0:T(8,128)(2,1)S(1)} %collective-permute-done.11.far, f32[2,2,128]{2,1,0:T(2,128)S(1)} %get-tuple-element.32.cosine, ...), custom_call_target="tpu_custom_call" | custom-call | tf_op jit(solution)/shard_map/attend/pallas_call | solution.py:154
  34.2 0.9 %collective-permute-start.13 = (bf16[80,128]{1,0:T(8,128)(2,1)S(1)}, bf16[80,128]{1,0:T(8,128)(2,1)S(1)}, u32[]{:S(2)}, u32[]{:S(2)}) collective-permute-start(bf16[80,128]{1,0:T(8,128)(2,1)S(1)} %get-tuple-element.23), channel_id=1, source_target_pairs={{0,1},{1,0},{2,5},{3,4},{4,3},{5,2},{6,7},{7,6},{8,9},{9,8},{10,13... | collective-permute-start | bytes 61448 | tf_op jit(solution)/shard_map/ppermute | solution.py:447
  35.1 1.8 %collective-permute-start.14 = (bf16[80,128]{1,0:T(8,128)(2,1)S(1)}, bf16[80,128]{1,0:T(8,128)(2,1)S(1)}, u32[]{:S(2)}, u32[]{:S(2)}) collective-permute-start(bf16[80,128]{1,0:T(8,128)(2,1)S(1)} %get-tuple-element.24), channel_id=1, source_target_pairs={{0,8},{1,9},{2,12},{3,13},{4,10},{5,11},{6,14},{7,15},{8,0},{9,1},... | collective-permute-start | bytes 61448 | tf_op jit(solution)/shard_map/ppermute | solution.py:447
  39.2 5.2 %collective-permute-start.16 = (bf16[2,64,128]{2,1,0:T(8,128)(2,1)S(1)}, bf16[2,64,128]{2,1,0:T(8,128)(2,1)S(1)}, u32[]{:S(2)}, u32[]{:S(2)}) collective-permute-start(bf16[2,64,128]{2,1,0:T(8,128)(2,1)S(1)} %settle.1.near), channel_id=1, source_target_pairs={{0,4},{4,0},{8,12},{12,8},{1,5},{5,1},{9,13},{13,9},{2,6},{6,2},{1... | collective-permute-start | bytes 98312 | tf_op jit(solution)/shard_map/ppermute | solution.py:431
  45.3 1.2 %output.1 = (f32[64,128]{1,0:T(8,128)S(1)}, bf16[64,128]{1,0:T(8,128)(2,1)S(1)}, bf16[64,128]{1,0:T(8,128)(2,1)S(1)}, bf16[64,128]{1,0:T(8,128)(2,1)S(1)}) custom-call(bf16[2,64,128]{2,1,0:T(8,128)(2,1)S(1)} %settle.1.near, bf16[2,64,128]{2,1,0:T(8,128)(2,1)S(1)} %collective-permute-done.16.far, bf16[2048,2048]{1,0:T(8,128)(2,1)S(1)} %bitcast.1), custom_call_target="tpu_custom_call" | custom-call | tf_op jit(solution)/shard_map/output/pallas_call | solution.py:154
  46.5 2.5 %collective-permute-start.17 = (bf16[64,128]{1,0:T(8,128)(2,1)S(1)}, bf16[64,128]{1,0:T(8,128)(2,1)S(1)}, u32[]{:S(2)}, u32[]{:S(2)}) collective-permute-start(bf16[64,128]{1,0:T(8,128)(2,1)S(1)} %get-tuple-element.25), channel_id=1, source_target_pairs={{0,3},{1,2},{2,1},{3,0},{4,7},{5,6},{6,5},{7,4},{8,11},{9,10},{10,... | collective-permute-start | bytes 49160 | tf_op jit(solution)/shard_map/ppermute | solution.py:431
  48.9 1.8 %collective-permute-start.18 = (bf16[64,128]{1,0:T(8,128)(2,1)S(1)}, bf16[64,128]{1,0:T(8,128)(2,1)S(1)}, u32[]{:S(2)}, u32[]{:S(2)}) collective-permute-start(bf16[64,128]{1,0:T(8,128)(2,1)S(1)} %get-tuple-element.26), channel_id=1, source_target_pairs={{0,2},{1,3},{2,0},{3,1},{4,6},{5,7},{6,4},{7,5},{8,10},{9,11},{10,... | collective-permute-start | bytes 49160 | tf_op jit(solution)/shard_map/ppermute | solution.py:431
  50.9 1.1 %collective-permute-done.17.d = bf16[64,128]{1,0:T(8,128)(2,1)S(1)} collective-permute-done((bf16[64,128]{1,0:T(8,128)(2,1)S(1)}, bf16[64,128]{1,0:T(8,128)(2,1)S(1)}, u32[]{:S(2)}, u32[]{:S(2)}) %collective-permute-start.17) | collective-permute-done | bytes 16416 | tf_op jit(solution)/shard_map/ppermute | solution.py:431
  52.1 1.5 %collective-permute-done.18.c = bf16[64,128]{1,0:T(8,128)(2,1)S(1)} collective-permute-done((bf16[64,128]{1,0:T(8,128)(2,1)S(1)}, bf16[64,128]{1,0:T(8,128)(2,1)S(1)}, u32[]{:S(2)}, u32[]{:S(2)}) %collective-permute-start.18) | collective-permute-done | bytes 16416 | tf_op jit(solution)/shard_map/ppermute | solution.py:431
  53.6 0.9 %collective-permute-done.19.b = bf16[64,128]{1,0:T(8,128)(2,1)S(1)} collective-permute-done((bf16[64,128]{1,0:T(8,128)(2,1)S(1)}, bf16[64,128]{1,0:T(8,128)(2,1)S(1)}, u32[]{:S(2)}, u32[]{:S(2)}) %collective-permute-start.19) | collective-permute-done | bytes 16416 | tf_op jit(solution)/shard_map/ppermute | solution.py:431
  (50 shorter events, 9.5 us)
Async XLA Ops:
  0.0 1.5 %collective-permute-start = (bf16[2,2,2048]{2,1,0:T(2,128)(2,1)}, bf16[2,2,2048]{2,1,0:T(2,128)(2,1)S(1)}, u32[]{:S(2)}, u32[]{:S(2)}) collective-permute-start(bf16[2,2,2048]{2,1,0:T(2,128)(2,1)} %hidden.1), channel_id=1, source_target_pairs={{0,4},{4,0},{8,12},{12,8},{1,5},{5,1},{9,13},{13,9},{2,6},{6,2},{1... | collective-permute-start | bytes 49160 | tf_op jit(solution)/shard_map/ppermute | solution.py:431
  2.3 42.9 %slice-start = ((s8[8388608]{0:T(1024)(128)(4,1)}), s8[4194304]{0:T(1024)(128)(4,1)S(1)}, s32[]{:S(2)}) async-start(s8[8388608]{0:T(1024)(128)(4,1)} %bitcast), calls=%async_computation | async-start | bytes 8388608
  3.9 13.6 %collective-permute-start.5 = (bf16[2,2,384,512]{3,2,1,0:T(8,128)(2,1)S(1)}, bf16[2,2,384,512]{3,2,1,0:T(8,128)(2,1)S(1)}, u32[]{:S(2)}, u32[]{:S(2)}) collective-permute-start(bf16[2,2,384,512]{3,2,1,0:T(8,128)(2,1)S(1)} %cut.1), channel_id=1, source_target_pairs={{0,4},{4,0},{8,12},{12,8},{1,5},{5,1},{9,13},{13,9},{2,6},{6,2},{1... | collective-permute-start | bytes 4718600 | tf_op jit(solution)/shard_map/ppermute | solution.py:431
  4.3 4.2 %collective-permute-start.1 = (f32[8,128]{1,0:T(8,128)S(1)}, f32[8,128]{1,0:T(8,128)S(1)}, u32[]{:S(2)}, u32[]{:S(2)}) collective-permute-start(f32[8,128]{1,0:T(8,128)S(1)} %get-tuple-element.18.a.squares), channel_id=1, source_target_pairs={{0,8},{4,12},{8,0},{12,4},{1,9},{5,13},{9,1},{13,5},{2,10},{6,14},... | collective-permute-start | bytes 12296 | tf_op jit(solution)/shard_map/ppermute | solution.py:431
  8.6 6.1 %collective-permute-start.2 = (bf16[2,2,2048]{2,1,0:T(2,128)(2,1)S(1)}, bf16[2,2,2048]{2,1,0:T(2,128)(2,1)S(1)}, u32[]{:S(2)}, u32[]{:S(2)}) collective-permute-start(bf16[2,2,2048]{2,1,0:T(2,128)(2,1)S(1)} %norm.1.n0), channel_id=1, source_target_pairs={{0,3},{1,2},{2,1},{3,0},{4,7},{5,6},{6,5},{7,4},{8,11},{9,10},{10,... | collective-permute-start | bytes 49160 | tf_op jit(solution)/shard_map/ppermute | solution.py:431
  12.8 4.6 %collective-permute-start.3 = (bf16[2,2,2048]{2,1,0:T(2,128)(2,1)S(1)}, bf16[2,2,2048]{2,1,0:T(2,128)(2,1)S(1)}, u32[]{:S(2)}, u32[]{:S(2)}) collective-permute-start(bf16[2,2,2048]{2,1,0:T(2,128)(2,1)S(1)} %norm.1.n0), channel_id=1, source_target_pairs={{0,2},{1,3},{2,0},{3,1},{4,6},{5,7},{6,4},{7,5},{8,10},{9,11},{10,... | collective-permute-start | bytes 49160 | tf_op jit(solution)/shard_map/ppermute | solution.py:431
  12.8 4.6 %collective-permute-start.4 = (bf16[2,2,2048]{2,1,0:T(2,128)(2,1)S(1)}, bf16[2,2,2048]{2,1,0:T(2,128)(2,1)S(1)}, u32[]{:S(2)}, u32[]{:S(2)}) collective-permute-start(bf16[2,2,2048]{2,1,0:T(2,128)(2,1)S(1)} %norm.1.n0), channel_id=1, source_target_pairs={{0,1},{1,0},{2,3},{3,2},{4,5},{5,4},{6,7},{7,6},{8,9},{9,8},{10,11... | collective-permute-start | bytes 49160 | tf_op jit(solution)/shard_map/ppermute | solution.py:431
  13.6 18.0 %copy-start.2 = (bf16[2,384,1024]{2,1,0:T(8,128)(2,1)S(1)}, bf16[2,384,1024]{2,1,0:T(8,128)(2,1)}, u32[]{:S(2)}) copy-start(bf16[2,384,1024]{2,1,0:T(8,128)(2,1)} %values.3) | copy-start | bytes 4718596
  13.6 18.0 %copy-start.4 = (s32[2]{0:T(128)S(1)}, s32[2]{0:T(128)}, u32[]{:S(2)}) copy-start(s32[2]{0:T(128)} %lengths.1) | copy-start | bytes 28
  13.6 31.7 %slice-start.1 = ((s8[8388608]{0:T(1024)(128)(4,1)}), s8[4194304]{0:T(1024)(128)(4,1)S(1)}, s32[]{:S(2)}) async-start(s8[8388608]{0:T(1024)(128)(4,1)} %bitcast), calls=%async_computation.1 | async-start | bytes 8388608
  19.0 1.3 %collective-permute-start.6 = (f32[2,80,128]{2,1,0:T(8,128)S(1)}, f32[2,80,128]{2,1,0:T(8,128)S(1)}, u32[]{:S(2)}, u32[]{:S(2)}) collective-permute-start(f32[2,80,128]{2,1,0:T(8,128)S(1)} %get-tuple-element.20), channel_id=1, source_target_pairs={{0,4},{4,0},{8,12},{12,8},{1,5},{5,1},{9,13},{13,9},{2,6},{6,2},{1... | collective-permute-start | bytes 245768 | tf_op jit(solution)/shard_map/ppermute | solution.py:431
  20.3 6.8 %collective-permute-start.7 = (f32[80,128]{1,0:T(8,128)S(1)}, f32[80,128]{1,0:T(8,128)S(1)}, u32[]{:S(2)}, u32[]{:S(2)}) collective-permute-start(f32[80,128]{1,0:T(8,128)S(1)} %get-tuple-element.21), channel_id=1, source_target_pairs={{0,11},{1,10},{2,9},{3,8},{4,14},{5,15},{6,12},{7,13},{8,3},{9,2},... | collective-permute-start | bytes 122888 | tf_op jit(solution)/shard_map/ppermute | solution.py:447
  22.8 5.8 %collective-permute-start.8 = (f32[80,128]{1,0:T(8,128)S(1)}, f32[80,128]{1,0:T(8,128)S(1)}, u32[]{:S(2)}, u32[]{:S(2)}) collective-permute-start(f32[80,128]{1,0:T(8,128)S(1)} %get-tuple-element.21), channel_id=1, source_target_pairs={{0,3},{1,2},{2,1},{3,0},{4,6},{5,7},{6,4},{7,5},{8,11},{9,10},{10,... | collective-permute-start | bytes 122888 | tf_op jit(solution)/shard_map/ppermute | solution.py:447
  25.2 1.4 %collective-permute-start.10 = (f32[80,128]{1,0:T(8,128)S(1)}, f32[80,128]{1,0:T(8,128)S(1)}, u32[]{:S(2)}, u32[]{:S(2)}) collective-permute-start(f32[80,128]{1,0:T(8,128)S(1)} %get-tuple-element.22), channel_id=1, source_target_pairs={{0,0},{1,1},{2,2},{3,3},{4,5},{5,4},{6,7},{7,6},{8,8},{9,9},{10,10... | collective-permute-start | bytes 122888 | tf_op jit(solution)/shard_map/ppermute | solution.py:447
  25.8 4.4 %collective-permute-start.9 = (f32[80,128]{1,0:T(8,128)S(1)}, f32[80,128]{1,0:T(8,128)S(1)}, u32[]{:S(2)}, u32[]{:S(2)}) collective-permute-start(f32[80,128]{1,0:T(8,128)S(1)} %get-tuple-element.22), channel_id=1, source_target_pairs={{0,8},{1,9},{2,10},{3,11},{4,13},{5,12},{6,15},{7,14},{8,0},{9,1},... | collective-permute-start | bytes 122888 | tf_op jit(solution)/shard_map/ppermute | solution.py:447
  30.2 1.3 %collective-permute-start.11 = (bf16[2,80,128]{2,1,0:T(8,128)(2,1)S(1)}, bf16[2,80,128]{2,1,0:T(8,128)(2,1)S(1)}, u32[]{:S(2)}, u32[]{:S(2)}) collective-permute-start(bf16[2,80,128]{2,1,0:T(8,128)(2,1)S(1)} %round.1.near), channel_id=1, source_target_pairs={{0,4},{4,0},{8,12},{12,8},{1,5},{5,1},{9,13},{13,9},{2,6},{6,2},{1... | collective-permute-start | bytes 122888 | tf_op jit(solution)/shard_map/ppermute | solution.py:431
  33.4 4.7 %collective-permute-start.12 = (bf16[80,128]{1,0:T(8,128)(2,1)S(1)}, bf16[80,128]{1,0:T(8,128)(2,1)S(1)}, u32[]{:S(2)}, u32[]{:S(2)}) collective-permute-start(bf16[80,128]{1,0:T(8,128)(2,1)S(1)} %get-tuple-element.23), channel_id=1, source_target_pairs={{0,9},{1,8},{2,13},{3,12},{4,11},{5,10},{6,15},{7,14},{8,1},{9,0},... | collective-permute-start | bytes 61448 | tf_op jit(solution)/shard_map/ppermute | solution.py:447
  34.2 4.0 %collective-permute-start.13 = (bf16[80,128]{1,0:T(8,128)(2,1)S(1)}, bf16[80,128]{1,0:T(8,128)(2,1)S(1)}, u32[]{:S(2)}, u32[]{:S(2)}) collective-permute-start(bf16[80,128]{1,0:T(8,128)(2,1)S(1)} %get-tuple-element.23), channel_id=1, source_target_pairs={{0,1},{1,0},{2,5},{3,4},{4,3},{5,2},{6,7},{7,6},{8,9},{9,8},{10,13... | collective-permute-start | bytes 61448 | tf_op jit(solution)/shard_map/ppermute | solution.py:447
  35.1 3.8 %collective-permute-start.14 = (bf16[80,128]{1,0:T(8,128)(2,1)S(1)}, bf16[80,128]{1,0:T(8,128)(2,1)S(1)}, u32[]{:S(2)}, u32[]{:S(2)}) collective-permute-start(bf16[80,128]{1,0:T(8,128)(2,1)S(1)} %get-tuple-element.24), channel_id=1, source_target_pairs={{0,8},{1,9},{2,12},{3,13},{4,10},{5,11},{6,14},{7,15},{8,0},{9,1},... | collective-permute-start | bytes 61448 | tf_op jit(solution)/shard_map/ppermute | solution.py:447
  37.0 2.0 %collective-permute-start.15 = (bf16[80,128]{1,0:T(8,128)(2,1)S(1)}, bf16[80,128]{1,0:T(8,128)(2,1)S(1)}, u32[]{:S(2)}, u32[]{:S(2)}) collective-permute-start(bf16[80,128]{1,0:T(8,128)(2,1)S(1)} %get-tuple-element.24), channel_id=1, source_target_pairs={{0,0},{1,1},{2,4},{3,5},{4,2},{5,3},{6,6},{7,7},{8,8},{9,9},{10,12... | collective-permute-start | bytes 61448 | tf_op jit(solution)/shard_map/ppermute | solution.py:447
  39.2 6.1 %collective-permute-start.16 = (bf16[2,64,128]{2,1,0:T(8,128)(2,1)S(1)}, bf16[2,64,128]{2,1,0:T(8,128)(2,1)S(1)}, u32[]{:S(2)}, u32[]{:S(2)}) collective-permute-start(bf16[2,64,128]{2,1,0:T(8,128)(2,1)S(1)} %settle.1.near), channel_id=1, source_target_pairs={{0,4},{4,0},{8,12},{12,8},{1,5},{5,1},{9,13},{13,9},{2,6},{6,2},{1... | collective-permute-start | bytes 98312 | tf_op jit(solution)/shard_map/ppermute | solution.py:431
  46.5 5.6 %collective-permute-start.17 = (bf16[64,128]{1,0:T(8,128)(2,1)S(1)}, bf16[64,128]{1,0:T(8,128)(2,1)S(1)}, u32[]{:S(2)}, u32[]{:S(2)}) collective-permute-start(bf16[64,128]{1,0:T(8,128)(2,1)S(1)} %get-tuple-element.25), channel_id=1, source_target_pairs={{0,3},{1,2},{2,1},{3,0},{4,7},{5,6},{6,5},{7,4},{8,11},{9,10},{10,... | collective-permute-start | bytes 49160 | tf_op jit(solution)/shard_map/ppermute | solution.py:431
  48.9 4.6 %collective-permute-start.18 = (bf16[64,128]{1,0:T(8,128)(2,1)S(1)}, bf16[64,128]{1,0:T(8,128)(2,1)S(1)}, u32[]{:S(2)}, u32[]{:S(2)}) collective-permute-start(bf16[64,128]{1,0:T(8,128)(2,1)S(1)} %get-tuple-element.26), channel_id=1, source_target_pairs={{0,2},{1,3},{2,0},{3,1},{4,6},{5,7},{6,4},{7,5},{8,10},{9,11},{10,... | collective-permute-start | bytes 49160 | tf_op jit(solution)/shard_map/ppermute | solution.py:431
  50.7 3.7 %collective-permute-start.19 = (bf16[64,128]{1,0:T(8,128)(2,1)S(1)}, bf16[64,128]{1,0:T(8,128)(2,1)S(1)}, u32[]{:S(2)}, u32[]{:S(2)}) collective-permute-start(bf16[64,128]{1,0:T(8,128)(2,1)S(1)} %get-tuple-element.27), channel_id=1, source_target_pairs={{0,1},{1,0},{2,3},{3,2},{4,5},{5,4},{6,7},{7,6},{8,9},{9,8},{10,11... | collective-permute-start | bytes 49160 | tf_op jit(solution)/shard_map/ppermute | solution.py:431
  (5 other events, 49.7 us)

commit v8 on v5

--- a/solution.py
+++ b/solution.py
@@ -169,25 +169,26 @@
     return high, values - high
 
 
+def squares_of(hidden, timeline):
+    wide = hidden[timeline].astype(F32)
+    return jnp.sum(wide * wide, axis=-1, keepdims=True)
+
+
 def square_kernel(hidden, later, out, held):
+    held[...] = hidden[...]
     out[...] = jnp.zeros_like(out)
-    held[...] = hidden[...]
     for timeline in range(2):
-        wide = hidden[timeline].astype(F32)
-        total = jnp.sum(wide * wide, axis=-1, keepdims=True)
-        out[2 * timeline : 2 * timeline + 2, :] = jnp.broadcast_to(total, (2, HD))
-
-
-def add_kernel(a, b, out):
-    out[...] = a[...] + b[...]
-
-
-def norm_kernel(hidden, a, b, gain, out):
-    squares = (a[...] + b[...])[:, 0:1]
+        total = jnp.broadcast_to(squares_of(hidden, timeline), (2, HD))
+        out[2 * timeline : 2 * timeline + 2, :] = total
+
+
+def norm_kernel(h3, h2, h1, h0, squares, gain, out):
     wide_gain = gain[...].astype(F32)
     for timeline in range(2):
-        scale = lax.rsqrt(squares[2 * timeline : 2 * timeline + 2] / D + EPSILON)
-        out[timeline] = (hidden[timeline].astype(F32) * scale * wide_gain).astype(BF16)
+        total = squares[2 * timeline : 2 * timeline + 2, 0:1] + squares_of(h1, timeline)
+        total += squares_of(h2, timeline) + squares_of(h3, timeline)
+        scale = lax.rsqrt(total / D + EPSILON)
+        out[timeline] = (h0[timeline].astype(F32) * scale * wide_gain).astype(BF16)
 
 
 def project_kernel(n3, n2, n1, n0, w, kept, sent, rows, sums):
@@ -261,10 +262,10 @@
         ]
         table[at, :] = jnp.where(first, both[0], both[1])
     scaling = HD ** (-0.5)
-    scores = table[...] * scaling
     slot = my_x * SPAN_DEV + lax.broadcasted_iota(jnp.int32, (QUERIES, SPAN_DEV), 1)
     usable = slot < jnp.where(timeline == 0, lengths[0], lengths[1])
-    maxima = jnp.max(jnp.where(usable, scores, NEGATIVE), axis=-1, keepdims=True)
+    scores = jnp.where(usable, table[...] * scaling, NEGATIVE)
+    maxima = jnp.maximum(jnp.max(scores, axis=-1, keepdims=True), NEGATIVE / 10)
 
     wide_queries = queries.astype(F32)
     column = lax.broadcasted_iota(jnp.int32, (QUERIES, KVH * ROWS), 1)
@@ -278,7 +279,7 @@
         allowed = (token >= j) & (my_x == 0)
         maxima = jnp.maximum(maxima, jnp.where(allowed, score, NEGATIVE))
         fresh.append((score, allowed, value))
-    weights = jnp.exp(jnp.where(usable, scores - maxima, NEGATIVE))
+    weights = jnp.exp(scores - maxima)
     totals = jnp.sum(weights, axis=-1, keepdims=True)
     rounded = weights.astype(BF16)
     added = jnp.zeros((QUERIES, HD), F32)
@@ -286,16 +287,14 @@
         weight = jnp.exp(jnp.where(allowed, score - maxima, NEGATIVE))
         totals += weight
         added += weight.astype(BF16).astype(F32) * value
-    mine = [jnp.where(timeline == t, rounded, jnp.zeros_like(rounded)) for t in range(2)]
     for g in range(KVH):
         at = slice(GROUP_ROWS * g, GROUP_ROWS * (g + 1))
-        total = added[at]
-        for t in range(2):
-            total += jnp.dot(
-                mine[t][at], values[t, :, HD * g : HD * (g + 1)], preferred_element_type=F32
-            )
+        both = [
+            jnp.dot(rounded[at], values[t, :, HD * g : HD * (g + 1)], preferred_element_type=F32)
+            for t in range(2)
+        ]
         inside = GROUP_ROWS * (g % 2)
-        parts[g // 2, inside : inside + GROUP_ROWS, :] = total
+        parts[g // 2, inside : inside + GROUP_ROWS, :] = added[at] + jnp.where(first, *both)
 
     lane = lax.broadcasted_iota(jnp.int32, (QUERIES, HD), 1)
     sheet = jnp.where(lane == 0, maxima, jnp.where(lane == 1, totals, 0.0))
@@ -431,19 +430,22 @@
     features = hidden.shape[2]
     count = columns // HD * ROWS
     pinned_w_qkv = pinned(w_qkv)
-    hidden, w_out, k_cache, v_cache = map(pinned, (hidden, w_out, k_cache, v_cache))
+    w_out, k_cache, v_cache = map(pinned, (w_out, k_cache, v_cache))
     cosine, sine = rotation(positions)
 
-    line = shape(8, HD, dtype=F32)
-    squares, hidden = call(
-        square_kernel, "square", [line, shape(*hidden.shape)], [hidden], later=[w_qkv]
-    )
-    squares = call(add_kernel, "add", line, [squares, partner(squares, "gx", 1)])
+    others = [partner(hidden, "gx", x) for x in (3, 2, 1)]
+    squares, held = call(
+        square_kernel,
+        "square",
+        [shape(8, HD, dtype=F32), shape(*hidden.shape)],
+        [pinned(hidden)],
+        later=[w_qkv],
+    )
     normed = call(
         norm_kernel,
         "norm",
         shape(*hidden.shape),
-        [hidden, squares, partner(squares, "gx", 2), norm_gain[None]],
+        [*others, held, squares, norm_gain[None]],
     )
     half = shape(2, QKV_ROWS, HD, dtype=F32)
     kept, sent = call(

time: 51.4 us -> 50.4 us (0.981)
  waiting for transfers between devices: 16.6 us -> 15.9 us
    broadcast_in_dim x1, local copies, waits for them, and re-layouts: 1.44 us -> 0.84 us  [small_body(): norm_gain[None]]
    unnamed x12, local copies, waits for them, and re-layouts: 0.89 us -> 1.48 us
    ppermute x12 -> x13, starting transfers between devices: 13.2 us -> 12.8 us  [partner(): lax.ppermute(part, axis, [(k, k ^ distance) for k in range(lax.axis_size(...]
    ppermute x12 -> x13, waiting for transfers between devices: 11 us -> 10.7 us  [partner(): lax.ppermute(part, axis, [(k, k ^ distance) for k in range(lax.axis_size(...]
    pallas_call x11 -> x10, Pallas kernels: 6.04 us -> 6.13 us  [call(): pl.pallas_call(kernel, in_specs=[SMEM_SPEC] * scalars + [VMEM_SPEC] * (le...]
  transfers between devices with their start and end apart: 20 -> 21, of which waited for: 15 -> 14; matrix products, arithmetic and copies ran while one was open for 5% -> 4% of each run, Pallas kernels for 0% -> 0%
where the time goes in v8:
time: 50.4 us; the launch traced here: 50.1 us
  starting transfers between devices  24.8 us (49%)
  waiting for transfers between devices  15.9 us (32%)
  Pallas kernels  6.13 us (12%)
  local copies, waits for them, and re-layouts  2.32 us (5%)
  other arithmetic  0.93 us (2%)
    ppermute x13, starting transfers between devices, partner(): lax.ppermute(part, axis, [(k, k ^ distance) for k in range(lax.axis_size(...  12.8 us
    ppermute x8, starting transfers between devices, on_chips(): received[k, far_x] = lax.ppermute(parts[k], ('gx', 'gy'), pairs)  12 us
    ppermute x13, waiting for transfers between devices, partner(): lax.ppermute(part, axis, [(k, k ^ distance) for k in range(lax.axis_size(...  10.7 us
    pallas_call x10, Pallas kernels, call(): pl.pallas_call(kernel, in_specs=[SMEM_SPEC] * scalars + [VMEM_SPEC] * (le...  6.13 us
    ppermute x8, waiting for transfers between devices, on_chips(): received[k, far_x] = lax.ppermute(parts[k], ('gx', 'gy'), pairs)  5.18 us
    unnamed x12, local copies, waits for them, and re-layouts  1.48 us
  transfers between devices with their start and end apart: 21, of which 14 were waited for; matrix products, arithmetic and copies ran while one was open for 4% of the time, Pallas kernels for 0%

profile of v8, /device:TPU:0, one launch (start us, length us, event | category | flops | bytes accessed | tf_op | source)
XLA Modules:
  0.0 50.1 jit_solution(12745103064770210198)
XLA Ops:
  0.0 2.4 %collective-permute-start = (bf16[2,2,2048]{2,1,0:T(2,128)(2,1)}, bf16[2,2,2048]{2,1,0:T(2,128)(2,1)S(1)}, u32[]{:S(2)}, u32[]{:S(2)}) collective-permute-start(bf16[2,2,2048]{2,1,0:T(2,128)(2,1)} %hidden.1), channel_id=1, source_target_pairs={{0,12},{4,8},{8,4},{12,0},{1,13},{5,9},{9,5},{13,1},{2,14},{6,10},... | collective-permute-start | bytes 49160 | tf_op jit(solution)/shard_map/ppermute | solution.py:402
  3.1 1.5 %copy-done.4 = bf16[2,2,2048]{2,1,0:T(2,128)(2,1)S(1)} copy-done((bf16[2,2,2048]{2,1,0:T(2,128)(2,1)S(1)}, bf16[2,2,2048]{2,1,0:T(2,128)(2,1)}, u32[]{:S(2)}) %copy-start.4) | copy-done | bytes 16408
  5.5 0.9 %collective-permute-done.1.h2 = bf16[2,2,2048]{2,1,0:T(2,128)(2,1)S(1)} collective-permute-done((bf16[2,2,2048]{2,1,0:T(2,128)(2,1)}, bf16[2,2,2048]{2,1,0:T(2,128)(2,1)S(1)}, u32[]{:S(2)}, u32[]{:S(2)}) %collective-permute-start.1) | collective-permute-done | bytes 16416 | tf_op jit(solution)/shard_map/ppermute | solution.py:402
  6.7 3.7 %collective-permute-start.3 = (bf16[2,2,2048]{2,1,0:T(2,128)(2,1)S(1)}, bf16[2,2,2048]{2,1,0:T(2,128)(2,1)S(1)}, u32[]{:S(2)}, u32[]{:S(2)}) collective-permute-start(bf16[2,2,2048]{2,1,0:T(2,128)(2,1)S(1)} %norm.1.n0), channel_id=1, source_target_pairs={{0,3},{1,2},{2,1},{3,0},{4,7},{5,6},{6,5},{7,4},{8,11},{9,10},{10,... | collective-permute-start | bytes 49160 | tf_op jit(solution)/shard_map/ppermute | solution.py:402
  12.3 2.6 %collective-permute-done.4.n2 = bf16[2,2,2048]{2,1,0:T(2,128)(2,1)S(1)} collective-permute-done((bf16[2,2,2048]{2,1,0:T(2,128)(2,1)S(1)}, bf16[2,2,2048]{2,1,0:T(2,128)(2,1)S(1)}, u32[]{:S(2)}, u32[]{:S(2)}) %collective-permute-start.4) | collective-permute-done | bytes 16416 | tf_op jit(solution)/shard_map/ppermute | solution.py:402
  15.0 1.5 %project.1 = (f32[2,80,128]{2,1,0:T(8,128)S(1)}, f32[2,80,128]{2,1,0:T(8,128)S(1)}) custom-call(bf16[2,2,2048]{2,1,0:T(2,128)(2,1)S(1)} %collective-permute-done.3.n3, bf16[2,2,2048]{2,1,0:T(2,128)(2,1)S(1)} %collective-permute-done.4.n2, bf16[2,2,2048]{2,1,0:T(2,128)(2,1)S(1)} %collective-permute-done.5.n1, bf16[2,2,2048]{2,1,0:T(2,128)(2,1)S(1)} %norm.1.n0, ...), custom_call_target="tpu_custom_call" | custom-call | tf_op jit(solution)/shard_map/project/pallas_call | solution.py:154
  16.6 1.2 %collective-permute-done.6.b = f32[2,80,128]{2,1,0:T(8,128)S(1)} collective-permute-done((f32[2,80,128]{2,1,0:T(8,128)S(1)}, f32[2,80,128]{2,1,0:T(8,128)S(1)}, u32[]{:S(2)}, u32[]{:S(2)}) %collective-permute-start.6) | collective-permute-done | bytes 81952 | tf_op jit(solution)/shard_map/ppermute | solution.py:402
  17.8 2.1 %collective-permute-start.7 = (f32[80,128]{1,0:T(8,128)S(1)}, f32[80,128]{1,0:T(8,128)S(1)}, u32[]{:S(2)}, u32[]{:S(2)}) collective-permute-start(f32[80,128]{1,0:T(8,128)S(1)} %get-tuple-element.23), channel_id=1, source_target_pairs={{0,11},{1,10},{2,9},{3,8},{4,14},{5,15},{6,12},{7,13},{8,3},{9,2},... | collective-permute-start | bytes 122888 | tf_op jit(solution)/shard_map/ppermute | solution.py:418
  19.9 2.4 %collective-permute-start.8 = (f32[80,128]{1,0:T(8,128)S(1)}, f32[80,128]{1,0:T(8,128)S(1)}, u32[]{:S(2)}, u32[]{:S(2)}) collective-permute-start(f32[80,128]{1,0:T(8,128)S(1)} %get-tuple-element.23), channel_id=1, source_target_pairs={{0,3},{1,2},{2,1},{3,0},{4,6},{5,7},{6,4},{7,5},{8,11},{9,10},{10,... | collective-permute-start | bytes 122888 | tf_op jit(solution)/shard_map/ppermute | solution.py:418
  22.3 0.9 %collective-permute-start.9 = (f32[80,128]{1,0:T(8,128)S(1)}, f32[80,128]{1,0:T(8,128)S(1)}, u32[]{:S(2)}, u32[]{:S(2)}) collective-permute-start(f32[80,128]{1,0:T(8,128)S(1)} %get-tuple-element.24), channel_id=1, source_target_pairs={{0,8},{1,9},{2,10},{3,11},{4,13},{5,12},{6,15},{7,14},{8,0},{9,1},... | collective-permute-start | bytes 122888 | tf_op jit(solution)/shard_map/ppermute | solution.py:418
  24.7 1.4 %collective-permute-done.8.a1 = f32[80,128]{1,0:T(8,128)S(1)} collective-permute-done((f32[80,128]{1,0:T(8,128)S(1)}, f32[80,128]{1,0:T(8,128)S(1)}, u32[]{:S(2)}, u32[]{:S(2)}) %collective-permute-start.8) | collective-permute-done | bytes 40992 | tf_op jit(solution)/shard_map/ppermute | solution.py:418
  26.6 1.0 %collective-permute-done.11.far = bf16[2,80,128]{2,1,0:T(8,128)(2,1)S(1)} collective-permute-done((bf16[2,80,128]{2,1,0:T(8,128)(2,1)S(1)}, bf16[2,80,128]{2,1,0:T(8,128)(2,1)S(1)}, u32[]{:S(2)}, u32[]{:S(2)}) %collective-permute-start.11) | collective-permute-done | bytes 40992 | tf_op jit(solution)/shard_map/ppermute | solution.py:402
  27.6 2.0 %attend.1 = (f32[2,72,128]{2,1,0:T(8,128)S(1)}, f32[2,72,128]{2,1,0:T(8,128)S(1)}) custom-call(s32[2]{0:T(128)S(1)} %copy-done.5, bf16[2,80,128]{2,1,0:T(8,128)(2,1)S(1)} %round.1.near, bf16[2,80,128]{2,1,0:T(8,128)(2,1)S(1)} %collective-permute-done.11.far, f32[2,2,128]{2,1,0:T(2,128)S(1)} %get-tuple-element.36.cosine, ...), custom_call_target="tpu_custom_call" | custom-call | tf_op jit(solution)/shard_map/attend/pallas_call | solution.py:154
  29.8 1.1 %collective-permute-done.12.b = f32[2,72,128]{2,1,0:T(8,128)S(1)} collective-permute-done((f32[2,72,128]{2,1,0:T(8,128)S(1)}, f32[2,72,128]{2,1,0:T(8,128)S(1)}, u32[]{:S(2)}, u32[]{:S(2)}) %collective-permute-start.12) | collective-permute-done | bytes 73760 | tf_op jit(solution)/shard_map/ppermute | solution.py:402
  31.2 3.2 %collective-permute-start.13 = (bf16[80,128]{1,0:T(8,128)(2,1)S(1)}, bf16[80,128]{1,0:T(8,128)(2,1)S(1)}, u32[]{:S(2)}, u32[]{:S(2)}) collective-permute-start(bf16[80,128]{1,0:T(8,128)(2,1)S(1)} %get-tuple-element.27), channel_id=1, source_target_pairs={{0,11},{1,10},{2,9},{3,8},{4,14},{5,15},{6,12},{7,13},{8,3},{9,2},... | collective-permute-start | bytes 61448 | tf_op jit(solution)/shard_map/ppermute | solution.py:418
  34.4 0.9 %collective-permute-start.14 = (bf16[80,128]{1,0:T(8,128)(2,1)S(1)}, bf16[80,128]{1,0:T(8,128)(2,1)S(1)}, u32[]{:S(2)}, u32[]{:S(2)}) collective-permute-start(bf16[80,128]{1,0:T(8,128)(2,1)S(1)} %get-tuple-element.27), channel_id=1, source_target_pairs={{0,3},{1,2},{2,1},{3,0},{4,6},{5,7},{6,4},{7,5},{8,11},{9,10},{10,... | collective-permute-start | bytes 61448 | tf_op jit(solution)/shard_map/ppermute | solution.py:418
  35.3 1.2 %collective-permute-start.15 = (bf16[80,128]{1,0:T(8,128)(2,1)S(1)}, bf16[80,128]{1,0:T(8,128)(2,1)S(1)}, u32[]{:S(2)}, u32[]{:S(2)}) collective-permute-start(bf16[80,128]{1,0:T(8,128)(2,1)S(1)} %get-tuple-element.28), channel_id=1, source_target_pairs={{0,8},{1,9},{2,10},{3,11},{4,13},{5,12},{6,15},{7,14},{8,0},{9,1},... | collective-permute-start | bytes 61448 | tf_op jit(solution)/shard_map/ppermute | solution.py:418
  37.9 2.1 %collective-permute-done.14.a1 = bf16[80,128]{1,0:T(8,128)(2,1)S(1)} collective-permute-done((bf16[80,128]{1,0:T(8,128)(2,1)S(1)}, bf16[80,128]{1,0:T(8,128)(2,1)S(1)}, u32[]{:S(2)}, u32[]{:S(2)}) %collective-permute-start.14) | collective-permute-done | bytes 20512 | tf_op jit(solution)/shard_map/ppermute | solution.py:418
  40.5 1.0 %collective-permute-done.17.far = bf16[2,64,128]{2,1,0:T(8,128)(2,1)S(1)} collective-permute-done((bf16[2,64,128]{2,1,0:T(8,128)(2,1)S(1)}, bf16[2,64,128]{2,1,0:T(8,128)(2,1)S(1)}, u32[]{:S(2)}, u32[]{:S(2)}) %collective-permute-start.17) | collective-permute-done | bytes 32800 | tf_op jit(solution)/shard_map/ppermute | solution.py:402
  41.5 1.2 %output.1 = (f32[64,128]{1,0:T(8,128)S(1)}, bf16[64,128]{1,0:T(8,128)(2,1)S(1)}, bf16[64,128]{1,0:T(8,128)(2,1)S(1)}, bf16[64,128]{1,0:T(8,128)(2,1)S(1)}) custom-call(bf16[2,64,128]{2,1,0:T(8,128)(2,1)S(1)} %settle.1.near, bf16[2,64,128]{2,1,0:T(8,128)(2,1)S(1)} %collective-permute-done.17.far, bf16[2048,2048]{1,0:T(8,128)(2,1)S(1)} %copy-done.1), custom_call_target="tpu_custom_call" | custom-call | tf_op jit(solution)/shard_map/output/pallas_call | solution.py:154
  42.7 2.1 %collective-permute-start.18 = (bf16[64,128]{1,0:T(8,128)(2,1)S(1)}, bf16[64,128]{1,0:T(8,128)(2,1)S(1)}, u32[]{:S(2)}, u32[]{:S(2)}) collective-permute-start(bf16[64,128]{1,0:T(8,128)(2,1)S(1)} %get-tuple-element.29), channel_id=1, source_target_pairs={{0,3},{1,2},{2,1},{3,0},{4,7},{5,6},{6,5},{7,4},{8,11},{9,10},{10,... | collective-permute-start | bytes 49160 | tf_op jit(solution)/shard_map/ppermute | solution.py:402
  44.8 2.4 %collective-permute-start.20 = (bf16[64,128]{1,0:T(8,128)(2,1)S(1)}, bf16[64,128]{1,0:T(8,128)(2,1)S(1)}, u32[]{:S(2)}, u32[]{:S(2)}) collective-permute-start(bf16[64,128]{1,0:T(8,128)(2,1)S(1)} %get-tuple-element.31), channel_id=1, source_target_pairs={{0,1},{1,0},{2,3},{3,2},{4,5},{5,4},{6,7},{7,6},{8,9},{9,8},{10,11... | collective-permute-start | bytes 49160 | tf_op jit(solution)/shard_map/ppermute | solution.py:402
  47.2 1.3 %collective-permute-done.18.d = bf16[64,128]{1,0:T(8,128)(2,1)S(1)} collective-permute-done((bf16[64,128]{1,0:T(8,128)(2,1)S(1)}, bf16[64,128]{1,0:T(8,128)(2,1)S(1)}, u32[]{:S(2)}, u32[]{:S(2)}) %collective-permute-start.18) | collective-permute-done | bytes 16416 | tf_op jit(solution)/shard_map/ppermute | solution.py:402
  48.5 1.0 %collective-permute-done.19.c = bf16[64,128]{1,0:T(8,128)(2,1)S(1)} collective-permute-done((bf16[64,128]{1,0:T(8,128)(2,1)S(1)}, bf16[64,128]{1,0:T(8,128)(2,1)S(1)}, u32[]{:S(2)}, u32[]{:S(2)}) %collective-permute-start.19) | collective-permute-done | bytes 16416 | tf_op jit(solution)/shard_map/ppermute | solution.py:402
  (45 shorter events, 8.9 us)
Async XLA Ops:
  0.0 27.6 %copy-start.2 = (bf16[2,384,1024]{2,1,0:T(8,128)(2,1)S(1)}, bf16[2,384,1024]{2,1,0:T(8,128)(2,1)}, u32[]{:S(2)}) copy-start(bf16[2,384,1024]{2,1,0:T(8,128)(2,1)} %keys.1) | copy-start | bytes 4718596
  0.0 27.6 %copy-start.3 = (bf16[2,384,1024]{2,1,0:T(8,128)(2,1)S(1)}, bf16[2,384,1024]{2,1,0:T(8,128)(2,1)}, u32[]{:S(2)}) copy-start(bf16[2,384,1024]{2,1,0:T(8,128)(2,1)} %values.1) | copy-start | bytes 4718596
  0.0 5.5 %collective-permute-start = (bf16[2,2,2048]{2,1,0:T(2,128)(2,1)}, bf16[2,2,2048]{2,1,0:T(2,128)(2,1)S(1)}, u32[]{:S(2)}, u32[]{:S(2)}) collective-permute-start(bf16[2,2,2048]{2,1,0:T(2,128)(2,1)} %hidden.1), channel_id=1, source_target_pairs={{0,12},{4,8},{8,4},{12,0},{1,13},{5,9},{9,5},{13,1},{2,14},{6,10},... | collective-permute-start | bytes 49160 | tf_op jit(solution)/shard_map/ppermute | solution.py:402
  2.5 3.9 %collective-permute-start.1 = (bf16[2,2,2048]{2,1,0:T(2,128)(2,1)}, bf16[2,2,2048]{2,1,0:T(2,128)(2,1)S(1)}, u32[]{:S(2)}, u32[]{:S(2)}) collective-permute-start(bf16[2,2,2048]{2,1,0:T(2,128)(2,1)} %hidden.1), channel_id=1, source_target_pairs={{0,8},{4,12},{8,0},{12,4},{1,9},{5,13},{9,1},{13,5},{2,10},{6,14},... | collective-permute-start | bytes 49160 | tf_op jit(solution)/shard_map/ppermute | solution.py:402
  3.1 3.3 %collective-permute-start.2 = (bf16[2,2,2048]{2,1,0:T(2,128)(2,1)}, bf16[2,2,2048]{2,1,0:T(2,128)(2,1)S(1)}, u32[]{:S(2)}, u32[]{:S(2)}) collective-permute-start(bf16[2,2,2048]{2,1,0:T(2,128)(2,1)} %hidden.1), channel_id=1, source_target_pairs={{0,4},{4,0},{8,12},{12,8},{1,5},{5,1},{9,13},{13,9},{2,6},{6,2},{1... | collective-permute-start | bytes 49160 | tf_op jit(solution)/shard_map/ppermute | solution.py:402
  4.7 36.8 %copy-start.1 = (bf16[2048,2048]{1,0:T(8,128)(2,1)S(1)}, bf16[2048,2048]{1,0:T(8,128)(2,1)}, u32[]{:S(2)}) copy-start(bf16[2048,2048]{1,0:T(8,128)(2,1)} %w.3) | copy-start | bytes 25165828
  6.7 5.7 %collective-permute-start.3 = (bf16[2,2,2048]{2,1,0:T(2,128)(2,1)S(1)}, bf16[2,2,2048]{2,1,0:T(2,128)(2,1)S(1)}, u32[]{:S(2)}, u32[]{:S(2)}) collective-permute-start(bf16[2,2,2048]{2,1,0:T(2,128)(2,1)S(1)} %norm.1.n0), channel_id=1, source_target_pairs={{0,3},{1,2},{2,1},{3,0},{4,7},{5,6},{6,5},{7,4},{8,11},{9,10},{10,... | collective-permute-start | bytes 49160 | tf_op jit(solution)/shard_map/ppermute | solution.py:402
  10.3 4.6 %collective-permute-start.4 = (bf16[2,2,2048]{2,1,0:T(2,128)(2,1)S(1)}, bf16[2,2,2048]{2,1,0:T(2,128)(2,1)S(1)}, u32[]{:S(2)}, u32[]{:S(2)}) collective-permute-start(bf16[2,2,2048]{2,1,0:T(2,128)(2,1)S(1)} %norm.1.n0), channel_id=1, source_target_pairs={{0,2},{1,3},{2,0},{3,1},{4,6},{5,7},{6,4},{7,5},{8,10},{9,11},{10,... | collective-permute-start | bytes 49160 | tf_op jit(solution)/shard_map/ppermute | solution.py:402
  10.3 4.6 %collective-permute-start.5 = (bf16[2,2,2048]{2,1,0:T(2,128)(2,1)S(1)}, bf16[2,2,2048]{2,1,0:T(2,128)(2,1)S(1)}, u32[]{:S(2)}, u32[]{:S(2)}) collective-permute-start(bf16[2,2,2048]{2,1,0:T(2,128)(2,1)S(1)} %norm.1.n0), channel_id=1, source_target_pairs={{0,1},{1,0},{2,3},{3,2},{4,5},{5,4},{6,7},{7,6},{8,9},{9,8},{10,11... | collective-permute-start | bytes 49160 | tf_op jit(solution)/shard_map/ppermute | solution.py:402
  16.5 1.3 %collective-permute-start.6 = (f32[2,80,128]{2,1,0:T(8,128)S(1)}, f32[2,80,128]{2,1,0:T(8,128)S(1)}, u32[]{:S(2)}, u32[]{:S(2)}) collective-permute-start(f32[2,80,128]{2,1,0:T(8,128)S(1)} %get-tuple-element.22), channel_id=1, source_target_pairs={{0,4},{4,0},{8,12},{12,8},{1,5},{5,1},{9,13},{13,9},{2,6},{6,2},{1... | collective-permute-start | bytes 245768 | tf_op jit(solution)/shard_map/ppermute | solution.py:402
  17.8 6.9 %collective-permute-start.7 = (f32[80,128]{1,0:T(8,128)S(1)}, f32[80,128]{1,0:T(8,128)S(1)}, u32[]{:S(2)}, u32[]{:S(2)}) collective-permute-start(f32[80,128]{1,0:T(8,128)S(1)} %get-tuple-element.23), channel_id=1, source_target_pairs={{0,11},{1,10},{2,9},{3,8},{4,14},{5,15},{6,12},{7,13},{8,3},{9,2},... | collective-permute-start | bytes 122888 | tf_op jit(solution)/shard_map/ppermute | solution.py:418
  19.9 6.2 %collective-permute-start.8 = (f32[80,128]{1,0:T(8,128)S(1)}, f32[80,128]{1,0:T(8,128)S(1)}, u32[]{:S(2)}, u32[]{:S(2)}) collective-permute-start(f32[80,128]{1,0:T(8,128)S(1)} %get-tuple-element.23), channel_id=1, source_target_pairs={{0,3},{1,2},{2,1},{3,0},{4,6},{5,7},{6,4},{7,5},{8,11},{9,10},{10,... | collective-permute-start | bytes 122888 | tf_op jit(solution)/shard_map/ppermute | solution.py:418
  22.3 4.0 %collective-permute-start.9 = (f32[80,128]{1,0:T(8,128)S(1)}, f32[80,128]{1,0:T(8,128)S(1)}, u32[]{:S(2)}, u32[]{:S(2)}) collective-permute-start(f32[80,128]{1,0:T(8,128)S(1)} %get-tuple-element.24), channel_id=1, source_target_pairs={{0,8},{1,9},{2,10},{3,11},{4,13},{5,12},{6,15},{7,14},{8,0},{9,1},... | collective-permute-start | bytes 122888 | tf_op jit(solution)/shard_map/ppermute | solution.py:418
  23.2 3.1 %collective-permute-start.10 = (f32[80,128]{1,0:T(8,128)S(1)}, f32[80,128]{1,0:T(8,128)S(1)}, u32[]{:S(2)}, u32[]{:S(2)}) collective-permute-start(f32[80,128]{1,0:T(8,128)S(1)} %get-tuple-element.24), channel_id=1, source_target_pairs={{0,0},{1,1},{2,2},{3,3},{4,5},{5,4},{6,7},{7,6},{8,8},{9,9},{10,10... | collective-permute-start | bytes 122888 | tf_op jit(solution)/shard_map/ppermute | solution.py:418
  26.3 1.3 %collective-permute-start.11 = (bf16[2,80,128]{2,1,0:T(8,128)(2,1)S(1)}, bf16[2,80,128]{2,1,0:T(8,128)(2,1)S(1)}, u32[]{:S(2)}, u32[]{:S(2)}) collective-permute-start(bf16[2,80,128]{2,1,0:T(8,128)(2,1)S(1)} %round.1.near), channel_id=1, source_target_pairs={{0,4},{4,0},{8,12},{12,8},{1,5},{5,1},{9,13},{13,9},{2,6},{6,2},{1... | collective-permute-start | bytes 122888 | tf_op jit(solution)/shard_map/ppermute | solution.py:402
  29.6 1.3 %collective-permute-start.12 = (f32[2,72,128]{2,1,0:T(8,128)S(1)}, f32[2,72,128]{2,1,0:T(8,128)S(1)}, u32[]{:S(2)}, u32[]{:S(2)}) collective-permute-start(f32[2,72,128]{2,1,0:T(8,128)S(1)} %get-tuple-element.26), channel_id=1, source_target_pairs={{0,4},{4,0},{8,12},{12,8},{1,5},{5,1},{9,13},{13,9},{2,6},{6,2},{1... | collective-permute-start | bytes 221192 | tf_op jit(solution)/shard_map/ppermute | solution.py:402
  31.2 6.7 %collective-permute-start.13 = (bf16[80,128]{1,0:T(8,128)(2,1)S(1)}, bf16[80,128]{1,0:T(8,128)(2,1)S(1)}, u32[]{:S(2)}, u32[]{:S(2)}) collective-permute-start(bf16[80,128]{1,0:T(8,128)(2,1)S(1)} %get-tuple-element.27), channel_id=1, source_target_pairs={{0,11},{1,10},{2,9},{3,8},{4,14},{5,15},{6,12},{7,13},{8,3},{9,2},... | collective-permute-start | bytes 61448 | tf_op jit(solution)/shard_map/ppermute | solution.py:418
  34.4 5.6 %collective-permute-start.14 = (bf16[80,128]{1,0:T(8,128)(2,1)S(1)}, bf16[80,128]{1,0:T(8,128)(2,1)S(1)}, u32[]{:S(2)}, u32[]{:S(2)}) collective-permute-start(bf16[80,128]{1,0:T(8,128)(2,1)S(1)} %get-tuple-element.27), channel_id=1, source_target_pairs={{0,3},{1,2},{2,1},{3,0},{4,6},{5,7},{6,4},{7,5},{8,11},{9,10},{10,... | collective-permute-start | bytes 61448 | tf_op jit(solution)/shard_map/ppermute | solution.py:418
  35.3 4.6 %collective-permute-start.15 = (bf16[80,128]{1,0:T(8,128)(2,1)S(1)}, bf16[80,128]{1,0:T(8,128)(2,1)S(1)}, u32[]{:S(2)}, u32[]{:S(2)}) collective-permute-start(bf16[80,128]{1,0:T(8,128)(2,1)S(1)} %get-tuple-element.28), channel_id=1, source_target_pairs={{0,8},{1,9},{2,10},{3,11},{4,13},{5,12},{6,15},{7,14},{8,0},{9,1},... | collective-permute-start | bytes 61448 | tf_op jit(solution)/shard_map/ppermute | solution.py:418
  36.5 3.5 %collective-permute-start.16 = (bf16[80,128]{1,0:T(8,128)(2,1)S(1)}, bf16[80,128]{1,0:T(8,128)(2,1)S(1)}, u32[]{:S(2)}, u32[]{:S(2)}) collective-permute-start(bf16[80,128]{1,0:T(8,128)(2,1)S(1)} %get-tuple-element.28), channel_id=1, source_target_pairs={{0,0},{1,1},{2,2},{3,3},{4,5},{5,4},{6,7},{7,6},{8,8},{9,9},{10,10... | collective-permute-start | bytes 61448 | tf_op jit(solution)/shard_map/ppermute | solution.py:418
  40.2 1.3 %collective-permute-start.17 = (bf16[2,64,128]{2,1,0:T(8,128)(2,1)S(1)}, bf16[2,64,128]{2,1,0:T(8,128)(2,1)S(1)}, u32[]{:S(2)}, u32[]{:S(2)}) collective-permute-start(bf16[2,64,128]{2,1,0:T(8,128)(2,1)S(1)} %settle.1.near), channel_id=1, source_target_pairs={{0,4},{4,0},{8,12},{12,8},{1,5},{5,1},{9,13},{13,9},{2,6},{6,2},{1... | collective-permute-start | bytes 98312 | tf_op jit(solution)/shard_map/ppermute | solution.py:402
  42.7 5.7 %collective-permute-start.18 = (bf16[64,128]{1,0:T(8,128)(2,1)S(1)}, bf16[64,128]{1,0:T(8,128)(2,1)S(1)}, u32[]{:S(2)}, u32[]{:S(2)}) collective-permute-start(bf16[64,128]{1,0:T(8,128)(2,1)S(1)} %get-tuple-element.29), channel_id=1, source_target_pairs={{0,3},{1,2},{2,1},{3,0},{4,7},{5,6},{6,5},{7,4},{8,11},{9,10},{10,... | collective-permute-start | bytes 49160 | tf_op jit(solution)/shard_map/ppermute | solution.py:402
  44.8 4.7 %collective-permute-start.19 = (bf16[64,128]{1,0:T(8,128)(2,1)S(1)}, bf16[64,128]{1,0:T(8,128)(2,1)S(1)}, u32[]{:S(2)}, u32[]{:S(2)}) collective-permute-start(bf16[64,128]{1,0:T(8,128)(2,1)S(1)} %get-tuple-element.30), channel_id=1, source_target_pairs={{0,2},{1,3},{2,0},{3,1},{4,6},{5,7},{6,4},{7,5},{8,10},{9,11},{10,... | collective-permute-start | bytes 49160 | tf_op jit(solution)/shard_map/ppermute | solution.py:402
  44.8 4.7 %collective-permute-start.20 = (bf16[64,128]{1,0:T(8,128)(2,1)S(1)}, bf16[64,128]{1,0:T(8,128)(2,1)S(1)}, u32[]{:S(2)}, u32[]{:S(2)}) collective-permute-start(bf16[64,128]{1,0:T(8,128)(2,1)S(1)} %get-tuple-element.31), channel_id=1, source_target_pairs={{0,1},{1,0},{2,3},{3,2},{4,5},{5,4},{6,7},{7,6},{8,9},{9,8},{10,11... | collective-permute-start | bytes 49160 | tf_op jit(solution)/shard_map/ppermute | solution.py:402
  (3 other events, 39.4 us)

commit v9 on v8

--- a/solution.py
+++ b/solution.py
@@ -144,18 +144,15 @@
 GROUP_ROWS = QUERIES // KVH
 VMEM_SPEC = pl.BlockSpec(memory_space=pltpu.VMEM)
 HBM_SPEC = pl.BlockSpec(memory_space=pltpu.HBM)
-SMEM_SPEC = pl.BlockSpec(memory_space=pltpu.SMEM)
 F32 = jnp.float32
 BF16 = jnp.bfloat16
 
 
-def call(kernel, name, out_shape, operands, scratch=(), scalars=0, mib=8, later=()):
+def call(kernel, name, out_shape, operands, scratch=(), mib=8, later=()):
     many = isinstance(out_shape, (list, tuple))
     return pl.pallas_call(
         kernel,
-        in_specs=[SMEM_SPEC] * scalars
-        + [VMEM_SPEC] * (len(operands) - scalars)
-        + [HBM_SPEC] * len(later),
+        in_specs=[VMEM_SPEC] * len(operands) + [HBM_SPEC] * len(later),
         out_specs=[VMEM_SPEC] * len(out_shape) if many else VMEM_SPEC,
         out_shape=out_shape,
         scratch_shapes=list(scratch),
@@ -174,7 +171,7 @@
     return jnp.sum(wide * wide, axis=-1, keepdims=True)
 
 
-def square_kernel(hidden, later, out, held):
+def square_kernel(hidden, out, held):
     held[...] = hidden[...]
     out[...] = jnp.zeros_like(out)
     for timeline in range(2):
@@ -182,7 +179,7 @@
         out[2 * timeline : 2 * timeline + 2, :] = total
 
 
-def norm_kernel(h3, h2, h1, h0, squares, gain, out):
+def norm_kernel(h3, h2, h1, h0, squares, gain, later, out):
     wide_gain = gain[...].astype(F32)
     for timeline in range(2):
         total = squares[2 * timeline : 2 * timeline + 2, 0:1] + squares_of(h1, timeline)
@@ -198,7 +195,7 @@
             at = ROWS * shift + 2 * timeline
             rows[at : at + 2, :] = normed[timeline].astype(F32)
     left = rows[...].astype(BF16)
-    width = 512
+    width = 1280
     for step in range(w.shape[1] // width):
         part = jnp.dot(left, w[:, width * step : width * (step + 1)], preferred_element_type=F32)
         for head in range(width // HD):
@@ -223,7 +220,7 @@
 
 
 def attend_kernel(
-    lengths, near, far, cosine, sine, keys, values, kept, sent, projected, turns, table, parts
+    near, far, cosine, sine, lengths, keys, values, kept, sent, projected, turns, live, table, parts
 ):
     my_x = lax.axis_index("gx")
     my_y = lax.axis_index("gy")
@@ -235,6 +232,7 @@
     for t in range(4):
         turns[0, 2 * t : 2 * t + 2, :] = cosine[t % 2]
         turns[1, 2 * t : 2 * t + 2, :] = sine[t % 2]
+        live[2 * t : 2 * t + 2, :] = lengths[t % 2]
     turned = projected[: QUERIES + KVH * ROWS, :]
     swapped = pltpu.roll(turned, HD // 2, 1)
     turned = (
@@ -262,9 +260,13 @@
         ]
         table[at, :] = jnp.where(first, both[0], both[1])
     scaling = HD ** (-0.5)
-    slot = my_x * SPAN_DEV + lax.broadcasted_iota(jnp.int32, (QUERIES, SPAN_DEV), 1)
-    usable = slot < jnp.where(timeline == 0, lengths[0], lengths[1])
-    scores = jnp.where(usable, table[...] * scaling, NEGATIVE)
+    scores = []
+    for start in range(0, SPAN_DEV, HD):
+        slot = my_x * SPAN_DEV + start + lax.broadcasted_iota(jnp.int32, (8, HD), 1)
+        usable = (slot < live[...])[None]
+        part = table[:, start : start + HD].reshape(-1, 8, HD) * scaling
+        scores.append(jnp.where(usable, part, NEGATIVE).reshape(QUERIES, HD))
+    scores = jnp.concatenate(scores, axis=1)
     maxima = jnp.maximum(jnp.max(scores, axis=-1, keepdims=True), NEGATIVE / 10)
 
     wide_queries = queries.astype(F32)
@@ -367,7 +369,7 @@
                 shift, ROWS * head : ROWS * (head + 1), :
             ]
     left = wide[...].astype(BF16)
-    width = 512
+    width = 1024
     for step in range(w.shape[1] // width):
         part = jnp.dot(left, w[:, width * step : width * (step + 1)], preferred_element_type=F32)
         for chunk in range(width // HD):
@@ -432,6 +434,7 @@
     pinned_w_qkv = pinned(w_qkv)
     w_out, k_cache, v_cache = map(pinned, (w_out, k_cache, v_cache))
     cosine, sine = rotation(positions)
+    lengths = jnp.broadcast_to(cache_len[:, None, None], (2, 2, HD))
 
     others = [partner(hidden, "gx", x) for x in (3, 2, 1)]
     squares, held = call(
@@ -439,13 +442,13 @@
         "square",
         [shape(8, HD, dtype=F32), shape(*hidden.shape)],
         [pinned(hidden)],
-        later=[w_qkv],
     )
     normed = call(
         norm_kernel,
         "norm",
         shape(*hidden.shape),
         [*others, held, squares, norm_gain[None]],
+        later=[w_qkv],
     )
     half = shape(2, QKV_ROWS, HD, dtype=F32)
     kept, sent = call(
@@ -464,14 +467,14 @@
         attend_kernel,
         "attend",
         [half, half],
-        [cache_len, near, partner(near, "gx", 1), cosine, sine, k_cache, v_cache],
+        [near, partner(near, "gx", 1), cosine, sine, lengths, k_cache, v_cache],
         [
             pltpu.VMEM((NY * QKV_ROWS, HD), F32),
             pltpu.VMEM((2, 8, HD), F32),
+            pltpu.VMEM((8, HD), jnp.int32),
             pltpu.VMEM((QUERIES, SPAN_DEV), F32),
             pltpu.VMEM((NY, OUT_ROWS + 8, HD), F32),
         ],
-        scalars=1,
         mib=16,
     )
     block = shape(OUT_ROWS + 16, HD)

time: 50.4 us -> 49.5 us (0.982)
  local copies, waits for them, and re-layouts: 2.32 us -> 1.52 us
  waiting for transfers between devices: 15.9 us -> 16.6 us
  other arithmetic: 0.93 us -> 0.28 us
  Pallas kernels: 6.13 us -> 5.59 us
    ppermute x13, waiting for transfers between devices: 10.7 us -> 11.8 us  [partner(): lax.ppermute(part, axis, [(k, k ^ distance) for k in range(lax.axis_size(...]
    unnamed x12 -> x14, local copies, waits for them, and re-layouts: 1.48 us -> 0.76 us
    convert_element_type x1, other arithmetic: 0.73 us -> 0.07 us  [rotation(): angles = places.astype(F32)[:, :, None] * frequency[None, None, :]]
    pallas_call x10, Pallas kernels: 6.13 us -> 5.59 us  [call(): pl.pallas_call(kernel, in_specs=[VMEM_SPEC] * len(operands) + [HBM_SPEC]...]
  transfers between devices with their start and end apart: 21 -> 21, of which waited for: 14 -> 14; matrix products, arithmetic and copies ran while one was open for 4% -> 2% of each run, Pallas kernels for 0% -> 0%
where the time goes in v9:
time: 49.5 us; the launch traced here: 49.2 us
  starting transfers between devices  25.1 us (51%)
  waiting for transfers between devices  16.6 us (34%)
  Pallas kernels  5.59 us (11%)
  local copies, waits for them, and re-layouts  1.52 us (3%)
    ppermute x13, starting transfers between devices, partner(): lax.ppermute(part, axis, [(k, k ^ distance) for k in range(lax.axis_size(...  13.1 us
    ppermute x8, starting transfers between devices, on_chips(): received[k, far_x] = lax.ppermute(parts[k], ('gx', 'gy'), pairs)  12 us
    ppermute x13, waiting for transfers between devices, partner(): lax.ppermute(part, axis, [(k, k ^ distance) for k in range(lax.axis_size(...  11.8 us
    pallas_call x10, Pallas kernels, call(): pl.pallas_call(kernel, in_specs=[VMEM_SPEC] * len(operands) + [HBM_SPEC]...  5.59 us
    ppermute x8, waiting for transfers between devices, on_chips(): received[k, far_x] = lax.ppermute(parts[k], ('gx', 'gy'), pairs)  4.8 us
  transfers between devices with their start and end apart: 21, of which 14 were waited for; matrix products, arithmetic and copies ran while one was open for 2% of the time, Pallas kernels for 0%

profile of v9, /device:TPU:0, one launch (start us, length us, event | category | flops | bytes accessed | tf_op | source)
XLA Modules:
  0.0 49.2 jit_solution(6883132695384180760)
XLA Ops:
  0.0 2.4 %collective-permute-start = (bf16[2,2,2048]{2,1,0:T(2,128)(2,1)}, bf16[2,2,2048]{2,1,0:T(2,128)(2,1)S(1)}, u32[]{:S(2)}, u32[]{:S(2)}) collective-permute-start(bf16[2,2,2048]{2,1,0:T(2,128)(2,1)} %hidden.1), channel_id=1, source_target_pairs={{0,12},{4,8},{8,4},{12,0},{1,13},{5,9},{9,5},{13,1},{2,14},{6,10},... | collective-permute-start | bytes 49160 | tf_op jit(solution)/shard_map/ppermute | solution.py:404
  4.6 1.7 %collective-permute-done.1.h2 = bf16[2,2,2048]{2,1,0:T(2,128)(2,1)S(1)} collective-permute-done((bf16[2,2,2048]{2,1,0:T(2,128)(2,1)}, bf16[2,2,2048]{2,1,0:T(2,128)(2,1)S(1)}, u32[]{:S(2)}, u32[]{:S(2)}) %collective-permute-start.1) | collective-permute-done | bytes 16416 | tf_op jit(solution)/shard_map/ppermute | solution.py:404
  6.6 3.7 %collective-permute-start.3 = (bf16[2,2,2048]{2,1,0:T(2,128)(2,1)S(1)}, bf16[2,2,2048]{2,1,0:T(2,128)(2,1)S(1)}, u32[]{:S(2)}, u32[]{:S(2)}) collective-permute-start(bf16[2,2,2048]{2,1,0:T(2,128)(2,1)S(1)} %norm.1.n0), channel_id=1, source_target_pairs={{0,3},{1,2},{2,1},{3,0},{4,7},{5,6},{6,5},{7,4},{8,11},{9,10},{10,... | collective-permute-start | bytes 49160 | tf_op jit(solution)/shard_map/ppermute | solution.py:404
  10.3 0.8 %collective-permute-start.5 = (bf16[2,2,2048]{2,1,0:T(2,128)(2,1)S(1)}, bf16[2,2,2048]{2,1,0:T(2,128)(2,1)S(1)}, u32[]{:S(2)}, u32[]{:S(2)}) collective-permute-start(bf16[2,2,2048]{2,1,0:T(2,128)(2,1)S(1)} %norm.1.n0), channel_id=1, source_target_pairs={{0,1},{1,0},{2,3},{3,2},{4,5},{5,4},{6,7},{7,6},{8,9},{9,8},{10,11... | collective-permute-start | bytes 49160 | tf_op jit(solution)/shard_map/ppermute | solution.py:404
  11.1 1.3 %collective-permute-done.3.n3 = bf16[2,2,2048]{2,1,0:T(2,128)(2,1)S(1)} collective-permute-done((bf16[2,2,2048]{2,1,0:T(2,128)(2,1)S(1)}, bf16[2,2,2048]{2,1,0:T(2,128)(2,1)S(1)}, u32[]{:S(2)}, u32[]{:S(2)}) %collective-permute-start.3) | collective-permute-done | bytes 16416 | tf_op jit(solution)/shard_map/ppermute | solution.py:404
  12.4 2.5 %collective-permute-done.4.n2 = bf16[2,2,2048]{2,1,0:T(2,128)(2,1)S(1)} collective-permute-done((bf16[2,2,2048]{2,1,0:T(2,128)(2,1)S(1)}, bf16[2,2,2048]{2,1,0:T(2,128)(2,1)S(1)}, u32[]{:S(2)}, u32[]{:S(2)}) %collective-permute-start.4) | collective-permute-done | bytes 16416 | tf_op jit(solution)/shard_map/ppermute | solution.py:404
  14.9 1.5 %project.1 = (f32[2,80,128]{2,1,0:T(8,128)S(1)}, f32[2,80,128]{2,1,0:T(8,128)S(1)}) custom-call(bf16[2,2,2048]{2,1,0:T(2,128)(2,1)S(1)} %collective-permute-done.3.n3, bf16[2,2,2048]{2,1,0:T(2,128)(2,1)S(1)} %collective-permute-done.4.n2, bf16[2,2,2048]{2,1,0:T(2,128)(2,1)S(1)} %collective-permute-done.5.n1, bf16[2,2,2048]{2,1,0:T(2,128)(2,1)S(1)} %norm.1.n0, ...), custom_call_target="tpu_custom_call" | custom-call | tf_op jit(solution)/shard_map/project/pallas_call | solution.py:153
  16.5 1.2 %collective-permute-done.6.b = f32[2,80,128]{2,1,0:T(8,128)S(1)} collective-permute-done((f32[2,80,128]{2,1,0:T(8,128)S(1)}, f32[2,80,128]{2,1,0:T(8,128)S(1)}, u32[]{:S(2)}, u32[]{:S(2)}) %collective-permute-start.6) | collective-permute-done | bytes 81952 | tf_op jit(solution)/shard_map/ppermute | solution.py:404
  17.8 1.7 %collective-permute-start.7 = (f32[80,128]{1,0:T(8,128)S(1)}, f32[80,128]{1,0:T(8,128)S(1)}, u32[]{:S(2)}, u32[]{:S(2)}) collective-permute-start(f32[80,128]{1,0:T(8,128)S(1)} %get-tuple-element.23), channel_id=1, source_target_pairs={{0,11},{1,10},{2,9},{3,8},{4,14},{5,15},{6,12},{7,13},{8,3},{9,2},... | collective-permute-start | bytes 122888 | tf_op jit(solution)/shard_map/ppermute | solution.py:420
  19.5 2.4 %collective-permute-start.8 = (f32[80,128]{1,0:T(8,128)S(1)}, f32[80,128]{1,0:T(8,128)S(1)}, u32[]{:S(2)}, u32[]{:S(2)}) collective-permute-start(f32[80,128]{1,0:T(8,128)S(1)} %get-tuple-element.23), channel_id=1, source_target_pairs={{0,3},{1,2},{2,1},{3,0},{4,6},{5,7},{6,4},{7,5},{8,11},{9,10},{10,... | collective-permute-start | bytes 122888 | tf_op jit(solution)/shard_map/ppermute | solution.py:420
  21.9 1.2 %collective-permute-start.9 = (f32[80,128]{1,0:T(8,128)S(1)}, f32[80,128]{1,0:T(8,128)S(1)}, u32[]{:S(2)}, u32[]{:S(2)}) collective-permute-start(f32[80,128]{1,0:T(8,128)S(1)} %get-tuple-element.24), channel_id=1, source_target_pairs={{0,8},{1,9},{2,10},{3,11},{4,13},{5,12},{6,15},{7,14},{8,0},{9,1},... | collective-permute-start | bytes 122888 | tf_op jit(solution)/shard_map/ppermute | solution.py:420
  26.2 1.0 %collective-permute-done.11.far = bf16[2,80,128]{2,1,0:T(8,128)(2,1)S(1)} collective-permute-done((bf16[2,80,128]{2,1,0:T(8,128)(2,1)S(1)}, bf16[2,80,128]{2,1,0:T(8,128)(2,1)S(1)}, u32[]{:S(2)}, u32[]{:S(2)}) %collective-permute-start.11) | collective-permute-done | bytes 40992 | tf_op jit(solution)/shard_map/ppermute | solution.py:404
  27.3 1.4 %attend.1 = (f32[2,72,128]{2,1,0:T(8,128)S(1)}, f32[2,72,128]{2,1,0:T(8,128)S(1)}) custom-call(bf16[2,80,128]{2,1,0:T(8,128)(2,1)S(1)} %round.1.near, bf16[2,80,128]{2,1,0:T(8,128)(2,1)S(1)} %collective-permute-done.11.far, f32[2,2,128]{2,1,0:T(2,128)S(1)} %get-tuple-element.36.cosine, f32[2,2,128]{2,1,0:T(2,128)S(1)} %get-tuple-element.37.sine, ...), custom_call_target="tpu_custom_call" | custom-call | tf_op jit(solution)/shard_map/attend/pallas_call | solution.py:153
  28.9 1.1 %collective-permute-done.12.b = f32[2,72,128]{2,1,0:T(8,128)S(1)} collective-permute-done((f32[2,72,128]{2,1,0:T(8,128)S(1)}, f32[2,72,128]{2,1,0:T(8,128)S(1)}, u32[]{:S(2)}, u32[]{:S(2)}) %collective-permute-start.12) | collective-permute-done | bytes 73760 | tf_op jit(solution)/shard_map/ppermute | solution.py:404
  30.3 3.2 %collective-permute-start.13 = (bf16[80,128]{1,0:T(8,128)(2,1)S(1)}, bf16[80,128]{1,0:T(8,128)(2,1)S(1)}, u32[]{:S(2)}, u32[]{:S(2)}) collective-permute-start(bf16[80,128]{1,0:T(8,128)(2,1)S(1)} %get-tuple-element.27), channel_id=1, source_target_pairs={{0,11},{1,10},{2,9},{3,8},{4,14},{5,15},{6,12},{7,13},{8,3},{9,2},... | collective-permute-start | bytes 61448 | tf_op jit(solution)/shard_map/ppermute | solution.py:420
  33.5 1.3 %collective-permute-start.14 = (bf16[80,128]{1,0:T(8,128)(2,1)S(1)}, bf16[80,128]{1,0:T(8,128)(2,1)S(1)}, u32[]{:S(2)}, u32[]{:S(2)}) collective-permute-start(bf16[80,128]{1,0:T(8,128)(2,1)S(1)} %get-tuple-element.27), channel_id=1, source_target_pairs={{0,3},{1,2},{2,1},{3,0},{4,6},{5,7},{6,4},{7,5},{8,11},{9,10},{10,... | collective-permute-start | bytes 61448 | tf_op jit(solution)/shard_map/ppermute | solution.py:420
  34.8 0.8 %collective-permute-start.15 = (bf16[80,128]{1,0:T(8,128)(2,1)S(1)}, bf16[80,128]{1,0:T(8,128)(2,1)S(1)}, u32[]{:S(2)}, u32[]{:S(2)}) collective-permute-start(bf16[80,128]{1,0:T(8,128)(2,1)S(1)} %get-tuple-element.28), channel_id=1, source_target_pairs={{0,8},{1,9},{2,10},{3,11},{4,13},{5,12},{6,15},{7,14},{8,0},{9,1},... | collective-permute-start | bytes 61448 | tf_op jit(solution)/shard_map/ppermute | solution.py:420
  36.9 2.2 %collective-permute-done.14.a1 = bf16[80,128]{1,0:T(8,128)(2,1)S(1)} collective-permute-done((bf16[80,128]{1,0:T(8,128)(2,1)S(1)}, bf16[80,128]{1,0:T(8,128)(2,1)S(1)}, u32[]{:S(2)}, u32[]{:S(2)}) %collective-permute-start.14) | collective-permute-done | bytes 20512 | tf_op jit(solution)/shard_map/ppermute | solution.py:420
  40.0 0.9 %collective-permute-done.17.far = bf16[2,64,128]{2,1,0:T(8,128)(2,1)S(1)} collective-permute-done((bf16[2,64,128]{2,1,0:T(8,128)(2,1)S(1)}, bf16[2,64,128]{2,1,0:T(8,128)(2,1)S(1)}, u32[]{:S(2)}, u32[]{:S(2)}) %collective-permute-start.17) | collective-permute-done | bytes 32800 | tf_op jit(solution)/shard_map/ppermute | solution.py:404
  40.8 1.2 %output.1 = (f32[64,128]{1,0:T(8,128)S(1)}, bf16[64,128]{1,0:T(8,128)(2,1)S(1)}, bf16[64,128]{1,0:T(8,128)(2,1)S(1)}, bf16[64,128]{1,0:T(8,128)(2,1)S(1)}) custom-call(bf16[2,64,128]{2,1,0:T(8,128)(2,1)S(1)} %settle.1.near, bf16[2,64,128]{2,1,0:T(8,128)(2,1)S(1)} %collective-permute-done.17.far, bf16[2048,2048]{1,0:T(8,128)(2,1)S(1)} %copy-done.1), custom_call_target="tpu_custom_call" | custom-call | tf_op jit(solution)/shard_map/output/pallas_call | solution.py:153
  42.1 1.9 %collective-permute-start.18 = (bf16[64,128]{1,0:T(8,128)(2,1)S(1)}, bf16[64,128]{1,0:T(8,128)(2,1)S(1)}, u32[]{:S(2)}, u32[]{:S(2)}) collective-permute-start(bf16[64,128]{1,0:T(8,128)(2,1)S(1)} %get-tuple-element.29), channel_id=1, source_target_pairs={{0,3},{1,2},{2,1},{3,0},{4,7},{5,6},{6,5},{7,4},{8,11},{9,10},{10,... | collective-permute-start | bytes 49160 | tf_op jit(solution)/shard_map/ppermute | solution.py:404
  44.2 2.3 %collective-permute-start.20 = (bf16[64,128]{1,0:T(8,128)(2,1)S(1)}, bf16[64,128]{1,0:T(8,128)(2,1)S(1)}, u32[]{:S(2)}, u32[]{:S(2)}) collective-permute-start(bf16[64,128]{1,0:T(8,128)(2,1)S(1)} %get-tuple-element.31), channel_id=1, source_target_pairs={{0,1},{1,0},{2,3},{3,2},{4,5},{5,4},{6,7},{7,6},{8,9},{9,8},{10,11... | collective-permute-start | bytes 49160 | tf_op jit(solution)/shard_map/ppermute | solution.py:404
  46.5 1.3 %collective-permute-done.18.d = bf16[64,128]{1,0:T(8,128)(2,1)S(1)} collective-permute-done((bf16[64,128]{1,0:T(8,128)(2,1)S(1)}, bf16[64,128]{1,0:T(8,128)(2,1)S(1)}, u32[]{:S(2)}, u32[]{:S(2)}) %collective-permute-start.18) | collective-permute-done | bytes 16416 | tf_op jit(solution)/shard_map/ppermute | solution.py:404
  47.8 0.8 %collective-permute-done.19.c = bf16[64,128]{1,0:T(8,128)(2,1)S(1)} collective-permute-done((bf16[64,128]{1,0:T(8,128)(2,1)S(1)}, bf16[64,128]{1,0:T(8,128)(2,1)S(1)}, u32[]{:S(2)}, u32[]{:S(2)}) %collective-permute-start.19) | collective-permute-done | bytes 16416 | tf_op jit(solution)/shard_map/ppermute | solution.py:404
  (48 shorter events, 9.3 us)
Async XLA Ops:
  0.0 4.6 %collective-permute-start = (bf16[2,2,2048]{2,1,0:T(2,128)(2,1)}, bf16[2,2,2048]{2,1,0:T(2,128)(2,1)S(1)}, u32[]{:S(2)}, u32[]{:S(2)}) collective-permute-start(bf16[2,2,2048]{2,1,0:T(2,128)(2,1)} %hidden.1), channel_id=1, source_target_pairs={{0,12},{4,8},{8,4},{12,0},{1,13},{5,9},{9,5},{13,1},{2,14},{6,10},... | collective-permute-start | bytes 49160 | tf_op jit(solution)/shard_map/ppermute | solution.py:404
  2.4 3.9 %collective-permute-start.1 = (bf16[2,2,2048]{2,1,0:T(2,128)(2,1)}, bf16[2,2,2048]{2,1,0:T(2,128)(2,1)S(1)}, u32[]{:S(2)}, u32[]{:S(2)}) collective-permute-start(bf16[2,2,2048]{2,1,0:T(2,128)(2,1)} %hidden.1), channel_id=1, source_target_pairs={{0,8},{4,12},{8,0},{12,4},{1,9},{5,13},{9,1},{13,5},{2,10},{6,14},... | collective-permute-start | bytes 49160 | tf_op jit(solution)/shard_map/ppermute | solution.py:404
  3.0 3.3 %collective-permute-start.2 = (bf16[2,2,2048]{2,1,0:T(2,128)(2,1)}, bf16[2,2,2048]{2,1,0:T(2,128)(2,1)S(1)}, u32[]{:S(2)}, u32[]{:S(2)}) collective-permute-start(bf16[2,2,2048]{2,1,0:T(2,128)(2,1)} %hidden.1), channel_id=1, source_target_pairs={{0,4},{4,0},{8,12},{12,8},{1,5},{5,1},{9,13},{13,9},{2,6},{6,2},{1... | collective-permute-start | bytes 49160 | tf_op jit(solution)/shard_map/ppermute | solution.py:404
  6.3 20.9 %copy-start.2 = (bf16[2,384,1024]{2,1,0:T(8,128)(2,1)S(1)}, bf16[2,384,1024]{2,1,0:T(8,128)(2,1)}, u32[]{:S(2)}) copy-start(bf16[2,384,1024]{2,1,0:T(8,128)(2,1)} %keys.1) | copy-start | bytes 4718596
  6.3 20.9 %copy-start.3 = (bf16[2,384,1024]{2,1,0:T(8,128)(2,1)S(1)}, bf16[2,384,1024]{2,1,0:T(8,128)(2,1)}, u32[]{:S(2)}) copy-start(bf16[2,384,1024]{2,1,0:T(8,128)(2,1)} %values.1) | copy-start | bytes 4718596
  6.6 34.3 %copy-start.1 = (bf16[2048,2048]{1,0:T(8,128)(2,1)S(1)}, bf16[2048,2048]{1,0:T(8,128)(2,1)}, u32[]{:S(2)}) copy-start(bf16[2048,2048]{1,0:T(8,128)(2,1)} %w.3) | copy-start | bytes 25165828
  6.6 5.8 %collective-permute-start.3 = (bf16[2,2,2048]{2,1,0:T(2,128)(2,1)S(1)}, bf16[2,2,2048]{2,1,0:T(2,128)(2,1)S(1)}, u32[]{:S(2)}, u32[]{:S(2)}) collective-permute-start(bf16[2,2,2048]{2,1,0:T(2,128)(2,1)S(1)} %norm.1.n0), channel_id=1, source_target_pairs={{0,3},{1,2},{2,1},{3,0},{4,7},{5,6},{6,5},{7,4},{8,11},{9,10},{10,... | collective-permute-start | bytes 49160 | tf_op jit(solution)/shard_map/ppermute | solution.py:404
  10.3 4.6 %collective-permute-start.4 = (bf16[2,2,2048]{2,1,0:T(2,128)(2,1)S(1)}, bf16[2,2,2048]{2,1,0:T(2,128)(2,1)S(1)}, u32[]{:S(2)}, u32[]{:S(2)}) collective-permute-start(bf16[2,2,2048]{2,1,0:T(2,128)(2,1)S(1)} %norm.1.n0), channel_id=1, source_target_pairs={{0,2},{1,3},{2,0},{3,1},{4,6},{5,7},{6,4},{7,5},{8,10},{9,11},{10,... | collective-permute-start | bytes 49160 | tf_op jit(solution)/shard_map/ppermute | solution.py:404
  10.3 4.6 %collective-permute-start.5 = (bf16[2,2,2048]{2,1,0:T(2,128)(2,1)S(1)}, bf16[2,2,2048]{2,1,0:T(2,128)(2,1)S(1)}, u32[]{:S(2)}, u32[]{:S(2)}) collective-permute-start(bf16[2,2,2048]{2,1,0:T(2,128)(2,1)S(1)} %norm.1.n0), channel_id=1, source_target_pairs={{0,1},{1,0},{2,3},{3,2},{4,5},{5,4},{6,7},{7,6},{8,9},{9,8},{10,11... | collective-permute-start | bytes 49160 | tf_op jit(solution)/shard_map/ppermute | solution.py:404
  16.4 1.3 %collective-permute-start.6 = (f32[2,80,128]{2,1,0:T(8,128)S(1)}, f32[2,80,128]{2,1,0:T(8,128)S(1)}, u32[]{:S(2)}, u32[]{:S(2)}) collective-permute-start(f32[2,80,128]{2,1,0:T(8,128)S(1)} %get-tuple-element.22), channel_id=1, source_target_pairs={{0,4},{4,0},{8,12},{12,8},{1,5},{5,1},{9,13},{13,9},{2,6},{6,2},{1... | collective-permute-start | bytes 245768 | tf_op jit(solution)/shard_map/ppermute | solution.py:404
  17.8 6.9 %collective-permute-start.7 = (f32[80,128]{1,0:T(8,128)S(1)}, f32[80,128]{1,0:T(8,128)S(1)}, u32[]{:S(2)}, u32[]{:S(2)}) collective-permute-start(f32[80,128]{1,0:T(8,128)S(1)} %get-tuple-element.23), channel_id=1, source_target_pairs={{0,11},{1,10},{2,9},{3,8},{4,14},{5,15},{6,12},{7,13},{8,3},{9,2},... | collective-permute-start | bytes 122888 | tf_op jit(solution)/shard_map/ppermute | solution.py:420
  19.5 5.9 %collective-permute-start.8 = (f32[80,128]{1,0:T(8,128)S(1)}, f32[80,128]{1,0:T(8,128)S(1)}, u32[]{:S(2)}, u32[]{:S(2)}) collective-permute-start(f32[80,128]{1,0:T(8,128)S(1)} %get-tuple-element.23), channel_id=1, source_target_pairs={{0,3},{1,2},{2,1},{3,0},{4,6},{5,7},{6,4},{7,5},{8,11},{9,10},{10,... | collective-permute-start | bytes 122888 | tf_op jit(solution)/shard_map/ppermute | solution.py:420
  21.9 4.0 %collective-permute-start.9 = (f32[80,128]{1,0:T(8,128)S(1)}, f32[80,128]{1,0:T(8,128)S(1)}, u32[]{:S(2)}, u32[]{:S(2)}) collective-permute-start(f32[80,128]{1,0:T(8,128)S(1)} %get-tuple-element.24), channel_id=1, source_target_pairs={{0,8},{1,9},{2,10},{3,11},{4,13},{5,12},{6,15},{7,14},{8,0},{9,1},... | collective-permute-start | bytes 122888 | tf_op jit(solution)/shard_map/ppermute | solution.py:420
  23.1 2.8 %collective-permute-start.10 = (f32[80,128]{1,0:T(8,128)S(1)}, f32[80,128]{1,0:T(8,128)S(1)}, u32[]{:S(2)}, u32[]{:S(2)}) collective-permute-start(f32[80,128]{1,0:T(8,128)S(1)} %get-tuple-element.24), channel_id=1, source_target_pairs={{0,0},{1,1},{2,2},{3,3},{4,5},{5,4},{6,7},{7,6},{8,8},{9,9},{10,10... | collective-permute-start | bytes 122888 | tf_op jit(solution)/shard_map/ppermute | solution.py:420
  25.9 1.3 %collective-permute-start.11 = (bf16[2,80,128]{2,1,0:T(8,128)(2,1)S(1)}, bf16[2,80,128]{2,1,0:T(8,128)(2,1)S(1)}, u32[]{:S(2)}, u32[]{:S(2)}) collective-permute-start(bf16[2,80,128]{2,1,0:T(8,128)(2,1)S(1)} %round.1.near), channel_id=1, source_target_pairs={{0,4},{4,0},{8,12},{12,8},{1,5},{5,1},{9,13},{13,9},{2,6},{6,2},{1... | collective-permute-start | bytes 122888 | tf_op jit(solution)/shard_map/ppermute | solution.py:404
  28.7 1.3 %collective-permute-start.12 = (f32[2,72,128]{2,1,0:T(8,128)S(1)}, f32[2,72,128]{2,1,0:T(8,128)S(1)}, u32[]{:S(2)}, u32[]{:S(2)}) collective-permute-start(f32[2,72,128]{2,1,0:T(8,128)S(1)} %get-tuple-element.26), channel_id=1, source_target_pairs={{0,4},{4,0},{8,12},{12,8},{1,5},{5,1},{9,13},{13,9},{2,6},{6,2},{1... | collective-permute-start | bytes 221192 | tf_op jit(solution)/shard_map/ppermute | solution.py:404
  30.3 6.6 %collective-permute-start.13 = (bf16[80,128]{1,0:T(8,128)(2,1)S(1)}, bf16[80,128]{1,0:T(8,128)(2,1)S(1)}, u32[]{:S(2)}, u32[]{:S(2)}) collective-permute-start(bf16[80,128]{1,0:T(8,128)(2,1)S(1)} %get-tuple-element.27), channel_id=1, source_target_pairs={{0,11},{1,10},{2,9},{3,8},{4,14},{5,15},{6,12},{7,13},{8,3},{9,2},... | collective-permute-start | bytes 61448 | tf_op jit(solution)/shard_map/ppermute | solution.py:420
  33.5 5.6 %collective-permute-start.14 = (bf16[80,128]{1,0:T(8,128)(2,1)S(1)}, bf16[80,128]{1,0:T(8,128)(2,1)S(1)}, u32[]{:S(2)}, u32[]{:S(2)}) collective-permute-start(bf16[80,128]{1,0:T(8,128)(2,1)S(1)} %get-tuple-element.27), channel_id=1, source_target_pairs={{0,3},{1,2},{2,1},{3,0},{4,6},{5,7},{6,4},{7,5},{8,11},{9,10},{10,... | collective-permute-start | bytes 61448 | tf_op jit(solution)/shard_map/ppermute | solution.py:420
  34.8 4.3 %collective-permute-start.15 = (bf16[80,128]{1,0:T(8,128)(2,1)S(1)}, bf16[80,128]{1,0:T(8,128)(2,1)S(1)}, u32[]{:S(2)}, u32[]{:S(2)}) collective-permute-start(bf16[80,128]{1,0:T(8,128)(2,1)S(1)} %get-tuple-element.28), channel_id=1, source_target_pairs={{0,8},{1,9},{2,10},{3,11},{4,13},{5,12},{6,15},{7,14},{8,0},{9,1},... | collective-permute-start | bytes 61448 | tf_op jit(solution)/shard_map/ppermute | solution.py:420
  35.6 3.5 %collective-permute-start.16 = (bf16[80,128]{1,0:T(8,128)(2,1)S(1)}, bf16[80,128]{1,0:T(8,128)(2,1)S(1)}, u32[]{:S(2)}, u32[]{:S(2)}) collective-permute-start(bf16[80,128]{1,0:T(8,128)(2,1)S(1)} %get-tuple-element.28), channel_id=1, source_target_pairs={{0,0},{1,1},{2,2},{3,3},{4,5},{5,4},{6,7},{7,6},{8,8},{9,9},{10,10... | collective-permute-start | bytes 61448 | tf_op jit(solution)/shard_map/ppermute | solution.py:420
  39.3 1.5 %collective-permute-start.17 = (bf16[2,64,128]{2,1,0:T(8,128)(2,1)S(1)}, bf16[2,64,128]{2,1,0:T(8,128)(2,1)S(1)}, u32[]{:S(2)}, u32[]{:S(2)}) collective-permute-start(bf16[2,64,128]{2,1,0:T(8,128)(2,1)S(1)} %settle.1.near), channel_id=1, source_target_pairs={{0,4},{4,0},{8,12},{12,8},{1,5},{5,1},{9,13},{13,9},{2,6},{6,2},{1... | collective-permute-start | bytes 98312 | tf_op jit(solution)/shard_map/ppermute | solution.py:404
  42.1 5.7 %collective-permute-start.18 = (bf16[64,128]{1,0:T(8,128)(2,1)S(1)}, bf16[64,128]{1,0:T(8,128)(2,1)S(1)}, u32[]{:S(2)}, u32[]{:S(2)}) collective-permute-start(bf16[64,128]{1,0:T(8,128)(2,1)S(1)} %get-tuple-element.29), channel_id=1, source_target_pairs={{0,3},{1,2},{2,1},{3,0},{4,7},{5,6},{6,5},{7,4},{8,11},{9,10},{10,... | collective-permute-start | bytes 49160 | tf_op jit(solution)/shard_map/ppermute | solution.py:404
  43.9 4.6 %collective-permute-start.19 = (bf16[64,128]{1,0:T(8,128)(2,1)S(1)}, bf16[64,128]{1,0:T(8,128)(2,1)S(1)}, u32[]{:S(2)}, u32[]{:S(2)}) collective-permute-start(bf16[64,128]{1,0:T(8,128)(2,1)S(1)} %get-tuple-element.30), channel_id=1, source_target_pairs={{0,2},{1,3},{2,0},{3,1},{4,6},{5,7},{6,4},{7,5},{8,10},{9,11},{10,... | collective-permute-start | bytes 49160 | tf_op jit(solution)/shard_map/ppermute | solution.py:404
  44.2 4.3 %collective-permute-start.20 = (bf16[64,128]{1,0:T(8,128)(2,1)S(1)}, bf16[64,128]{1,0:T(8,128)(2,1)S(1)}, u32[]{:S(2)}, u32[]{:S(2)}) collective-permute-start(bf16[64,128]{1,0:T(8,128)(2,1)S(1)} %get-tuple-element.31), channel_id=1, source_target_pairs={{0,1},{1,0},{2,3},{3,2},{4,5},{5,4},{6,7},{7,6},{8,9},{9,8},{10,11... | collective-permute-start | bytes 49160 | tf_op jit(solution)/shard_map/ppermute | solution.py:404
  (4 other events, 43.8 us)

commit v10 on v9

--- a/solution.py
+++ b/solution.py
@@ -171,7 +171,8 @@
     return jnp.sum(wide * wide, axis=-1, keepdims=True)
 
 
-def square_kernel(hidden, out, held):
+def square_kernel(hidden, gain, out, held, wide_gain):
+    wide_gain[...] = gain[...].astype(F32)[None]
     held[...] = hidden[...]
     out[...] = jnp.zeros_like(out)
     for timeline in range(2):
@@ -180,12 +181,11 @@
 
 
 def norm_kernel(h3, h2, h1, h0, squares, gain, later, out):
-    wide_gain = gain[...].astype(F32)
     for timeline in range(2):
         total = squares[2 * timeline : 2 * timeline + 2, 0:1] + squares_of(h1, timeline)
         total += squares_of(h2, timeline) + squares_of(h3, timeline)
         scale = lax.rsqrt(total / D + EPSILON)
-        out[timeline] = (h0[timeline].astype(F32) * scale * wide_gain).astype(BF16)
+        out[timeline] = (h0[timeline].astype(F32) * scale * gain[...]).astype(BF16)
 
 
 def project_kernel(n3, n2, n1, n0, w, kept, sent, rows, sums):
@@ -195,9 +195,12 @@
             at = ROWS * shift + 2 * timeline
             rows[at : at + 2, :] = normed[timeline].astype(F32)
     left = rows[...].astype(BF16)
-    width = 1280
+    width = 512
+    deep = w.shape[0] // 2
     for step in range(w.shape[1] // width):
-        part = jnp.dot(left, w[:, width * step : width * (step + 1)], preferred_element_type=F32)
+        at = slice(width * step, width * (step + 1))
+        part = jnp.dot(left[:, :deep], w[:deep, at], preferred_element_type=F32)
+        part += jnp.dot(left[:, deep:], w[deep:, at], preferred_element_type=F32)
         for head in range(width // HD):
             at = (step * (width // HD) + head) * ROWS
             for shift in range(NY):
@@ -437,17 +440,17 @@
     lengths = jnp.broadcast_to(cache_len[:, None, None], (2, 2, HD))
 
     others = [partner(hidden, "gx", x) for x in (3, 2, 1)]
-    squares, held = call(
+    squares, held, wide_gain = call(
         square_kernel,
         "square",
-        [shape(8, HD, dtype=F32), shape(*hidden.shape)],
-        [pinned(hidden)],
+        [shape(8, HD, dtype=F32), shape(*hidden.shape), shape(1, features, dtype=F32)],
+        [pinned(hidden), pinned(norm_gain)],
     )
     normed = call(
         norm_kernel,
         "norm",
         shape(*hidden.shape),
-        [*others, held, squares, norm_gain[None]],
+        [*others, held, squares, wide_gain],
         later=[w_qkv],
     )
     half = shape(2, QKV_ROWS, HD, dtype=F32)

time: 49.5 us -> 49.5 us (level)
    broadcast_in_dim x1 -> x0, local copies, waits for them, and re-layouts: 0.69 us -> none  [small_body(): norm_gain[None]]
    unnamed x14 -> x16, local copies, waits for them, and re-layouts: 0.76 us -> 1.44 us
  transfers between devices with their start and end apart: 21 -> 21, of which waited for: 14 -> 14; matrix products, arithmetic and copies ran while one was open for 2% -> 1% of each run, Pallas kernels for 0% -> 0%
where the time goes in v10:
time: 49.5 us; the launch traced here: 49.2 us
  starting transfers between devices  25.1 us (51%)
  waiting for transfers between devices  16.6 us (34%)
  Pallas kernels  5.6 us (11%)
  local copies, waits for them, and re-layouts  1.51 us (3%)
    ppermute x13, starting transfers between devices, partner(): lax.ppermute(part, axis, [(k, k ^ distance) for k in range(lax.axis_size(...  13.1 us
    ppermute x8, starting transfers between devices, on_chips(): received[k, far_x] = lax.ppermute(parts[k], ('gx', 'gy'), pairs)  12 us
    ppermute x13, waiting for transfers between devices, partner(): lax.ppermute(part, axis, [(k, k ^ distance) for k in range(lax.axis_size(...  11.8 us
    pallas_call x10, Pallas kernels, call(): pl.pallas_call(kernel, in_specs=[VMEM_SPEC] * len(operands) + [HBM_SPEC]...  5.6 us
    ppermute x8, waiting for transfers between devices, on_chips(): received[k, far_x] = lax.ppermute(parts[k], ('gx', 'gy'), pairs)  4.79 us
    unnamed x16, local copies, waits for them, and re-layouts  1.44 us
  transfers between devices with their start and end apart: 21, of which 14 were waited for; matrix products, arithmetic and copies ran while one was open for 1% of the time, Pallas kernels for 0%

profile of v10, /device:TPU:0, one launch (start us, length us, event | category | flops | bytes accessed | tf_op | source)
XLA Modules:
  0.0 49.2 jit_solution(13612769930838195763)
XLA Ops:
  0.0 2.4 %collective-permute-start = (bf16[2,2,2048]{2,1,0:T(2,128)(2,1)}, bf16[2,2,2048]{2,1,0:T(2,128)(2,1)S(1)}, u32[]{:S(2)}, u32[]{:S(2)}) collective-permute-start(bf16[2,2,2048]{2,1,0:T(2,128)(2,1)} %hidden.1), channel_id=1, source_target_pairs={{0,12},{4,8},{8,4},{12,0},{1,13},{5,9},{9,5},{13,1},{2,14},{6,10},... | collective-permute-start | bytes 49160 | tf_op jit(solution)/shard_map/ppermute | solution.py:407
  4.6 1.7 %collective-permute-done.1.h2 = bf16[2,2,2048]{2,1,0:T(2,128)(2,1)S(1)} collective-permute-done((bf16[2,2,2048]{2,1,0:T(2,128)(2,1)}, bf16[2,2,2048]{2,1,0:T(2,128)(2,1)S(1)}, u32[]{:S(2)}, u32[]{:S(2)}) %collective-permute-start.1) | collective-permute-done | bytes 16416 | tf_op jit(solution)/shard_map/ppermute | solution.py:407
  6.6 3.7 %collective-permute-start.3 = (bf16[2,2,2048]{2,1,0:T(2,128)(2,1)S(1)}, bf16[2,2,2048]{2,1,0:T(2,128)(2,1)S(1)}, u32[]{:S(2)}, u32[]{:S(2)}) collective-permute-start(bf16[2,2,2048]{2,1,0:T(2,128)(2,1)S(1)} %norm.1.n0), channel_id=1, source_target_pairs={{0,3},{1,2},{2,1},{3,0},{4,7},{5,6},{6,5},{7,4},{8,11},{9,10},{10,... | collective-permute-start | bytes 49160 | tf_op jit(solution)/shard_map/ppermute | solution.py:407
  10.3 0.8 %collective-permute-start.5 = (bf16[2,2,2048]{2,1,0:T(2,128)(2,1)S(1)}, bf16[2,2,2048]{2,1,0:T(2,128)(2,1)S(1)}, u32[]{:S(2)}, u32[]{:S(2)}) collective-permute-start(bf16[2,2,2048]{2,1,0:T(2,128)(2,1)S(1)} %norm.1.n0), channel_id=1, source_target_pairs={{0,1},{1,0},{2,3},{3,2},{4,5},{5,4},{6,7},{7,6},{8,9},{9,8},{10,11... | collective-permute-start | bytes 49160 | tf_op jit(solution)/shard_map/ppermute | solution.py:407
  11.1 1.3 %collective-permute-done.3.n3 = bf16[2,2,2048]{2,1,0:T(2,128)(2,1)S(1)} collective-permute-done((bf16[2,2,2048]{2,1,0:T(2,128)(2,1)S(1)}, bf16[2,2,2048]{2,1,0:T(2,128)(2,1)S(1)}, u32[]{:S(2)}, u32[]{:S(2)}) %collective-permute-start.3) | collective-permute-done | bytes 16416 | tf_op jit(solution)/shard_map/ppermute | solution.py:407
  12.4 2.5 %collective-permute-done.4.n2 = bf16[2,2,2048]{2,1,0:T(2,128)(2,1)S(1)} collective-permute-done((bf16[2,2,2048]{2,1,0:T(2,128)(2,1)S(1)}, bf16[2,2,2048]{2,1,0:T(2,128)(2,1)S(1)}, u32[]{:S(2)}, u32[]{:S(2)}) %collective-permute-start.4) | collective-permute-done | bytes 16416 | tf_op jit(solution)/shard_map/ppermute | solution.py:407
  14.9 1.5 %project.1 = (f32[2,80,128]{2,1,0:T(8,128)S(1)}, f32[2,80,128]{2,1,0:T(8,128)S(1)}) custom-call(bf16[2,2,2048]{2,1,0:T(2,128)(2,1)S(1)} %collective-permute-done.3.n3, bf16[2,2,2048]{2,1,0:T(2,128)(2,1)S(1)} %collective-permute-done.4.n2, bf16[2,2,2048]{2,1,0:T(2,128)(2,1)S(1)} %collective-permute-done.5.n1, bf16[2,2,2048]{2,1,0:T(2,128)(2,1)S(1)} %norm.1.n0, ...), custom_call_target="tpu_custom_call" | custom-call | tf_op jit(solution)/shard_map/project/pallas_call | solution.py:153
  16.5 1.2 %collective-permute-done.6.b = f32[2,80,128]{2,1,0:T(8,128)S(1)} collective-permute-done((f32[2,80,128]{2,1,0:T(8,128)S(1)}, f32[2,80,128]{2,1,0:T(8,128)S(1)}, u32[]{:S(2)}, u32[]{:S(2)}) %collective-permute-start.6) | collective-permute-done | bytes 81952 | tf_op jit(solution)/shard_map/ppermute | solution.py:407
  17.8 1.7 %collective-permute-start.7 = (f32[80,128]{1,0:T(8,128)S(1)}, f32[80,128]{1,0:T(8,128)S(1)}, u32[]{:S(2)}, u32[]{:S(2)}) collective-permute-start(f32[80,128]{1,0:T(8,128)S(1)} %get-tuple-element.25), channel_id=1, source_target_pairs={{0,11},{1,10},{2,9},{3,8},{4,14},{5,15},{6,12},{7,13},{8,3},{9,2},... | collective-permute-start | bytes 122888 | tf_op jit(solution)/shard_map/ppermute | solution.py:423
  19.5 2.4 %collective-permute-start.8 = (f32[80,128]{1,0:T(8,128)S(1)}, f32[80,128]{1,0:T(8,128)S(1)}, u32[]{:S(2)}, u32[]{:S(2)}) collective-permute-start(f32[80,128]{1,0:T(8,128)S(1)} %get-tuple-element.25), channel_id=1, source_target_pairs={{0,3},{1,2},{2,1},{3,0},{4,6},{5,7},{6,4},{7,5},{8,11},{9,10},{10,... | collective-permute-start | bytes 122888 | tf_op jit(solution)/shard_map/ppermute | solution.py:423
  21.9 1.3 %collective-permute-start.9 = (f32[80,128]{1,0:T(8,128)S(1)}, f32[80,128]{1,0:T(8,128)S(1)}, u32[]{:S(2)}, u32[]{:S(2)}) collective-permute-start(f32[80,128]{1,0:T(8,128)S(1)} %get-tuple-element.26), channel_id=1, source_target_pairs={{0,8},{1,9},{2,10},{3,11},{4,13},{5,12},{6,15},{7,14},{8,0},{9,1},... | collective-permute-start | bytes 122888 | tf_op jit(solution)/shard_map/ppermute | solution.py:423
  26.2 1.0 %collective-permute-done.11.far = bf16[2,80,128]{2,1,0:T(8,128)(2,1)S(1)} collective-permute-done((bf16[2,80,128]{2,1,0:T(8,128)(2,1)S(1)}, bf16[2,80,128]{2,1,0:T(8,128)(2,1)S(1)}, u32[]{:S(2)}, u32[]{:S(2)}) %collective-permute-start.11) | collective-permute-done | bytes 40992 | tf_op jit(solution)/shard_map/ppermute | solution.py:407
  27.3 1.4 %attend.1 = (f32[2,72,128]{2,1,0:T(8,128)S(1)}, f32[2,72,128]{2,1,0:T(8,128)S(1)}) custom-call(bf16[2,80,128]{2,1,0:T(8,128)(2,1)S(1)} %round.1.near, bf16[2,80,128]{2,1,0:T(8,128)(2,1)S(1)} %collective-permute-done.11.far, f32[2,2,128]{2,1,0:T(2,128)S(1)} %get-tuple-element.38.cosine, f32[2,2,128]{2,1,0:T(2,128)S(1)} %get-tuple-element.39.sine, ...), custom_call_target="tpu_custom_call" | custom-call | tf_op jit(solution)/shard_map/attend/pallas_call | solution.py:153
  28.9 1.1 %collective-permute-done.12.b = f32[2,72,128]{2,1,0:T(8,128)S(1)} collective-permute-done((f32[2,72,128]{2,1,0:T(8,128)S(1)}, f32[2,72,128]{2,1,0:T(8,128)S(1)}, u32[]{:S(2)}, u32[]{:S(2)}) %collective-permute-start.12) | collective-permute-done | bytes 73760 | tf_op jit(solution)/shard_map/ppermute | solution.py:407
  30.2 3.3 %collective-permute-start.13 = (bf16[80,128]{1,0:T(8,128)(2,1)S(1)}, bf16[80,128]{1,0:T(8,128)(2,1)S(1)}, u32[]{:S(2)}, u32[]{:S(2)}) collective-permute-start(bf16[80,128]{1,0:T(8,128)(2,1)S(1)} %get-tuple-element.29), channel_id=1, source_target_pairs={{0,11},{1,10},{2,9},{3,8},{4,14},{5,15},{6,12},{7,13},{8,3},{9,2},... | collective-permute-start | bytes 61448 | tf_op jit(solution)/shard_map/ppermute | solution.py:423
  33.5 1.3 %collective-permute-start.14 = (bf16[80,128]{1,0:T(8,128)(2,1)S(1)}, bf16[80,128]{1,0:T(8,128)(2,1)S(1)}, u32[]{:S(2)}, u32[]{:S(2)}) collective-permute-start(bf16[80,128]{1,0:T(8,128)(2,1)S(1)} %get-tuple-element.29), channel_id=1, source_target_pairs={{0,3},{1,2},{2,1},{3,0},{4,6},{5,7},{6,4},{7,5},{8,11},{9,10},{10,... | collective-permute-start | bytes 61448 | tf_op jit(solution)/shard_map/ppermute | solution.py:423
  34.8 0.8 %collective-permute-start.15 = (bf16[80,128]{1,0:T(8,128)(2,1)S(1)}, bf16[80,128]{1,0:T(8,128)(2,1)S(1)}, u32[]{:S(2)}, u32[]{:S(2)}) collective-permute-start(bf16[80,128]{1,0:T(8,128)(2,1)S(1)} %get-tuple-element.30), channel_id=1, source_target_pairs={{0,8},{1,9},{2,10},{3,11},{4,13},{5,12},{6,15},{7,14},{8,0},{9,1},... | collective-permute-start | bytes 61448 | tf_op jit(solution)/shard_map/ppermute | solution.py:423
  36.8 2.3 %collective-permute-done.14.a1 = bf16[80,128]{1,0:T(8,128)(2,1)S(1)} collective-permute-done((bf16[80,128]{1,0:T(8,128)(2,1)S(1)}, bf16[80,128]{1,0:T(8,128)(2,1)S(1)}, u32[]{:S(2)}, u32[]{:S(2)}) %collective-permute-start.14) | collective-permute-done | bytes 20512 | tf_op jit(solution)/shard_map/ppermute | solution.py:423
  40.0 0.9 %collective-permute-done.17.far = bf16[2,64,128]{2,1,0:T(8,128)(2,1)S(1)} collective-permute-done((bf16[2,64,128]{2,1,0:T(8,128)(2,1)S(1)}, bf16[2,64,128]{2,1,0:T(8,128)(2,1)S(1)}, u32[]{:S(2)}, u32[]{:S(2)}) %collective-permute-start.17) | collective-permute-done | bytes 32800 | tf_op jit(solution)/shard_map/ppermute | solution.py:407
  40.8 1.2 %output.1 = (f32[64,128]{1,0:T(8,128)S(1)}, bf16[64,128]{1,0:T(8,128)(2,1)S(1)}, bf16[64,128]{1,0:T(8,128)(2,1)S(1)}, bf16[64,128]{1,0:T(8,128)(2,1)S(1)}) custom-call(bf16[2,64,128]{2,1,0:T(8,128)(2,1)S(1)} %settle.1.near, bf16[2,64,128]{2,1,0:T(8,128)(2,1)S(1)} %collective-permute-done.17.far, bf16[2048,2048]{1,0:T(8,128)(2,1)S(1)} %copy-done.1), custom_call_target="tpu_custom_call" | custom-call | tf_op jit(solution)/shard_map/output/pallas_call | solution.py:153
  42.1 1.9 %collective-permute-start.18 = (bf16[64,128]{1,0:T(8,128)(2,1)S(1)}, bf16[64,128]{1,0:T(8,128)(2,1)S(1)}, u32[]{:S(2)}, u32[]{:S(2)}) collective-permute-start(bf16[64,128]{1,0:T(8,128)(2,1)S(1)} %get-tuple-element.31), channel_id=1, source_target_pairs={{0,3},{1,2},{2,1},{3,0},{4,7},{5,6},{6,5},{7,4},{8,11},{9,10},{10,... | collective-permute-start | bytes 49160 | tf_op jit(solution)/shard_map/ppermute | solution.py:407
  44.2 2.3 %collective-permute-start.20 = (bf16[64,128]{1,0:T(8,128)(2,1)S(1)}, bf16[64,128]{1,0:T(8,128)(2,1)S(1)}, u32[]{:S(2)}, u32[]{:S(2)}) collective-permute-start(bf16[64,128]{1,0:T(8,128)(2,1)S(1)} %get-tuple-element.33), channel_id=1, source_target_pairs={{0,1},{1,0},{2,3},{3,2},{4,5},{5,4},{6,7},{7,6},{8,9},{9,8},{10,11... | collective-permute-start | bytes 49160 | tf_op jit(solution)/shard_map/ppermute | solution.py:407
  46.5 1.3 %collective-permute-done.18.d = bf16[64,128]{1,0:T(8,128)(2,1)S(1)} collective-permute-done((bf16[64,128]{1,0:T(8,128)(2,1)S(1)}, bf16[64,128]{1,0:T(8,128)(2,1)S(1)}, u32[]{:S(2)}, u32[]{:S(2)}) %collective-permute-start.18) | collective-permute-done | bytes 16416 | tf_op jit(solution)/shard_map/ppermute | solution.py:407
  47.8 0.8 %collective-permute-done.19.c = bf16[64,128]{1,0:T(8,128)(2,1)S(1)} collective-permute-done((bf16[64,128]{1,0:T(8,128)(2,1)S(1)}, bf16[64,128]{1,0:T(8,128)(2,1)S(1)}, u32[]{:S(2)}, u32[]{:S(2)}) %collective-permute-start.19) | collective-permute-done | bytes 16416 | tf_op jit(solution)/shard_map/ppermute | solution.py:407
  (49 shorter events, 9.2 us)
Async XLA Ops:
  0.0 4.6 %collective-permute-start = (bf16[2,2,2048]{2,1,0:T(2,128)(2,1)}, bf16[2,2,2048]{2,1,0:T(2,128)(2,1)S(1)}, u32[]{:S(2)}, u32[]{:S(2)}) collective-permute-start(bf16[2,2,2048]{2,1,0:T(2,128)(2,1)} %hidden.1), channel_id=1, source_target_pairs={{0,12},{4,8},{8,4},{12,0},{1,13},{5,9},{9,5},{13,1},{2,14},{6,10},... | collective-permute-start | bytes 49160 | tf_op jit(solution)/shard_map/ppermute | solution.py:407
  2.4 3.9 %collective-permute-start.1 = (bf16[2,2,2048]{2,1,0:T(2,128)(2,1)}, bf16[2,2,2048]{2,1,0:T(2,128)(2,1)S(1)}, u32[]{:S(2)}, u32[]{:S(2)}) collective-permute-start(bf16[2,2,2048]{2,1,0:T(2,128)(2,1)} %hidden.1), channel_id=1, source_target_pairs={{0,8},{4,12},{8,0},{12,4},{1,9},{5,13},{9,1},{13,5},{2,10},{6,14},... | collective-permute-start | bytes 49160 | tf_op jit(solution)/shard_map/ppermute | solution.py:407
  3.0 3.3 %collective-permute-start.2 = (bf16[2,2,2048]{2,1,0:T(2,128)(2,1)}, bf16[2,2,2048]{2,1,0:T(2,128)(2,1)S(1)}, u32[]{:S(2)}, u32[]{:S(2)}) collective-permute-start(bf16[2,2,2048]{2,1,0:T(2,128)(2,1)} %hidden.1), channel_id=1, source_target_pairs={{0,4},{4,0},{8,12},{12,8},{1,5},{5,1},{9,13},{13,9},{2,6},{6,2},{1... | collective-permute-start | bytes 49160 | tf_op jit(solution)/shard_map/ppermute | solution.py:407
  6.3 20.9 %copy-start.2 = (bf16[2,384,1024]{2,1,0:T(8,128)(2,1)S(1)}, bf16[2,384,1024]{2,1,0:T(8,128)(2,1)}, u32[]{:S(2)}) copy-start(bf16[2,384,1024]{2,1,0:T(8,128)(2,1)} %keys.1) | copy-start | bytes 4718596
  6.3 20.9 %copy-start.3 = (bf16[2,384,1024]{2,1,0:T(8,128)(2,1)S(1)}, bf16[2,384,1024]{2,1,0:T(8,128)(2,1)}, u32[]{:S(2)}) copy-start(bf16[2,384,1024]{2,1,0:T(8,128)(2,1)} %values.1) | copy-start | bytes 4718596
  6.6 34.3 %copy-start.1 = (bf16[2048,2048]{1,0:T(8,128)(2,1)S(1)}, bf16[2048,2048]{1,0:T(8,128)(2,1)}, u32[]{:S(2)}) copy-start(bf16[2048,2048]{1,0:T(8,128)(2,1)} %w.3) | copy-start | bytes 25165828
  6.6 5.8 %collective-permute-start.3 = (bf16[2,2,2048]{2,1,0:T(2,128)(2,1)S(1)}, bf16[2,2,2048]{2,1,0:T(2,128)(2,1)S(1)}, u32[]{:S(2)}, u32[]{:S(2)}) collective-permute-start(bf16[2,2,2048]{2,1,0:T(2,128)(2,1)S(1)} %norm.1.n0), channel_id=1, source_target_pairs={{0,3},{1,2},{2,1},{3,0},{4,7},{5,6},{6,5},{7,4},{8,11},{9,10},{10,... | collective-permute-start | bytes 49160 | tf_op jit(solution)/shard_map/ppermute | solution.py:407
  10.3 4.6 %collective-permute-start.4 = (bf16[2,2,2048]{2,1,0:T(2,128)(2,1)S(1)}, bf16[2,2,2048]{2,1,0:T(2,128)(2,1)S(1)}, u32[]{:S(2)}, u32[]{:S(2)}) collective-permute-start(bf16[2,2,2048]{2,1,0:T(2,128)(2,1)S(1)} %norm.1.n0), channel_id=1, source_target_pairs={{0,2},{1,3},{2,0},{3,1},{4,6},{5,7},{6,4},{7,5},{8,10},{9,11},{10,... | collective-permute-start | bytes 49160 | tf_op jit(solution)/shard_map/ppermute | solution.py:407
  10.3 4.6 %collective-permute-start.5 = (bf16[2,2,2048]{2,1,0:T(2,128)(2,1)S(1)}, bf16[2,2,2048]{2,1,0:T(2,128)(2,1)S(1)}, u32[]{:S(2)}, u32[]{:S(2)}) collective-permute-start(bf16[2,2,2048]{2,1,0:T(2,128)(2,1)S(1)} %norm.1.n0), channel_id=1, source_target_pairs={{0,1},{1,0},{2,3},{3,2},{4,5},{5,4},{6,7},{7,6},{8,9},{9,8},{10,11... | collective-permute-start | bytes 49160 | tf_op jit(solution)/shard_map/ppermute | solution.py:407
  16.4 1.3 %collective-permute-start.6 = (f32[2,80,128]{2,1,0:T(8,128)S(1)}, f32[2,80,128]{2,1,0:T(8,128)S(1)}, u32[]{:S(2)}, u32[]{:S(2)}) collective-permute-start(f32[2,80,128]{2,1,0:T(8,128)S(1)} %get-tuple-element.24), channel_id=1, source_target_pairs={{0,4},{4,0},{8,12},{12,8},{1,5},{5,1},{9,13},{13,9},{2,6},{6,2},{1... | collective-permute-start | bytes 245768 | tf_op jit(solution)/shard_map/ppermute | solution.py:407
  17.8 6.9 %collective-permute-start.7 = (f32[80,128]{1,0:T(8,128)S(1)}, f32[80,128]{1,0:T(8,128)S(1)}, u32[]{:S(2)}, u32[]{:S(2)}) collective-permute-start(f32[80,128]{1,0:T(8,128)S(1)} %get-tuple-element.25), channel_id=1, source_target_pairs={{0,11},{1,10},{2,9},{3,8},{4,14},{5,15},{6,12},{7,13},{8,3},{9,2},... | collective-permute-start | bytes 122888 | tf_op jit(solution)/shard_map/ppermute | solution.py:423
  19.5 5.8 %collective-permute-start.8 = (f32[80,128]{1,0:T(8,128)S(1)}, f32[80,128]{1,0:T(8,128)S(1)}, u32[]{:S(2)}, u32[]{:S(2)}) collective-permute-start(f32[80,128]{1,0:T(8,128)S(1)} %get-tuple-element.25), channel_id=1, source_target_pairs={{0,3},{1,2},{2,1},{3,0},{4,6},{5,7},{6,4},{7,5},{8,11},{9,10},{10,... | collective-permute-start | bytes 122888 | tf_op jit(solution)/shard_map/ppermute | solution.py:423
  21.9 4.0 %collective-permute-start.9 = (f32[80,128]{1,0:T(8,128)S(1)}, f32[80,128]{1,0:T(8,128)S(1)}, u32[]{:S(2)}, u32[]{:S(2)}) collective-permute-start(f32[80,128]{1,0:T(8,128)S(1)} %get-tuple-element.26), channel_id=1, source_target_pairs={{0,8},{1,9},{2,10},{3,11},{4,13},{5,12},{6,15},{7,14},{8,0},{9,1},... | collective-permute-start | bytes 122888 | tf_op jit(solution)/shard_map/ppermute | solution.py:423
  23.1 2.8 %collective-permute-start.10 = (f32[80,128]{1,0:T(8,128)S(1)}, f32[80,128]{1,0:T(8,128)S(1)}, u32[]{:S(2)}, u32[]{:S(2)}) collective-permute-start(f32[80,128]{1,0:T(8,128)S(1)} %get-tuple-element.26), channel_id=1, source_target_pairs={{0,0},{1,1},{2,2},{3,3},{4,5},{5,4},{6,7},{7,6},{8,8},{9,9},{10,10... | collective-permute-start | bytes 122888 | tf_op jit(solution)/shard_map/ppermute | solution.py:423
  25.9 1.3 %collective-permute-start.11 = (bf16[2,80,128]{2,1,0:T(8,128)(2,1)S(1)}, bf16[2,80,128]{2,1,0:T(8,128)(2,1)S(1)}, u32[]{:S(2)}, u32[]{:S(2)}) collective-permute-start(bf16[2,80,128]{2,1,0:T(8,128)(2,1)S(1)} %round.1.near), channel_id=1, source_target_pairs={{0,4},{4,0},{8,12},{12,8},{1,5},{5,1},{9,13},{13,9},{2,6},{6,2},{1... | collective-permute-start | bytes 122888 | tf_op jit(solution)/shard_map/ppermute | solution.py:407
  28.7 1.3 %collective-permute-start.12 = (f32[2,72,128]{2,1,0:T(8,128)S(1)}, f32[2,72,128]{2,1,0:T(8,128)S(1)}, u32[]{:S(2)}, u32[]{:S(2)}) collective-permute-start(f32[2,72,128]{2,1,0:T(8,128)S(1)} %get-tuple-element.28), channel_id=1, source_target_pairs={{0,4},{4,0},{8,12},{12,8},{1,5},{5,1},{9,13},{13,9},{2,6},{6,2},{1... | collective-permute-start | bytes 221192 | tf_op jit(solution)/shard_map/ppermute | solution.py:407
  30.2 6.6 %collective-permute-start.13 = (bf16[80,128]{1,0:T(8,128)(2,1)S(1)}, bf16[80,128]{1,0:T(8,128)(2,1)S(1)}, u32[]{:S(2)}, u32[]{:S(2)}) collective-permute-start(bf16[80,128]{1,0:T(8,128)(2,1)S(1)} %get-tuple-element.29), channel_id=1, source_target_pairs={{0,11},{1,10},{2,9},{3,8},{4,14},{5,15},{6,12},{7,13},{8,3},{9,2},... | collective-permute-start | bytes 61448 | tf_op jit(solution)/shard_map/ppermute | solution.py:423
  33.5 5.6 %collective-permute-start.14 = (bf16[80,128]{1,0:T(8,128)(2,1)S(1)}, bf16[80,128]{1,0:T(8,128)(2,1)S(1)}, u32[]{:S(2)}, u32[]{:S(2)}) collective-permute-start(bf16[80,128]{1,0:T(8,128)(2,1)S(1)} %get-tuple-element.29), channel_id=1, source_target_pairs={{0,3},{1,2},{2,1},{3,0},{4,6},{5,7},{6,4},{7,5},{8,11},{9,10},{10,... | collective-permute-start | bytes 61448 | tf_op jit(solution)/shard_map/ppermute | solution.py:423
  34.8 4.3 %collective-permute-start.15 = (bf16[80,128]{1,0:T(8,128)(2,1)S(1)}, bf16[80,128]{1,0:T(8,128)(2,1)S(1)}, u32[]{:S(2)}, u32[]{:S(2)}) collective-permute-start(bf16[80,128]{1,0:T(8,128)(2,1)S(1)} %get-tuple-element.30), channel_id=1, source_target_pairs={{0,8},{1,9},{2,10},{3,11},{4,13},{5,12},{6,15},{7,14},{8,0},{9,1},... | collective-permute-start | bytes 61448 | tf_op jit(solution)/shard_map/ppermute | solution.py:423
  35.6 3.5 %collective-permute-start.16 = (bf16[80,128]{1,0:T(8,128)(2,1)S(1)}, bf16[80,128]{1,0:T(8,128)(2,1)S(1)}, u32[]{:S(2)}, u32[]{:S(2)}) collective-permute-start(bf16[80,128]{1,0:T(8,128)(2,1)S(1)} %get-tuple-element.30), channel_id=1, source_target_pairs={{0,0},{1,1},{2,2},{3,3},{4,5},{5,4},{6,7},{7,6},{8,8},{9,9},{10,10... | collective-permute-start | bytes 61448 | tf_op jit(solution)/shard_map/ppermute | solution.py:423
  39.3 1.5 %collective-permute-start.17 = (bf16[2,64,128]{2,1,0:T(8,128)(2,1)S(1)}, bf16[2,64,128]{2,1,0:T(8,128)(2,1)S(1)}, u32[]{:S(2)}, u32[]{:S(2)}) collective-permute-start(bf16[2,64,128]{2,1,0:T(8,128)(2,1)S(1)} %settle.1.near), channel_id=1, source_target_pairs={{0,4},{4,0},{8,12},{12,8},{1,5},{5,1},{9,13},{13,9},{2,6},{6,2},{1... | collective-permute-start | bytes 98312 | tf_op jit(solution)/shard_map/ppermute | solution.py:407
  42.1 5.7 %collective-permute-start.18 = (bf16[64,128]{1,0:T(8,128)(2,1)S(1)}, bf16[64,128]{1,0:T(8,128)(2,1)S(1)}, u32[]{:S(2)}, u32[]{:S(2)}) collective-permute-start(bf16[64,128]{1,0:T(8,128)(2,1)S(1)} %get-tuple-element.31), channel_id=1, source_target_pairs={{0,3},{1,2},{2,1},{3,0},{4,7},{5,6},{6,5},{7,4},{8,11},{9,10},{10,... | collective-permute-start | bytes 49160 | tf_op jit(solution)/shard_map/ppermute | solution.py:407
  43.9 4.6 %collective-permute-start.19 = (bf16[64,128]{1,0:T(8,128)(2,1)S(1)}, bf16[64,128]{1,0:T(8,128)(2,1)S(1)}, u32[]{:S(2)}, u32[]{:S(2)}) collective-permute-start(bf16[64,128]{1,0:T(8,128)(2,1)S(1)} %get-tuple-element.32), channel_id=1, source_target_pairs={{0,2},{1,3},{2,0},{3,1},{4,6},{5,7},{6,4},{7,5},{8,10},{9,11},{10,... | collective-permute-start | bytes 49160 | tf_op jit(solution)/shard_map/ppermute | solution.py:407
  44.2 4.3 %collective-permute-start.20 = (bf16[64,128]{1,0:T(8,128)(2,1)S(1)}, bf16[64,128]{1,0:T(8,128)(2,1)S(1)}, u32[]{:S(2)}, u32[]{:S(2)}) collective-permute-start(bf16[64,128]{1,0:T(8,128)(2,1)S(1)} %get-tuple-element.33), channel_id=1, source_target_pairs={{0,1},{1,0},{2,3},{3,2},{4,5},{5,4},{6,7},{7,6},{8,9},{9,8},{10,11... | collective-permute-start | bytes 49160 | tf_op jit(solution)/shard_map/ppermute | solution.py:407
  (5 other events, 43.8 us)
